TPU v7x, 256 devices: a whole 4x4x8 slice. The times are simulated.
256 devices in a mesh: ctx: 32 (over y, z_lo, core), tp: 8 (over x, z_hi).
Axes of the slice: x: 4, y: 4, z: 8 (z_hi: 2, z_lo: 4; z = z_hi * 4 + z_lo), core: 2. Of those that a mesh axis runs over, the one named last changes fastest.
Arguments:
- inputs: bfloat16 [16384, 1024], P('ctx', 'tp'), may hold values from -0.09375 to 0.09375
- grad_out: bfloat16 [16384, 1024], P('ctx', 'tp'), may hold values from -6 to 6
- filters: bfloat16 [12, 4096], replicated, may hold values from -0.09375 to 0.09375
- projection: bfloat16 [1024, 12, 1024], P(None, None, 'tp'), may hold values from -0.078125 to 0.078125
Outputs:
- grad_input: bfloat16 [16384, 1024], P('ctx', 'tp')
- grad_proj: float32 [1024, 12, 1024], P('ctx', None, 'tp')
All inputs are finite; a program needn't handle non-finite values.
Results may differ from a plain program's by a relative error of at most 0.0049.
Values may be sent and summed in bfloat16 or wider, within the bound.
No kernel may reach another device: no remote copies, remote signals or barrier semaphores. Data moves between devices by JAX's collectives and lax.ppermute only.
A program may use at most 128 MiB of HBM per device.

v0:
```python
import jax
import jax.numpy as jnp
from jax import lax
from jax.sharding import PartitionSpec as P


def passed_along(value, axis, steps):
    count = lax.axis_size(axis)
    first, last = (max(0, -steps), min(count, count - steps))
    return lax.ppermute(value, axis, [(source, source + steps) for source in range(first, last)])


def lag_table(padded, lag_index, tok_rows):
    segment = lax.dynamic_slice_in_dim(padded, lag_index * tok_rows, 2 * tok_rows, 1)
    rotated = jnp.concatenate([segment[:, tok_rows:], segment[:, :tok_rows]], axis=1)
    filt_count = rotated.shape[0]
    repeated = jnp.broadcast_to(rotated[:, None, :], (filt_count, tok_rows, 2 * tok_rows))
    repeated = repeated.reshape(filt_count, 2 * tok_rows * tok_rows)
    trimmed = repeated[:, : tok_rows * (2 * tok_rows - 1)].reshape(
        filt_count, tok_rows, 2 * tok_rows - 1
    )
    return trimmed[:, :, :tok_rows]


def lag_term(padded, lag_index, grad_block, tok_rows):
    return jnp.einsum(
        "kab,bc->kac",
        lag_table(padded, lag_index, tok_rows),
        grad_block,
        preferred_element_type=jnp.float32,
    )


def per_device(inputs, grad_out, filters, projection):
    tok_rows = grad_out.shape[0]
    filt_count = filters.shape[0]
    lag_reach = filters.shape[1] // tok_rows
    zero_edge = jnp.zeros((filt_count, tok_rows), filters.dtype)
    padded = jnp.concatenate([zero_edge, filters, zero_edge], axis=1)

    def follow(lag_index, carried):
        running, current = carried
        current = passed_along(current, "ctx", -1)
        return (running + lag_term(padded, lag_index, current, tok_rows), current)

    first_term = lag_term(padded, 0, grad_out, tok_rows)
    running, current = lax.fori_loop(1, lag_reach + 1, follow, (first_term, grad_out))
    correlated = running.astype(jnp.bfloat16)
    input_share = lax.psum_scatter(
        jnp.einsum("ikc,ktc->it", projection, correlated, preferred_element_type=jnp.float32),
        "tp",
        scatter_dimension=0,
        tiled=True,
    )
    grad_input = input_share.T.astype(jnp.bfloat16)
    full_inputs = lax.all_gather(inputs, "tp", axis=1, tiled=True)
    grad_proj = lax.psum_scatter(
        jnp.einsum("ti,ktc->ikc", full_inputs, correlated, preferred_element_type=jnp.float32),
        "ctx",
        scatter_dimension=0,
        tiled=True,
    )
    return (grad_input, grad_proj)


def solution(mesh):
    return jax.shard_map(
        per_device,
        mesh=mesh,
        in_specs=(P("ctx", "tp"), P("ctx", "tp"), P(), P(None, None, "tp")),
        out_specs=(P("ctx", "tp"), P("ctx", None, "tp")),
        check_vma=False,
    )
```

profile of v0, /device:TPU:2, one launch (start us, length us, event | category | flops | bytes accessed | tf_op | source)
XLA Modules:
  0.0 1141.9 jit_solution(5958274989680195779)
XLA Ops:
  7.2 1.7 copy.26
  9.8 6.1 broadcast_in_dim.25
  15.9 5.8 pad.8
  21.7 29.2 %copy.13 = bf16[2,8,512,1024]{3,1,2,0:T(8,128)(2,1)S(1)} copy(bf16[2,8,512,1024]{3,2,1,0:T(8,128)(2,1)S(1)} %bitcast.32) | data formatting | bytes 33554432
  50.9 6.5 slice.48
  57.5 36.0 %reshape.27 = bf16[12,512,1023]{2,1,0:T(8,128)(2,1)} reshape(bf16[12,523776]{1,0:T(8,128)(2,1)} %slice.48) | data formatting | bytes 25141248 | tf_op jit(solution)/shard_map/reshape | solution.py:19
  93.5 6.3 fusion.6
  99.8 758.6 %while.15 = (s32[]{:T(128)}, f32[12,512,128]{2,1,0:T(8,128)}, bf16[512,128]{1,0:T(8,128)(2,1)}, bf16[12,5120]{1,0:T(8,128)(2,1)S(1)}, s32[]{:T(128)}, /*index=5*...) while((s32[]{:T(128)}, f32[12,512,128]{2,1,0:T(8,128)}, bf16[512,128]{1,0:T(8,128)(2,1)}, ...), condition=%wide.region_1.0_spmd, body=%wide.region_0.0_spmd.sunk | while | flops 806141952 | bytes 139403488 | solution.py:47
  116.1 1.3 collective-permute-start
  117.4 6.1 broadcast_in_dim.28
  123.5 5.8 pad.19
  129.3 29.2 %copy.15 = bf16[2,8,512,1024]{3,1,2,0:T(8,128)(2,1)S(1)} copy(bf16[2,8,512,1024]{3,2,1,0:T(8,128)(2,1)S(1)} %bitcast.30) | data formatting | bytes 33554432 | tf_op jit(solution)/shard_map/while
  158.5 6.5 slice.60
  165.1 36.0 %reshape.33 = bf16[12,512,1023]{2,1,0:T(8,128)(2,1)} reshape(bf16[12,523776]{1,0:T(8,128)(2,1)} %slice.60) | data formatting | bytes 25141248 | tf_op jit(solution)/shard_map/while/body/eval_jaxpr/reshape | solution.py:19
  201.7 7.2 fusion.18
  210.2 6.1 broadcast_in_dim.28
  216.3 5.8 pad.19
  222.1 29.2 %copy.15 = bf16[2,8,512,1024]{3,1,2,0:T(8,128)(2,1)S(1)} copy(bf16[2,8,512,1024]{3,2,1,0:T(8,128)(2,1)S(1)} %bitcast.30) | data formatting | bytes 33554432 | tf_op jit(solution)/shard_map/while
  251.3 6.5 slice.60
  257.8 36.0 %reshape.33 = bf16[12,512,1023]{2,1,0:T(8,128)(2,1)} reshape(bf16[12,523776]{1,0:T(8,128)(2,1)} %slice.60) | data formatting | bytes 25141248 | tf_op jit(solution)/shard_map/while/body/eval_jaxpr/reshape | solution.py:19
  294.5 7.1 fusion.18
  302.9 6.1 broadcast_in_dim.28
  309.1 5.8 pad.19
  314.9 29.2 %copy.15 = bf16[2,8,512,1024]{3,1,2,0:T(8,128)(2,1)S(1)} copy(bf16[2,8,512,1024]{3,2,1,0:T(8,128)(2,1)S(1)} %bitcast.30) | data formatting | bytes 33554432 | tf_op jit(solution)/shard_map/while
  344.1 6.5 slice.60
  350.6 36.0 %reshape.33 = bf16[12,512,1023]{2,1,0:T(8,128)(2,1)} reshape(bf16[12,523776]{1,0:T(8,128)(2,1)} %slice.60) | data formatting | bytes 25141248 | tf_op jit(solution)/shard_map/while/body/eval_jaxpr/reshape | solution.py:19
  387.2 7.2 fusion.18
  395.7 6.1 broadcast_in_dim.28
  401.8 5.8 pad.19
  407.6 29.2 %copy.15 = bf16[2,8,512,1024]{3,1,2,0:T(8,128)(2,1)S(1)} copy(bf16[2,8,512,1024]{3,2,1,0:T(8,128)(2,1)S(1)} %bitcast.30) | data formatting | bytes 33554432 | tf_op jit(solution)/shard_map/while
  436.8 6.5 slice.60
  443.4 36.0 %reshape.33 = bf16[12,512,1023]{2,1,0:T(8,128)(2,1)} reshape(bf16[12,523776]{1,0:T(8,128)(2,1)} %slice.60) | data formatting | bytes 25141248 | tf_op jit(solution)/shard_map/while/body/eval_jaxpr/reshape | solution.py:19
  480.0 7.1 fusion.18
  488.5 6.1 broadcast_in_dim.28
  494.6 5.8 pad.19
  500.4 29.2 %copy.15 = bf16[2,8,512,1024]{3,1,2,0:T(8,128)(2,1)S(1)} copy(bf16[2,8,512,1024]{3,2,1,0:T(8,128)(2,1)S(1)} %bitcast.30) | data formatting | bytes 33554432 | tf_op jit(solution)/shard_map/while
  529.6 6.5 slice.60
  536.1 36.0 %reshape.33 = bf16[12,512,1023]{2,1,0:T(8,128)(2,1)} reshape(bf16[12,523776]{1,0:T(8,128)(2,1)} %slice.60) | data formatting | bytes 25141248 | tf_op jit(solution)/shard_map/while/body/eval_jaxpr/reshape | solution.py:19
  572.7 7.2 fusion.18
  581.2 6.1 broadcast_in_dim.28
  587.4 5.8 pad.19
  593.1 29.2 %copy.15 = bf16[2,8,512,1024]{3,1,2,0:T(8,128)(2,1)S(1)} copy(bf16[2,8,512,1024]{3,2,1,0:T(8,128)(2,1)S(1)} %bitcast.30) | data formatting | bytes 33554432 | tf_op jit(solution)/shard_map/while
  622.4 6.5 slice.60
  628.9 36.0 %reshape.33 = bf16[12,512,1023]{2,1,0:T(8,128)(2,1)} reshape(bf16[12,523776]{1,0:T(8,128)(2,1)} %slice.60) | data formatting | bytes 25141248 | tf_op jit(solution)/shard_map/while/body/eval_jaxpr/reshape | solution.py:19
  665.5 7.1 fusion.18
  674.0 6.1 broadcast_in_dim.28
  680.1 5.8 pad.19
  685.9 29.2 %copy.15 = bf16[2,8,512,1024]{3,1,2,0:T(8,128)(2,1)S(1)} copy(bf16[2,8,512,1024]{3,2,1,0:T(8,128)(2,1)S(1)} %bitcast.30) | data formatting | bytes 33554432 | tf_op jit(solution)/shard_map/while
  715.1 6.5 slice.60
  721.6 36.0 %reshape.33 = bf16[12,512,1023]{2,1,0:T(8,128)(2,1)} reshape(bf16[12,523776]{1,0:T(8,128)(2,1)} %slice.60) | data formatting | bytes 25141248 | tf_op jit(solution)/shard_map/while/body/eval_jaxpr/reshape | solution.py:19
  758.3 7.2 fusion.18
  766.7 6.1 broadcast_in_dim.28
  772.9 5.8 pad.19
  778.7 29.2 %copy.15 = bf16[2,8,512,1024]{3,1,2,0:T(8,128)(2,1)S(1)} copy(bf16[2,8,512,1024]{3,2,1,0:T(8,128)(2,1)S(1)} %bitcast.30) | data formatting | bytes 33554432 | tf_op jit(solution)/shard_map/while
  807.9 6.5 slice.60
  814.4 36.0 %reshape.33 = bf16[12,512,1023]{2,1,0:T(8,128)(2,1)} reshape(bf16[12,523776]{1,0:T(8,128)(2,1)} %slice.60) | data formatting | bytes 25141248 | tf_op jit(solution)/shard_map/while/body/eval_jaxpr/reshape | solution.py:19
  851.0 7.1 fusion.18
  858.4 5.0 convolution_bitcast_fusion.1
  863.5 6.7 convolution_bitcast_fusion
  870.2 9.0 copy.9
  879.2 93.0 %reduce-scatter.3.cloned.1.call-done = f32[128,512]{0,1:T(8,128)} async-done(((f32[1024,512]{0,1:T(8,128)}), f32[128,512]{0,1:T(8,128)}) %reduce-scatter.3.cloned.1.call-update) | async-done | bytes 262160 | tf_op jit(solution)/shard_map/reduce_scatter | solution.py:49
  972.2 1.6 convert_bitcast_fusion
  973.8 159.5 %reduce-scatter.5.cloned.1.call-done = f32[32,12,128]{2,1,0:T(8,128)} async-done(((f32[1024,12,128]{2,1,0:T(8,128)}), f32[32,12,128]{2,1,0:T(8,128)}) %reduce-scatter.5.cloned.1.call-update) | async-done | bytes 196624 | tf_op jit(solution)/shard_map/reduce_scatter | solution.py:57
  1133.3 1.7 copy.10
  (53 shorter events, 15.4 us)
Async XLA Ops:
  7.2 851.2 %copy-start = (bf16[1024,12,128]{2,0,1:T(8,128)(2,1)S(1)}, bf16[1024,12,128]{2,0,1:T(8,128)(2,1)}, u32[]{:S(2)}) copy-start(bf16[1024,12,128]{2,0,1:T(8,128)(2,1)} %param.9) | copy-start | bytes 9437188
  7.2 856.3 %all-gather.2.cloned.1.call-start = ((), (), s32[]{:S(2)}) async-start(), calls=%async_computation.3 | async-start | bytes 1179648 | tf_op jit(solution)/shard_map/all_gather | solution.py:56
  9.0 963.2 %reduce-scatter.3.cloned.1.call-start = ((), (), s32[]{:S(2)}) async-start(), calls=%async_computation.2 | async-start | bytes 2359296 | tf_op jit(solution)/shard_map/reduce_scatter | solution.py:49
  57.5 36.0 %copy-start.1 = (bf16[12,4096]{1,0:T(8,128)(2,1)S(1)}, bf16[12,4096]{1,0:T(8,128)(2,1)}, u32[]{:S(2)}) copy-start(bf16[12,4096]{1,0:T(8,128)(2,1)} %param.8) | copy-start | bytes 294916
  116.1 85.0 %collective-permute-start = (bf16[512,128]{1,0:T(8,128)(2,1)}, bf16[512,128]{1,0:T(8,128)(2,1)S(1)}, u32[]{:S(2)}, u32[]{:S(2)}) collective-permute-start(bf16[512,128]{1,0:T(8,128)(2,1)} %get-tuple-element.137), channel_id=1, source_target_pairs={{8,0},{16,8},{24,16},{32,24},{40,32},{48,40},{56,48},{64,56},{72,6... | collective-permute-start | bytes 393224 | tf_op jit(solution)/shard_map/while/body/eval_jaxpr/ppermute | solution.py:10
  208.8 85.0 %collective-permute-start = (bf16[512,128]{1,0:T(8,128)(2,1)}, bf16[512,128]{1,0:T(8,128)(2,1)S(1)}, u32[]{:S(2)}, u32[]{:S(2)}) collective-permute-start(bf16[512,128]{1,0:T(8,128)(2,1)} %get-tuple-element.137), channel_id=1, source_target_pairs={{8,0},{16,8},{24,16},{32,24},{40,32},{48,40},{56,48},{64,56},{72,6... | collective-permute-start | bytes 393224 | tf_op jit(solution)/shard_map/while/body/eval_jaxpr/ppermute | solution.py:10
  301.6 85.0 %collective-permute-start = (bf16[512,128]{1,0:T(8,128)(2,1)}, bf16[512,128]{1,0:T(8,128)(2,1)S(1)}, u32[]{:S(2)}, u32[]{:S(2)}) collective-permute-start(bf16[512,128]{1,0:T(8,128)(2,1)} %get-tuple-element.137), channel_id=1, source_target_pairs={{8,0},{16,8},{24,16},{32,24},{40,32},{48,40},{56,48},{64,56},{72,6... | collective-permute-start | bytes 393224 | tf_op jit(solution)/shard_map/while/body/eval_jaxpr/ppermute | solution.py:10
  394.4 85.0 %collective-permute-start = (bf16[512,128]{1,0:T(8,128)(2,1)}, bf16[512,128]{1,0:T(8,128)(2,1)S(1)}, u32[]{:S(2)}, u32[]{:S(2)}) collective-permute-start(bf16[512,128]{1,0:T(8,128)(2,1)} %get-tuple-element.137), channel_id=1, source_target_pairs={{8,0},{16,8},{24,16},{32,24},{40,32},{48,40},{56,48},{64,56},{72,6... | collective-permute-start | bytes 393224 | tf_op jit(solution)/shard_map/while/body/eval_jaxpr/ppermute | solution.py:10
  487.1 85.0 %collective-permute-start = (bf16[512,128]{1,0:T(8,128)(2,1)}, bf16[512,128]{1,0:T(8,128)(2,1)S(1)}, u32[]{:S(2)}, u32[]{:S(2)}) collective-permute-start(bf16[512,128]{1,0:T(8,128)(2,1)} %get-tuple-element.137), channel_id=1, source_target_pairs={{8,0},{16,8},{24,16},{32,24},{40,32},{48,40},{56,48},{64,56},{72,6... | collective-permute-start | bytes 393224 | tf_op jit(solution)/shard_map/while/body/eval_jaxpr/ppermute | solution.py:10
  579.9 85.0 %collective-permute-start = (bf16[512,128]{1,0:T(8,128)(2,1)}, bf16[512,128]{1,0:T(8,128)(2,1)S(1)}, u32[]{:S(2)}, u32[]{:S(2)}) collective-permute-start(bf16[512,128]{1,0:T(8,128)(2,1)} %get-tuple-element.137), channel_id=1, source_target_pairs={{8,0},{16,8},{24,16},{32,24},{40,32},{48,40},{56,48},{64,56},{72,6... | collective-permute-start | bytes 393224 | tf_op jit(solution)/shard_map/while/body/eval_jaxpr/ppermute | solution.py:10
  672.6 85.0 %collective-permute-start = (bf16[512,128]{1,0:T(8,128)(2,1)}, bf16[512,128]{1,0:T(8,128)(2,1)S(1)}, u32[]{:S(2)}, u32[]{:S(2)}) collective-permute-start(bf16[512,128]{1,0:T(8,128)(2,1)} %get-tuple-element.137), channel_id=1, source_target_pairs={{8,0},{16,8},{24,16},{32,24},{40,32},{48,40},{56,48},{64,56},{72,6... | collective-permute-start | bytes 393224 | tf_op jit(solution)/shard_map/while/body/eval_jaxpr/ppermute | solution.py:10
  765.4 85.0 %collective-permute-start = (bf16[512,128]{1,0:T(8,128)(2,1)}, bf16[512,128]{1,0:T(8,128)(2,1)S(1)}, u32[]{:S(2)}, u32[]{:S(2)}) collective-permute-start(bf16[512,128]{1,0:T(8,128)(2,1)} %get-tuple-element.137), channel_id=1, source_target_pairs={{8,0},{16,8},{24,16},{32,24},{40,32},{48,40},{56,48},{64,56},{72,6... | collective-permute-start | bytes 393224 | tf_op jit(solution)/shard_map/while/body/eval_jaxpr/ppermute | solution.py:10
  863.4 269.9 %reduce-scatter.5.cloned.1.call-start = ((), (), s32[]{:S(2)}) async-start(), calls=%async_computation.4 | async-start | bytes 8650752 | tf_op jit(solution)/shard_map/reduce_scatter | solution.py:57
Sparse Core Ops, SparseCore 0:
  10.5 64.2 all-gather.1
  863.5 108.6 reduce-scatter.2
  974.9 158.3 reduce-scatter.4
where the time goes:
time: 1160 us; the launch traced here: 1140 us
  local copies, waits for them, and re-layouts  770 us (66%)
  waiting for transfers between devices  253 us (22%)
  matrix products  75.2 us (6%)
  loops' own time  16.9 us (1%)
  between operations  14.2 us (1%)
    reshape x9, local copies, waits for them, and re-layouts, lag_table(): repeated[:, :tok_rows * (2 * tok_rows - 1)]  324 us
    while x24, local copies, waits for them, and re-layouts  285 us
    reduce_scatter x1, waiting for transfers between devices, per_device(): lax.psum_scatter(jnp.einsum('ti,ktc->ikc', full_inputs, correlated, prefe...  159 us
    reduce_scatter x1, waiting for transfers between devices, per_device(): lax.psum_scatter(jnp.einsum('ikc,ktc->it', projection, correlated, prefer...  93 us
    dot_general x9, matrix products, lag_term(): jnp.einsum('kab,bc->kac', lag_table(padded, lag_index, tok_rows), grad_bl...  63.5 us
    slice x9, local copies, waits for them, and re-layouts, lag_table(): repeated[:, :tok_rows * (2 * tok_rows - 1)]  58.8 us
    broadcast_in_dim x9, local copies, waits for them, and re-layouts, lag_table(): jnp.broadcast_to(rotated[:, None, :], (filt_count, tok_rows, 2 * tok_rows))  55.3 us
    unnamed x8, local copies, waits for them, and re-layouts  38.4 us
  transfers between devices with their start and end apart: 11, of which 2 were waited for; matrix products, arithmetic and copies ran while one was open for 74% of the time, Pallas kernels for 0%

commit v1 on v0

v1 whole, which is shorter than its diff:
```python
import functools

import jax
import jax.numpy as jnp
from jax import lax
from jax.experimental import pallas as pl
from jax.experimental.pallas import tpu as pltpu
from jax.sharding import PartitionSpec as P

BF16, F32 = jnp.bfloat16, jnp.float32
ROWS = 64
LANE = 128
NX, NZ_HI, NY, NZ_LO, NCORE = 4, 2, 4, 4, 2
CHIPS = NY * NZ_LO
VMEM_LIMIT = 48 * 1024 * 1024


def ctx_of(y, z, core):
    return (y * NZ_LO + z) * NCORE + core


CTX = [(y, z, core) for y in range(NY) for z in range(NZ_LO) for core in range(NCORE)]
TP = [(x, z) for x in range(NX) for z in range(NZ_HI)]
CORE_SWAP = [(ctx_of(y, z, c), ctx_of(y, z, 1 - c)) for y, z, c in CTX]
Z_HI_SWAP = [(x * NZ_HI + z, x * NZ_HI + 1 - z) for x, z in TP]


def along_y(steps):
    return [(ctx_of(y, z, c), ctx_of((y + steps) % NY, z, c)) for y, z, c in CTX]


def along_z(steps):
    return [(ctx_of(y, z, c), ctx_of(y, (z + steps) % NZ_LO, c)) for y, z, c in CTX]


def along_x(steps):
    return [(x * NZ_HI + z, (x + steps) % NX * NZ_HI + z) for x, z in TP]


def from_later_chip(steps):
    return [
        (NCORE * (chip + steps) + core, NCORE * chip + core)
        for chip in range(CHIPS - steps)
        for core in range(NCORE)
    ]


def table_kernel(filters_ref, table_ref):
    filt_count, rows, width = table_ref.shape
    taps = filters_ref.shape[1]
    for k in range(filt_count):
        line = filters_ref[k : k + 1, :].astype(F32)
        line = jnp.concatenate([line, jnp.zeros((1, width - taps), F32)], axis=1)
        block = jnp.broadcast_to(line, (rows, width))
        table_ref[k] = pltpu.roll(block, 0, 1, stride=1, stride_axis=0).astype(BF16)


def toeplitz_tables(filters):
    filt_count, taps = filters.shape
    width = taps + LANE
    return pl.pallas_call(
        table_kernel,
        out_shape=jax.ShapeDtypeStruct((filt_count, ROWS, width), BF16),
        in_specs=[pl.BlockSpec(memory_space=pltpu.VMEM)],
        out_specs=pl.BlockSpec(memory_space=pltpu.VMEM),
        compiler_params=pltpu.CompilerParams(vmem_limit_bytes=VMEM_LIMIT),
        cost_estimate=pl.CostEstimate(flops=30_000_000, bytes_accessed=7_000_000, transcendentals=0),
        name="tables",
    )(filters)


def conv_kernel(
    pos_ref, table_ref, own_ref, r1_ref, r2_ref, r3_ref, r4_ref, swapped_ref,
    x0_ref, x1_ref, x2_ref, x3_ref,
    corr_ref, keep_ref, send_ref, grad_ref, full_ref,
):
    filt_count, rows, width = table_ref.shape
    tok = own_ref.shape[0]
    x, z_hi, y, z_lo, core = (pos_ref[i] for i in range(5))
    received = (own_ref, r1_ref, r2_ref, r3_ref, r4_ref)
    for s, part in enumerate(received):
        grad_ref[2 * s * tok : (2 * s + 1) * tok, :] = part[...]
    for s in range(4):
        grad_ref[(2 * s + 1) * tok : (2 * s + 2) * tok, :] = swapped_ref[s]
    grad_ref[9 * tok :, :] = jnp.zeros((grad_ref.shape[0] - 9 * tok, LANE), BF16)

    table = table_ref[...].reshape(filt_count * rows, width)

    @pl.loop(0, tok // (2 * rows))
    def _(pair):
        start = pl.multiple_of(pair * (2 * rows), 2 * rows)
        first = grad_ref[pl.ds(start, width), :]
        second = grad_ref[pl.ds(start + rows, width), :]
        both = jnp.concatenate([first, second], axis=1)
        result = jnp.dot(table, both, preferred_element_type=F32).astype(BF16)
        for k in range(filt_count):
            for half in range(2):
                corr_ref[pl.ds(start + half * rows, rows), k * LANE : (k + 1) * LANE] = result[
                    k * rows : (k + 1) * rows, half * LANE : (half + 1) * LANE
                ]

    for s, part in enumerate((x0_ref, x1_ref, x2_ref, x3_ref)):
        for h in range(NZ_HI):
            at = lax.rem(x + NX - s, NX) * NZ_HI + lax.rem(z_hi + h, NZ_HI)
            full_ref[:, pl.ds(pl.multiple_of(at * LANE, LANE), LANE)] = part[h]

    deep = NZ_LO * NCORE * 32

    @pl.loop(0, NY)
    def _(s):
        at = lax.rem(y + s, NY)
        part = full_ref[:, pl.ds(pl.multiple_of(at * deep, deep), deep)]
        result = lax.dot_general(
            part, corr_ref[...], (((0,), (0,)), ((), ())), preferred_element_type=F32
        ).astype(BF16)
        for z in range(NZ_LO):
            slot = lax.rem(z + NZ_LO - z_lo, NZ_LO)
            for k in range(filt_count):
                columns = slice(k * LANE, (k + 1) * LANE)
                even = result[z * 64 : z * 64 + 32, columns]
                odd = result[z * 64 + 32 : z * 64 + 64, columns]
                keep_ref[s, slot, k] = jnp.where(core == 0, even, odd)
                send_ref[s, slot, k] = jnp.where(core == 0, odd, even)


def conv_and_product(pos, table, halo, swapped, gathered):
    filt_count, rows, width = table.shape
    tok = halo[0].shape[0]
    part = jax.ShapeDtypeStruct((NY, NZ_LO, filt_count, 32, LANE), BF16)
    vmem = pl.BlockSpec(memory_space=pltpu.VMEM)
    flops = 2 * filt_count * (rows * width * (tok // rows) * LANE + tok * LANE * 1024)
    return pl.pallas_call(
        conv_kernel,
        out_shape=(jax.ShapeDtypeStruct((tok, filt_count * LANE), BF16), part, part),
        in_specs=[pl.BlockSpec(memory_space=pltpu.SMEM)] + [vmem] * 11,
        out_specs=(vmem,) * 3,
        scratch_shapes=[
            pltpu.VMEM((9 * tok + rows, LANE), BF16),
            pltpu.VMEM((tok, 1024), BF16),
        ],
        compiler_params=pltpu.CompilerParams(vmem_limit_bytes=VMEM_LIMIT),
        cost_estimate=pl.CostEstimate(flops=flops, bytes_accessed=8_000_000, transcendentals=0),
        name="conv_product",
    )(pos, table, *halo, swapped, *gathered)


def share_kernel(pos_ref, *refs):
    corr_refs, proj_ref, slot_refs, all_ref = refs[:-6], refs[-6], refs[-5:-1], refs[-1]
    filt_count = proj_ref.shape[0]
    x, z_hi = pos_ref[0], pos_ref[1]
    at = 0
    for part in corr_refs:
        all_ref[:, at : at + part.shape[1]] = part[...]
        at += part.shape[1]
    wide = NZ_HI * LANE
    for s, slot_ref in enumerate(slot_refs):
        base = pl.multiple_of(lax.rem(x + s, NX) * wide, wide)
        weights = jnp.concatenate(
            [proj_ref[k, pl.ds(base, wide), :] for k in range(filt_count)], axis=1
        )
        result = lax.dot_general(
            all_ref[...], weights, (((1,), (1,)), ((), ())), preferred_element_type=F32
        ).astype(BF16)
        low, high = result[:, :LANE], result[:, LANE:]
        slot_ref[0] = jnp.where(z_hi == 0, low, high)
        slot_ref[1] = jnp.where(z_hi == 0, high, low)


def input_shares(pos, corrs, projection):
    tok = corrs[0].shape[0]
    filt_count, channels, _ = projection.shape
    vmem = pl.BlockSpec(memory_space=pltpu.VMEM)
    return pl.pallas_call(
        share_kernel,
        out_shape=(jax.ShapeDtypeStruct((NZ_HI, tok, LANE), BF16),) * NX,
        in_specs=[pl.BlockSpec(memory_space=pltpu.SMEM)] + [vmem] * (len(corrs) + 1),
        out_specs=(vmem,) * NX,
        scratch_shapes=[pltpu.VMEM((tok, filt_count * LANE), BF16)],
        compiler_params=pltpu.CompilerParams(vmem_limit_bytes=VMEM_LIMIT),
        cost_estimate=pl.CostEstimate(
            flops=2 * tok * filt_count * LANE * channels, bytes_accessed=6_000_000, transcendentals=0
        ),
        name="input_shares",
    )(pos, *corrs, projection)


GROUPS = 2


def per_device(inputs, grad_out, filters, projection):
    filt_count = filters.shape[0]
    tp, ctx = lax.axis_index("tp"), lax.axis_index("ctx")
    core = ctx % NCORE
    pos = jnp.stack(
        [tp // NZ_HI, tp % NZ_HI, ctx // (NCORE * NZ_LO), ctx // NCORE % NZ_LO, core]
    ).astype(jnp.int32)

    later = [lax.ppermute(grad_out, "ctx", from_later_chip(s)) for s in range(1, 5)]
    pair = jnp.stack([inputs, lax.ppermute(inputs, "tp", Z_HI_SWAP)])
    gathered = [pair] + [lax.ppermute(pair, "tp", along_x(s)) for s in range(1, NX)]
    tables = toeplitz_tables(filters)
    halo = [grad_out] + later
    sent = jnp.stack([jnp.where(core == 0, halo[s + 1], halo[s]) for s in range(4)])
    swapped = lax.ppermute(sent, "ctx", CORE_SWAP)

    per_group = filt_count // GROUPS
    corrs, gradients = [], []
    for group in range(GROUPS):
        table = tables[group * per_group : (group + 1) * per_group]
        corr, keep, send = conv_and_product(pos, table, halo, swapped, gathered)
        corrs.append(corr)
        other = lax.ppermute(send, "ctx", CORE_SWAP)
        chip_sum = [keep[s].astype(F32) + other[s].astype(F32) for s in range(NY)]
        column = chip_sum[0]
        for s in range(1, NY):
            column += lax.ppermute(chip_sum[s].astype(BF16), "ctx", along_y(s)).astype(F32)
        total = column[0]
        for s in range(1, NZ_LO):
            total += lax.ppermute(column[s].astype(BF16), "ctx", along_z(s)).astype(F32)
        gradients.append(total)
    grad_proj = jnp.concatenate(gradients, axis=0).transpose(1, 0, 2)

    shares = input_shares(pos, corrs, projection.transpose(1, 0, 2))
    both = shares[0].astype(F32)
    for s in range(1, NX):
        both += lax.ppermute(shares[s], "tp", along_x(s)).astype(F32)
    far = lax.ppermute(both[1].astype(BF16), "tp", Z_HI_SWAP)
    grad_input = (both[0] + far.astype(F32)).astype(BF16)
    return grad_input, grad_proj


def solution(mesh):
    return jax.shard_map(
        per_device,
        mesh=mesh,
        in_specs=(P("ctx", "tp"), P("ctx", "tp"), P(), P(None, None, "tp")),
        out_specs=(P("ctx", "tp"), P("ctx", None, "tp")),
        check_vma=False,
    )
```

time: 1160 us -> 121 us (0.10)
  the two profiles are of different devices: /device:TPU:2 before, /device:TPU:24 now
where the time goes in v1:
time: 121 us; the launch traced here: 120 us
  starting transfers between devices  50.1 us (41%)
  waiting for transfers between devices  35.7 us (30%)
  Pallas kernels  23.9 us (20%)
  local copies, waits for them, and re-layouts  7.13 us (6%)
  other arithmetic  2.28 us (2%)
    pallas_call x2, Pallas kernels, conv_and_product(): pl.pallas_call(conv_kernel, out_shape=(jax.ShapeDtypeStruct((tok, filt_co...  17.1 us
    ppermute x6, starting transfers between devices, per_device(): total += lax.ppermute(column[s].astype(BF16), 'ctx', along_z(s)).astype(F32)  12.2 us
    ppermute x3, waiting for transfers between devices, per_device(): both += lax.ppermute(shares[s], 'tp', along_x(s)).astype(F32)  11.7 us
    ppermute x4, starting transfers between devices, per_device(): lax.ppermute(grad_out, 'ctx', from_later_chip(s))  11.6 us
    ppermute x1, waiting for transfers between devices, per_device(): far = lax.ppermute(both[1].astype(BF16), 'tp', Z_HI_SWAP)  8.24 us
    ppermute x6, waiting for transfers between devices, per_device(): lax.ppermute(chip_sum[s].astype(BF16), 'ctx', along_y(s)).astype(F32)  8.23 us
    ppermute x1, starting transfers between devices, per_device(): pair = jnp.stack([inputs, lax.ppermute(inputs, 'tp', Z_HI_SWAP)])  7.28 us
    ppermute x6, starting transfers between devices, per_device(): lax.ppermute(chip_sum[s].astype(BF16), 'ctx', along_y(s)).astype(F32)  6.47 us
  transfers between devices with their start and end apart: 27, of which 11 were waited for; matrix products, arithmetic and copies ran while one was open for 6% of the time, Pallas kernels for 4%

profile of v1, /device:TPU:24, one launch (start us, length us, event | category | flops | bytes accessed | tf_op | source)
XLA Modules:
  0.0 120.0 jit_solution(12929022864246662569)
XLA Ops:
  0.6 7.3 %collective-permute-start.5 = (bf16[512,128]{1,0:T(8,128)(2,1)}, bf16[512,128]{1,0:T(8,128)(2,1)S(1)}, u32[]{:S(2)}, u32[]{:S(2)}) collective-permute-start(bf16[512,128]{1,0:T(8,128)(2,1)} %param.4), channel_id=1, source_target_pairs={{0,1},{1,0},{2,3},{3,2},{4,5},{5,4},{6,7},{7,6},{8,9},{9,8},{10,11... | collective-permute-start | bytes 393224 | tf_op jit(solution)/shard_map/ppermute | solution.py:199
  7.9 4.0 %collective-permute-start = (bf16[512,128]{1,0:T(8,128)(2,1)}, bf16[512,128]{1,0:T(8,128)(2,1)S(1)}, u32[]{:S(2)}, u32[]{:S(2)}) collective-permute-start(bf16[512,128]{1,0:T(8,128)(2,1)} %own_ref.3), channel_id=1, source_target_pairs={{16,0},{24,8},{32,16},{40,24},{48,32},{56,40},{64,48},{72,56},{80,... | collective-permute-start | bytes 393224 | tf_op jit(solution)/shard_map/ppermute | solution.py:198
  11.9 2.5 %collective-permute-start.1 = (bf16[512,128]{1,0:T(8,128)(2,1)}, bf16[512,128]{1,0:T(8,128)(2,1)S(1)}, u32[]{:S(2)}, u32[]{:S(2)}) collective-permute-start(bf16[512,128]{1,0:T(8,128)(2,1)} %own_ref.3), channel_id=1, source_target_pairs={{32,0},{40,8},{48,16},{56,24},{64,32},{72,40},{80,48},{88,56},{96,... | collective-permute-start | bytes 393224 | tf_op jit(solution)/shard_map/ppermute | solution.py:198
  14.4 2.8 %collective-permute-start.2 = (bf16[512,128]{1,0:T(8,128)(2,1)}, bf16[512,128]{1,0:T(8,128)(2,1)S(1)}, u32[]{:S(2)}, u32[]{:S(2)}) collective-permute-start(bf16[512,128]{1,0:T(8,128)(2,1)} %own_ref.3), channel_id=1, source_target_pairs={{48,0},{56,8},{64,16},{72,24},{80,32},{88,40},{96,48},{104,56},{11... | collective-permute-start | bytes 393224 | tf_op jit(solution)/shard_map/ppermute | solution.py:198
  17.2 2.4 %collective-permute-start.3 = (bf16[512,128]{1,0:T(8,128)(2,1)}, bf16[512,128]{1,0:T(8,128)(2,1)S(1)}, u32[]{:S(2)}, u32[]{:S(2)}) collective-permute-start(bf16[512,128]{1,0:T(8,128)(2,1)} %own_ref.3), channel_id=1, source_target_pairs={{64,0},{72,8},{80,16},{88,24},{96,32},{104,40},{112,48},{120,56},{... | collective-permute-start | bytes 393224 | tf_op jit(solution)/shard_map/ppermute | solution.py:198
  19.6 0.9 copy-done
  20.5 4.5 %tables.1 = bf16[12,64,4224]{2,1,0:T(8,128)(2,1)} custom-call(bf16[12,4096]{1,0:T(8,128)(2,1)S(1)} %copy-done), custom_call_target="tpu_custom_call" | custom-call | flops 30000000 | bytes 7000000 | tf_op jit(solution)/shard_map/tables/pallas_call | solution.py:61
  25.0 0.0 collective-permute-done.5
  25.0 1.6 %collective-permute-start.6 = (bf16[2,512,128]{2,1,0:T(8,128)(2,1)S(1)}, bf16[2,512,128]{2,1,0:T(8,128)(2,1)S(1)}, u32[]{:S(2)}, u32[]{:S(2)}) collective-permute-start(bf16[2,512,128]{2,1,0:T(8,128)(2,1)S(1)} %pad_maximum_fusion.1.x0_ref), channel_id=1, source_target_pairs={{0,2},{1,3},{2,4},{3,5},{4,6},{5,7},{6,0},{7,1},{8,10},{9,11},{10,... | collective-permute-start | bytes 786440 | tf_op jit(solution)/shard_map/ppermute | solution.py:200
  26.6 0.0 collective-permute-done.r1_ref
  26.6 2.7 %collective-permute-start.7 = (bf16[2,512,128]{2,1,0:T(8,128)(2,1)S(1)}, bf16[2,512,128]{2,1,0:T(8,128)(2,1)S(1)}, u32[]{:S(2)}, u32[]{:S(2)}) collective-permute-start(bf16[2,512,128]{2,1,0:T(8,128)(2,1)S(1)} %pad_maximum_fusion.1.x0_ref), channel_id=1, source_target_pairs={{0,4},{1,5},{2,6},{3,7},{4,0},{5,1},{6,2},{7,3},{8,12},{9,13},{10,... | collective-permute-start | bytes 786440 | tf_op jit(solution)/shard_map/ppermute | solution.py:200
  29.3 0.0 collective-permute-done.1.r2_ref
  29.3 1.4 %collective-permute-start.8 = (bf16[2,512,128]{2,1,0:T(8,128)(2,1)S(1)}, bf16[2,512,128]{2,1,0:T(8,128)(2,1)S(1)}, u32[]{:S(2)}, u32[]{:S(2)}) collective-permute-start(bf16[2,512,128]{2,1,0:T(8,128)(2,1)S(1)} %pad_maximum_fusion.1.x0_ref), channel_id=1, source_target_pairs={{0,6},{1,7},{2,0},{3,1},{4,2},{5,3},{6,4},{7,5},{8,14},{9,15},{10,... | collective-permute-start | bytes 786440 | tf_op jit(solution)/shard_map/ppermute | solution.py:200
  30.7 0.0 collective-permute-done.2.r3_ref
  30.8 0.0 collective-permute-done.3.r4_ref
  30.8 0.1 pad_maximum_fusion
  30.9 0.1 collective-permute-start.4
  31.0 6.1 %fusion.23 = (bf16[6,64,4224]{2,1,0:T(8,128)(2,1)}, bf16[6,64,4224]{2,1,0:T(8,128)(2,1)}) fusion(bf16[12,64,4224]{2,1,0:T(8,128)(2,1)} %tables.1), kind=kLoop, calls=%fused_computation.47 | loop fusion | bytes 12976128 | tf_op jit(solution)/shard_map/slice | solution.py:209
  37.1 0.1 stack.47.pos_ref
  37.2 0.0 collective-permute-done.6.x1_ref
  37.2 2.4 %collective-permute-done.7.x2_ref = bf16[2,512,128]{2,1,0:T(8,128)(2,1)S(1)} collective-permute-done((bf16[2,512,128]{2,1,0:T(8,128)(2,1)S(1)}, bf16[2,512,128]{2,1,0:T(8,128)(2,1)S(1)}, u32[]{:S(2)}, u32[]{:S(2)}) %collective-permute-start.7) | collective-permute-done | bytes 262176 | tf_op jit(solution)/shard_map/ppermute | solution.py:200
  39.5 0.0 collective-permute-done.8.x3_ref
  39.5 0.0 collective-permute-done.4.swapped_ref
  39.5 8.5 %conv_product.2 = (bf16[512,768]{1,0:T(8,128)(2,1)S(1)}, bf16[4,4,6,32,128]{4,3,2,1,0:T(8,128)(2,1)S(1)}, bf16[4,4,6,32,128]{4,3,2,1,0:T(8,128)(2,1)S(1)}) custom-call(s32[5]{0:T(128)S(1)} %stack.47.pos_ref, bf16[6,64,4224]{2,1,0:T(8,128)(2,1)} %get-tuple-element.27.table_ref, bf16[512,128]{1,0:T(8,128)(2,1)S(1)} %copy-done.1, ...), custom_call_target="tpu_custom_call" | custom-call | flops 4127195136 | bytes 8000000 | tf_op jit(solution)/shard_map/conv_product/pallas_call | solution.py:132
  48.0 0.0 copy-start.2
  48.0 8.6 %conv_product.3 = (bf16[512,768]{1,0:T(8,128)(2,1)S(1)}, bf16[4,4,6,32,128]{4,3,2,1,0:T(8,128)(2,1)S(1)}, bf16[4,4,6,32,128]{4,3,2,1,0:T(8,128)(2,1)S(1)}) custom-call(s32[5]{0:T(128)S(1)} %stack.47.pos_ref, bf16[6,64,4224]{2,1,0:T(8,128)(2,1)} %get-tuple-element.26.table_ref, bf16[512,128]{1,0:T(8,128)(2,1)S(1)} %copy-done.1, ...), custom_call_target="tpu_custom_call" | custom-call | flops 4127195136 | bytes 8000000 | tf_op jit(solution)/shard_map/conv_product/pallas_call | solution.py:132
  56.7 2.4 %input_shares.1 = (bf16[2,512,128]{2,1,0:T(8,128)(2,1)S(1)}, bf16[2,512,128]{2,1,0:T(8,128)(2,1)S(1)}, bf16[2,512,128]{2,1,0:T(8,128)(2,1)S(1)}, bf16[2,512,128]{2,1,0:T(8,128)(2,1)S(1)}) custom-call(s32[5]{0:T(128)S(1)} %stack.47.pos_ref, bf16[512,768]{1,0:T(8,128)(2,1)S(1)} %get-tuple-element.12.refs_0_, bf16[512,768]{1,0:T(8,128)(2,1)S(1)} %get-tuple-element.13.refs_1_, ...), custom_call_target="tpu_custom_call" | custom-call | flops 1610612736 | bytes 6000000 | tf_op jit(solution)/shard_map/input_shares/pallas_call | solution.py:173
  59.1 2.3 %collective-permute-start.11 = (bf16[2,512,128]{2,1,0:T(8,128)(2,1)S(1)}, bf16[2,512,128]{2,1,0:T(8,128)(2,1)S(1)}, u32[]{:S(2)}, u32[]{:S(2)}) collective-permute-start(bf16[2,512,128]{2,1,0:T(8,128)(2,1)S(1)} %get-tuple-element.17), channel_id=1, source_target_pairs={{0,6},{1,7},{2,0},{3,1},{4,2},{5,3},{6,4},{7,5},{8,14},{9,15},{10,... | collective-permute-start | bytes 786440 | tf_op jit(solution)/shard_map/ppermute | solution.py:226
  61.4 1.8 %collective-permute-start.10 = (bf16[2,512,128]{2,1,0:T(8,128)(2,1)S(1)}, bf16[2,512,128]{2,1,0:T(8,128)(2,1)S(1)}, u32[]{:S(2)}, u32[]{:S(2)}) collective-permute-start(bf16[2,512,128]{2,1,0:T(8,128)(2,1)S(1)} %get-tuple-element.16), channel_id=1, source_target_pairs={{0,4},{1,5},{2,6},{3,7},{4,0},{5,1},{6,2},{7,3},{8,12},{9,13},{10,... | collective-permute-start | bytes 786440 | tf_op jit(solution)/shard_map/ppermute | solution.py:226
  63.2 0.1 collective-permute-start.9
  63.2 0.0 collective-permute-start.20
  63.2 0.5 collective-permute-start.13
  63.7 4.5 %collective-permute-done.11 = bf16[2,512,128]{2,1,0:T(8,128)(2,1)S(1)} collective-permute-done((bf16[2,512,128]{2,1,0:T(8,128)(2,1)S(1)}, bf16[2,512,128]{2,1,0:T(8,128)(2,1)S(1)}, u32[]{:S(2)}, u32[]{:S(2)}) %collective-permute-start.11) | collective-permute-done | bytes 262176 | tf_op jit(solution)/shard_map/ppermute | solution.py:226
  68.3 3.9 %collective-permute-done.10 = bf16[2,512,128]{2,1,0:T(8,128)(2,1)S(1)} collective-permute-done((bf16[2,512,128]{2,1,0:T(8,128)(2,1)S(1)}, bf16[2,512,128]{2,1,0:T(8,128)(2,1)S(1)}, u32[]{:S(2)}, u32[]{:S(2)}) %collective-permute-start.10) | collective-permute-done | bytes 262176 | tf_op jit(solution)/shard_map/ppermute | solution.py:226
  72.1 3.3 %collective-permute-done.9 = bf16[2,512,128]{2,1,0:T(8,128)(2,1)S(1)} collective-permute-done((bf16[2,512,128]{2,1,0:T(8,128)(2,1)S(1)}, bf16[2,512,128]{2,1,0:T(8,128)(2,1)S(1)}, u32[]{:S(2)}, u32[]{:S(2)}) %collective-permute-start.9) | collective-permute-done | bytes 262176 | tf_op jit(solution)/shard_map/ppermute | solution.py:226
  75.4 0.1 convert_add_fusion
  75.5 2.0 %collective-permute-start.12 = (bf16[512,128]{1,0:T(8,128)(2,1)S(1)}, bf16[512,128]{1,0:T(8,128)(2,1)S(1)}, u32[]{:S(2)}, u32[]{:S(2)}) collective-permute-start(bf16[512,128]{1,0:T(8,128)(2,1)S(1)} %fusion.12), channel_id=1, source_target_pairs={{0,1},{1,0},{2,3},{3,2},{4,5},{5,4},{6,7},{7,6},{8,9},{9,8},{10,11... | collective-permute-start | bytes 393224 | tf_op jit(solution)/shard_map/ppermute | solution.py:227
  77.5 8.2 %collective-permute-done.12 = bf16[512,128]{1,0:T(8,128)(2,1)S(1)} collective-permute-done((bf16[512,128]{1,0:T(8,128)(2,1)S(1)}, bf16[512,128]{1,0:T(8,128)(2,1)S(1)}, u32[]{:S(2)}, u32[]{:S(2)}) %collective-permute-start.12) | collective-permute-done | bytes 131104 | tf_op jit(solution)/shard_map/ppermute | solution.py:227
  85.8 0.7 fusion.5
  86.5 0.2 fusion.9
  86.6 0.8 collective-permute-start.23
  87.5 0.0 collective-permute-start.22
  87.5 2.8 %collective-permute-start.21 = (bf16[4,6,32,128]{3,2,1,0:T(8,128)(2,1)S(1)}, bf16[4,6,32,128]{3,2,1,0:T(8,128)(2,1)S(1)}, u32[]{:S(2)}, u32[]{:S(2)}) collective-permute-start(bf16[4,6,32,128]{3,2,1,0:T(8,128)(2,1)S(1)} %get-tuple-element.31), channel_id=1, source_target_pairs={{0,64},{8,72},{16,80},{24,88},{32,96},{40,104},{48,112},{56,120},{... | collective-permute-start | bytes 589832 | tf_op jit(solution)/shard_map/ppermute | solution.py:216
  90.2 0.0 collective-permute-done.13
  90.3 0.2 fusion.6
  90.4 0.6 collective-permute-start.16
  91.1 2.2 %collective-permute-start.15 = (bf16[4,6,32,128]{3,2,1,0:T(8,128)(2,1)S(1)}, bf16[4,6,32,128]{3,2,1,0:T(8,128)(2,1)S(1)}, u32[]{:S(2)}, u32[]{:S(2)}) collective-permute-start(bf16[4,6,32,128]{3,2,1,0:T(8,128)(2,1)S(1)} %get-tuple-element.30), channel_id=1, source_target_pairs={{0,128},{8,136},{16,144},{24,152},{32,160},{40,168},{48,176},{56,1... | collective-permute-start | bytes 589832 | tf_op jit(solution)/shard_map/ppermute | solution.py:216
  93.3 7.4 %collective-permute-done.23 = bf16[4,6,32,128]{3,2,1,0:T(8,128)(2,1)S(1)} collective-permute-done((bf16[4,6,32,128]{3,2,1,0:T(8,128)(2,1)S(1)}, bf16[4,6,32,128]{3,2,1,0:T(8,128)(2,1)S(1)}, u32[]{:S(2)}, u32[]{:S(2)}) %collective-permute-start.23) | collective-permute-done | bytes 196640 | tf_op jit(solution)/shard_map/ppermute | solution.py:216
  100.7 0.2 collective-permute-done.21
  100.8 0.1 fusion.21
  101.0 3.2 %collective-permute-start.26 = (bf16[6,32,128]{2,1,0:T(8,128)(2,1)S(1)}, bf16[6,32,128]{2,1,0:T(8,128)(2,1)S(1)}, u32[]{:S(2)}, u32[]{:S(2)}) collective-permute-start(bf16[6,32,128]{2,1,0:T(8,128)(2,1)S(1)} %get-tuple-element.38), channel_id=1, source_target_pairs={{0,48},{8,56},{16,0},{24,8},{32,16},{40,24},{48,32},{56,40},{64,11... | collective-permute-start | bytes 147464 | tf_op jit(solution)/shard_map/ppermute | solution.py:219
  104.2 1.6 %collective-permute-start.25 = (bf16[6,32,128]{2,1,0:T(8,128)(2,1)S(1)}, bf16[6,32,128]{2,1,0:T(8,128)(2,1)S(1)}, u32[]{:S(2)}, u32[]{:S(2)}) collective-permute-start(bf16[6,32,128]{2,1,0:T(8,128)(2,1)S(1)} %get-tuple-element.39), channel_id=1, source_target_pairs={{0,32},{8,40},{16,48},{24,56},{32,0},{40,8},{48,16},{56,24},{64,96... | collective-permute-start | bytes 147464 | tf_op jit(solution)/shard_map/ppermute | solution.py:219
  105.9 0.7 collective-permute-done.16
  106.5 1.2 collective-permute-start.24
  107.7 0.1 fusion.19
  107.9 3.5 %collective-permute-start.19 = (bf16[6,32,128]{2,1,0:T(8,128)(2,1)S(1)}, bf16[6,32,128]{2,1,0:T(8,128)(2,1)S(1)}, u32[]{:S(2)}, u32[]{:S(2)}) collective-permute-start(bf16[6,32,128]{2,1,0:T(8,128)(2,1)S(1)} %get-tuple-element.35), channel_id=1, source_target_pairs={{0,48},{8,56},{16,0},{24,8},{32,16},{40,24},{48,32},{56,40},{64,11... | collective-permute-start | bytes 147464 | tf_op jit(solution)/shard_map/ppermute | solution.py:219
  111.4 2.0 %collective-permute-start.18 = (bf16[6,32,128]{2,1,0:T(8,128)(2,1)S(1)}, bf16[6,32,128]{2,1,0:T(8,128)(2,1)S(1)}, u32[]{:S(2)}, u32[]{:S(2)}) collective-permute-start(bf16[6,32,128]{2,1,0:T(8,128)(2,1)S(1)} %get-tuple-element.36), channel_id=1, source_target_pairs={{0,32},{8,40},{16,48},{24,56},{32,0},{40,8},{48,16},{56,24},{64,96... | collective-permute-start | bytes 147464 | tf_op jit(solution)/shard_map/ppermute | solution.py:219
  113.4 0.7 collective-permute-start.17
  114.0 0.0 collective-permute-done.25
  114.0 0.0 collective-permute-done.24
  114.1 0.1 collective-permute-done.19
  114.2 3.2 %collective-permute-done.18 = bf16[6,32,128]{2,1,0:T(8,128)(2,1)S(1)} collective-permute-done((bf16[6,32,128]{2,1,0:T(8,128)(2,1)S(1)}, bf16[6,32,128]{2,1,0:T(8,128)(2,1)S(1)}, u32[]{:S(2)}, u32[]{:S(2)}) %collective-permute-start.18) | collective-permute-done | bytes 49184 | tf_op jit(solution)/shard_map/ppermute | solution.py:219
  117.4 1.9 %collective-permute-done.17 = bf16[6,32,128]{2,1,0:T(8,128)(2,1)S(1)} collective-permute-done((bf16[6,32,128]{2,1,0:T(8,128)(2,1)S(1)}, bf16[6,32,128]{2,1,0:T(8,128)(2,1)S(1)}, u32[]{:S(2)}, u32[]{:S(2)}) %collective-permute-start.17) | collective-permute-done | bytes 49184 | tf_op jit(solution)/shard_map/ppermute | solution.py:219
  119.3 0.7 maximum_bitcast_fusion
  (19 shorter events, 0.2 us)
Async XLA Ops:
  0.6 24.3 %collective-permute-start.5 = (bf16[512,128]{1,0:T(8,128)(2,1)}, bf16[512,128]{1,0:T(8,128)(2,1)S(1)}, u32[]{:S(2)}, u32[]{:S(2)}) collective-permute-start(bf16[512,128]{1,0:T(8,128)(2,1)} %param.4), channel_id=1, source_target_pairs={{0,1},{1,0},{2,3},{3,2},{4,5},{5,4},{6,7},{7,6},{8,9},{9,8},{10,11... | collective-permute-start | bytes 393224 | tf_op jit(solution)/shard_map/ppermute | solution.py:199
  7.9 18.7 %collective-permute-start = (bf16[512,128]{1,0:T(8,128)(2,1)}, bf16[512,128]{1,0:T(8,128)(2,1)S(1)}, u32[]{:S(2)}, u32[]{:S(2)}) collective-permute-start(bf16[512,128]{1,0:T(8,128)(2,1)} %own_ref.3), channel_id=1, source_target_pairs={{16,0},{24,8},{32,16},{40,24},{48,32},{56,40},{64,48},{72,56},{80,... | collective-permute-start | bytes 393224 | tf_op jit(solution)/shard_map/ppermute | solution.py:198
  11.9 17.4 %collective-permute-start.1 = (bf16[512,128]{1,0:T(8,128)(2,1)}, bf16[512,128]{1,0:T(8,128)(2,1)S(1)}, u32[]{:S(2)}, u32[]{:S(2)}) collective-permute-start(bf16[512,128]{1,0:T(8,128)(2,1)} %own_ref.3), channel_id=1, source_target_pairs={{32,0},{40,8},{48,16},{56,24},{64,32},{72,40},{80,48},{88,56},{96,... | collective-permute-start | bytes 393224 | tf_op jit(solution)/shard_map/ppermute | solution.py:198
  14.4 16.4 %collective-permute-start.2 = (bf16[512,128]{1,0:T(8,128)(2,1)}, bf16[512,128]{1,0:T(8,128)(2,1)S(1)}, u32[]{:S(2)}, u32[]{:S(2)}) collective-permute-start(bf16[512,128]{1,0:T(8,128)(2,1)} %own_ref.3), channel_id=1, source_target_pairs={{48,0},{56,8},{64,16},{72,24},{80,32},{88,40},{96,48},{104,56},{11... | collective-permute-start | bytes 393224 | tf_op jit(solution)/shard_map/ppermute | solution.py:198
  17.2 13.5 %collective-permute-start.3 = (bf16[512,128]{1,0:T(8,128)(2,1)}, bf16[512,128]{1,0:T(8,128)(2,1)S(1)}, u32[]{:S(2)}, u32[]{:S(2)}) collective-permute-start(bf16[512,128]{1,0:T(8,128)(2,1)} %own_ref.3), channel_id=1, source_target_pairs={{64,0},{72,8},{80,16},{88,24},{96,32},{104,40},{112,48},{120,56},{... | collective-permute-start | bytes 393224 | tf_op jit(solution)/shard_map/ppermute | solution.py:198
  19.6 0.9 copy-start
  20.5 4.5 %copy-start.3 = (bf16[512,128]{1,0:T(8,128)(2,1)S(1)}, bf16[512,128]{1,0:T(8,128)(2,1)}, u32[]{:S(2)}) copy-start(bf16[512,128]{1,0:T(8,128)(2,1)} %param.4) | copy-start | bytes 393220
  20.5 10.3 %copy-start.1 = (bf16[512,128]{1,0:T(8,128)(2,1)S(1)}, bf16[512,128]{1,0:T(8,128)(2,1)}, u32[]{:S(2)}) copy-start(bf16[512,128]{1,0:T(8,128)(2,1)} %own_ref.3) | copy-start | bytes 393220
  25.0 12.2 %collective-permute-start.6 = (bf16[2,512,128]{2,1,0:T(8,128)(2,1)S(1)}, bf16[2,512,128]{2,1,0:T(8,128)(2,1)S(1)}, u32[]{:S(2)}, u32[]{:S(2)}) collective-permute-start(bf16[2,512,128]{2,1,0:T(8,128)(2,1)S(1)} %pad_maximum_fusion.1.x0_ref), channel_id=1, source_target_pairs={{0,2},{1,3},{2,4},{3,5},{4,6},{5,7},{6,0},{7,1},{8,10},{9,11},{10,... | collective-permute-start | bytes 786440 | tf_op jit(solution)/shard_map/ppermute | solution.py:200
  26.6 13.0 %collective-permute-start.7 = (bf16[2,512,128]{2,1,0:T(8,128)(2,1)S(1)}, bf16[2,512,128]{2,1,0:T(8,128)(2,1)S(1)}, u32[]{:S(2)}, u32[]{:S(2)}) collective-permute-start(bf16[2,512,128]{2,1,0:T(8,128)(2,1)S(1)} %pad_maximum_fusion.1.x0_ref), channel_id=1, source_target_pairs={{0,4},{1,5},{2,6},{3,7},{4,0},{5,1},{6,2},{7,3},{8,12},{9,13},{10,... | collective-permute-start | bytes 786440 | tf_op jit(solution)/shard_map/ppermute | solution.py:200
  29.3 10.2 %collective-permute-start.8 = (bf16[2,512,128]{2,1,0:T(8,128)(2,1)S(1)}, bf16[2,512,128]{2,1,0:T(8,128)(2,1)S(1)}, u32[]{:S(2)}, u32[]{:S(2)}) collective-permute-start(bf16[2,512,128]{2,1,0:T(8,128)(2,1)S(1)} %pad_maximum_fusion.1.x0_ref), channel_id=1, source_target_pairs={{0,6},{1,7},{2,0},{3,1},{4,2},{5,3},{6,4},{7,5},{8,14},{9,15},{10,... | collective-permute-start | bytes 786440 | tf_op jit(solution)/shard_map/ppermute | solution.py:200
  30.9 8.7 %collective-permute-start.4 = (bf16[4,512,128]{2,1,0:T(8,128)(2,1)S(1)}, bf16[4,512,128]{2,1,0:T(8,128)(2,1)S(1)}, u32[]{:S(2)}, u32[]{:S(2)}) collective-permute-start(bf16[4,512,128]{2,1,0:T(8,128)(2,1)S(1)} %pad_maximum_fusion), channel_id=1, source_target_pairs={{0,8},{8,0},{16,24},{24,16},{32,40},{40,32},{48,56},{56,48},{64,72... | collective-permute-start | bytes 1572872 | tf_op jit(solution)/shard_map/ppermute | solution.py:204
  48.0 8.6 %copy-start.2 = (bf16[1024,12,128]{2,0,1:T(8,128)(2,1)S(1)}, bf16[1024,12,128]{2,0,1:T(8,128)(2,1)}, u32[]{:S(2)}) copy-start(bf16[1024,12,128]{2,0,1:T(8,128)(2,1)} %param.7) | copy-start | bytes 9437188
  59.1 9.2 %collective-permute-start.11 = (bf16[2,512,128]{2,1,0:T(8,128)(2,1)S(1)}, bf16[2,512,128]{2,1,0:T(8,128)(2,1)S(1)}, u32[]{:S(2)}, u32[]{:S(2)}) collective-permute-start(bf16[2,512,128]{2,1,0:T(8,128)(2,1)S(1)} %get-tuple-element.17), channel_id=1, source_target_pairs={{0,6},{1,7},{2,0},{3,1},{4,2},{5,3},{6,4},{7,5},{8,14},{9,15},{10,... | collective-permute-start | bytes 786440 | tf_op jit(solution)/shard_map/ppermute | solution.py:226
  61.4 10.7 %collective-permute-start.10 = (bf16[2,512,128]{2,1,0:T(8,128)(2,1)S(1)}, bf16[2,512,128]{2,1,0:T(8,128)(2,1)S(1)}, u32[]{:S(2)}, u32[]{:S(2)}) collective-permute-start(bf16[2,512,128]{2,1,0:T(8,128)(2,1)S(1)} %get-tuple-element.16), channel_id=1, source_target_pairs={{0,4},{1,5},{2,6},{3,7},{4,0},{5,1},{6,2},{7,3},{8,12},{9,13},{10,... | collective-permute-start | bytes 786440 | tf_op jit(solution)/shard_map/ppermute | solution.py:226
  63.2 12.2 %collective-permute-start.9 = (bf16[2,512,128]{2,1,0:T(8,128)(2,1)S(1)}, bf16[2,512,128]{2,1,0:T(8,128)(2,1)S(1)}, u32[]{:S(2)}, u32[]{:S(2)}) collective-permute-start(bf16[2,512,128]{2,1,0:T(8,128)(2,1)S(1)} %get-tuple-element.15), channel_id=1, source_target_pairs={{0,2},{1,3},{2,4},{3,5},{4,6},{5,7},{6,0},{7,1},{8,10},{9,11},{10,... | collective-permute-start | bytes 786440 | tf_op jit(solution)/shard_map/ppermute | solution.py:226
  63.2 23.2 %collective-permute-start.20 = (bf16[4,4,6,32,128]{4,3,2,1,0:T(8,128)(2,1)S(1)}, bf16[4,4,6,32,128]{4,3,2,1,0:T(8,128)(2,1)S(1)}, u32[]{:S(2)}, u32[]{:S(2)}) collective-permute-start(bf16[4,4,6,32,128]{4,3,2,1,0:T(8,128)(2,1)S(1)} %get-tuple-element.21), channel_id=1, source_target_pairs={{0,8},{8,0},{16,24},{24,16},{32,40},{40,32},{48,56},{56,48},{64,72... | collective-permute-start | bytes 2359304 | tf_op jit(solution)/shard_map/ppermute | solution.py:212
  63.2 27.0 %collective-permute-start.13 = (bf16[4,4,6,32,128]{4,3,2,1,0:T(8,128)(2,1)S(1)}, bf16[4,4,6,32,128]{4,3,2,1,0:T(8,128)(2,1)S(1)}, u32[]{:S(2)}, u32[]{:S(2)}) collective-permute-start(bf16[4,4,6,32,128]{4,3,2,1,0:T(8,128)(2,1)S(1)} %get-tuple-element.19), channel_id=1, source_target_pairs={{0,8},{8,0},{16,24},{24,16},{32,40},{40,32},{48,56},{56,48},{64,72... | collective-permute-start | bytes 2359304 | tf_op jit(solution)/shard_map/ppermute | solution.py:212
  75.5 10.2 %collective-permute-start.12 = (bf16[512,128]{1,0:T(8,128)(2,1)S(1)}, bf16[512,128]{1,0:T(8,128)(2,1)S(1)}, u32[]{:S(2)}, u32[]{:S(2)}) collective-permute-start(bf16[512,128]{1,0:T(8,128)(2,1)S(1)} %fusion.12), channel_id=1, source_target_pairs={{0,1},{1,0},{2,3},{3,2},{4,5},{5,4},{6,7},{7,6},{8,9},{9,8},{10,11... | collective-permute-start | bytes 393224 | tf_op jit(solution)/shard_map/ppermute | solution.py:227
  86.6 14.0 %collective-permute-start.23 = (bf16[4,6,32,128]{3,2,1,0:T(8,128)(2,1)S(1)}, bf16[4,6,32,128]{3,2,1,0:T(8,128)(2,1)S(1)}, u32[]{:S(2)}, u32[]{:S(2)}) collective-permute-start(bf16[4,6,32,128]{3,2,1,0:T(8,128)(2,1)S(1)} %get-tuple-element.32), channel_id=1, source_target_pairs={{0,192},{8,200},{16,208},{24,216},{32,224},{40,232},{48,240},{56,2... | collective-permute-start | bytes 589832 | tf_op jit(solution)/shard_map/ppermute | solution.py:216
  87.5 13.2 %collective-permute-start.22 = (bf16[4,6,32,128]{3,2,1,0:T(8,128)(2,1)S(1)}, bf16[4,6,32,128]{3,2,1,0:T(8,128)(2,1)S(1)}, u32[]{:S(2)}, u32[]{:S(2)}) collective-permute-start(bf16[4,6,32,128]{3,2,1,0:T(8,128)(2,1)S(1)} %get-tuple-element.33), channel_id=1, source_target_pairs={{0,128},{8,136},{16,144},{24,152},{32,160},{40,168},{48,176},{56,1... | collective-permute-start | bytes 589832 | tf_op jit(solution)/shard_map/ppermute | solution.py:216
  87.5 13.4 %collective-permute-start.21 = (bf16[4,6,32,128]{3,2,1,0:T(8,128)(2,1)S(1)}, bf16[4,6,32,128]{3,2,1,0:T(8,128)(2,1)S(1)}, u32[]{:S(2)}, u32[]{:S(2)}) collective-permute-start(bf16[4,6,32,128]{3,2,1,0:T(8,128)(2,1)S(1)} %get-tuple-element.31), channel_id=1, source_target_pairs={{0,64},{8,72},{16,80},{24,88},{32,96},{40,104},{48,112},{56,120},{... | collective-permute-start | bytes 589832 | tf_op jit(solution)/shard_map/ppermute | solution.py:216
  90.4 16.1 %collective-permute-start.16 = (bf16[4,6,32,128]{3,2,1,0:T(8,128)(2,1)S(1)}, bf16[4,6,32,128]{3,2,1,0:T(8,128)(2,1)S(1)}, u32[]{:S(2)}, u32[]{:S(2)}) collective-permute-start(bf16[4,6,32,128]{3,2,1,0:T(8,128)(2,1)S(1)} %get-tuple-element.29), channel_id=1, source_target_pairs={{0,192},{8,200},{16,208},{24,216},{32,224},{40,232},{48,240},{56,2... | collective-permute-start | bytes 589832 | tf_op jit(solution)/shard_map/ppermute | solution.py:216
  91.1 16.7 %collective-permute-start.15 = (bf16[4,6,32,128]{3,2,1,0:T(8,128)(2,1)S(1)}, bf16[4,6,32,128]{3,2,1,0:T(8,128)(2,1)S(1)}, u32[]{:S(2)}, u32[]{:S(2)}) collective-permute-start(bf16[4,6,32,128]{3,2,1,0:T(8,128)(2,1)S(1)} %get-tuple-element.30), channel_id=1, source_target_pairs={{0,128},{8,136},{16,144},{24,152},{32,160},{40,168},{48,176},{56,1... | collective-permute-start | bytes 589832 | tf_op jit(solution)/shard_map/ppermute | solution.py:216
  100.7 7.1 %collective-permute-start.14 = (bf16[4,6,32,128]{3,2,1,0:T(8,128)(2,1)S(1)}, bf16[4,6,32,128]{3,2,1,0:T(8,128)(2,1)S(1)}, u32[]{:S(2)}, u32[]{:S(2)}) collective-permute-start(bf16[4,6,32,128]{3,2,1,0:T(8,128)(2,1)S(1)} %get-tuple-element.28), channel_id=1, source_target_pairs={{0,64},{8,72},{16,80},{24,88},{32,96},{40,104},{48,112},{56,120},{... | collective-permute-start | bytes 589832 | tf_op jit(solution)/shard_map/ppermute | solution.py:216
  101.0 12.4 %collective-permute-start.26 = (bf16[6,32,128]{2,1,0:T(8,128)(2,1)S(1)}, bf16[6,32,128]{2,1,0:T(8,128)(2,1)S(1)}, u32[]{:S(2)}, u32[]{:S(2)}) collective-permute-start(bf16[6,32,128]{2,1,0:T(8,128)(2,1)S(1)} %get-tuple-element.38), channel_id=1, source_target_pairs={{0,48},{8,56},{16,0},{24,8},{32,16},{40,24},{48,32},{56,40},{64,11... | collective-permute-start | bytes 147464 | tf_op jit(solution)/shard_map/ppermute | solution.py:219
  104.2 9.8 %collective-permute-start.25 = (bf16[6,32,128]{2,1,0:T(8,128)(2,1)S(1)}, bf16[6,32,128]{2,1,0:T(8,128)(2,1)S(1)}, u32[]{:S(2)}, u32[]{:S(2)}) collective-permute-start(bf16[6,32,128]{2,1,0:T(8,128)(2,1)S(1)} %get-tuple-element.39), channel_id=1, source_target_pairs={{0,32},{8,40},{16,48},{24,56},{32,0},{40,8},{48,16},{56,24},{64,96... | collective-permute-start | bytes 147464 | tf_op jit(solution)/shard_map/ppermute | solution.py:219
  106.5 7.5 %collective-permute-start.24 = (bf16[6,32,128]{2,1,0:T(8,128)(2,1)S(1)}, bf16[6,32,128]{2,1,0:T(8,128)(2,1)S(1)}, u32[]{:S(2)}, u32[]{:S(2)}) collective-permute-start(bf16[6,32,128]{2,1,0:T(8,128)(2,1)S(1)} %get-tuple-element.37), channel_id=1, source_target_pairs={{0,16},{8,24},{16,32},{24,40},{32,48},{40,56},{48,0},{56,8},{64,80... | collective-permute-start | bytes 147464 | tf_op jit(solution)/shard_map/ppermute | solution.py:219
  107.9 6.3 %collective-permute-start.19 = (bf16[6,32,128]{2,1,0:T(8,128)(2,1)S(1)}, bf16[6,32,128]{2,1,0:T(8,128)(2,1)S(1)}, u32[]{:S(2)}, u32[]{:S(2)}) collective-permute-start(bf16[6,32,128]{2,1,0:T(8,128)(2,1)S(1)} %get-tuple-element.35), channel_id=1, source_target_pairs={{0,48},{8,56},{16,0},{24,8},{32,16},{40,24},{48,32},{56,40},{64,11... | collective-permute-start | bytes 147464 | tf_op jit(solution)/shard_map/ppermute | solution.py:219
  111.4 6.0 %collective-permute-start.18 = (bf16[6,32,128]{2,1,0:T(8,128)(2,1)S(1)}, bf16[6,32,128]{2,1,0:T(8,128)(2,1)S(1)}, u32[]{:S(2)}, u32[]{:S(2)}) collective-permute-start(bf16[6,32,128]{2,1,0:T(8,128)(2,1)S(1)} %get-tuple-element.36), channel_id=1, source_target_pairs={{0,32},{8,40},{16,48},{24,56},{32,0},{40,8},{48,16},{56,24},{64,96... | collective-permute-start | bytes 147464 | tf_op jit(solution)/shard_map/ppermute | solution.py:219
  113.4 5.9 %collective-permute-start.17 = (bf16[6,32,128]{2,1,0:T(8,128)(2,1)S(1)}, bf16[6,32,128]{2,1,0:T(8,128)(2,1)S(1)}, u32[]{:S(2)}, u32[]{:S(2)}) collective-permute-start(bf16[6,32,128]{2,1,0:T(8,128)(2,1)S(1)} %get-tuple-element.34), channel_id=1, source_target_pairs={{0,16},{8,24},{16,32},{24,40},{32,48},{40,56},{48,0},{56,8},{64,80... | collective-permute-start | bytes 147464 | tf_op jit(solution)/shard_map/ppermute | solution.py:219

commit v2 on v1

v2 whole, which is shorter than its diff:
```python
import functools

import jax
import jax.numpy as jnp
from jax import lax
from jax.experimental import pallas as pl
from jax.experimental.pallas import tpu as pltpu
from jax.sharding import PartitionSpec as P

BF16, F32 = jnp.bfloat16, jnp.float32
ROWS = 64
LANE = 128
NX, NZ_HI, NY, NZ_LO, NCORE = 4, 2, 4, 4, 2
CHIPS = NY * NZ_LO
VMEM_LIMIT = 20 * 1024 * 1024
LARGE_COST = pl.CostEstimate(flops=4_000_000_000, bytes_accessed=8_000_000, transcendentals=0)
SMALL_COST = pl.CostEstimate(flops=1000, bytes_accessed=1000, transcendentals=0)


def ctx_of(y, z, core):
    return (y * NZ_LO + z) * NCORE + core


CTX = [(y, z, core) for y in range(NY) for z in range(NZ_LO) for core in range(NCORE)]
TP = [(x, z) for x in range(NX) for z in range(NZ_HI)]
CORE_SWAP = [(ctx_of(y, z, c), ctx_of(y, z, 1 - c)) for y, z, c in CTX]
Z_HI_SWAP = [(x * NZ_HI + z, x * NZ_HI + 1 - z) for x, z in TP]


def ring_partner(at, crossed):
    return NX - 1 - at if crossed else at ^ 1


def ring_slots(at, crossed):
    near, far = ring_partner(at, crossed), ring_partner(at, not crossed)
    return at, far, near, ring_partner(near, not crossed)


def y_swap(crossed):
    return [(ctx_of(y, z, c), ctx_of(ring_partner(y, crossed), z, c)) for y, z, c in CTX]


def x_swap(crossed):
    return [(x * NZ_HI + z, ring_partner(x, crossed) * NZ_HI + z) for x, z in TP]


def z_swap(bit):
    return [(ctx_of(y, z, c), ctx_of(y, z ^ bit, c)) for y, z, c in CTX]


def along_x(steps):
    return [(x * NZ_HI + z, (x + steps) % NX * NZ_HI + z) for x, z in TP]


def from_later_chip(steps):
    return [
        (NCORE * (chip + steps) + core, NCORE * chip + core)
        for chip in range(CHIPS - steps)
        for core in range(NCORE)
    ]


def table_kernel(filters_ref, near_ref, *far_refs):
    filt_count, rows, near = near_ref.shape
    per_group, _, far = far_refs[0].shape
    taps = filters_ref.shape[1]
    width = near + far
    for k in range(filt_count):
        line = filters_ref[k : k + 1, :].astype(F32)
        line = jnp.concatenate([line, jnp.zeros((1, width - taps), F32)], axis=1)
        block = jnp.broadcast_to(line, (rows, width))
        block = pltpu.roll(block, 0, 1, stride=1, stride_axis=0).astype(BF16)
        near_ref[k] = block[:, :near]
        far_refs[k // per_group][k % per_group] = block[:, near:]


def toeplitz_tables(filters, groups):
    filt_count, taps = filters.shape
    near, far = taps // 2, taps // 2 + LANE
    vmem = pl.BlockSpec(memory_space=pltpu.VMEM)
    outs = [jax.ShapeDtypeStruct((filt_count, ROWS, near), BF16)]
    outs += [jax.ShapeDtypeStruct((filt_count // groups, ROWS, far), BF16)] * groups
    return pl.pallas_call(
        table_kernel,
        out_shape=outs,
        in_specs=[vmem],
        out_specs=[vmem] * (1 + groups),
        compiler_params=pltpu.CompilerParams(vmem_limit_bytes=VMEM_LIMIT),
        cost_estimate=LARGE_COST,
        name="tables",
    )(filters)


def pair_of_blocks(grad_ref, start, rows, width):
    first = grad_ref[pl.ds(start, width), :]
    second = grad_ref[pl.ds(start + rows, width), :]
    return jnp.concatenate([first, second], axis=1)


def near_kernel(table_ref, own_ref, r1_ref, r2_ref, swapped_ref, *refs):
    acc_refs, grad_ref = refs[:-1], refs[-1]
    filt_count, rows, width = table_ref.shape
    tok = own_ref.shape[0]
    for s, part in enumerate((own_ref, r1_ref, r2_ref)):
        grad_ref[2 * s * tok : (2 * s + 1) * tok, :] = part[...]
    for s in range(2):
        grad_ref[(2 * s + 1) * tok : (2 * s + 2) * tok, :] = swapped_ref[s]
    table = table_ref[...].reshape(filt_count * rows, width)

    @pl.loop(0, tok // (2 * rows))
    def _(pair):
        start = pl.multiple_of(pair * (2 * rows), 2 * rows)
        both = pair_of_blocks(grad_ref, start, rows, width)
        result = jnp.dot(table, both, preferred_element_type=F32)
        part = acc_refs[0].shape[1]
        for group, acc_ref in enumerate(acc_refs):
            acc_ref[pair] = result[group * part : (group + 1) * part]


def near_conv(table, near_halo, swapped, groups):
    filt_count, rows, width = table.shape
    tok = near_halo[0].shape[0]
    vmem = pl.BlockSpec(memory_space=pltpu.VMEM)
    acc = jax.ShapeDtypeStruct((tok // (2 * rows), filt_count // groups * rows, 2 * LANE), F32)
    return pl.pallas_call(
        near_kernel,
        out_shape=[acc] * groups,
        in_specs=[vmem] * 5,
        out_specs=[vmem] * groups,
        scratch_shapes=[pltpu.VMEM((5 * tok, LANE), BF16)],
        compiler_params=pltpu.CompilerParams(vmem_limit_bytes=VMEM_LIMIT),
        cost_estimate=LARGE_COST,
        name="near_conv",
    )(table, *near_halo, swapped)


def conv_kernel(
    crossed, pos_ref, table_ref, acc_ref, r2_ref, r3_ref, r4_ref, swapped_ref,
    x0_ref, x1_ref, x2_ref, x3_ref,
    corr_ref, keep_ref, send_ref, grad_ref, full_ref,
):
    filt_count, rows, width = table_ref.shape
    tok = r2_ref.shape[0]
    x, z_hi = pos_ref[0] // NZ_HI, lax.rem(pos_ref[0], NZ_HI)
    y, z_lo, core = pos_ref[1] // (NZ_LO * NCORE), lax.rem(pos_ref[1] // NCORE, NZ_LO), lax.rem(pos_ref[1], NCORE)
    for s, part in enumerate((r2_ref, r3_ref, r4_ref)):
        grad_ref[2 * s * tok : (2 * s + 1) * tok, :] = part[...]
    for s in range(2):
        grad_ref[(2 * s + 1) * tok : (2 * s + 2) * tok, :] = swapped_ref[s]
    grad_ref[5 * tok :, :] = jnp.zeros((grad_ref.shape[0] - 5 * tok, LANE), BF16)
    table = table_ref[...].reshape(filt_count * rows, width)

    @pl.loop(0, tok // (2 * rows))
    def _(pair):
        start = pl.multiple_of(pair * (2 * rows), 2 * rows)
        both = pair_of_blocks(grad_ref, start, rows, width)
        result = jnp.dot(table, both, preferred_element_type=F32)
        result = (result + acc_ref[pair]).astype(BF16)
        for k in range(filt_count):
            for half in range(2):
                corr_ref[pl.ds(start + half * rows, rows), k * LANE : (k + 1) * LANE] = result[
                    k * rows : (k + 1) * rows, half * LANE : (half + 1) * LANE
                ]

    for s, part in enumerate((x0_ref, x1_ref, x2_ref, x3_ref)):
        for h in range(NZ_HI):
            at = lax.rem(x + NX - s, NX) * NZ_HI + lax.rem(z_hi + h, NZ_HI)
            full_ref[:, pl.ds(pl.multiple_of(at * LANE, LANE), LANE)] = part[h]

    deep = NZ_LO * NCORE * 32

    for s, at in enumerate(ring_slots(y, crossed)):
        part = full_ref[:, pl.ds(pl.multiple_of(at * deep, deep), deep)]
        result = lax.dot_general(
            part, corr_ref[...], (((0,), (0,)), ((), ())), preferred_element_type=F32
        ).astype(BF16)
        for z in range(NZ_LO):
            slot = z ^ z_lo
            for k in range(filt_count):
                columns = slice(k * LANE, (k + 1) * LANE)
                even = result[z * 64 : z * 64 + 32, columns]
                odd = result[z * 64 + 32 : z * 64 + 64, columns]
                keep_ref[s, slot, k] = jnp.where(core == 0, even, odd)
                send_ref[s, slot, k] = jnp.where(core == 0, odd, even)


def conv_and_product(crossed, pos, table, acc, far_halo, swapped, gathered):
    filt_count, rows, width = table.shape
    tok = far_halo[0].shape[0]
    part = jax.ShapeDtypeStruct((NY, NZ_LO, filt_count, 32, LANE), BF16)
    vmem = pl.BlockSpec(memory_space=pltpu.VMEM)
    return pl.pallas_call(
        functools.partial(conv_kernel, crossed),
        out_shape=(jax.ShapeDtypeStruct((tok, filt_count * LANE), BF16), part, part),
        in_specs=[pl.BlockSpec(memory_space=pltpu.SMEM)] + [vmem] * 10,
        out_specs=(vmem,) * 3,
        scratch_shapes=[
            pltpu.VMEM((5 * tok + rows, LANE), BF16),
            pltpu.VMEM((tok, 1024), BF16),
        ],
        compiler_params=pltpu.CompilerParams(vmem_limit_bytes=VMEM_LIMIT),
        cost_estimate=SMALL_COST,
        name="conv_product",
    )(pos, table, acc, *far_halo, swapped, *gathered)


def share_kernel(pos_ref, _, *refs):
    corr_refs, proj_ref = refs[:-6], refs[-6]
    near_keep, near_send, far_keep, far_send, all_ref = refs[-5:]
    filt_count = proj_ref.shape[0]
    x, z_hi = pos_ref[0] // NZ_HI, lax.rem(pos_ref[0], NZ_HI)
    at = 0
    for part in corr_refs:
        all_ref[:, at : at + part.shape[1]] = part[...]
        at += part.shape[1]
    wide = NZ_HI * LANE
    near_slots = (near_keep, 0), (near_send, 0), (near_keep, 1), (near_send, 1)
    far_slots = (far_keep, 0), (far_keep, 1), (far_send, 0), (far_send, 1)
    for at, near, far in zip(ring_slots(x, False), near_slots, far_slots):
        base = pl.multiple_of(at * wide, wide)
        weights = jnp.concatenate(
            [proj_ref[k, pl.ds(base, wide), :] for k in range(filt_count)], axis=1
        )
        result = lax.dot_general(
            all_ref[...], weights, (((1,), (1,)), ((), ())), preferred_element_type=F32
        )
        low, high = result[:, :LANE], result[:, LANE:]
        near[0][near[1]] = jnp.where(z_hi == 0, low, high).astype(near[0].dtype)
        far[0][far[1]] = jnp.where(z_hi == 0, high, low).astype(far[0].dtype)


def input_shares(pos, after, corrs, projection):
    tok = corrs[0].shape[0]
    filt_count = projection.shape[0]
    vmem = pl.BlockSpec(memory_space=pltpu.VMEM)
    keep = jax.ShapeDtypeStruct((2, tok, LANE), F32)
    send = jax.ShapeDtypeStruct((2, tok, LANE), BF16)
    return pl.pallas_call(
        share_kernel,
        out_shape=(keep, send, keep, send),
        in_specs=[pl.BlockSpec(memory_space=pltpu.SMEM), pl.BlockSpec(memory_space=pl.ANY)]
        + [vmem] * (len(corrs) + 1),
        out_specs=(vmem,) * 4,
        scratch_shapes=[pltpu.VMEM((tok, filt_count * LANE), BF16)],
        compiler_params=pltpu.CompilerParams(vmem_limit_bytes=VMEM_LIMIT),
        cost_estimate=SMALL_COST,
        name="input_shares",
    )(pos, after, *corrs, projection)


GROUPS = 2


def per_device(inputs, grad_out, filters, projection):
    tp, ctx = lax.axis_index("tp"), lax.axis_index("ctx")
    first_core = lax.rem(ctx, NCORE) == 0
    pos = jnp.stack([tp, ctx]).astype(jnp.int32)

    halo = [grad_out] + [lax.ppermute(grad_out, "ctx", from_later_chip(s)) for s in range(1, 5)]
    pair = jnp.stack([inputs, lax.ppermute(inputs, "tp", Z_HI_SWAP)])
    gathered = [pair] + [lax.ppermute(pair, "tp", along_x(s)) for s in range(1, NX)]
    near_table, *far_tables = toeplitz_tables(filters, GROUPS)
    swapped = []
    for at in (0, 2):
        sent = jnp.stack([jnp.where(first_core, halo[s + 1], halo[s]) for s in (at, at + 1)])
        swapped.append(lax.ppermute(sent, "ctx", CORE_SWAP))
    accs = near_conv(near_table, halo[:3], swapped[0], GROUPS)

    corrs, columns = [], []
    for group, (table, acc) in enumerate(zip(far_tables, accs)):
        crossed = group % 2 == 1
        corr, keep, send = conv_and_product(
            crossed, pos, table, acc, halo[2:], swapped[1], gathered
        )
        corrs.append(corr)
        other = lax.ppermute(send, "ctx", CORE_SWAP)
        leave = (keep[2:].astype(F32) + other[2:].astype(F32)).astype(BF16)
        stay = keep[:2].astype(F32) + other[:2].astype(F32)
        columns.append((crossed, stay, leave))

    near, near_send, far, far_send = input_shares(
        pos, columns[0][2], corrs, projection.transpose(1, 0, 2)
    )
    gradients = []
    for crossed, stay, leave in columns:
        stay = stay + lax.ppermute(leave, "ctx", y_swap(crossed)).astype(F32)
        leave = stay[1].astype(BF16)
        stay = stay[0] + lax.ppermute(leave, "ctx", y_swap(not crossed)).astype(F32)
        leave = jnp.stack([stay[1], stay[3]]).astype(BF16)
        stay = jnp.stack([stay[0], stay[2]])
        stay = stay + lax.ppermute(leave, "ctx", z_swap(1)).astype(F32)
        leave = stay[1].astype(BF16)
        gradients.append(stay[0] + lax.ppermute(leave, "ctx", z_swap(2)).astype(F32))
    grad_proj = jnp.concatenate(gradients, axis=0).transpose(1, 0, 2)

    far = far + lax.ppermute(far_send, "tp", x_swap(False)).astype(F32)
    far = far[0] + lax.ppermute(far[1].astype(BF16), "tp", x_swap(True)).astype(F32)
    near = near + lax.ppermute(near_send, "tp", x_swap(True)).astype(F32)
    near = near[0] + lax.ppermute(near[1].astype(BF16), "tp", x_swap(False)).astype(F32)
    far = lax.ppermute(far.astype(BF16), "tp", Z_HI_SWAP)
    grad_input = (near + far.astype(F32)).astype(BF16)
    return grad_input, grad_proj


def solution(mesh):
    return jax.shard_map(
        per_device,
        mesh=mesh,
        in_specs=(P("ctx", "tp"), P("ctx", "tp"), P(), P(None, None, "tp")),
        out_specs=(P("ctx", "tp"), P("ctx", None, "tp")),
        check_vma=False,
    )
```

time: 121 us -> 98.5 us (0.81)
  waiting for transfers between devices: 35.7 us -> 21.3 us
  Pallas kernels: 23.9 us -> 19.5 us
  starting transfers between devices: 50.1 us -> 46.8 us
  local copies, waits for them, and re-layouts: 7.13 us -> 4.6 us
  other arithmetic: 2.28 us -> 4.42 us
    ppermute x17 -> x15, waiting for transfers between devices: 33.3 us -> 17.6 us  [the longest x1 4.82 us: per_device(): far = far + lax.ppermute(far_send, 'tp', x_swap(False)).astype(F32)]
    slice x1 -> x4, local copies, waits for them, and re-layouts: 6.09 us -> 0.05 us  [the longest x2 0.03 us: per_device(): stay = jnp.stack([stay[0], stay[2]])]
    pallas_call x4 -> x5, Pallas kernels: 23.9 us -> 19.5 us  [the longest x2 10.4 us: conv_and_product(): pl.pallas_call(functools.partial(conv_kernel, crossed), out_shape=(jax.Sh...]
    ppermute x17 -> x15, starting transfers between devices: 24.9 us -> 20.7 us  [the longest x1 4.62 us: per_device(): far = lax.ppermute(far.astype(BF16), 'tp', Z_HI_SWAP)]
    unnamed x8 -> x12, local copies, waits for them, and re-layouts: 0.91 us -> 4.44 us
    ppermute x4, starting transfers between devices: 11.6 us -> 14.1 us  [per_device(): lax.ppermute(grad_out, 'ctx', from_later_chip(s))]
    ppermute x1, starting transfers between devices: 7.28 us -> 5.39 us  [per_device(): pair = jnp.stack([inputs, lax.ppermute(inputs, 'tp', Z_HI_SWAP)])]
    ppermute x3, waiting for transfers between devices: 2.38 us -> 3.74 us  [per_device(): lax.ppermute(pair, 'tp', along_x(s))]
  transfers between devices with their start and end apart: 27 -> 25, of which waited for: 11 -> 9; matrix products, arithmetic and copies ran while one was open for 6% -> 4% of each run, Pallas kernels for 4% -> 15%
where the time goes in v2:
time: 98.5 us; the launch traced here: 97.8 us
  starting transfers between devices  46.8 us (48%)
  waiting for transfers between devices  21.3 us (22%)
  Pallas kernels  19.5 us (20%)
  local copies, waits for them, and re-layouts  4.6 us (5%)
  other arithmetic  4.42 us (4%)
  between operations  1.01 us (1%)
    ppermute x4, starting transfers between devices, per_device(): lax.ppermute(grad_out, 'ctx', from_later_chip(s))  14.1 us
    pallas_call x2, Pallas kernels, conv_and_product(): pl.pallas_call(functools.partial(conv_kernel, crossed), out_shape=(jax.Sh...  10.4 us
    ppermute x3, starting transfers between devices, per_device(): lax.ppermute(pair, 'tp', along_x(s))  5.73 us
    ppermute x1, starting transfers between devices, per_device(): pair = jnp.stack([inputs, lax.ppermute(inputs, 'tp', Z_HI_SWAP)])  5.39 us
    pallas_call x1, Pallas kernels, near_conv(): pl.pallas_call(near_kernel, out_shape=[acc] * groups, in_specs=[vmem] * 5...  5.06 us
    ppermute x1, waiting for transfers between devices, per_device(): far = far + lax.ppermute(far_send, 'tp', x_swap(False)).astype(F32)  4.82 us
    ppermute x1, starting transfers between devices, per_device(): far = lax.ppermute(far.astype(BF16), 'tp', Z_HI_SWAP)  4.62 us
    unnamed x12, local copies, waits for them, and re-layouts  4.44 us
  transfers between devices with their start and end apart: 25, of which 9 were waited for; matrix products, arithmetic and copies ran while one was open for 4% of the time, Pallas kernels for 15%

profile of v2, /device:TPU:24, one launch (start us, length us, event | category | flops | bytes accessed | tf_op | source)
XLA Modules:
  0.0 97.8 jit_solution(9039058737432387776)
XLA Ops:
  0.6 6.7 %collective-permute-start = (bf16[512,128]{1,0:T(8,128)(2,1)}, bf16[512,128]{1,0:T(8,128)(2,1)}, u32[]{:S(2)}, u32[]{:S(2)}) collective-permute-start(bf16[512,128]{1,0:T(8,128)(2,1)} %own_ref.1), channel_id=1, source_target_pairs={{16,0},{24,8},{32,16},{40,24},{48,32},{56,40},{64,48},{72,56},{80,... | collective-permute-start | bytes 393224 | tf_op jit(solution)/shard_map/ppermute | solution.py:259
  7.4 1.9 %collective-permute-start.1 = (bf16[512,128]{1,0:T(8,128)(2,1)}, bf16[512,128]{1,0:T(8,128)(2,1)S(1)}, u32[]{:S(2)}, u32[]{:S(2)}) collective-permute-start(bf16[512,128]{1,0:T(8,128)(2,1)} %own_ref.1), channel_id=1, source_target_pairs={{32,0},{40,8},{48,16},{56,24},{64,32},{72,40},{80,48},{88,56},{96,... | collective-permute-start | bytes 393224 | tf_op jit(solution)/shard_map/ppermute | solution.py:259
  9.3 2.5 %collective-permute-start.3 = (bf16[512,128]{1,0:T(8,128)(2,1)}, bf16[512,128]{1,0:T(8,128)(2,1)}, u32[]{:S(2)}, u32[]{:S(2)}) collective-permute-start(bf16[512,128]{1,0:T(8,128)(2,1)} %own_ref.1), channel_id=1, source_target_pairs={{48,0},{56,8},{64,16},{72,24},{80,32},{88,40},{96,48},{104,56},{11... | collective-permute-start | bytes 393224 | tf_op jit(solution)/shard_map/ppermute | solution.py:259
  11.7 3.0 %collective-permute-start.4 = (bf16[512,128]{1,0:T(8,128)(2,1)}, bf16[512,128]{1,0:T(8,128)(2,1)}, u32[]{:S(2)}, u32[]{:S(2)}) collective-permute-start(bf16[512,128]{1,0:T(8,128)(2,1)} %own_ref.1), channel_id=1, source_target_pairs={{64,0},{72,8},{80,16},{88,24},{96,32},{104,40},{112,48},{120,56},{... | collective-permute-start | bytes 393224 | tf_op jit(solution)/shard_map/ppermute | solution.py:259
  14.8 5.4 %collective-permute-start.6 = (bf16[512,128]{1,0:T(8,128)(2,1)}, bf16[512,128]{1,0:T(8,128)(2,1)}, u32[]{:S(2)}, u32[]{:S(2)}) collective-permute-start(bf16[512,128]{1,0:T(8,128)(2,1)} %param.4), channel_id=1, source_target_pairs={{0,1},{1,0},{2,3},{3,2},{4,5},{5,4},{6,7},{7,6},{8,9},{9,8},{10,11... | collective-permute-start | bytes 393224 | tf_op jit(solution)/shard_map/ppermute | solution.py:260
  20.2 0.9 copy-done.2
  21.1 1.7 %tables.1 = (bf16[12,64,2048]{2,1,0:T(8,128)(2,1)S(1)}, bf16[6,64,2176]{2,1,0:T(8,128)(2,1)S(1)}, bf16[6,64,2176]{2,1,0:T(8,128)(2,1)S(1)}) custom-call(bf16[12,4096]{1,0:T(8,128)(2,1)S(1)} %copy-done.2), custom_call_target="tpu_custom_call" | custom-call | flops 4000000000 | bytes 8000000 | tf_op jit(solution)/shard_map/tables/pallas_call | solution.py:83
  22.8 1.6 %copy-done.3 = bf16[12,64,2048]{2,1,0:T(8,128)(2,1)} copy-done((bf16[12,64,2048]{2,1,0:T(8,128)(2,1)}, bf16[12,64,2048]{2,1,0:T(8,128)(2,1)S(1)}, u32[]{:S(2)}) %copy-start.3) | copy-done | bytes 3145752
  24.4 0.0 collective-permute-done.r1_ref
  24.5 0.0 collective-permute-done.1.r2_ref
  24.5 0.0 collective-permute-done.3.r3_ref
  24.5 0.0 collective-permute-done.4.r4_ref
  24.5 1.1 %select_bitcast_fusion.1 = (bf16[1,512,128]{2,1,0:T(8,128)(2,1)S(1)}, bf16[1,512,128]{2,1,0:T(8,128)(2,1)S(1)}, bf16[1,512,128]{2,1,0:T(8,128)(2,1)S(1)}, bf16[1,512,128]{2,1,0:T(8,128)(2,1)S(1)}) fusion(bf16[512,128]{1,0:T(8,128)(2,1)} %collective-permute-done.3.r3_ref, bf16[512,128]{1,0:T(8,128)(2,1)S(1)} %collective-permute-done.1.r2_ref, pred[]{:T(512)S(6)} %eq.3, ...), kind=kLoop, calls=%fused_computation.32 | loop fusion | flops 262144 | bytes 1179649 | tf_op jit(solution)/shard_map/stack | solution.py:265
  25.6 0.1 collective-permute-start.2
  25.8 0.1 pad_add_fusion.pos_ref
  25.8 0.0 collective-permute-done.6
  25.8 0.9 pad_maximum_fusion.2.x0_ref
  26.8 1.6 %collective-permute-start.7 = (bf16[2,512,128]{2,1,0:T(8,128)(2,1)S(1)}, bf16[2,512,128]{2,1,0:T(8,128)(2,1)S(1)}, u32[]{:S(2)}, u32[]{:S(2)}) collective-permute-start(bf16[2,512,128]{2,1,0:T(8,128)(2,1)S(1)} %pad_maximum_fusion.2.x0_ref), channel_id=1, source_target_pairs={{0,2},{1,3},{2,4},{3,5},{4,6},{5,7},{6,0},{7,1},{8,10},{9,11},{10,... | collective-permute-start | bytes 786440 | tf_op jit(solution)/shard_map/ppermute | solution.py:261
  28.3 2.7 %collective-permute-start.8 = (bf16[2,512,128]{2,1,0:T(8,128)(2,1)S(1)}, bf16[2,512,128]{2,1,0:T(8,128)(2,1)S(1)}, u32[]{:S(2)}, u32[]{:S(2)}) collective-permute-start(bf16[2,512,128]{2,1,0:T(8,128)(2,1)S(1)} %pad_maximum_fusion.2.x0_ref), channel_id=1, source_target_pairs={{0,4},{1,5},{2,6},{3,7},{4,0},{5,1},{6,2},{7,3},{8,12},{9,13},{10,... | collective-permute-start | bytes 786440 | tf_op jit(solution)/shard_map/ppermute | solution.py:261
  31.1 1.4 %collective-permute-start.9 = (bf16[2,512,128]{2,1,0:T(8,128)(2,1)S(1)}, bf16[2,512,128]{2,1,0:T(8,128)(2,1)S(1)}, u32[]{:S(2)}, u32[]{:S(2)}) collective-permute-start(bf16[2,512,128]{2,1,0:T(8,128)(2,1)S(1)} %pad_maximum_fusion.2.x0_ref), channel_id=1, source_target_pairs={{0,6},{1,7},{2,0},{3,1},{4,2},{5,3},{6,4},{7,5},{8,14},{9,15},{10,... | collective-permute-start | bytes 786440 | tf_op jit(solution)/shard_map/ppermute | solution.py:261
  32.5 0.1 collective-permute-start.5
  32.6 0.0 collective-permute-done.2.swapped_ref
  32.7 1.9 %copy-done.4 = bf16[12,64,2048]{2,1,0:T(8,128)(2,1)S(1)} copy-done((bf16[12,64,2048]{2,1,0:T(8,128)(2,1)S(1)}, bf16[12,64,2048]{2,1,0:T(8,128)(2,1)}, u32[]{:S(2)}) %copy-start.4) | copy-done | bytes 3145752
  34.5 5.1 %near_conv.1 = (f32[4,384,256]{2,1,0:T(8,128)S(1)}, f32[4,384,256]{2,1,0:T(8,128)S(1)}) custom-call(bf16[12,64,2048]{2,1,0:T(8,128)(2,1)S(1)} %copy-done.4, bf16[512,128]{1,0:T(8,128)(2,1)S(1)} %copy-done.1, bf16[512,128]{1,0:T(8,128)(2,1)} %collective-permute-done.r1_ref, bf16[512,128]{1,0:T(8,128)(2,1)S(1)} %collective-permute-done.1.r2_ref, ...), custom_call_target="tpu_custom_call" | custom-call | flops 4000000000 | bytes 8000000 | tf_op jit(solution)/shard_map/near_conv/pallas_call | solution.py:125
  39.6 0.0 collective-permute-done.5.swapped_ref
  39.6 0.0 collective-permute-done.7.x1_ref
  39.6 3.7 %collective-permute-done.8.x2_ref = bf16[2,512,128]{2,1,0:T(8,128)(2,1)S(1)} collective-permute-done((bf16[2,512,128]{2,1,0:T(8,128)(2,1)S(1)}, bf16[2,512,128]{2,1,0:T(8,128)(2,1)S(1)}, u32[]{:S(2)}, u32[]{:S(2)}) %collective-permute-start.8) | collective-permute-done | bytes 262176 | tf_op jit(solution)/shard_map/ppermute | solution.py:261
  43.4 0.0 collective-permute-done.9.x3_ref
  43.4 5.1 %conv_product.2 = (bf16[512,768]{1,0:T(8,128)(2,1)S(1)}, bf16[4,4,6,32,128]{4,3,2,1,0:T(8,128)(2,1)S(1)}, bf16[4,4,6,32,128]{4,3,2,1,0:T(8,128)(2,1)S(1)}) custom-call(s32[2]{0:T(128)S(1)} %pad_add_fusion.pos_ref, bf16[6,64,2176]{2,1,0:T(8,128)(2,1)S(1)} %get-tuple-element.17.table_ref, f32[4,384,256]{2,1,0:T(8,128)S(1)} %get-tuple-element.19.acc_ref, ...), custom_call_target="tpu_custom_call" | custom-call | flops 1000 | bytes 1000 | tf_op jit(solution)/shard_map/conv_product/pallas_call | solution.py:192
  48.5 0.1 collective-permute-start.10
  48.6 0.0 copy-start
  48.6 5.3 %conv_product.3 = (bf16[512,768]{1,0:T(8,128)(2,1)S(1)}, bf16[4,4,6,32,128]{4,3,2,1,0:T(8,128)(2,1)S(1)}, bf16[4,4,6,32,128]{4,3,2,1,0:T(8,128)(2,1)S(1)}) custom-call(s32[2]{0:T(128)S(1)} %pad_add_fusion.pos_ref, bf16[6,64,2176]{2,1,0:T(8,128)(2,1)S(1)} %get-tuple-element.23.table_ref, f32[4,384,256]{2,1,0:T(8,128)S(1)} %get-tuple-element.24.acc_ref, ...), custom_call_target="tpu_custom_call" | custom-call | flops 1000 | bytes 1000 | tf_op jit(solution)/shard_map/conv_product/pallas_call | solution.py:192
  53.9 0.8 collective-permute-start.20
  54.7 0.1 add_convert_fusion.1._
  54.8 2.4 %input_shares.1 = (f32[2,512,128]{2,1,0:T(8,128)S(1)}, bf16[2,512,128]{2,1,0:T(8,128)(2,1)S(1)}, f32[2,512,128]{2,1,0:T(8,128)S(1)}, bf16[2,512,128]{2,1,0:T(8,128)(2,1)S(1)}) custom-call(s32[2]{0:T(128)S(1)} %pad_add_fusion.pos_ref, bf16[2,4,6,32,128]{4,3,2,1,0:T(8,128)(2,1)S(1)} %add_convert_fusion.1._, bf16[512,768]{1,0:T(8,128)(2,1)S(1)} %get-tuple-element.22.refs_0_, ...), custom_call_target="tpu_custom_call" | custom-call | flops 1000 | bytes 1000 | tf_op jit(solution)/shard_map/input_shares/pallas_call | solution.py:238
  57.2 1.4 %collective-permute-start.13 = (bf16[2,512,128]{2,1,0:T(8,128)(2,1)S(1)}, bf16[2,512,128]{2,1,0:T(8,128)(2,1)S(1)}, u32[]{:S(2)}, u32[]{:S(2)}) collective-permute-start(bf16[2,512,128]{2,1,0:T(8,128)(2,1)S(1)} %get-tuple-element.29), channel_id=1, source_target_pairs={{0,2},{1,3},{2,0},{3,1},{4,6},{5,7},{6,4},{7,5},{8,10},{9,11},{10,... | collective-permute-start | bytes 786440 | tf_op jit(solution)/shard_map/ppermute | solution.py:296
  58.6 1.9 %collective-permute-start.11 = (bf16[2,512,128]{2,1,0:T(8,128)(2,1)S(1)}, bf16[2,512,128]{2,1,0:T(8,128)(2,1)S(1)}, u32[]{:S(2)}, u32[]{:S(2)}) collective-permute-start(bf16[2,512,128]{2,1,0:T(8,128)(2,1)S(1)} %get-tuple-element.27), channel_id=1, source_target_pairs={{0,6},{1,7},{2,4},{3,5},{4,2},{5,3},{6,0},{7,1},{8,14},{9,15},{10,... | collective-permute-start | bytes 786440 | tf_op jit(solution)/shard_map/ppermute | solution.py:298
  60.5 0.1 add_convert_fusion
  60.6 0.1 collective-permute-start.21
  60.7 4.8 %collective-permute-done.13 = bf16[2,512,128]{2,1,0:T(8,128)(2,1)S(1)} collective-permute-done((bf16[2,512,128]{2,1,0:T(8,128)(2,1)S(1)}, bf16[2,512,128]{2,1,0:T(8,128)(2,1)S(1)}, u32[]{:S(2)}, u32[]{:S(2)}) %collective-permute-start.13) | collective-permute-done | bytes 262176 | tf_op jit(solution)/shard_map/ppermute | solution.py:296
  65.6 2.3 %collective-permute-start.14 = (bf16[512,128]{1,0:T(8,128)(2,1)S(1)}, bf16[512,128]{1,0:T(8,128)(2,1)S(1)}, u32[]{:S(2)}, u32[]{:S(2)}) collective-permute-start(bf16[512,128]{1,0:T(8,128)(2,1)S(1)} %fusion.10), channel_id=1, source_target_pairs={{0,6},{1,7},{2,4},{3,5},{4,2},{5,3},{6,0},{7,1},{8,14},{9,15},{10,... | collective-permute-start | bytes 393224 | tf_op jit(solution)/shard_map/ppermute | solution.py:297
  67.9 0.0 collective-permute-done.11
  68.0 0.4 collective-permute-start.12
  68.4 3.4 %collective-permute-done.14 = bf16[512,128]{1,0:T(8,128)(2,1)S(1)} collective-permute-done((bf16[512,128]{1,0:T(8,128)(2,1)S(1)}, bf16[512,128]{1,0:T(8,128)(2,1)S(1)}, u32[]{:S(2)}, u32[]{:S(2)}) %collective-permute-start.14) | collective-permute-done | bytes 131104 | tf_op jit(solution)/shard_map/ppermute | solution.py:297
  71.9 4.6 %collective-permute-start.15 = (bf16[512,128]{1,0:T(8,128)(2,1)S(1)}, bf16[512,128]{1,0:T(8,128)(2,1)S(1)}, u32[]{:S(2)}, u32[]{:S(2)}) collective-permute-start(bf16[512,128]{1,0:T(8,128)(2,1)S(1)} %fusion.3), channel_id=1, source_target_pairs={{0,1},{1,0},{2,3},{3,2},{4,5},{5,4},{6,7},{7,6},{8,9},{9,8},{10,11... | collective-permute-start | bytes 393224 | tf_op jit(solution)/shard_map/ppermute | solution.py:300
  76.5 0.1 convert_add_fusion
  76.7 1.6 %collective-permute-start.22 = (bf16[4,6,32,128]{3,2,1,0:T(8,128)(2,1)S(1)}, bf16[4,6,32,128]{3,2,1,0:T(8,128)(2,1)S(1)}, u32[]{:S(2)}, u32[]{:S(2)}) collective-permute-start(bf16[4,6,32,128]{3,2,1,0:T(8,128)(2,1)S(1)} %fusion.8), channel_id=1, source_target_pairs={{0,64},{8,72},{16,80},{24,88},{32,96},{40,104},{48,112},{56,120},{... | collective-permute-start | bytes 589832 | tf_op jit(solution)/shard_map/ppermute | solution.py:288
  78.3 0.1 convert_add_fusion.1
  78.5 1.7 %collective-permute-start.17 = (bf16[4,6,32,128]{3,2,1,0:T(8,128)(2,1)S(1)}, bf16[4,6,32,128]{3,2,1,0:T(8,128)(2,1)S(1)}, u32[]{:S(2)}, u32[]{:S(2)}) collective-permute-start(bf16[4,6,32,128]{3,2,1,0:T(8,128)(2,1)S(1)} %fusion.7), channel_id=1, source_target_pairs={{0,192},{8,200},{16,208},{24,216},{32,224},{40,232},{48,240},{56,2... | collective-permute-start | bytes 589832 | tf_op jit(solution)/shard_map/ppermute | solution.py:288
  80.2 0.0 collective-permute-done.12
  80.2 0.7 collective-permute-done.15
  80.9 0.7 fusion.6
  81.6 0.8 collective-permute-done.22
  82.4 0.1 fusion.17
  82.5 4.0 %collective-permute-start.23 = (bf16[2,6,32,128]{3,2,1,0:T(8,128)(2,1)S(1)}, bf16[2,6,32,128]{3,2,1,0:T(8,128)(2,1)S(1)}, u32[]{:S(2)}, u32[]{:S(2)}) collective-permute-start(bf16[2,6,32,128]{3,2,1,0:T(8,128)(2,1)S(1)} %pad_maximum_fusion.4), channel_id=1, source_target_pairs={{0,16},{8,24},{16,0},{24,8},{32,48},{40,56},{48,32},{56,40},{64,80... | collective-permute-start | bytes 294920 | tf_op jit(solution)/shard_map/ppermute | solution.py:291
  86.6 0.1 fusion.15
  86.7 0.1 collective-permute-start.18
  86.8 2.7 %collective-permute-done.23 = bf16[2,6,32,128]{3,2,1,0:T(8,128)(2,1)S(1)} collective-permute-done((bf16[2,6,32,128]{3,2,1,0:T(8,128)(2,1)S(1)}, bf16[2,6,32,128]{3,2,1,0:T(8,128)(2,1)S(1)}, u32[]{:S(2)}, u32[]{:S(2)}) %collective-permute-start.23) | collective-permute-done | bytes 98336 | tf_op jit(solution)/shard_map/ppermute | solution.py:291
  89.5 0.9 collective-permute-start.24
  90.4 1.4 %collective-permute-done.18 = bf16[2,6,32,128]{3,2,1,0:T(8,128)(2,1)S(1)} collective-permute-done((bf16[2,6,32,128]{3,2,1,0:T(8,128)(2,1)S(1)}, bf16[2,6,32,128]{3,2,1,0:T(8,128)(2,1)S(1)}, u32[]{:S(2)}, u32[]{:S(2)}) %collective-permute-start.18) | collective-permute-done | bytes 98336 | tf_op jit(solution)/shard_map/ppermute | solution.py:291
  91.9 1.4 %collective-permute-start.19 = (bf16[6,32,128]{2,1,0:T(8,128)(2,1)S(1)}, bf16[6,32,128]{2,1,0:T(8,128)(2,1)S(1)}, u32[]{:S(2)}, u32[]{:S(2)}) collective-permute-start(bf16[6,32,128]{2,1,0:T(8,128)(2,1)S(1)} %fusion.13), channel_id=1, source_target_pairs={{0,32},{8,40},{16,48},{24,56},{32,0},{40,8},{48,16},{56,24},{64,96... | collective-permute-start | bytes 147464 | tf_op jit(solution)/shard_map/ppermute | solution.py:293
  93.3 1.3 %collective-permute-done.24 = bf16[6,32,128]{2,1,0:T(8,128)(2,1)S(1)} collective-permute-done((bf16[6,32,128]{2,1,0:T(8,128)(2,1)S(1)}, bf16[6,32,128]{2,1,0:T(8,128)(2,1)S(1)}, u32[]{:S(2)}, u32[]{:S(2)}) %collective-permute-start.24) | collective-permute-done | bytes 49184 | tf_op jit(solution)/shard_map/ppermute | solution.py:293
  94.6 2.4 %collective-permute-done.19 = bf16[6,32,128]{2,1,0:T(8,128)(2,1)S(1)} collective-permute-done((bf16[6,32,128]{2,1,0:T(8,128)(2,1)S(1)}, bf16[6,32,128]{2,1,0:T(8,128)(2,1)S(1)}, u32[]{:S(2)}, u32[]{:S(2)}) %collective-permute-start.19) | collective-permute-done | bytes 49184 | tf_op jit(solution)/shard_map/ppermute | solution.py:293
  97.1 0.7 maximum_bitcast_fusion
  (35 shorter events, 0.4 us)
Async XLA Ops:
  0.6 23.8 %collective-permute-start = (bf16[512,128]{1,0:T(8,128)(2,1)}, bf16[512,128]{1,0:T(8,128)(2,1)}, u32[]{:S(2)}, u32[]{:S(2)}) collective-permute-start(bf16[512,128]{1,0:T(8,128)(2,1)} %own_ref.1), channel_id=1, source_target_pairs={{16,0},{24,8},{32,16},{40,24},{48,32},{56,40},{64,48},{72,56},{80,... | collective-permute-start | bytes 393224 | tf_op jit(solution)/shard_map/ppermute | solution.py:259
  7.4 17.1 %collective-permute-start.1 = (bf16[512,128]{1,0:T(8,128)(2,1)}, bf16[512,128]{1,0:T(8,128)(2,1)S(1)}, u32[]{:S(2)}, u32[]{:S(2)}) collective-permute-start(bf16[512,128]{1,0:T(8,128)(2,1)} %own_ref.1), channel_id=1, source_target_pairs={{32,0},{40,8},{48,16},{56,24},{64,32},{72,40},{80,48},{88,56},{96,... | collective-permute-start | bytes 393224 | tf_op jit(solution)/shard_map/ppermute | solution.py:259
  9.3 15.2 %collective-permute-start.3 = (bf16[512,128]{1,0:T(8,128)(2,1)}, bf16[512,128]{1,0:T(8,128)(2,1)}, u32[]{:S(2)}, u32[]{:S(2)}) collective-permute-start(bf16[512,128]{1,0:T(8,128)(2,1)} %own_ref.1), channel_id=1, source_target_pairs={{48,0},{56,8},{64,16},{72,24},{80,32},{88,40},{96,48},{104,56},{11... | collective-permute-start | bytes 393224 | tf_op jit(solution)/shard_map/ppermute | solution.py:259
  11.7 12.7 %collective-permute-start.4 = (bf16[512,128]{1,0:T(8,128)(2,1)}, bf16[512,128]{1,0:T(8,128)(2,1)}, u32[]{:S(2)}, u32[]{:S(2)}) collective-permute-start(bf16[512,128]{1,0:T(8,128)(2,1)} %own_ref.1), channel_id=1, source_target_pairs={{64,0},{72,8},{80,16},{88,24},{96,32},{104,40},{112,48},{120,56},{... | collective-permute-start | bytes 393224 | tf_op jit(solution)/shard_map/ppermute | solution.py:259
  14.8 11.1 %collective-permute-start.6 = (bf16[512,128]{1,0:T(8,128)(2,1)}, bf16[512,128]{1,0:T(8,128)(2,1)}, u32[]{:S(2)}, u32[]{:S(2)}) collective-permute-start(bf16[512,128]{1,0:T(8,128)(2,1)} %param.4), channel_id=1, source_target_pairs={{0,1},{1,0},{2,3},{3,2},{4,5},{5,4},{6,7},{7,6},{8,9},{9,8},{10,11... | collective-permute-start | bytes 393224 | tf_op jit(solution)/shard_map/ppermute | solution.py:260
  20.2 0.9 copy-start.2
  22.8 1.6 %copy-start.3 = (bf16[12,64,2048]{2,1,0:T(8,128)(2,1)}, bf16[12,64,2048]{2,1,0:T(8,128)(2,1)S(1)}, u32[]{:S(2)}) copy-start(bf16[12,64,2048]{2,1,0:T(8,128)(2,1)S(1)} %get-tuple-element.18.table_ref) | copy-start | bytes 9437188
  24.4 1.4 %copy-start.5 = (bf16[512,128]{1,0:T(8,128)(2,1)S(1)}, bf16[512,128]{1,0:T(8,128)(2,1)}, u32[]{:S(2)}) copy-start(bf16[512,128]{1,0:T(8,128)(2,1)} %param.4) | copy-start | bytes 393220
  24.4 8.2 %copy-start.1 = (bf16[512,128]{1,0:T(8,128)(2,1)S(1)}, bf16[512,128]{1,0:T(8,128)(2,1)}, u32[]{:S(2)}) copy-start(bf16[512,128]{1,0:T(8,128)(2,1)} %own_ref.1) | copy-start | bytes 393220
  25.6 7.0 %collective-permute-start.2 = (bf16[2,512,128]{2,1,0:T(8,128)(2,1)S(1)}, bf16[2,512,128]{2,1,0:T(8,128)(2,1)S(1)}, u32[]{:S(2)}, u32[]{:S(2)}) collective-permute-start(bf16[2,512,128]{2,1,0:T(8,128)(2,1)S(1)} %pad_maximum_fusion), channel_id=1, source_target_pairs={{0,8},{8,0},{16,24},{24,16},{32,40},{40,32},{48,56},{56,48},{64,72... | collective-permute-start | bytes 786440 | tf_op jit(solution)/shard_map/ppermute | solution.py:266
  26.8 12.9 %collective-permute-start.7 = (bf16[2,512,128]{2,1,0:T(8,128)(2,1)S(1)}, bf16[2,512,128]{2,1,0:T(8,128)(2,1)S(1)}, u32[]{:S(2)}, u32[]{:S(2)}) collective-permute-start(bf16[2,512,128]{2,1,0:T(8,128)(2,1)S(1)} %pad_maximum_fusion.2.x0_ref), channel_id=1, source_target_pairs={{0,2},{1,3},{2,4},{3,5},{4,6},{5,7},{6,0},{7,1},{8,10},{9,11},{10,... | collective-permute-start | bytes 786440 | tf_op jit(solution)/shard_map/ppermute | solution.py:261
  28.3 15.0 %collective-permute-start.8 = (bf16[2,512,128]{2,1,0:T(8,128)(2,1)S(1)}, bf16[2,512,128]{2,1,0:T(8,128)(2,1)S(1)}, u32[]{:S(2)}, u32[]{:S(2)}) collective-permute-start(bf16[2,512,128]{2,1,0:T(8,128)(2,1)S(1)} %pad_maximum_fusion.2.x0_ref), channel_id=1, source_target_pairs={{0,4},{1,5},{2,6},{3,7},{4,0},{5,1},{6,2},{7,3},{8,12},{9,13},{10,... | collective-permute-start | bytes 786440 | tf_op jit(solution)/shard_map/ppermute | solution.py:261
  31.1 12.3 %collective-permute-start.9 = (bf16[2,512,128]{2,1,0:T(8,128)(2,1)S(1)}, bf16[2,512,128]{2,1,0:T(8,128)(2,1)S(1)}, u32[]{:S(2)}, u32[]{:S(2)}) collective-permute-start(bf16[2,512,128]{2,1,0:T(8,128)(2,1)S(1)} %pad_maximum_fusion.2.x0_ref), channel_id=1, source_target_pairs={{0,6},{1,7},{2,0},{3,1},{4,2},{5,3},{6,4},{7,5},{8,14},{9,15},{10,... | collective-permute-start | bytes 786440 | tf_op jit(solution)/shard_map/ppermute | solution.py:261
  32.5 7.1 %collective-permute-start.5 = (bf16[2,512,128]{2,1,0:T(8,128)(2,1)S(1)}, bf16[2,512,128]{2,1,0:T(8,128)(2,1)S(1)}, u32[]{:S(2)}, u32[]{:S(2)}) collective-permute-start(bf16[2,512,128]{2,1,0:T(8,128)(2,1)S(1)} %pad_maximum_fusion.1), channel_id=1, source_target_pairs={{0,8},{8,0},{16,24},{24,16},{32,40},{40,32},{48,56},{56,48},{64,72... | collective-permute-start | bytes 786440 | tf_op jit(solution)/shard_map/ppermute | solution.py:266
  32.7 1.9 %copy-start.4 = (bf16[12,64,2048]{2,1,0:T(8,128)(2,1)S(1)}, bf16[12,64,2048]{2,1,0:T(8,128)(2,1)}, u32[]{:S(2)}) copy-start(bf16[12,64,2048]{2,1,0:T(8,128)(2,1)} %copy-done.3) | copy-start | bytes 9437188
  48.5 6.1 %collective-permute-start.10 = (bf16[4,4,6,32,128]{4,3,2,1,0:T(8,128)(2,1)S(1)}, bf16[4,4,6,32,128]{4,3,2,1,0:T(8,128)(2,1)S(1)}, u32[]{:S(2)}, u32[]{:S(2)}) collective-permute-start(bf16[4,4,6,32,128]{4,3,2,1,0:T(8,128)(2,1)S(1)} %get-tuple-element.21), channel_id=1, source_target_pairs={{0,8},{8,0},{16,24},{24,16},{32,40},{40,32},{48,56},{56,48},{64,72... | collective-permute-start | bytes 2359304 | tf_op jit(solution)/shard_map/ppermute | solution.py:276
  48.6 6.2 %copy-start = (bf16[1024,12,128]{2,0,1:T(8,128)(2,1)S(1)}, bf16[1024,12,128]{2,0,1:T(8,128)(2,1)}, u32[]{:S(2)}) copy-start(bf16[1024,12,128]{2,0,1:T(8,128)(2,1)} %param.7) | copy-start | bytes 9437188
  53.9 6.6 %collective-permute-start.20 = (bf16[4,4,6,32,128]{4,3,2,1,0:T(8,128)(2,1)S(1)}, bf16[4,4,6,32,128]{4,3,2,1,0:T(8,128)(2,1)S(1)}, u32[]{:S(2)}, u32[]{:S(2)}) collective-permute-start(bf16[4,4,6,32,128]{4,3,2,1,0:T(8,128)(2,1)S(1)} %get-tuple-element.31), channel_id=1, source_target_pairs={{0,8},{8,0},{16,24},{24,16},{32,40},{40,32},{48,56},{56,48},{64,72... | collective-permute-start | bytes 2359304 | tf_op jit(solution)/shard_map/ppermute | solution.py:276
  57.2 8.3 %collective-permute-start.13 = (bf16[2,512,128]{2,1,0:T(8,128)(2,1)S(1)}, bf16[2,512,128]{2,1,0:T(8,128)(2,1)S(1)}, u32[]{:S(2)}, u32[]{:S(2)}) collective-permute-start(bf16[2,512,128]{2,1,0:T(8,128)(2,1)S(1)} %get-tuple-element.29), channel_id=1, source_target_pairs={{0,2},{1,3},{2,0},{3,1},{4,6},{5,7},{6,4},{7,5},{8,10},{9,11},{10,... | collective-permute-start | bytes 786440 | tf_op jit(solution)/shard_map/ppermute | solution.py:296
  58.6 19.7 %collective-permute-start.16 = (bf16[2,4,6,32,128]{4,3,2,1,0:T(8,128)(2,1)S(1)}, bf16[2,4,6,32,128]{4,3,2,1,0:T(8,128)(2,1)S(1)}, u32[]{:S(2)}, u32[]{:S(2)}) collective-permute-start(bf16[2,4,6,32,128]{4,3,2,1,0:T(8,128)(2,1)S(1)} %add_convert_fusion.1._), channel_id=1, source_target_pairs={{0,64},{8,72},{16,80},{24,88},{32,96},{40,104},{48,112},{56,120},{... | collective-permute-start | bytes 1179656 | tf_op jit(solution)/shard_map/ppermute | solution.py:286
  58.6 9.3 %collective-permute-start.11 = (bf16[2,512,128]{2,1,0:T(8,128)(2,1)S(1)}, bf16[2,512,128]{2,1,0:T(8,128)(2,1)S(1)}, u32[]{:S(2)}, u32[]{:S(2)}) collective-permute-start(bf16[2,512,128]{2,1,0:T(8,128)(2,1)S(1)} %get-tuple-element.27), channel_id=1, source_target_pairs={{0,6},{1,7},{2,4},{3,5},{4,2},{5,3},{6,0},{7,1},{8,14},{9,15},{10,... | collective-permute-start | bytes 786440 | tf_op jit(solution)/shard_map/ppermute | solution.py:298
  60.6 15.9 %collective-permute-start.21 = (bf16[2,4,6,32,128]{4,3,2,1,0:T(8,128)(2,1)S(1)}, bf16[2,4,6,32,128]{4,3,2,1,0:T(8,128)(2,1)S(1)}, u32[]{:S(2)}, u32[]{:S(2)}) collective-permute-start(bf16[2,4,6,32,128]{4,3,2,1,0:T(8,128)(2,1)S(1)} %add_convert_fusion), channel_id=1, source_target_pairs={{0,192},{8,200},{16,208},{24,216},{32,224},{40,232},{48,240},{56,2... | collective-permute-start | bytes 1179656 | tf_op jit(solution)/shard_map/ppermute | solution.py:286
  65.6 6.3 %collective-permute-start.14 = (bf16[512,128]{1,0:T(8,128)(2,1)S(1)}, bf16[512,128]{1,0:T(8,128)(2,1)S(1)}, u32[]{:S(2)}, u32[]{:S(2)}) collective-permute-start(bf16[512,128]{1,0:T(8,128)(2,1)S(1)} %fusion.10), channel_id=1, source_target_pairs={{0,6},{1,7},{2,4},{3,5},{4,2},{5,3},{6,0},{7,1},{8,14},{9,15},{10,... | collective-permute-start | bytes 393224 | tf_op jit(solution)/shard_map/ppermute | solution.py:297
  68.0 12.3 %collective-permute-start.12 = (bf16[512,128]{1,0:T(8,128)(2,1)S(1)}, bf16[512,128]{1,0:T(8,128)(2,1)S(1)}, u32[]{:S(2)}, u32[]{:S(2)}) collective-permute-start(bf16[512,128]{1,0:T(8,128)(2,1)S(1)} %fusion.9), channel_id=1, source_target_pairs={{0,2},{1,3},{2,0},{3,1},{4,6},{5,7},{6,4},{7,5},{8,10},{9,11},{10,... | collective-permute-start | bytes 393224 | tf_op jit(solution)/shard_map/ppermute | solution.py:299
  71.9 9.1 %collective-permute-start.15 = (bf16[512,128]{1,0:T(8,128)(2,1)S(1)}, bf16[512,128]{1,0:T(8,128)(2,1)S(1)}, u32[]{:S(2)}, u32[]{:S(2)}) collective-permute-start(bf16[512,128]{1,0:T(8,128)(2,1)S(1)} %fusion.3), channel_id=1, source_target_pairs={{0,1},{1,0},{2,3},{3,2},{4,5},{5,4},{6,7},{7,6},{8,9},{9,8},{10,11... | collective-permute-start | bytes 393224 | tf_op jit(solution)/shard_map/ppermute | solution.py:300
  76.7 5.8 %collective-permute-start.22 = (bf16[4,6,32,128]{3,2,1,0:T(8,128)(2,1)S(1)}, bf16[4,6,32,128]{3,2,1,0:T(8,128)(2,1)S(1)}, u32[]{:S(2)}, u32[]{:S(2)}) collective-permute-start(bf16[4,6,32,128]{3,2,1,0:T(8,128)(2,1)S(1)} %fusion.8), channel_id=1, source_target_pairs={{0,64},{8,72},{16,80},{24,88},{32,96},{40,104},{48,112},{56,120},{... | collective-permute-start | bytes 589832 | tf_op jit(solution)/shard_map/ppermute | solution.py:288
  78.5 8.1 %collective-permute-start.17 = (bf16[4,6,32,128]{3,2,1,0:T(8,128)(2,1)S(1)}, bf16[4,6,32,128]{3,2,1,0:T(8,128)(2,1)S(1)}, u32[]{:S(2)}, u32[]{:S(2)}) collective-permute-start(bf16[4,6,32,128]{3,2,1,0:T(8,128)(2,1)S(1)} %fusion.7), channel_id=1, source_target_pairs={{0,192},{8,200},{16,208},{24,216},{32,224},{40,232},{48,240},{56,2... | collective-permute-start | bytes 589832 | tf_op jit(solution)/shard_map/ppermute | solution.py:288
  82.5 6.9 %collective-permute-start.23 = (bf16[2,6,32,128]{3,2,1,0:T(8,128)(2,1)S(1)}, bf16[2,6,32,128]{3,2,1,0:T(8,128)(2,1)S(1)}, u32[]{:S(2)}, u32[]{:S(2)}) collective-permute-start(bf16[2,6,32,128]{3,2,1,0:T(8,128)(2,1)S(1)} %pad_maximum_fusion.4), channel_id=1, source_target_pairs={{0,16},{8,24},{16,0},{24,8},{32,48},{40,56},{48,32},{56,40},{64,80... | collective-permute-start | bytes 294920 | tf_op jit(solution)/shard_map/ppermute | solution.py:291
  86.7 5.2 %collective-permute-start.18 = (bf16[2,6,32,128]{3,2,1,0:T(8,128)(2,1)S(1)}, bf16[2,6,32,128]{3,2,1,0:T(8,128)(2,1)S(1)}, u32[]{:S(2)}, u32[]{:S(2)}) collective-permute-start(bf16[2,6,32,128]{3,2,1,0:T(8,128)(2,1)S(1)} %pad_maximum_fusion.3), channel_id=1, source_target_pairs={{0,16},{8,24},{16,0},{24,8},{32,48},{40,56},{48,32},{56,40},{64,80... | collective-permute-start | bytes 294920 | tf_op jit(solution)/shard_map/ppermute | solution.py:291
  89.5 5.1 %collective-permute-start.24 = (bf16[6,32,128]{2,1,0:T(8,128)(2,1)S(1)}, bf16[6,32,128]{2,1,0:T(8,128)(2,1)S(1)}, u32[]{:S(2)}, u32[]{:S(2)}) collective-permute-start(bf16[6,32,128]{2,1,0:T(8,128)(2,1)S(1)} %fusion.14), channel_id=1, source_target_pairs={{0,32},{8,40},{16,48},{24,56},{32,0},{40,8},{48,16},{56,24},{64,96... | collective-permute-start | bytes 147464 | tf_op jit(solution)/shard_map/ppermute | solution.py:293
  91.9 5.1 %collective-permute-start.19 = (bf16[6,32,128]{2,1,0:T(8,128)(2,1)S(1)}, bf16[6,32,128]{2,1,0:T(8,128)(2,1)S(1)}, u32[]{:S(2)}, u32[]{:S(2)}) collective-permute-start(bf16[6,32,128]{2,1,0:T(8,128)(2,1)S(1)} %fusion.13), channel_id=1, source_target_pairs={{0,32},{8,40},{16,48},{24,56},{32,0},{40,8},{48,16},{56,24},{64,96... | collective-permute-start | bytes 147464 | tf_op jit(solution)/shard_map/ppermute | solution.py:293

commit v3 on v2

v3 whole, which is shorter than its diff:
```python
import functools

import jax
import jax.numpy as jnp
from jax import lax
from jax.experimental import pallas as pl
from jax.experimental.pallas import tpu as pltpu
from jax.sharding import PartitionSpec as P

BF16, F32 = jnp.bfloat16, jnp.float32
ROWS = 64
LANE = 128
NX, NZ_HI, NY, NZ_LO, NCORE = 4, 2, 4, 4, 2
CHIPS = NY * NZ_LO
VMEM_LIMIT = 20 * 1024 * 1024
LARGE_COST = pl.CostEstimate(flops=4_000_000_000, bytes_accessed=8_000_000, transcendentals=0)
SMALL_COST = pl.CostEstimate(flops=1000, bytes_accessed=1000, transcendentals=0)


def ctx_of(y, z, core):
    return (y * NZ_LO + z) * NCORE + core


CTX = [(y, z, core) for y in range(NY) for z in range(NZ_LO) for core in range(NCORE)]
TP = [(x, z) for x in range(NX) for z in range(NZ_HI)]
CORE_SWAP = [(ctx_of(y, z, c), ctx_of(y, z, 1 - c)) for y, z, c in CTX]
Z_HI_SWAP = [(x * NZ_HI + z, x * NZ_HI + 1 - z) for x, z in TP]


def ring_partner(at, crossed):
    return NX - 1 - at if crossed else at ^ 1


def ring_slots(at, crossed):
    near, far = ring_partner(at, crossed), ring_partner(at, not crossed)
    return at, far, near, ring_partner(near, not crossed)


def y_swap(crossed):
    return [(ctx_of(y, z, c), ctx_of(ring_partner(y, crossed), z, c)) for y, z, c in CTX]


def x_swap(crossed):
    return [(x * NZ_HI + z, ring_partner(x, crossed) * NZ_HI + z) for x, z in TP]


def z_swap(bit):
    return [(ctx_of(y, z, c), ctx_of(y, z ^ bit, c)) for y, z, c in CTX]


def along_x(steps):
    return [(x * NZ_HI + z, (x + steps) % NX * NZ_HI + z) for x, z in TP]


def from_later_chip(steps):
    return [
        (NCORE * (chip + steps) + core, NCORE * chip + core)
        for chip in range(CHIPS - steps)
        for core in range(NCORE)
    ]


def table_kernel(filters_ref, grad_ref, near_ref, copy_ref, *far_refs):
    copy_ref[...] = grad_ref[...]
    filt_count, rows, near = near_ref.shape
    per_group, _, far = far_refs[0].shape
    taps = filters_ref.shape[1]
    width = near + far
    for k in range(filt_count):
        line = filters_ref[k : k + 1, :].astype(F32)
        line = jnp.concatenate([line, jnp.zeros((1, width - taps), F32)], axis=1)
        block = jnp.broadcast_to(line, (rows, width))
        block = pltpu.roll(block, 0, 1, stride=1, stride_axis=0).astype(BF16)
        near_ref[k] = block[:, :near]
        far_refs[k // per_group][k % per_group] = block[:, near:]


def toeplitz_tables(filters, grad_out, groups):
    filt_count, taps = filters.shape
    near, far = taps // 2, taps // 2 + LANE
    vmem = pl.BlockSpec(memory_space=pltpu.VMEM)
    outs = [jax.ShapeDtypeStruct((filt_count, ROWS, near), BF16)]
    outs += [jax.ShapeDtypeStruct(grad_out.shape, BF16)]
    outs += [jax.ShapeDtypeStruct((filt_count // groups, ROWS, far), BF16)] * groups
    return pl.pallas_call(
        table_kernel,
        out_shape=outs,
        in_specs=[vmem] * 2,
        out_specs=[vmem] * (2 + groups),
        compiler_params=pltpu.CompilerParams(vmem_limit_bytes=VMEM_LIMIT),
        cost_estimate=LARGE_COST,
        name="tables",
    )(filters, grad_out)


def pair_of_blocks(grad_ref, start, rows, width):
    first = grad_ref[pl.ds(start, width), :]
    second = grad_ref[pl.ds(start + rows, width), :]
    return jnp.concatenate([first, second], axis=1)


def coords(pos_ref):
    x, z_hi = pos_ref[0] // NZ_HI, lax.rem(pos_ref[0], NZ_HI)
    chip, core = pos_ref[1] // NCORE, lax.rem(pos_ref[1], NCORE)
    return x, z_hi, chip // NZ_LO, lax.rem(chip, NZ_LO), core


def lay_out(core, grad_ref, even_refs, odd_refs):
    tok = even_refs[0].shape[0]
    for s, part in enumerate(even_refs):
        grad_ref[2 * s * tok : (2 * s + 1) * tok, :] = part[...]
    for s in range(len(even_refs) - 1):
        grad_ref[(2 * s + 1) * tok : (2 * s + 2) * tok, :] = jnp.where(
            core == 0, odd_refs[s][...], odd_refs[s + 1][...]
        )


def near_kernel(pos_ref, table_ref, own_ref, r1_ref, r2_ref, s0_ref, s1_ref, s2_ref, *refs):
    acc_refs, grad_ref = refs[:-1], refs[-1]
    filt_count, rows, width = table_ref.shape
    tok = own_ref.shape[0]
    core = coords(pos_ref)[-1]
    lay_out(core, grad_ref, (own_ref, r1_ref, r2_ref), (s0_ref, s1_ref, s2_ref))
    table = table_ref[...].reshape(filt_count * rows, width)

    @pl.loop(0, tok // (2 * rows))
    def _(pair):
        start = pl.multiple_of(pair * (2 * rows), 2 * rows)
        both = pair_of_blocks(grad_ref, start, rows, width)
        result = jnp.dot(table, both, preferred_element_type=F32)
        part = acc_refs[0].shape[1]
        for group, acc_ref in enumerate(acc_refs):
            acc_ref[pair] = result[group * part : (group + 1) * part]


def near_conv(pos, table, halo, swapped, groups):
    filt_count, rows, width = table.shape
    tok = halo[0].shape[0]
    vmem = pl.BlockSpec(memory_space=pltpu.VMEM)
    acc = jax.ShapeDtypeStruct((tok // (2 * rows), filt_count // groups * rows, 2 * LANE), F32)
    return pl.pallas_call(
        near_kernel,
        out_shape=[acc] * groups,
        in_specs=[pl.BlockSpec(memory_space=pltpu.SMEM)] + [vmem] * 7,
        out_specs=[vmem] * groups,
        scratch_shapes=[pltpu.VMEM((5 * tok, LANE), BF16)],
        compiler_params=pltpu.CompilerParams(vmem_limit_bytes=VMEM_LIMIT),
        cost_estimate=LARGE_COST,
        name="near_conv",
    )(pos, table, *halo, *swapped)


def far_kernel(
    pos_ref, _, table_ref, acc_ref, r2_ref, r3_ref, r4_ref, s2_ref, s3_ref, s4_ref,
    corr_ref, grad_ref,
):
    filt_count, rows, width = table_ref.shape
    tok = r2_ref.shape[0]
    core = coords(pos_ref)[-1]
    lay_out(core, grad_ref, (r2_ref, r3_ref, r4_ref), (s2_ref, s3_ref, s4_ref))
    grad_ref[5 * tok :, :] = jnp.zeros((grad_ref.shape[0] - 5 * tok, LANE), BF16)
    table = table_ref[...].reshape(filt_count * rows, width)

    @pl.loop(0, tok // (2 * rows))
    def _(pair):
        start = pl.multiple_of(pair * (2 * rows), 2 * rows)
        both = pair_of_blocks(grad_ref, start, rows, width)
        result = jnp.dot(table, both, preferred_element_type=F32)
        result = (result + acc_ref[pair]).astype(BF16)
        for k in range(filt_count):
            for half in range(2):
                corr_ref[pl.ds(start + half * rows, rows), k * LANE : (k + 1) * LANE] = result[
                    k * rows : (k + 1) * rows, half * LANE : (half + 1) * LANE
                ]


def far_conv(pos, after, table, acc, halo, swapped):
    filt_count, rows, width = table.shape
    tok = halo[0].shape[0]
    vmem = pl.BlockSpec(memory_space=pltpu.VMEM)
    return pl.pallas_call(
        far_kernel,
        out_shape=jax.ShapeDtypeStruct((tok, filt_count * LANE), BF16),
        in_specs=[pl.BlockSpec(memory_space=pltpu.SMEM), pl.BlockSpec(memory_space=pl.ANY)]
        + [vmem] * 8,
        out_specs=vmem,
        scratch_shapes=[pltpu.VMEM((5 * tok + rows, LANE), BF16)],
        compiler_params=pltpu.CompilerParams(vmem_limit_bytes=VMEM_LIMIT),
        cost_estimate=SMALL_COST,
        name="far_conv",
    )(pos, after, table, acc, *halo, *swapped)


def product_kernel(
    crossed, pos_ref, corr_ref, x0_ref, x1_ref, x2_ref, x3_ref, keep_ref, send_ref, full_ref
):
    x, z_hi, y, z_lo, core = coords(pos_ref)
    for s, part in enumerate((x0_ref, x1_ref, x2_ref, x3_ref)):
        for h in range(NZ_HI):
            at = lax.rem(x + NX - s, NX) * NZ_HI + lax.rem(z_hi + h, NZ_HI)
            full_ref[:, pl.ds(pl.multiple_of(at * LANE, LANE), LANE)] = part[h]

    deep = NZ_LO * NCORE * 32
    for s, at in enumerate(ring_slots(y, crossed)):
        part = full_ref[:, pl.ds(pl.multiple_of(at * deep, deep), deep)]
        result = lax.dot_general(
            part, corr_ref[...], (((0,), (0,)), ((), ())), preferred_element_type=F32
        ).astype(BF16)
        for z in range(NZ_LO):
            shift = z ^ z_lo
            slot = lax.rem(shift, 2) * 2 + shift // 2
            for k in range(keep_ref.shape[2]):
                columns = slice(k * LANE, (k + 1) * LANE)
                even = result[z * 64 : z * 64 + 32, columns]
                odd = result[z * 64 + 32 : z * 64 + 64, columns]
                keep_ref[s, slot, k] = jnp.where(core == 0, even, odd)
                send_ref[s, slot, k] = jnp.where(core == 0, odd, even)


def product(crossed, pos, corr, gathered):
    tok, width = corr.shape
    part = jax.ShapeDtypeStruct((NY, NZ_LO, width // LANE, 32, LANE), BF16)
    vmem = pl.BlockSpec(memory_space=pltpu.VMEM)
    return pl.pallas_call(
        functools.partial(product_kernel, crossed),
        out_shape=(part, part),
        in_specs=[pl.BlockSpec(memory_space=pltpu.SMEM)] + [vmem] * 5,
        out_specs=(vmem,) * 2,
        scratch_shapes=[pltpu.VMEM((tok, 1024), BF16)],
        compiler_params=pltpu.CompilerParams(vmem_limit_bytes=VMEM_LIMIT),
        cost_estimate=SMALL_COST,
        name="product",
    )(pos, corr, *gathered)


def halve_kernel(_, mine_ref, other_ref, stay_ref, leave_ref):
    half = leave_ref.shape[0]
    stay_ref[...] = mine_ref[:half].astype(F32) + other_ref[:half].astype(F32)
    leave_ref[...] = (mine_ref[half:].astype(F32) + other_ref[half:].astype(F32)).astype(BF16)


def halve(after, mine, other):
    half = (mine.shape[0] // 2,) + mine.shape[1:]
    vmem = pl.BlockSpec(memory_space=pltpu.VMEM)
    return pl.pallas_call(
        halve_kernel,
        out_shape=(jax.ShapeDtypeStruct(half, F32), jax.ShapeDtypeStruct(half, BF16)),
        in_specs=[pl.BlockSpec(memory_space=pl.ANY), vmem, vmem],
        out_specs=(vmem, vmem),
        compiler_params=pltpu.CompilerParams(vmem_limit_bytes=VMEM_LIMIT),
        cost_estimate=SMALL_COST,
        name="halve",
    )(after, mine, other)


def add_kernel(_, mine_ref, other_ref, sum_ref):
    sum_ref[...] = (mine_ref[...] + other_ref[...].astype(F32)).astype(BF16)


def add(after, mine, other):
    vmem = pl.BlockSpec(memory_space=pltpu.VMEM)
    return pl.pallas_call(
        add_kernel,
        out_shape=jax.ShapeDtypeStruct(mine.shape, BF16),
        in_specs=[pl.BlockSpec(memory_space=pl.ANY), vmem, vmem],
        out_specs=vmem,
        compiler_params=pltpu.CompilerParams(vmem_limit_bytes=VMEM_LIMIT),
        cost_estimate=SMALL_COST,
        name="add",
    )(after, mine, other)


def share_kernel(pos_ref, _, *refs):
    corr_refs, proj_ref = refs[:-6], refs[-6]
    near_keep, near_send, far_keep, far_send, all_ref = refs[-5:]
    filt_count = proj_ref.shape[0]
    x, z_hi = coords(pos_ref)[:2]
    at = 0
    for part in corr_refs:
        all_ref[:, at : at + part.shape[1]] = part[...]
        at += part.shape[1]
    wide = NZ_HI * LANE
    near_slots = (near_keep, 0), (near_send, 0), (near_keep, 1), (near_send, 1)
    far_slots = (far_keep, 0), (far_keep, 1), (far_send, 0), (far_send, 1)
    for at, near, far in zip(ring_slots(x, False), near_slots, far_slots):
        base = pl.multiple_of(at * wide, wide)
        weights = jnp.concatenate(
            [proj_ref[k, pl.ds(base, wide), :] for k in range(filt_count)], axis=1
        )
        result = lax.dot_general(
            all_ref[...], weights, (((1,), (1,)), ((), ())), preferred_element_type=F32
        )
        low, high = result[:, :LANE], result[:, LANE:]
        near[0][near[1]] = jnp.where(z_hi == 0, low, high).astype(near[0].dtype)
        far[0][far[1]] = jnp.where(z_hi == 0, high, low).astype(far[0].dtype)


def input_shares(pos, after, corrs, projection):
    tok = corrs[0].shape[0]
    filt_count = projection.shape[0]
    vmem = pl.BlockSpec(memory_space=pltpu.VMEM)
    keep = jax.ShapeDtypeStruct((2, tok, LANE), F32)
    send = jax.ShapeDtypeStruct((2, tok, LANE), BF16)
    return pl.pallas_call(
        share_kernel,
        out_shape=(keep, send, keep, send),
        in_specs=[pl.BlockSpec(memory_space=pltpu.SMEM), pl.BlockSpec(memory_space=pl.ANY)]
        + [vmem] * (len(corrs) + 1),
        out_specs=(vmem,) * 4,
        scratch_shapes=[pltpu.VMEM((tok, filt_count * LANE), BF16)],
        compiler_params=pltpu.CompilerParams(vmem_limit_bytes=VMEM_LIMIT),
        cost_estimate=SMALL_COST,
        name="input_shares",
    )(pos, after, *corrs, projection)


GROUPS = 2


def per_device(inputs, grad_out, filters, projection):
    tp, ctx = lax.axis_index("tp"), lax.axis_index("ctx")
    pos = jnp.stack([tp, ctx]).astype(jnp.int32)

    def later(value, steps):
        return lax.ppermute(value, "ctx", from_later_chip(steps))

    def sibling(value):
        return lax.ppermute(value, "ctx", CORE_SWAP)

    def y_swapped(value, crossed):
        return lax.ppermute(value, "ctx", y_swap(crossed))

    def z_swapped(value, bit):
        return lax.ppermute(value, "ctx", z_swap(bit))

    def x_swapped(value, crossed):
        return lax.ppermute(value, "tp", x_swap(crossed))

    pair = jnp.stack([inputs, lax.ppermute(inputs, "tp", Z_HI_SWAP)])
    gathered = [pair] + [lax.ppermute(pair, "tp", along_x(s)) for s in range(1, NX)]
    near_table, grad_copy, *far_tables = toeplitz_tables(filters, grad_out, GROUPS)
    halo = [grad_out, later(grad_out, 1), later(grad_out, 2)]
    halo += [later(grad_copy, 3), later(grad_copy, 4)]
    swapped = [sibling(part) for part in halo]
    accs = near_conv(pos, near_table, halo[:3], swapped[:3], GROUPS)

    def conv(group, after):
        return far_conv(pos, after, far_tables[group], accs[group], halo[2:], swapped[2:])

    corr_0 = conv(0, near_table)
    keep_0, send_0 = product(False, pos, corr_0, gathered)
    corr_1 = conv(1, send_0)
    keep_1, send_1 = product(True, pos, corr_1, gathered)

    stay_0, leave_0 = halve(send_1, keep_0, sibling(send_0))
    near, near_send, far, far_send = input_shares(
        pos, leave_0, [corr_0, corr_1], projection.transpose(1, 0, 2)
    )
    y_0 = y_swapped(leave_0, False)
    stay_1, leave_1 = halve(near_send, keep_1, sibling(send_1))
    y_1 = y_swapped(leave_1, True)
    far, leave = halve(leave_1, far, x_swapped(far_send, False))
    x_far = x_swapped(leave, True)
    stay_0, leave_0 = halve(leave, stay_0, y_0)
    y_0 = y_swapped(leave_0, True)
    near, leave = halve(leave_0, near, x_swapped(near_send, True))
    x_near = x_swapped(leave, False)
    stay_1, leave_1 = halve(leave, stay_1, y_1)
    y_1 = y_swapped(leave_1, False)
    far = add(leave_1, far, x_far)
    opposite = lax.ppermute(far, "tp", Z_HI_SWAP)

    stay_0, leave_0 = halve(far, stay_0[0], y_0[0])
    z_0 = z_swapped(leave_0, 1)
    stay_1, leave_1 = halve(leave_0, stay_1[0], y_1[0])
    z_1 = z_swapped(leave_1, 1)
    stay_0, leave_0 = halve(leave_1, stay_0, z_0)
    z_0 = z_swapped(leave_0, 2)
    stay_1, leave_1 = halve(leave_0, stay_1, z_1)
    z_1 = z_swapped(leave_1, 2)
    parts = [stay_0[0] + z_0[0].astype(F32), stay_1[0] + z_1[0].astype(F32)]
    grad_proj = jnp.concatenate(parts, axis=0).transpose(1, 0, 2)
    total = near[0] + x_near[0].astype(F32) + opposite[0].astype(F32)
    return total.astype(BF16), grad_proj


def solution(mesh):
    return jax.shard_map(
        per_device,
        mesh=mesh,
        in_specs=(P("ctx", "tp"), P("ctx", "tp"), P(), P(None, None, "tp")),
        out_specs=(P("ctx", "tp"), P("ctx", None, "tp")),
        check_vma=False,
    )
```

time: 98.5 us -> 94.1 us (0.955)
  starting transfers between devices: 46.8 us -> 43.1 us
  other arithmetic: 4.42 us -> 2.48 us
  Pallas kernels: 19.5 us -> 21.2 us
    ppermute x21 -> x24, starting transfers between devices: 35.7 us -> 31.4 us  [the longest x4 12.9 us: later(): return lax.ppermute(value, 'ctx', from_later_chip(steps))]
    ppermute x21 -> x24, waiting for transfers between devices: 17.6 us -> 20.2 us  [the longest x4 9.55 us: z_swapped(): return lax.ppermute(value, 'ctx', z_swap(bit))]
    ppermute x3, waiting for transfers between devices: 3.74 us -> 1.38 us  [per_device(): lax.ppermute(pair, 'tp', along_x(s))]
    pallas_call x4 -> x17, Pallas kernels: 17.2 us -> 18.9 us  [the longest x2 6.66 us: far_conv(): pl.pallas_call(far_kernel, out_shape=jax.ShapeDtypeStruct((tok, filt_coun...]
    another operation x7 -> x0, other arithmetic: 1.35 us -> none  [the longest x3 1.18 us: per_device(): jnp.stack([jnp.where(first_core, halo[s + 1], halo[s]) for s in (at, at +...]
    unnamed x12 -> x16, local copies, waits for them, and re-layouts: 4.44 us -> 4.2 us
  transfers between devices with their start and end apart: 25 -> 28, of which waited for: 9 -> 8; matrix products, arithmetic and copies ran while one was open for 4% -> 2% of each run, Pallas kernels for 15% -> 21%
where the time goes in v3:
time: 94.1 us; the launch traced here: 93.6 us
  starting transfers between devices  43.1 us (46%)
  waiting for transfers between devices  21.6 us (23%)
  Pallas kernels  21.2 us (23%)
  local copies, waits for them, and re-layouts  4.2 us (4%)
  other arithmetic  2.48 us (3%)
  between operations  0.95 us (1%)
    ppermute x4, starting transfers between devices, later(): return lax.ppermute(value, 'ctx', from_later_chip(steps))  12.9 us
    ppermute x4, waiting for transfers between devices, z_swapped(): return lax.ppermute(value, 'ctx', z_swap(bit))  9.55 us
    ppermute x4, waiting for transfers between devices, x_swapped(): return lax.ppermute(value, 'tp', x_swap(crossed))  8.04 us
    pallas_call x2, Pallas kernels, far_conv(): pl.pallas_call(far_kernel, out_shape=jax.ShapeDtypeStruct((tok, filt_coun...  6.66 us
    ppermute x4, starting transfers between devices, z_swapped(): return lax.ppermute(value, 'ctx', z_swap(bit))  6.1 us
    ppermute x1, starting transfers between devices, per_device(): pair = jnp.stack([inputs, lax.ppermute(inputs, 'tp', Z_HI_SWAP)])  6.02 us
    ppermute x3, starting transfers between devices, per_device(): lax.ppermute(pair, 'tp', along_x(s))  5.73 us
    ppermute x4, starting transfers between devices, x_swapped(): return lax.ppermute(value, 'tp', x_swap(crossed))  5.37 us
  transfers between devices with their start and end apart: 28, of which 8 were waited for; matrix products, arithmetic and copies ran while one was open for 2% of the time, Pallas kernels for 21%

profile of v3, /device:TPU:24, one launch (start us, length us, event | category | flops | bytes accessed | tf_op | source)
XLA Modules:
  0.0 93.6 jit_solution(4906037939454522399)
XLA Ops:
  0.6 5.4 %collective-permute-start.1 = (bf16[512,128]{1,0:T(8,128)(2,1)}, bf16[512,128]{1,0:T(8,128)(2,1)S(1)}, u32[]{:S(2)}, u32[]{:S(2)}) collective-permute-start(bf16[512,128]{1,0:T(8,128)(2,1)} %own_ref.1), channel_id=1, source_target_pairs={{32,0},{40,8},{48,16},{56,24},{64,32},{72,40},{80,48},{88,56},{96,... | collective-permute-start | bytes 393224 | tf_op jit(solution)/shard_map/ppermute | solution.py:325
  6.0 3.3 %collective-permute-start = (bf16[512,128]{1,0:T(8,128)(2,1)}, bf16[512,128]{1,0:T(8,128)(2,1)}, u32[]{:S(2)}, u32[]{:S(2)}) collective-permute-start(bf16[512,128]{1,0:T(8,128)(2,1)} %own_ref.1), channel_id=1, source_target_pairs={{16,0},{24,8},{32,16},{40,24},{48,32},{56,40},{64,48},{72,56},{80,... | collective-permute-start | bytes 393224 | tf_op jit(solution)/shard_map/ppermute | solution.py:325
  9.3 0.1 collective-permute-start.2
  9.4 6.0 %collective-permute-start.9 = (bf16[512,128]{1,0:T(8,128)(2,1)}, bf16[512,128]{1,0:T(8,128)(2,1)}, u32[]{:S(2)}, u32[]{:S(2)}) collective-permute-start(bf16[512,128]{1,0:T(8,128)(2,1)} %param.4), channel_id=1, source_target_pairs={{0,1},{1,0},{2,3},{3,2},{4,5},{5,4},{6,7},{7,6},{8,9},{9,8},{10,11... | collective-permute-start | bytes 393224 | tf_op jit(solution)/shard_map/ppermute | solution.py:339
  15.4 0.9 copy-done.5
  16.3 0.9 copy-done.6
  17.2 2.3 %tables.1 = (bf16[12,64,2048]{2,1,0:T(8,128)(2,1)S(1)}, bf16[512,128]{1,0:T(8,128)(2,1)}, bf16[6,64,2176]{2,1,0:T(8,128)(2,1)S(1)}, bf16[6,64,2176]{2,1,0:T(8,128)(2,1)S(1)}) custom-call(bf16[12,4096]{1,0:T(8,128)(2,1)S(1)} %copy-done.5, bf16[512,128]{1,0:T(8,128)(2,1)S(1)} %copy-done.6), custom_call_target="tpu_custom_call" | custom-call | flops 4000000000 | bytes 8000000 | tf_op jit(solution)/shard_map/tables/pallas_call | solution.py:85
  19.5 1.2 %copy-done.1 = bf16[6,64,2176]{2,1,0:T(8,128)(2,1)} copy-done((bf16[6,64,2176]{2,1,0:T(8,128)(2,1)}, bf16[6,64,2176]{2,1,0:T(8,128)(2,1)S(1)}, u32[]{:S(2)}) %copy-start.1) | copy-done | bytes 1671192
  20.7 1.2 %copy-done.3 = bf16[6,64,2176]{2,1,0:T(8,128)(2,1)} copy-done((bf16[6,64,2176]{2,1,0:T(8,128)(2,1)}, bf16[6,64,2176]{2,1,0:T(8,128)(2,1)S(1)}, u32[]{:S(2)}) %copy-start.3) | copy-done | bytes 1671192
  21.9 1.9 %collective-permute-start.5 = (bf16[512,128]{1,0:T(8,128)(2,1)}, bf16[512,128]{1,0:T(8,128)(2,1)S(1)}, u32[]{:S(2)}, u32[]{:S(2)}) collective-permute-start(bf16[512,128]{1,0:T(8,128)(2,1)} %get-tuple-element.39), channel_id=1, source_target_pairs={{48,0},{56,8},{64,16},{72,24},{80,32},{88,40},{96,48},{104,56},{11... | collective-permute-start | bytes 393224 | tf_op jit(solution)/shard_map/ppermute | solution.py:325
  23.8 2.4 %collective-permute-start.6 = (bf16[512,128]{1,0:T(8,128)(2,1)}, bf16[512,128]{1,0:T(8,128)(2,1)S(1)}, u32[]{:S(2)}, u32[]{:S(2)}) collective-permute-start(bf16[512,128]{1,0:T(8,128)(2,1)} %get-tuple-element.39), channel_id=1, source_target_pairs={{64,0},{72,8},{80,16},{88,24},{96,32},{104,40},{112,48},{120,56},{... | collective-permute-start | bytes 393224 | tf_op jit(solution)/shard_map/ppermute | solution.py:325
  26.2 0.0 collective-permute-done.r1_ref
  26.2 0.1 collective-permute-start.4
  26.3 0.5 collective-permute-start.3
  26.8 0.1 pad_add_fusion.pos_ref
  26.9 1.0 %pad_maximum_fusion.x0_ref = bf16[2,512,128]{2,1,0:T(8,128)(2,1)S(1)} fusion(bf16[1,512,128]{2,1,0:T(8,128)(2,1)} %bitcast.3, bf16[1,512,128]{2,1,0:T(8,128)(2,1)} %bitcast.22), kind=kLoop, calls=%fused_computation | loop fusion | flops 131072 | bytes 524288 | tf_op jit(solution)/shard_map/stack | solution.py:339
  27.9 0.0 collective-permute-done.2.s0_ref
  27.9 1.6 %collective-permute-start.10 = (bf16[2,512,128]{2,1,0:T(8,128)(2,1)S(1)}, bf16[2,512,128]{2,1,0:T(8,128)(2,1)S(1)}, u32[]{:S(2)}, u32[]{:S(2)}) collective-permute-start(bf16[2,512,128]{2,1,0:T(8,128)(2,1)S(1)} %pad_maximum_fusion.x0_ref), channel_id=1, source_target_pairs={{0,2},{1,3},{2,4},{3,5},{4,6},{5,7},{6,0},{7,1},{8,10},{9,11},{10,... | collective-permute-start | bytes 786440 | tf_op jit(solution)/shard_map/ppermute | solution.py:340
  29.5 1.9 %collective-permute-done.5.r3_ref = bf16[512,128]{1,0:T(8,128)(2,1)S(1)} collective-permute-done((bf16[512,128]{1,0:T(8,128)(2,1)}, bf16[512,128]{1,0:T(8,128)(2,1)S(1)}, u32[]{:S(2)}, u32[]{:S(2)}) %collective-permute-start.5) | collective-permute-done | bytes 131104 | tf_op jit(solution)/shard_map/ppermute | solution.py:325
  31.3 3.0 %collective-permute-start.11 = (bf16[2,512,128]{2,1,0:T(8,128)(2,1)S(1)}, bf16[2,512,128]{2,1,0:T(8,128)(2,1)S(1)}, u32[]{:S(2)}, u32[]{:S(2)}) collective-permute-start(bf16[2,512,128]{2,1,0:T(8,128)(2,1)S(1)} %pad_maximum_fusion.x0_ref), channel_id=1, source_target_pairs={{0,4},{1,5},{2,6},{3,7},{4,0},{5,1},{6,2},{7,3},{8,12},{9,13},{10,... | collective-permute-start | bytes 786440 | tf_op jit(solution)/shard_map/ppermute | solution.py:340
  34.4 1.1 %collective-permute-start.12 = (bf16[2,512,128]{2,1,0:T(8,128)(2,1)S(1)}, bf16[2,512,128]{2,1,0:T(8,128)(2,1)S(1)}, u32[]{:S(2)}, u32[]{:S(2)}) collective-permute-start(bf16[2,512,128]{2,1,0:T(8,128)(2,1)S(1)} %pad_maximum_fusion.x0_ref), channel_id=1, source_target_pairs={{0,6},{1,7},{2,0},{3,1},{4,2},{5,3},{6,4},{7,5},{8,14},{9,15},{10,... | collective-permute-start | bytes 786440 | tf_op jit(solution)/shard_map/ppermute | solution.py:340
  35.5 0.0 collective-permute-done.4.s2_ref
  35.5 0.0 collective-permute-start.7
  35.5 0.0 collective-permute-done.3.s1_ref
  35.5 0.5 collective-permute-start.8
  36.0 5.3 %near_conv.1 = (f32[4,384,256]{2,1,0:T(8,128)S(1)}, f32[4,384,256]{2,1,0:T(8,128)S(1)}) custom-call(s32[2]{0:T(128)S(1)} %pad_add_fusion.pos_ref, bf16[12,64,2048]{2,1,0:T(8,128)(2,1)S(1)} %get-tuple-element.36.table_ref._, bf16[512,128]{1,0:T(8,128)(2,1)S(1)} %copy-done.7, bf16[512,128]{1,0:T(8,128)(2,1)} %collective-permute-done.r1_ref, ...), custom_call_target="tpu_custom_call" | custom-call | flops 4000000000 | bytes 8000000 | tf_op jit(solution)/shard_map/near_conv/pallas_call | solution.py:141
  41.4 0.0 collective-permute-done.7.s3_ref
  41.4 0.0 collective-permute-done.8.s4_ref
  41.4 3.3 %far_conv.2.corr_ref.refs_0_ = bf16[512,768]{1,0:T(8,128)(2,1)S(1)} custom-call(s32[2]{0:T(128)S(1)} %pad_add_fusion.pos_ref, bf16[12,64,2048]{2,1,0:T(8,128)(2,1)S(1)} %get-tuple-element.36.table_ref._, bf16[6,64,2176]{2,1,0:T(8,128)(2,1)S(1)} %copy-done.4, f32[4,384,256]{2,1,0:T(8,128)S(1)} %get-tuple-element.38.acc_ref, ...), custom_call_target="tpu_custom_call" | custom-call | flops 1000 | bytes 1000 | tf_op jit(solution)/shard_map/far_conv/pallas_call | solution.py:181
  44.7 0.0 collective-permute-done.11.x2_ref
  44.8 1.4 %collective-permute-done.12.x3_ref = bf16[2,512,128]{2,1,0:T(8,128)(2,1)S(1)} collective-permute-done((bf16[2,512,128]{2,1,0:T(8,128)(2,1)S(1)}, bf16[2,512,128]{2,1,0:T(8,128)(2,1)S(1)}, u32[]{:S(2)}, u32[]{:S(2)}) %collective-permute-start.12) | collective-permute-done | bytes 262176 | tf_op jit(solution)/shard_map/ppermute | solution.py:340
  46.1 1.9 %product.2 = (bf16[4,4,6,32,128]{4,3,2,1,0:T(8,128)(2,1)S(1)}, bf16[4,4,6,32,128]{4,3,2,1,0:T(8,128)(2,1)S(1)}) custom-call(s32[2]{0:T(128)S(1)} %pad_add_fusion.pos_ref, bf16[512,768]{1,0:T(8,128)(2,1)S(1)} %far_conv.2.corr_ref.refs_0_, bf16[2,512,128]{2,1,0:T(8,128)(2,1)S(1)} %pad_maximum_fusion.x0_ref, ...), custom_call_target="tpu_custom_call" | custom-call | flops 1000 | bytes 1000 | tf_op jit(solution)/shard_map/product/pallas_call | solution.py:224
  48.1 0.3 collective-permute-start.13
  48.4 3.3 %far_conv.3.corr_ref.refs_1_ = bf16[512,768]{1,0:T(8,128)(2,1)S(1)} custom-call(s32[2]{0:T(128)S(1)} %pad_add_fusion.pos_ref, bf16[4,4,6,32,128]{4,3,2,1,0:T(8,128)(2,1)S(1)} %get-tuple-element.40._, bf16[6,64,2176]{2,1,0:T(8,128)(2,1)S(1)} %copy-done.2, f32[4,384,256]{2,1,0:T(8,128)S(1)} %get-tuple-element.42.acc_ref, ...), custom_call_target="tpu_custom_call" | custom-call | flops 1000 | bytes 1000 | tf_op jit(solution)/shard_map/far_conv/pallas_call | solution.py:181
  51.7 0.0 copy-start
  51.7 1.9 %product.3 = (bf16[4,4,6,32,128]{4,3,2,1,0:T(8,128)(2,1)S(1)}, bf16[4,4,6,32,128]{4,3,2,1,0:T(8,128)(2,1)S(1)}) custom-call(s32[2]{0:T(128)S(1)} %pad_add_fusion.pos_ref, bf16[512,768]{1,0:T(8,128)(2,1)S(1)} %far_conv.3.corr_ref.refs_1_, bf16[2,512,128]{2,1,0:T(8,128)(2,1)S(1)} %pad_maximum_fusion.x0_ref, ...), custom_call_target="tpu_custom_call" | custom-call | flops 1000 | bytes 1000 | tf_op jit(solution)/shard_map/product/pallas_call | solution.py:224
  53.7 0.6 collective-permute-start.14
  54.2 0.0 collective-permute-done.13.other_ref
  54.2 0.2 halve.10
  54.4 0.5 collective-permute-start.16
  55.0 2.4 %input_shares.1 = (f32[2,512,128]{2,1,0:T(8,128)S(1)}, bf16[2,512,128]{2,1,0:T(8,128)(2,1)S(1)}, f32[2,512,128]{2,1,0:T(8,128)S(1)}, bf16[2,512,128]{2,1,0:T(8,128)(2,1)S(1)}) custom-call(s32[2]{0:T(128)S(1)} %pad_add_fusion.pos_ref, bf16[2,4,6,32,128]{4,3,2,1,0:T(8,128)(2,1)S(1)} %get-tuple-element.45._, bf16[512,768]{1,0:T(8,128)(2,1)S(1)} %far_conv.2.corr_ref.refs_0_, ...), custom_call_target="tpu_custom_call" | custom-call | flops 1000 | bytes 1000 | tf_op jit(solution)/shard_map/input_shares/pallas_call | solution.py:304
  57.3 0.2 halve.11
  57.5 1.1 %collective-permute-start.19 = (bf16[2,4,6,32,128]{4,3,2,1,0:T(8,128)(2,1)S(1)}, bf16[2,4,6,32,128]{4,3,2,1,0:T(8,128)(2,1)S(1)}, u32[]{:S(2)}, u32[]{:S(2)}) collective-permute-start(bf16[2,4,6,32,128]{4,3,2,1,0:T(8,128)(2,1)S(1)} %get-tuple-element.48._), channel_id=1, source_target_pairs={{0,192},{8,200},{16,208},{24,216},{32,224},{40,232},{48,240},{56,2... | collective-permute-start | bytes 1179656 | tf_op jit(solution)/shard_map/ppermute | solution.py:331
  58.6 1.4 %collective-permute-start.15 = (bf16[2,512,128]{2,1,0:T(8,128)(2,1)S(1)}, bf16[2,512,128]{2,1,0:T(8,128)(2,1)S(1)}, u32[]{:S(2)}, u32[]{:S(2)}) collective-permute-start(bf16[2,512,128]{2,1,0:T(8,128)(2,1)S(1)} %get-tuple-element.50), channel_id=1, source_target_pairs={{0,2},{1,3},{2,0},{3,1},{4,6},{5,7},{6,4},{7,5},{8,10},{9,11},{10,... | collective-permute-start | bytes 786440 | tf_op jit(solution)/shard_map/ppermute | solution.py:337
  60.0 1.3 %collective-permute-start.17 = (bf16[2,512,128]{2,1,0:T(8,128)(2,1)S(1)}, bf16[2,512,128]{2,1,0:T(8,128)(2,1)S(1)}, u32[]{:S(2)}, u32[]{:S(2)}) collective-permute-start(bf16[2,512,128]{2,1,0:T(8,128)(2,1)S(1)} %get-tuple-element.46._), channel_id=1, source_target_pairs={{0,6},{1,7},{2,4},{3,5},{4,2},{5,3},{6,0},{7,1},{8,14},{9,15},{10,... | collective-permute-start | bytes 786440 | tf_op jit(solution)/shard_map/ppermute | solution.py:337
  61.3 5.1 %collective-permute-done.15.other_ref = bf16[2,512,128]{2,1,0:T(8,128)(2,1)S(1)} collective-permute-done((bf16[2,512,128]{2,1,0:T(8,128)(2,1)S(1)}, bf16[2,512,128]{2,1,0:T(8,128)(2,1)S(1)}, u32[]{:S(2)}, u32[]{:S(2)}) %collective-permute-start.15) | collective-permute-done | bytes 262176 | tf_op jit(solution)/shard_map/ppermute | solution.py:337
  66.4 0.1 halve.13
  66.5 2.3 %collective-permute-start.22 = (bf16[1,4,6,32,128]{4,3,2,1,0:T(8,128)(2,1)S(1)}, bf16[1,4,6,32,128]{4,3,2,1,0:T(8,128)(2,1)S(1)}, u32[]{:S(2)}, u32[]{:S(2)}) collective-permute-start(bf16[1,4,6,32,128]{4,3,2,1,0:T(8,128)(2,1)S(1)} %get-tuple-element.53._), channel_id=1, source_target_pairs={{0,192},{8,200},{16,208},{24,216},{32,224},{40,232},{48,240},{56,2... | collective-permute-start | bytes 589832 | tf_op jit(solution)/shard_map/ppermute | solution.py:331
  68.7 2.6 %collective-permute-start.20 = (bf16[1,512,128]{2,1,0:T(8,128)(2,1)S(1)}, bf16[1,512,128]{2,1,0:T(8,128)(2,1)S(1)}, u32[]{:S(2)}, u32[]{:S(2)}) collective-permute-start(bf16[1,512,128]{2,1,0:T(8,128)(2,1)S(1)} %get-tuple-element.51._), channel_id=1, source_target_pairs={{0,6},{1,7},{2,4},{3,5},{4,2},{5,3},{6,0},{7,1},{8,14},{9,15},{10,... | collective-permute-start | bytes 393224 | tf_op jit(solution)/shard_map/ppermute | solution.py:337
  71.4 0.1 halve.15
  71.5 0.4 collective-permute-start.23
  71.9 3.0 %collective-permute-done.20.other_ref = bf16[1,512,128]{2,1,0:T(8,128)(2,1)S(1)} collective-permute-done((bf16[1,512,128]{2,1,0:T(8,128)(2,1)S(1)}, bf16[1,512,128]{2,1,0:T(8,128)(2,1)S(1)}, u32[]{:S(2)}, u32[]{:S(2)}) %collective-permute-start.20) | collective-permute-done | bytes 131104 | tf_op jit(solution)/shard_map/ppermute | solution.py:337
  75.0 0.6 collective-permute-start.21
  75.5 0.1 collective-permute-start.18
  75.7 0.8 collective-permute-start.24
  76.5 0.7 collective-permute-done.23
  77.3 0.7 collective-permute-start.26
  78.0 4.8 %collective-permute-done.24.other_ref = bf16[2,6,32,128]{3,2,1,0:T(8,128)(2,1)S(1)} collective-permute-done((bf16[2,6,32,128]{3,2,1,0:T(8,128)(2,1)S(1)}, bf16[2,6,32,128]{3,2,1,0:T(8,128)(2,1)S(1)}, u32[]{:S(2)}, u32[]{:S(2)}) %collective-permute-start.24) | collective-permute-done | bytes 98336 | tf_op jit(solution)/shard_map/ppermute | solution.py:334
  82.8 4.3 %collective-permute-start.25 = (bf16[1,6,32,128]{3,2,1,0:T(8,128)(2,1)S(1)}, bf16[1,6,32,128]{3,2,1,0:T(8,128)(2,1)S(1)}, u32[]{:S(2)}, u32[]{:S(2)}) collective-permute-start(bf16[1,6,32,128]{3,2,1,0:T(8,128)(2,1)S(1)} %get-tuple-element.66._), channel_id=1, source_target_pairs={{0,32},{8,40},{16,48},{24,56},{32,0},{40,8},{48,16},{56,24},{64,96... | collective-permute-start | bytes 147464 | tf_op jit(solution)/shard_map/ppermute | solution.py:334
  87.1 0.7 fusion
  87.8 0.3 collective-permute-start.27
  88.1 1.0 %collective-permute-done.25 = bf16[1,6,32,128]{3,2,1,0:T(8,128)(2,1)S(1)} collective-permute-done((bf16[1,6,32,128]{3,2,1,0:T(8,128)(2,1)S(1)}, bf16[1,6,32,128]{3,2,1,0:T(8,128)(2,1)S(1)}, u32[]{:S(2)}, u32[]{:S(2)}) %collective-permute-start.25) | collective-permute-done | bytes 49184 | tf_op jit(solution)/shard_map/ppermute | solution.py:334
  89.2 3.7 %collective-permute-done.27 = bf16[1,6,32,128]{3,2,1,0:T(8,128)(2,1)S(1)} collective-permute-done((bf16[1,6,32,128]{3,2,1,0:T(8,128)(2,1)S(1)}, bf16[1,6,32,128]{3,2,1,0:T(8,128)(2,1)S(1)}, u32[]{:S(2)}, u32[]{:S(2)}) %collective-permute-start.27) | collective-permute-done | bytes 49184 | tf_op jit(solution)/shard_map/ppermute | solution.py:334
  92.9 0.7 maximum_bitcast_fusion
  (32 shorter events, 0.3 us)
Async XLA Ops:
  0.6 23.2 %collective-permute-start.1 = (bf16[512,128]{1,0:T(8,128)(2,1)}, bf16[512,128]{1,0:T(8,128)(2,1)S(1)}, u32[]{:S(2)}, u32[]{:S(2)}) collective-permute-start(bf16[512,128]{1,0:T(8,128)(2,1)} %own_ref.1), channel_id=1, source_target_pairs={{32,0},{40,8},{48,16},{56,24},{64,32},{72,40},{80,48},{88,56},{96,... | collective-permute-start | bytes 393224 | tf_op jit(solution)/shard_map/ppermute | solution.py:325
  6.0 20.2 %collective-permute-start = (bf16[512,128]{1,0:T(8,128)(2,1)}, bf16[512,128]{1,0:T(8,128)(2,1)}, u32[]{:S(2)}, u32[]{:S(2)}) collective-permute-start(bf16[512,128]{1,0:T(8,128)(2,1)} %own_ref.1), channel_id=1, source_target_pairs={{16,0},{24,8},{32,16},{40,24},{48,32},{56,40},{64,48},{72,56},{80,... | collective-permute-start | bytes 393224 | tf_op jit(solution)/shard_map/ppermute | solution.py:325
  9.3 18.6 %collective-permute-start.2 = (bf16[512,128]{1,0:T(8,128)(2,1)}, bf16[512,128]{1,0:T(8,128)(2,1)}, u32[]{:S(2)}, u32[]{:S(2)}) collective-permute-start(bf16[512,128]{1,0:T(8,128)(2,1)} %own_ref.1), channel_id=1, source_target_pairs={{0,8},{8,0},{16,24},{24,16},{32,40},{40,32},{48,56},{56,48},{64,72... | collective-permute-start | bytes 393224 | tf_op jit(solution)/shard_map/ppermute | solution.py:328
  9.4 16.9 %collective-permute-start.9 = (bf16[512,128]{1,0:T(8,128)(2,1)}, bf16[512,128]{1,0:T(8,128)(2,1)}, u32[]{:S(2)}, u32[]{:S(2)}) collective-permute-start(bf16[512,128]{1,0:T(8,128)(2,1)} %param.4), channel_id=1, source_target_pairs={{0,1},{1,0},{2,3},{3,2},{4,5},{5,4},{6,7},{7,6},{8,9},{9,8},{10,11... | collective-permute-start | bytes 393224 | tf_op jit(solution)/shard_map/ppermute | solution.py:339
  15.4 0.9 copy-start.5
  16.3 0.9 copy-start.6
  17.2 18.8 %copy-start.7 = (bf16[512,128]{1,0:T(8,128)(2,1)S(1)}, bf16[512,128]{1,0:T(8,128)(2,1)}, u32[]{:S(2)}) copy-start(bf16[512,128]{1,0:T(8,128)(2,1)} %own_ref.1) | copy-start | bytes 393220
  19.5 1.2 %copy-start.1 = (bf16[6,64,2176]{2,1,0:T(8,128)(2,1)}, bf16[6,64,2176]{2,1,0:T(8,128)(2,1)S(1)}, u32[]{:S(2)}) copy-start(bf16[6,64,2176]{2,1,0:T(8,128)(2,1)S(1)} %get-tuple-element.41.table_ref) | copy-start | bytes 5013508
  20.7 1.2 %copy-start.3 = (bf16[6,64,2176]{2,1,0:T(8,128)(2,1)}, bf16[6,64,2176]{2,1,0:T(8,128)(2,1)S(1)}, u32[]{:S(2)}) copy-start(bf16[6,64,2176]{2,1,0:T(8,128)(2,1)S(1)} %get-tuple-element.37.table_ref) | copy-start | bytes 5013508
  21.9 9.4 %collective-permute-start.5 = (bf16[512,128]{1,0:T(8,128)(2,1)}, bf16[512,128]{1,0:T(8,128)(2,1)S(1)}, u32[]{:S(2)}, u32[]{:S(2)}) collective-permute-start(bf16[512,128]{1,0:T(8,128)(2,1)} %get-tuple-element.39), channel_id=1, source_target_pairs={{48,0},{56,8},{64,16},{72,24},{80,32},{88,40},{96,48},{104,56},{11... | collective-permute-start | bytes 393224 | tf_op jit(solution)/shard_map/ppermute | solution.py:325
  23.8 10.5 %collective-permute-start.6 = (bf16[512,128]{1,0:T(8,128)(2,1)}, bf16[512,128]{1,0:T(8,128)(2,1)S(1)}, u32[]{:S(2)}, u32[]{:S(2)}) collective-permute-start(bf16[512,128]{1,0:T(8,128)(2,1)} %get-tuple-element.39), channel_id=1, source_target_pairs={{64,0},{72,8},{80,16},{88,24},{96,32},{104,40},{112,48},{120,56},{... | collective-permute-start | bytes 393224 | tf_op jit(solution)/shard_map/ppermute | solution.py:325
  26.2 9.3 %collective-permute-start.4 = (bf16[512,128]{1,0:T(8,128)(2,1)S(1)}, bf16[512,128]{1,0:T(8,128)(2,1)S(1)}, u32[]{:S(2)}, u32[]{:S(2)}) collective-permute-start(bf16[512,128]{1,0:T(8,128)(2,1)S(1)} %collective-permute-done.1.r2_ref), channel_id=1, source_target_pairs={{0,8},{8,0},{16,24},{24,16},{32,40},{40,32},{48,56},{56,48},{64,72... | collective-permute-start | bytes 393224 | tf_op jit(solution)/shard_map/ppermute | solution.py:328
  26.3 9.2 %collective-permute-start.3 = (bf16[512,128]{1,0:T(8,128)(2,1)}, bf16[512,128]{1,0:T(8,128)(2,1)S(1)}, u32[]{:S(2)}, u32[]{:S(2)}) collective-permute-start(bf16[512,128]{1,0:T(8,128)(2,1)} %collective-permute-done.r1_ref), channel_id=1, source_target_pairs={{0,8},{8,0},{16,24},{24,16},{32,40},{40,32},{48,56},{56,48},{64,72... | collective-permute-start | bytes 393224 | tf_op jit(solution)/shard_map/ppermute | solution.py:328
  27.9 16.8 %collective-permute-start.10 = (bf16[2,512,128]{2,1,0:T(8,128)(2,1)S(1)}, bf16[2,512,128]{2,1,0:T(8,128)(2,1)S(1)}, u32[]{:S(2)}, u32[]{:S(2)}) collective-permute-start(bf16[2,512,128]{2,1,0:T(8,128)(2,1)S(1)} %pad_maximum_fusion.x0_ref), channel_id=1, source_target_pairs={{0,2},{1,3},{2,4},{3,5},{4,6},{5,7},{6,0},{7,1},{8,10},{9,11},{10,... | collective-permute-start | bytes 786440 | tf_op jit(solution)/shard_map/ppermute | solution.py:340
  31.3 13.4 %collective-permute-start.11 = (bf16[2,512,128]{2,1,0:T(8,128)(2,1)S(1)}, bf16[2,512,128]{2,1,0:T(8,128)(2,1)S(1)}, u32[]{:S(2)}, u32[]{:S(2)}) collective-permute-start(bf16[2,512,128]{2,1,0:T(8,128)(2,1)S(1)} %pad_maximum_fusion.x0_ref), channel_id=1, source_target_pairs={{0,4},{1,5},{2,6},{3,7},{4,0},{5,1},{6,2},{7,3},{8,12},{9,13},{10,... | collective-permute-start | bytes 786440 | tf_op jit(solution)/shard_map/ppermute | solution.py:340
  34.4 11.8 %collective-permute-start.12 = (bf16[2,512,128]{2,1,0:T(8,128)(2,1)S(1)}, bf16[2,512,128]{2,1,0:T(8,128)(2,1)S(1)}, u32[]{:S(2)}, u32[]{:S(2)}) collective-permute-start(bf16[2,512,128]{2,1,0:T(8,128)(2,1)S(1)} %pad_maximum_fusion.x0_ref), channel_id=1, source_target_pairs={{0,6},{1,7},{2,0},{3,1},{4,2},{5,3},{6,4},{7,5},{8,14},{9,15},{10,... | collective-permute-start | bytes 786440 | tf_op jit(solution)/shard_map/ppermute | solution.py:340
  35.5 5.8 %collective-permute-start.7 = (bf16[512,128]{1,0:T(8,128)(2,1)S(1)}, bf16[512,128]{1,0:T(8,128)(2,1)S(1)}, u32[]{:S(2)}, u32[]{:S(2)}) collective-permute-start(bf16[512,128]{1,0:T(8,128)(2,1)S(1)} %collective-permute-done.5.r3_ref), channel_id=1, source_target_pairs={{0,8},{8,0},{16,24},{24,16},{32,40},{40,32},{48,56},{56,48},{64,72... | collective-permute-start | bytes 393224 | tf_op jit(solution)/shard_map/ppermute | solution.py:328
  35.5 5.8 %collective-permute-start.8 = (bf16[512,128]{1,0:T(8,128)(2,1)S(1)}, bf16[512,128]{1,0:T(8,128)(2,1)S(1)}, u32[]{:S(2)}, u32[]{:S(2)}) collective-permute-start(bf16[512,128]{1,0:T(8,128)(2,1)S(1)} %collective-permute-done.6.r4_ref), channel_id=1, source_target_pairs={{0,8},{8,0},{16,24},{24,16},{32,40},{40,32},{48,56},{56,48},{64,72... | collective-permute-start | bytes 393224 | tf_op jit(solution)/shard_map/ppermute | solution.py:328
  36.0 5.3 %copy-start.4 = (bf16[6,64,2176]{2,1,0:T(8,128)(2,1)S(1)}, bf16[6,64,2176]{2,1,0:T(8,128)(2,1)}, u32[]{:S(2)}) copy-start(bf16[6,64,2176]{2,1,0:T(8,128)(2,1)} %copy-done.3) | copy-start | bytes 5013508
  44.7 3.6 %copy-start.2 = (bf16[6,64,2176]{2,1,0:T(8,128)(2,1)S(1)}, bf16[6,64,2176]{2,1,0:T(8,128)(2,1)}, u32[]{:S(2)}) copy-start(bf16[6,64,2176]{2,1,0:T(8,128)(2,1)} %copy-done.1) | copy-start | bytes 5013508
  48.1 6.2 %collective-permute-start.13 = (bf16[4,4,6,32,128]{4,3,2,1,0:T(8,128)(2,1)S(1)}, bf16[4,4,6,32,128]{4,3,2,1,0:T(8,128)(2,1)S(1)}, u32[]{:S(2)}, u32[]{:S(2)}) collective-permute-start(bf16[4,4,6,32,128]{4,3,2,1,0:T(8,128)(2,1)S(1)} %get-tuple-element.40._), channel_id=1, source_target_pairs={{0,8},{8,0},{16,24},{24,16},{32,40},{40,32},{48,56},{56,48},{64,72... | collective-permute-start | bytes 2359304 | tf_op jit(solution)/shard_map/ppermute | solution.py:328
  51.7 3.3 %copy-start = (bf16[1024,12,128]{2,0,1:T(8,128)(2,1)S(1)}, bf16[1024,12,128]{2,0,1:T(8,128)(2,1)}, u32[]{:S(2)}) copy-start(bf16[1024,12,128]{2,0,1:T(8,128)(2,1)} %param.7) | copy-start | bytes 9437188
  53.7 3.7 %collective-permute-start.14 = (bf16[4,4,6,32,128]{4,3,2,1,0:T(8,128)(2,1)S(1)}, bf16[4,4,6,32,128]{4,3,2,1,0:T(8,128)(2,1)S(1)}, u32[]{:S(2)}, u32[]{:S(2)}) collective-permute-start(bf16[4,4,6,32,128]{4,3,2,1,0:T(8,128)(2,1)S(1)} %get-tuple-element.43._), channel_id=1, source_target_pairs={{0,8},{8,0},{16,24},{24,16},{32,40},{40,32},{48,56},{56,48},{64,72... | collective-permute-start | bytes 2359304 | tf_op jit(solution)/shard_map/ppermute | solution.py:328
  54.4 12.0 %collective-permute-start.16 = (bf16[2,4,6,32,128]{4,3,2,1,0:T(8,128)(2,1)S(1)}, bf16[2,4,6,32,128]{4,3,2,1,0:T(8,128)(2,1)S(1)}, u32[]{:S(2)}, u32[]{:S(2)}) collective-permute-start(bf16[2,4,6,32,128]{4,3,2,1,0:T(8,128)(2,1)S(1)} %get-tuple-element.45._), channel_id=1, source_target_pairs={{0,64},{8,72},{16,80},{24,88},{32,96},{40,104},{48,112},{56,120},{... | collective-permute-start | bytes 1179656 | tf_op jit(solution)/shard_map/ppermute | solution.py:331
  57.5 13.9 %collective-permute-start.19 = (bf16[2,4,6,32,128]{4,3,2,1,0:T(8,128)(2,1)S(1)}, bf16[2,4,6,32,128]{4,3,2,1,0:T(8,128)(2,1)S(1)}, u32[]{:S(2)}, u32[]{:S(2)}) collective-permute-start(bf16[2,4,6,32,128]{4,3,2,1,0:T(8,128)(2,1)S(1)} %get-tuple-element.48._), channel_id=1, source_target_pairs={{0,192},{8,200},{16,208},{24,216},{32,224},{40,232},{48,240},{56,2... | collective-permute-start | bytes 1179656 | tf_op jit(solution)/shard_map/ppermute | solution.py:331
  58.6 7.7 %collective-permute-start.15 = (bf16[2,512,128]{2,1,0:T(8,128)(2,1)S(1)}, bf16[2,512,128]{2,1,0:T(8,128)(2,1)S(1)}, u32[]{:S(2)}, u32[]{:S(2)}) collective-permute-start(bf16[2,512,128]{2,1,0:T(8,128)(2,1)S(1)} %get-tuple-element.50), channel_id=1, source_target_pairs={{0,2},{1,3},{2,0},{3,1},{4,6},{5,7},{6,4},{7,5},{8,10},{9,11},{10,... | collective-permute-start | bytes 786440 | tf_op jit(solution)/shard_map/ppermute | solution.py:337
  60.0 11.4 %collective-permute-start.17 = (bf16[2,512,128]{2,1,0:T(8,128)(2,1)S(1)}, bf16[2,512,128]{2,1,0:T(8,128)(2,1)S(1)}, u32[]{:S(2)}, u32[]{:S(2)}) collective-permute-start(bf16[2,512,128]{2,1,0:T(8,128)(2,1)S(1)} %get-tuple-element.46._), channel_id=1, source_target_pairs={{0,6},{1,7},{2,4},{3,5},{4,2},{5,3},{6,0},{7,1},{8,14},{9,15},{10,... | collective-permute-start | bytes 786440 | tf_op jit(solution)/shard_map/ppermute | solution.py:337
  66.5 9.2 %collective-permute-start.22 = (bf16[1,4,6,32,128]{4,3,2,1,0:T(8,128)(2,1)S(1)}, bf16[1,4,6,32,128]{4,3,2,1,0:T(8,128)(2,1)S(1)}, u32[]{:S(2)}, u32[]{:S(2)}) collective-permute-start(bf16[1,4,6,32,128]{4,3,2,1,0:T(8,128)(2,1)S(1)} %get-tuple-element.53._), channel_id=1, source_target_pairs={{0,192},{8,200},{16,208},{24,216},{32,224},{40,232},{48,240},{56,2... | collective-permute-start | bytes 589832 | tf_op jit(solution)/shard_map/ppermute | solution.py:331
  68.7 6.2 %collective-permute-start.20 = (bf16[1,512,128]{2,1,0:T(8,128)(2,1)S(1)}, bf16[1,512,128]{2,1,0:T(8,128)(2,1)S(1)}, u32[]{:S(2)}, u32[]{:S(2)}) collective-permute-start(bf16[1,512,128]{2,1,0:T(8,128)(2,1)S(1)} %get-tuple-element.51._), channel_id=1, source_target_pairs={{0,6},{1,7},{2,4},{3,5},{4,2},{5,3},{6,0},{7,1},{8,14},{9,15},{10,... | collective-permute-start | bytes 393224 | tf_op jit(solution)/shard_map/ppermute | solution.py:337
  71.5 5.8 %collective-permute-start.23 = (bf16[1,4,6,32,128]{4,3,2,1,0:T(8,128)(2,1)S(1)}, bf16[1,4,6,32,128]{4,3,2,1,0:T(8,128)(2,1)S(1)}, u32[]{:S(2)}, u32[]{:S(2)}) collective-permute-start(bf16[1,4,6,32,128]{4,3,2,1,0:T(8,128)(2,1)S(1)} %get-tuple-element.58._), channel_id=1, source_target_pairs={{0,64},{8,72},{16,80},{24,88},{32,96},{40,104},{48,112},{56,120},{... | collective-permute-start | bytes 589832 | tf_op jit(solution)/shard_map/ppermute | solution.py:331
  75.0 12.1 %collective-permute-start.21 = (bf16[1,512,128]{2,1,0:T(8,128)(2,1)S(1)}, bf16[1,512,128]{2,1,0:T(8,128)(2,1)S(1)}, u32[]{:S(2)}, u32[]{:S(2)}) collective-permute-start(bf16[1,512,128]{2,1,0:T(8,128)(2,1)S(1)} %add.37._), channel_id=1, source_target_pairs={{0,1},{1,0},{2,3},{3,2},{4,5},{5,4},{6,7},{7,6},{8,9},{9,8},{10,11... | collective-permute-start | bytes 393224 | tf_op jit(solution)/shard_map/ppermute | solution.py:371
  75.5 11.6 %collective-permute-start.18 = (bf16[1,512,128]{2,1,0:T(8,128)(2,1)S(1)}, bf16[1,512,128]{2,1,0:T(8,128)(2,1)S(1)}, u32[]{:S(2)}, u32[]{:S(2)}) collective-permute-start(bf16[1,512,128]{2,1,0:T(8,128)(2,1)S(1)} %get-tuple-element.56._), channel_id=1, source_target_pairs={{0,2},{1,3},{2,0},{3,1},{4,6},{5,7},{6,4},{7,5},{8,10},{9,11},{10,... | collective-permute-start | bytes 393224 | tf_op jit(solution)/shard_map/ppermute | solution.py:337
  75.7 7.0 %collective-permute-start.24 = (bf16[2,6,32,128]{3,2,1,0:T(8,128)(2,1)S(1)}, bf16[2,6,32,128]{3,2,1,0:T(8,128)(2,1)S(1)}, u32[]{:S(2)}, u32[]{:S(2)}) collective-permute-start(bf16[2,6,32,128]{3,2,1,0:T(8,128)(2,1)S(1)} %get-tuple-element.61._), channel_id=1, source_target_pairs={{0,16},{8,24},{16,0},{24,8},{32,48},{40,56},{48,32},{56,40},{64,80... | collective-permute-start | bytes 294920 | tf_op jit(solution)/shard_map/ppermute | solution.py:334
  77.3 10.5 %collective-permute-start.26 = (bf16[2,6,32,128]{3,2,1,0:T(8,128)(2,1)S(1)}, bf16[2,6,32,128]{3,2,1,0:T(8,128)(2,1)S(1)}, u32[]{:S(2)}, u32[]{:S(2)}) collective-permute-start(bf16[2,6,32,128]{3,2,1,0:T(8,128)(2,1)S(1)} %get-tuple-element.63._), channel_id=1, source_target_pairs={{0,16},{8,24},{16,0},{24,8},{32,48},{40,56},{48,32},{56,40},{64,80... | collective-permute-start | bytes 294920 | tf_op jit(solution)/shard_map/ppermute | solution.py:334
  82.8 6.4 %collective-permute-start.25 = (bf16[1,6,32,128]{3,2,1,0:T(8,128)(2,1)S(1)}, bf16[1,6,32,128]{3,2,1,0:T(8,128)(2,1)S(1)}, u32[]{:S(2)}, u32[]{:S(2)}) collective-permute-start(bf16[1,6,32,128]{3,2,1,0:T(8,128)(2,1)S(1)} %get-tuple-element.66._), channel_id=1, source_target_pairs={{0,32},{8,40},{16,48},{24,56},{32,0},{40,8},{48,16},{56,24},{64,96... | collective-permute-start | bytes 147464 | tf_op jit(solution)/shard_map/ppermute | solution.py:334
  87.8 5.1 %collective-permute-start.27 = (bf16[1,6,32,128]{3,2,1,0:T(8,128)(2,1)S(1)}, bf16[1,6,32,128]{3,2,1,0:T(8,128)(2,1)S(1)}, u32[]{:S(2)}, u32[]{:S(2)}) collective-permute-start(bf16[1,6,32,128]{3,2,1,0:T(8,128)(2,1)S(1)} %get-tuple-element.69), channel_id=1, source_target_pairs={{0,32},{8,40},{16,48},{24,56},{32,0},{40,8},{48,16},{56,24},{64,96... | collective-permute-start | bytes 147464 | tf_op jit(solution)/shard_map/ppermute | solution.py:334

commit v4 on v3

--- a/solution.py
+++ b/solution.py
@@ -60,37 +60,57 @@
     ]
 
 
-def table_kernel(filters_ref, grad_ref, near_ref, copy_ref, *far_refs):
-    copy_ref[...] = grad_ref[...]
+def shifted_rows(line, rows):
+    block = jnp.broadcast_to(line, (rows, line.shape[1]))
+    return pltpu.roll(block, 0, 1, stride=1, stride_axis=0).astype(BF16)
+
+
+def table_kernel(filters_ref, near_ref):
     filt_count, rows, near = near_ref.shape
-    per_group, _, far = far_refs[0].shape
-    taps = filters_ref.shape[1]
-    width = near + far
+    edge = jnp.zeros((1, LANE), F32)
     for k in range(filt_count):
-        line = filters_ref[k : k + 1, :].astype(F32)
-        line = jnp.concatenate([line, jnp.zeros((1, width - taps), F32)], axis=1)
-        block = jnp.broadcast_to(line, (rows, width))
-        block = pltpu.roll(block, 0, 1, stride=1, stride_axis=0).astype(BF16)
-        near_ref[k] = block[:, :near]
-        far_refs[k // per_group][k % per_group] = block[:, near:]
-
-
-def toeplitz_tables(filters, grad_out, groups):
+        line = filters_ref[k : k + 1, :near].astype(F32)
+        near_ref[k] = shifted_rows(jnp.concatenate([line, edge], axis=1), rows)[:, :near]
+
+
+def near_table(filters):
     filt_count, taps = filters.shape
-    near, far = taps // 2, taps // 2 + LANE
-    vmem = pl.BlockSpec(memory_space=pltpu.VMEM)
-    outs = [jax.ShapeDtypeStruct((filt_count, ROWS, near), BF16)]
-    outs += [jax.ShapeDtypeStruct(grad_out.shape, BF16)]
-    outs += [jax.ShapeDtypeStruct((filt_count // groups, ROWS, far), BF16)] * groups
+    vmem = pl.BlockSpec(memory_space=pltpu.VMEM)
     return pl.pallas_call(
         table_kernel,
-        out_shape=outs,
-        in_specs=[vmem] * 2,
-        out_specs=[vmem] * (2 + groups),
+        out_shape=jax.ShapeDtypeStruct((filt_count, ROWS, taps // 2), BF16),
+        in_specs=[vmem],
+        out_specs=vmem,
         compiler_params=pltpu.CompilerParams(vmem_limit_bytes=VMEM_LIMIT),
         cost_estimate=LARGE_COST,
-        name="tables",
-    )(filters, grad_out)
+        name="near_table",
+    )(filters)
+
+
+def prep_kernel(_, own_ref, r1_ref, r2_ref, r4_ref, in_ref, far_in_ref, stack_ref, pair_ref, copy_ref):
+    copy_ref[...] = own_ref[...]
+    for s, part in enumerate((own_ref, r1_ref, r2_ref, r4_ref)):
+        stack_ref[s] = part[...]
+    pair_ref[0] = in_ref[...]
+    pair_ref[1] = far_in_ref[...]
+
+
+def prepare(after, *parts):
+    block = parts[0].shape
+    vmem = pl.BlockSpec(memory_space=pltpu.VMEM)
+    return pl.pallas_call(
+        prep_kernel,
+        out_shape=[
+            jax.ShapeDtypeStruct((4,) + block, BF16),
+            jax.ShapeDtypeStruct((2,) + block, BF16),
+            jax.ShapeDtypeStruct(block, BF16),
+        ],
+        in_specs=[pl.BlockSpec(memory_space=pl.ANY)] + [vmem] * 6,
+        out_specs=[vmem] * 3,
+        compiler_params=pltpu.CompilerParams(vmem_limit_bytes=VMEM_LIMIT),
+        cost_estimate=SMALL_COST,
+        name="prepare",
+    )(after, *parts)
 
 
 def pair_of_blocks(grad_ref, start, rows, width):
@@ -115,12 +135,12 @@
         )
 
 
-def near_kernel(pos_ref, table_ref, own_ref, r1_ref, r2_ref, s0_ref, s1_ref, s2_ref, *refs):
+def near_kernel(pos_ref, table_ref, own_ref, r1_ref, r2_ref, sib_ref, *refs):
     acc_refs, grad_ref = refs[:-1], refs[-1]
     filt_count, rows, width = table_ref.shape
     tok = own_ref.shape[0]
     core = coords(pos_ref)[-1]
-    lay_out(core, grad_ref, (own_ref, r1_ref, r2_ref), (s0_ref, s1_ref, s2_ref))
+    lay_out(core, grad_ref, (own_ref, r1_ref, r2_ref), [sib_ref.at[s] for s in range(3)])
     table = table_ref[...].reshape(filt_count * rows, width)
 
     @pl.loop(0, tok // (2 * rows))
@@ -133,7 +153,7 @@
             acc_ref[pair] = result[group * part : (group + 1) * part]
 
 
-def near_conv(pos, table, halo, swapped, groups):
+def near_conv(pos, table, halo, sibling, groups):
     filt_count, rows, width = table.shape
     tok = halo[0].shape[0]
     vmem = pl.BlockSpec(memory_space=pltpu.VMEM)
@@ -141,30 +161,35 @@
     return pl.pallas_call(
         near_kernel,
         out_shape=[acc] * groups,
-        in_specs=[pl.BlockSpec(memory_space=pltpu.SMEM)] + [vmem] * 7,
+        in_specs=[pl.BlockSpec(memory_space=pltpu.SMEM)] + [vmem] * 5,
         out_specs=[vmem] * groups,
         scratch_shapes=[pltpu.VMEM((5 * tok, LANE), BF16)],
         compiler_params=pltpu.CompilerParams(vmem_limit_bytes=VMEM_LIMIT),
         cost_estimate=LARGE_COST,
         name="near_conv",
-    )(pos, table, *halo, *swapped)
+    )(pos, table, *halo, sibling)
 
 
 def far_kernel(
-    pos_ref, _, table_ref, acc_ref, r2_ref, r3_ref, r4_ref, s2_ref, s3_ref, s4_ref,
-    corr_ref, grad_ref,
+    first, pos_ref, _, filters_ref, acc_ref, r2_ref, r3_ref, r4_ref, sib_ref, sib_r3_ref,
+    corr_ref, grad_ref, table_ref,
 ):
     filt_count, rows, width = table_ref.shape
     tok = r2_ref.shape[0]
     core = coords(pos_ref)[-1]
-    lay_out(core, grad_ref, (r2_ref, r3_ref, r4_ref), (s2_ref, s3_ref, s4_ref))
+    edge = jnp.zeros((1, LANE), F32)
+    start = filters_ref.shape[1] + LANE - width - LANE
+    for k in range(filt_count):
+        line = filters_ref[first + k : first + k + 1, start:].astype(F32)
+        table_ref[k] = shifted_rows(jnp.concatenate([line, edge], axis=1), rows)[:, LANE:]
+    lay_out(core, grad_ref, (r2_ref, r3_ref, r4_ref), (sib_ref.at[2], sib_r3_ref, sib_ref.at[3]))
     grad_ref[5 * tok :, :] = jnp.zeros((grad_ref.shape[0] - 5 * tok, LANE), BF16)
-    table = table_ref[...].reshape(filt_count * rows, width)
 
     @pl.loop(0, tok // (2 * rows))
     def _(pair):
         start = pl.multiple_of(pair * (2 * rows), 2 * rows)
         both = pair_of_blocks(grad_ref, start, rows, width)
+        table = table_ref[...].reshape(filt_count * rows, width)
         result = jnp.dot(table, both, preferred_element_type=F32)
         result = (result + acc_ref[pair]).astype(BF16)
         for k in range(filt_count):
@@ -174,25 +199,28 @@
                 ]
 
 
-def far_conv(pos, after, table, acc, halo, swapped):
-    filt_count, rows, width = table.shape
+def far_conv(first, count, pos, after, filters, acc, halo, sibling, sibling_r3):
     tok = halo[0].shape[0]
-    vmem = pl.BlockSpec(memory_space=pltpu.VMEM)
-    return pl.pallas_call(
-        far_kernel,
-        out_shape=jax.ShapeDtypeStruct((tok, filt_count * LANE), BF16),
+    width = filters.shape[1] // 2 + LANE
+    vmem = pl.BlockSpec(memory_space=pltpu.VMEM)
+    return pl.pallas_call(
+        functools.partial(far_kernel, first),
+        out_shape=jax.ShapeDtypeStruct((tok, count * LANE), BF16),
         in_specs=[pl.BlockSpec(memory_space=pltpu.SMEM), pl.BlockSpec(memory_space=pl.ANY)]
-        + [vmem] * 8,
+        + [vmem] * 7,
         out_specs=vmem,
-        scratch_shapes=[pltpu.VMEM((5 * tok + rows, LANE), BF16)],
+        scratch_shapes=[
+            pltpu.VMEM((5 * tok + ROWS, LANE), BF16),
+            pltpu.VMEM((count, ROWS, width), BF16),
+        ],
         compiler_params=pltpu.CompilerParams(vmem_limit_bytes=VMEM_LIMIT),
         cost_estimate=SMALL_COST,
         name="far_conv",
-    )(pos, after, table, acc, *halo, *swapped)
+    )(pos, after, filters, acc, *halo, sibling, sibling_r3)
 
 
 def product_kernel(
-    crossed, pos_ref, corr_ref, x0_ref, x1_ref, x2_ref, x3_ref, keep_ref, send_ref, full_ref
+    crossed, pos_ref, _, corr_ref, x0_ref, x1_ref, x2_ref, x3_ref, keep_ref, send_ref, full_ref
 ):
     x, z_hi, y, z_lo, core = coords(pos_ref)
     for s, part in enumerate((x0_ref, x1_ref, x2_ref, x3_ref)):
@@ -217,20 +245,21 @@
                 send_ref[s, slot, k] = jnp.where(core == 0, odd, even)
 
 
-def product(crossed, pos, corr, gathered):
+def product(crossed, pos, after, corr, gathered):
     tok, width = corr.shape
     part = jax.ShapeDtypeStruct((NY, NZ_LO, width // LANE, 32, LANE), BF16)
     vmem = pl.BlockSpec(memory_space=pltpu.VMEM)
     return pl.pallas_call(
         functools.partial(product_kernel, crossed),
         out_shape=(part, part),
-        in_specs=[pl.BlockSpec(memory_space=pltpu.SMEM)] + [vmem] * 5,
+        in_specs=[pl.BlockSpec(memory_space=pltpu.SMEM), pl.BlockSpec(memory_space=pl.ANY)]
+        + [vmem] * 5,
         out_specs=(vmem,) * 2,
         scratch_shapes=[pltpu.VMEM((tok, 1024), BF16)],
         compiler_params=pltpu.CompilerParams(vmem_limit_bytes=VMEM_LIMIT),
         cost_estimate=SMALL_COST,
         name="product",
-    )(pos, corr, *gathered)
+    )(pos, after, corr, *gathered)
 
 
 def halve_kernel(_, mine_ref, other_ref, stay_ref, leave_ref):
@@ -336,27 +365,33 @@
     def x_swapped(value, crossed):
         return lax.ppermute(value, "tp", x_swap(crossed))
 
-    pair = jnp.stack([inputs, lax.ppermute(inputs, "tp", Z_HI_SWAP)])
+    count = filters.shape[0] // GROUPS
+    r1, r2, r4 = (later(grad_out, steps) for steps in (1, 2, 4))
+    table = near_table(filters)
+    stack, pair, grad_copy = prepare(
+        table, grad_out, r1, r2, r4, inputs, lax.ppermute(inputs, "tp", Z_HI_SWAP)
+    )
+    beside = sibling(stack)
     gathered = [pair] + [lax.ppermute(pair, "tp", along_x(s)) for s in range(1, NX)]
-    near_table, grad_copy, *far_tables = toeplitz_tables(filters, grad_out, GROUPS)
-    halo = [grad_out, later(grad_out, 1), later(grad_out, 2)]
-    halo += [later(grad_copy, 3), later(grad_copy, 4)]
-    swapped = [sibling(part) for part in halo]
-    accs = near_conv(pos, near_table, halo[:3], swapped[:3], GROUPS)
+    r3 = later(grad_copy, 3)
+    beside_r3 = sibling(r3)
+    accs = near_conv(pos, table, (grad_out, r1, r2), beside, GROUPS)
 
     def conv(group, after):
-        return far_conv(pos, after, far_tables[group], accs[group], halo[2:], swapped[2:])
-
-    corr_0 = conv(0, near_table)
-    keep_0, send_0 = product(False, pos, corr_0, gathered)
+        return far_conv(
+            group * count, count, pos, after, filters, accs[group], (r2, r3, r4), beside, beside_r3
+        )
+
+    corr_0 = conv(0, table)
+    keep_0, send_0 = product(False, pos, table, corr_0, gathered)
     corr_1 = conv(1, send_0)
-    keep_1, send_1 = product(True, pos, corr_1, gathered)
-
-    stay_0, leave_0 = halve(send_1, keep_0, sibling(send_0))
+    stay_0, leave_0 = halve(corr_1, keep_0, sibling(send_0))
+    y_0 = y_swapped(leave_0, False)
+    keep_1, send_1 = product(True, pos, leave_0, corr_1, gathered)
+
     near, near_send, far, far_send = input_shares(
-        pos, leave_0, [corr_0, corr_1], projection.transpose(1, 0, 2)
+        pos, send_1, [corr_0, corr_1], projection.transpose(1, 0, 2)
     )
-    y_0 = y_swapped(leave_0, False)
     stay_1, leave_1 = halve(near_send, keep_1, sibling(send_1))
     y_1 = y_swapped(leave_1, True)
     far, leave = halve(leave_1, far, x_swapped(far_send, False))

time: 94.1 us -> 99.1 us (1.053)
  waiting for transfers between devices: 21.6 us -> 28.5 us
  starting transfers between devices: 43.1 us -> 41.3 us
  Pallas kernels: 21.2 us -> 22.4 us
    ppermute x4, starting transfers between devices: 12.9 us -> 17.5 us  [later(): return lax.ppermute(value, 'ctx', from_later_chip(steps))]
    ppermute x1, waiting for transfers between devices: 0.01 us -> 4.23 us  [per_device(): lax.ppermute(inputs, 'tp', Z_HI_SWAP)]
    ppermute x4, starting transfers between devices: 5.37 us -> 2.06 us  [x_swapped(): return lax.ppermute(value, 'tp', x_swap(crossed))]
    ppermute x4, waiting for transfers between devices: 8.04 us -> 11.1 us  [x_swapped(): return lax.ppermute(value, 'tp', x_swap(crossed))]
    ppermute x4, waiting for transfers between devices: 1.89 us -> 0.01 us  [later(): return lax.ppermute(value, 'ctx', from_later_chip(steps))]
    ppermute x4, starting transfers between devices: 6.1 us -> 4.6 us  [z_swapped(): return lax.ppermute(value, 'ctx', z_swap(bit))]
    ppermute x1, starting transfers between devices: 0.59 us -> 2.07 us  [per_device(): opposite = lax.ppermute(far, 'tp', Z_HI_SWAP)]
    ppermute x7 -> x4, starting transfers between devices: 2.04 us -> 0.67 us  [sibling(): return lax.ppermute(value, 'ctx', CORE_SWAP)]
  transfers between devices with their start and end apart: 28 -> 25, of which waited for: 8 -> 9; matrix products, arithmetic and copies ran while one was open for 2% -> 1% of each run, Pallas kernels for 21% -> 18%
where the time goes in v4:
time: 99.1 us; the launch traced here: 98.1 us
  starting transfers between devices  41.3 us (42%)
  waiting for transfers between devices  28.5 us (29%)
  Pallas kernels  22.4 us (23%)
  local copies, waits for them, and re-layouts  3.44 us (3%)
  other arithmetic  1.49 us (2%)
    ppermute x4, starting transfers between devices, later(): return lax.ppermute(value, 'ctx', from_later_chip(steps))  17.5 us
    ppermute x4, waiting for transfers between devices, x_swapped(): return lax.ppermute(value, 'tp', x_swap(crossed))  11.1 us
    ppermute x4, waiting for transfers between devices, z_swapped(): return lax.ppermute(value, 'ctx', z_swap(bit))  8.74 us
    pallas_call x2, Pallas kernels, far_conv(): pl.pallas_call(functools.partial(far_kernel, first), out_shape=jax.ShapeD...  8.34 us
    ppermute x1, starting transfers between devices, per_device(): lax.ppermute(inputs, 'tp', Z_HI_SWAP)  6.02 us
    pallas_call x1, Pallas kernels, near_conv(): pl.pallas_call(near_kernel, out_shape=[acc] * groups, in_specs=[pl.BlockS...  5.27 us
    ppermute x4, starting transfers between devices, z_swapped(): return lax.ppermute(value, 'ctx', z_swap(bit))  4.6 us
    ppermute x3, starting transfers between devices, per_device(): lax.ppermute(pair, 'tp', along_x(s))  4.47 us
  transfers between devices with their start and end apart: 25, of which 9 were waited for; matrix products, arithmetic and copies ran while one was open for 1% of the time, Pallas kernels for 18%

profile of v4, /device:TPU:24, one launch (start us, length us, event | category | flops | bytes accessed | tf_op | source)
XLA Modules:
  0.0 98.1 jit_solution(7419915828298160094)
XLA Ops:
  0.6 2.7 %collective-permute-start.2 = (bf16[512,128]{1,0:T(8,128)(2,1)}, bf16[512,128]{1,0:T(8,128)(2,1)S(1)}, u32[]{:S(2)}, u32[]{:S(2)}) collective-permute-start(bf16[512,128]{1,0:T(8,128)(2,1)} %own_ref.3), channel_id=1, source_target_pairs={{64,0},{72,8},{80,16},{88,24},{96,32},{104,40},{112,48},{120,56},{... | collective-permute-start | bytes 393224 | tf_op jit(solution)/shard_map/ppermute | solution.py:354
  3.3 5.1 %collective-permute-start.1 = (bf16[512,128]{1,0:T(8,128)(2,1)}, bf16[512,128]{1,0:T(8,128)(2,1)S(1)}, u32[]{:S(2)}, u32[]{:S(2)}) collective-permute-start(bf16[512,128]{1,0:T(8,128)(2,1)} %own_ref.3), channel_id=1, source_target_pairs={{32,0},{40,8},{48,16},{56,24},{64,32},{72,40},{80,48},{88,56},{96,... | collective-permute-start | bytes 393224 | tf_op jit(solution)/shard_map/ppermute | solution.py:354
  8.4 3.3 %collective-permute-start = (bf16[512,128]{1,0:T(8,128)(2,1)}, bf16[512,128]{1,0:T(8,128)(2,1)S(1)}, u32[]{:S(2)}, u32[]{:S(2)}) collective-permute-start(bf16[512,128]{1,0:T(8,128)(2,1)} %own_ref.3), channel_id=1, source_target_pairs={{16,0},{24,8},{32,16},{40,24},{48,32},{56,40},{64,48},{72,56},{80,... | collective-permute-start | bytes 393224 | tf_op jit(solution)/shard_map/ppermute | solution.py:354
  11.7 6.0 %collective-permute-start.3 = (bf16[512,128]{1,0:T(8,128)(2,1)}, bf16[512,128]{1,0:T(8,128)(2,1)S(1)}, u32[]{:S(2)}, u32[]{:S(2)}) collective-permute-start(bf16[512,128]{1,0:T(8,128)(2,1)} %in_ref.1), channel_id=1, source_target_pairs={{0,1},{1,0},{2,3},{3,2},{4,5},{5,4},{6,7},{7,6},{8,9},{9,8},{10,11... | collective-permute-start | bytes 393224 | tf_op jit(solution)/shard_map/ppermute | solution.py:372
  17.7 0.9 copy-done.3
  18.6 0.9 near_table.1._.table_ref
  19.5 4.2 %collective-permute-done.3.far_in_ref = bf16[512,128]{1,0:T(8,128)(2,1)S(1)} collective-permute-done((bf16[512,128]{1,0:T(8,128)(2,1)}, bf16[512,128]{1,0:T(8,128)(2,1)S(1)}, u32[]{:S(2)}, u32[]{:S(2)}) %collective-permute-start.3) | collective-permute-done | bytes 131104 | tf_op jit(solution)/shard_map/ppermute | solution.py:372
  23.7 0.0 collective-permute-done.2.r4_ref
  23.7 0.0 collective-permute-done.1.r2_ref
  23.7 0.0 collective-permute-done.r1_ref
  23.8 0.0 copy-start.8
  23.8 0.9 prepare.1
  24.7 0.7 copy-done.1
  25.4 0.0 collective-permute-start.4
  25.4 6.5 %collective-permute-start.5 = (bf16[512,128]{1,0:T(8,128)(2,1)}, bf16[512,128]{1,0:T(8,128)(2,1)S(1)}, u32[]{:S(2)}, u32[]{:S(2)}) collective-permute-start(bf16[512,128]{1,0:T(8,128)(2,1)} %get-tuple-element.37), channel_id=1, source_target_pairs={{48,0},{56,8},{64,16},{72,24},{80,32},{88,40},{96,48},{104,56},{11... | collective-permute-start | bytes 393224 | tf_op jit(solution)/shard_map/ppermute | solution.py:354
  31.9 0.1 pad_add_fusion.pos_ref
  32.0 2.8 %collective-permute-start.9 = (bf16[2,512,128]{2,1,0:T(8,128)(2,1)}, bf16[2,512,128]{2,1,0:T(8,128)(2,1)S(1)}, u32[]{:S(2)}, u32[]{:S(2)}) collective-permute-start(bf16[2,512,128]{2,1,0:T(8,128)(2,1)} %copy-done.1), channel_id=1, source_target_pairs={{0,6},{1,7},{2,0},{3,1},{4,2},{5,3},{6,4},{7,5},{8,14},{9,15},{10,... | collective-permute-start | bytes 786440 | tf_op jit(solution)/shard_map/ppermute | solution.py:375
  34.8 0.8 collective-permute-start.8
  35.6 0.9 collective-permute-start.7
  36.5 0.0 collective-permute-done.5.r3_ref
  36.5 0.0 collective-permute-start.6
  36.5 0.0 copy-start.7
  36.5 0.9 copy-done.7
  37.4 0.9 copy-done.9
  38.3 5.3 %near_conv.1 = (f32[4,384,256]{2,1,0:T(8,128)S(1)}, f32[4,384,256]{2,1,0:T(8,128)S(1)}) custom-call(s32[2]{0:T(128)S(1)} %pad_add_fusion.pos_ref, bf16[12,64,2048]{2,1,0:T(8,128)(2,1)S(1)} %near_table.1._.table_ref, bf16[512,128]{1,0:T(8,128)(2,1)S(1)} %copy-done.7, bf16[512,128]{1,0:T(8,128)(2,1)S(1)} %copy-done.9, ...), custom_call_target="tpu_custom_call" | custom-call | flops 4000000000 | bytes 8000000 | tf_op jit(solution)/shard_map/near_conv/pallas_call | solution.py:161
  43.6 0.0 collective-permute-done.6.sib_r3_ref
  43.6 4.2 %far_conv.2.corr_ref.refs_0_ = bf16[512,768]{1,0:T(8,128)(2,1)S(1)} custom-call(s32[2]{0:T(128)S(1)} %pad_add_fusion.pos_ref, bf16[12,64,2048]{2,1,0:T(8,128)(2,1)S(1)} %near_table.1._.table_ref, bf16[12,4096]{1,0:T(8,128)(2,1)S(1)} %copy-done.4, f32[4,384,256]{2,1,0:T(8,128)S(1)} %get-tuple-element.36.acc_ref, ...), custom_call_target="tpu_custom_call" | custom-call | flops 1000 | bytes 1000 | tf_op jit(solution)/shard_map/far_conv/pallas_call | solution.py:206
  47.8 0.0 collective-permute-done.8.x2_ref
  47.8 2.5 %collective-permute-done.7.x1_ref = bf16[2,512,128]{2,1,0:T(8,128)(2,1)S(1)} collective-permute-done((bf16[2,512,128]{2,1,0:T(8,128)(2,1)}, bf16[2,512,128]{2,1,0:T(8,128)(2,1)S(1)}, u32[]{:S(2)}, u32[]{:S(2)}) %collective-permute-start.7) | collective-permute-done | bytes 262176 | tf_op jit(solution)/shard_map/ppermute | solution.py:375
  50.3 1.9 %product.2 = (bf16[4,4,6,32,128]{4,3,2,1,0:T(8,128)(2,1)S(1)}, bf16[4,4,6,32,128]{4,3,2,1,0:T(8,128)(2,1)S(1)}) custom-call(s32[2]{0:T(128)S(1)} %pad_add_fusion.pos_ref, bf16[12,64,2048]{2,1,0:T(8,128)(2,1)S(1)} %near_table.1._.table_ref, bf16[512,768]{1,0:T(8,128)(2,1)S(1)} %far_conv.2.corr_ref.refs_0_, bf16[2,512,128]{2,1,0:T(8,128)(2,1)S(1)} %copy-done.2, ...), custom_call_target="tpu_custom_call" | custom-call | flops 1000 | bytes 1000 | tf_op jit(solution)/shard_map/product/pallas_call | solution.py:252
  52.2 0.1 collective-permute-start.10
  52.3 4.1 %far_conv.3._.corr_ref.refs_1_ = bf16[512,768]{1,0:T(8,128)(2,1)S(1)} custom-call(s32[2]{0:T(128)S(1)} %pad_add_fusion.pos_ref, bf16[4,4,6,32,128]{4,3,2,1,0:T(8,128)(2,1)S(1)} %get-tuple-element.39._, bf16[12,4096]{1,0:T(8,128)(2,1)S(1)} %copy-done.4, f32[4,384,256]{2,1,0:T(8,128)S(1)} %get-tuple-element.40.acc_ref, ...), custom_call_target="tpu_custom_call" | custom-call | flops 1000 | bytes 1000 | tf_op jit(solution)/shard_map/far_conv/pallas_call | solution.py:206
  56.5 0.0 copy-start
  56.5 0.2 halve.10
  56.7 1.9 %product.3 = (bf16[4,4,6,32,128]{4,3,2,1,0:T(8,128)(2,1)S(1)}, bf16[4,4,6,32,128]{4,3,2,1,0:T(8,128)(2,1)S(1)}) custom-call(s32[2]{0:T(128)S(1)} %pad_add_fusion.pos_ref, bf16[2,4,6,32,128]{4,3,2,1,0:T(8,128)(2,1)S(1)} %get-tuple-element.42._, bf16[512,768]{1,0:T(8,128)(2,1)S(1)} %far_conv.3._.corr_ref.refs_1_, bf16[2,512,128]{2,1,0:T(8,128)(2,1)S(1)} %copy-done.2, ...), custom_call_target="tpu_custom_call" | custom-call | flops 1000 | bytes 1000 | tf_op jit(solution)/shard_map/product/pallas_call | solution.py:252
  58.6 0.6 collective-permute-start.11
  59.2 0.0 collective-permute-start.13
  59.2 2.4 %input_shares.1 = (f32[2,512,128]{2,1,0:T(8,128)S(1)}, bf16[2,512,128]{2,1,0:T(8,128)(2,1)S(1)}, f32[2,512,128]{2,1,0:T(8,128)S(1)}, bf16[2,512,128]{2,1,0:T(8,128)(2,1)S(1)}) custom-call(s32[2]{0:T(128)S(1)} %pad_add_fusion.pos_ref, bf16[4,4,6,32,128]{4,3,2,1,0:T(8,128)(2,1)S(1)} %get-tuple-element.43._, bf16[512,768]{1,0:T(8,128)(2,1)S(1)} %far_conv.2.corr_ref.refs_0_, ...), custom_call_target="tpu_custom_call" | custom-call | flops 1000 | bytes 1000 | tf_op jit(solution)/shard_map/input_shares/pallas_call | solution.py:333
  61.5 0.0 collective-permute-done.11.other_ref
  61.6 0.2 halve.11
  61.7 0.1 collective-permute-start.16
  61.8 0.1 collective-permute-start.12
  61.9 1.4 %collective-permute-start.14 = (bf16[2,512,128]{2,1,0:T(8,128)(2,1)S(1)}, bf16[2,512,128]{2,1,0:T(8,128)(2,1)S(1)}, u32[]{:S(2)}, u32[]{:S(2)}) collective-permute-start(bf16[2,512,128]{2,1,0:T(8,128)(2,1)S(1)} %get-tuple-element.44._), channel_id=1, source_target_pairs={{0,6},{1,7},{2,4},{3,5},{4,2},{5,3},{6,0},{7,1},{8,14},{9,15},{10,... | collective-permute-start | bytes 786440 | tf_op jit(solution)/shard_map/ppermute | solution.py:366
  63.3 7.1 %collective-permute-done.12.other_ref = bf16[2,512,128]{2,1,0:T(8,128)(2,1)S(1)} collective-permute-done((bf16[2,512,128]{2,1,0:T(8,128)(2,1)S(1)}, bf16[2,512,128]{2,1,0:T(8,128)(2,1)S(1)}, u32[]{:S(2)}, u32[]{:S(2)}) %collective-permute-start.12) | collective-permute-done | bytes 262176 | tf_op jit(solution)/shard_map/ppermute | solution.py:366
  70.5 0.0 collective-permute-done.13.other_ref
  70.5 0.1 halve.13
  70.6 2.9 %collective-permute-start.19 = (bf16[1,4,6,32,128]{4,3,2,1,0:T(8,128)(2,1)S(1)}, bf16[1,4,6,32,128]{4,3,2,1,0:T(8,128)(2,1)S(1)}, u32[]{:S(2)}, u32[]{:S(2)}) collective-permute-start(bf16[1,4,6,32,128]{4,3,2,1,0:T(8,128)(2,1)S(1)} %get-tuple-element.51._), channel_id=1, source_target_pairs={{0,192},{8,200},{16,208},{24,216},{32,224},{40,232},{48,240},{56,2... | collective-permute-start | bytes 589832 | tf_op jit(solution)/shard_map/ppermute | solution.py:360
  73.5 0.6 collective-permute-start.17
  74.2 0.5 collective-permute-done.16.other_ref
  74.7 0.1 halve.15
  74.8 0.9 collective-permute-start.20
  75.7 0.0 collective-permute-start.15
  75.7 4.0 %collective-permute-done.17.other_ref = bf16[1,512,128]{2,1,0:T(8,128)(2,1)S(1)} collective-permute-done((bf16[1,512,128]{2,1,0:T(8,128)(2,1)S(1)}, bf16[1,512,128]{2,1,0:T(8,128)(2,1)S(1)}, u32[]{:S(2)}, u32[]{:S(2)}) %collective-permute-start.17) | collective-permute-done | bytes 131104 | tf_op jit(solution)/shard_map/ppermute | solution.py:366
  79.7 2.1 %collective-permute-start.18 = (bf16[1,512,128]{2,1,0:T(8,128)(2,1)S(1)}, bf16[1,512,128]{2,1,0:T(8,128)(2,1)S(1)}, u32[]{:S(2)}, u32[]{:S(2)}) collective-permute-start(bf16[1,512,128]{2,1,0:T(8,128)(2,1)S(1)} %add.37._), channel_id=1, source_target_pairs={{0,1},{1,0},{2,3},{3,2},{4,5},{5,4},{6,7},{7,6},{8,9},{9,8},{10,11... | collective-permute-start | bytes 393224 | tf_op jit(solution)/shard_map/ppermute | solution.py:406
  81.8 1.3 %collective-permute-start.21 = (bf16[2,6,32,128]{3,2,1,0:T(8,128)(2,1)S(1)}, bf16[2,6,32,128]{3,2,1,0:T(8,128)(2,1)S(1)}, u32[]{:S(2)}, u32[]{:S(2)}) collective-permute-start(bf16[2,6,32,128]{3,2,1,0:T(8,128)(2,1)S(1)} %get-tuple-element.59._), channel_id=1, source_target_pairs={{0,16},{8,24},{16,0},{24,8},{32,48},{40,56},{48,32},{56,40},{64,80... | collective-permute-start | bytes 294920 | tf_op jit(solution)/shard_map/ppermute | solution.py:363
  83.2 0.9 collective-permute-start.23
  84.1 5.7 %collective-permute-done.21.other_ref = bf16[2,6,32,128]{3,2,1,0:T(8,128)(2,1)S(1)} collective-permute-done((bf16[2,6,32,128]{3,2,1,0:T(8,128)(2,1)S(1)}, bf16[2,6,32,128]{3,2,1,0:T(8,128)(2,1)S(1)}, u32[]{:S(2)}, u32[]{:S(2)}) %collective-permute-start.21) | collective-permute-done | bytes 98336 | tf_op jit(solution)/shard_map/ppermute | solution.py:363
  89.8 0.4 collective-permute-start.22
  90.2 1.4 %collective-permute-done.18 = bf16[1,512,128]{2,1,0:T(8,128)(2,1)S(1)} collective-permute-done((bf16[1,512,128]{2,1,0:T(8,128)(2,1)S(1)}, bf16[1,512,128]{2,1,0:T(8,128)(2,1)S(1)}, u32[]{:S(2)}, u32[]{:S(2)}) %collective-permute-start.18) | collective-permute-done | bytes 131104 | tf_op jit(solution)/shard_map/ppermute | solution.py:406
  91.6 0.7 fusion
  92.3 2.0 %collective-permute-start.24 = (bf16[1,6,32,128]{3,2,1,0:T(8,128)(2,1)S(1)}, bf16[1,6,32,128]{3,2,1,0:T(8,128)(2,1)S(1)}, u32[]{:S(2)}, u32[]{:S(2)}) collective-permute-start(bf16[1,6,32,128]{3,2,1,0:T(8,128)(2,1)S(1)} %get-tuple-element.67), channel_id=1, source_target_pairs={{0,32},{8,40},{16,48},{24,56},{32,0},{40,8},{48,16},{56,24},{64,96... | collective-permute-start | bytes 147464 | tf_op jit(solution)/shard_map/ppermute | solution.py:363
  94.3 1.0 %collective-permute-done.22 = bf16[1,6,32,128]{3,2,1,0:T(8,128)(2,1)S(1)} collective-permute-done((bf16[1,6,32,128]{3,2,1,0:T(8,128)(2,1)S(1)}, bf16[1,6,32,128]{3,2,1,0:T(8,128)(2,1)S(1)}, u32[]{:S(2)}, u32[]{:S(2)}) %collective-permute-start.22) | collective-permute-done | bytes 49184 | tf_op jit(solution)/shard_map/ppermute | solution.py:363
  95.4 2.0 %collective-permute-done.24 = bf16[1,6,32,128]{3,2,1,0:T(8,128)(2,1)S(1)} collective-permute-done((bf16[1,6,32,128]{3,2,1,0:T(8,128)(2,1)S(1)}, bf16[1,6,32,128]{3,2,1,0:T(8,128)(2,1)S(1)}, u32[]{:S(2)}, u32[]{:S(2)}) %collective-permute-start.24) | collective-permute-done | bytes 49184 | tf_op jit(solution)/shard_map/ppermute | solution.py:363
  97.4 0.7 maximum_bitcast_fusion
  (30 shorter events, 0.3 us)
Async XLA Ops:
  0.6 23.1 %collective-permute-start.2 = (bf16[512,128]{1,0:T(8,128)(2,1)}, bf16[512,128]{1,0:T(8,128)(2,1)S(1)}, u32[]{:S(2)}, u32[]{:S(2)}) collective-permute-start(bf16[512,128]{1,0:T(8,128)(2,1)} %own_ref.3), channel_id=1, source_target_pairs={{64,0},{72,8},{80,16},{88,24},{96,32},{104,40},{112,48},{120,56},{... | collective-permute-start | bytes 393224 | tf_op jit(solution)/shard_map/ppermute | solution.py:354
  3.3 20.4 %collective-permute-start.1 = (bf16[512,128]{1,0:T(8,128)(2,1)}, bf16[512,128]{1,0:T(8,128)(2,1)S(1)}, u32[]{:S(2)}, u32[]{:S(2)}) collective-permute-start(bf16[512,128]{1,0:T(8,128)(2,1)} %own_ref.3), channel_id=1, source_target_pairs={{32,0},{40,8},{48,16},{56,24},{64,32},{72,40},{80,48},{88,56},{96,... | collective-permute-start | bytes 393224 | tf_op jit(solution)/shard_map/ppermute | solution.py:354
  8.4 15.4 %collective-permute-start = (bf16[512,128]{1,0:T(8,128)(2,1)}, bf16[512,128]{1,0:T(8,128)(2,1)S(1)}, u32[]{:S(2)}, u32[]{:S(2)}) collective-permute-start(bf16[512,128]{1,0:T(8,128)(2,1)} %own_ref.3), channel_id=1, source_target_pairs={{16,0},{24,8},{32,16},{40,24},{48,32},{56,40},{64,48},{72,56},{80,... | collective-permute-start | bytes 393224 | tf_op jit(solution)/shard_map/ppermute | solution.py:354
  11.7 12.1 %collective-permute-start.3 = (bf16[512,128]{1,0:T(8,128)(2,1)}, bf16[512,128]{1,0:T(8,128)(2,1)S(1)}, u32[]{:S(2)}, u32[]{:S(2)}) collective-permute-start(bf16[512,128]{1,0:T(8,128)(2,1)} %in_ref.1), channel_id=1, source_target_pairs={{0,1},{1,0},{2,3},{3,2},{4,5},{5,4},{6,7},{7,6},{8,9},{9,8},{10,11... | collective-permute-start | bytes 393224 | tf_op jit(solution)/shard_map/ppermute | solution.py:372
  17.7 0.9 copy-start.3
  18.6 5.2 %copy-start.5 = (bf16[512,128]{1,0:T(8,128)(2,1)S(1)}, bf16[512,128]{1,0:T(8,128)(2,1)}, u32[]{:S(2)}) copy-start(bf16[512,128]{1,0:T(8,128)(2,1)} %in_ref.1) | copy-start | bytes 393220
  18.6 5.2 %copy-start.6 = (bf16[512,128]{1,0:T(8,128)(2,1)S(1)}, bf16[512,128]{1,0:T(8,128)(2,1)}, u32[]{:S(2)}) copy-start(bf16[512,128]{1,0:T(8,128)(2,1)} %own_ref.3) | copy-start | bytes 393220
  23.8 1.7 %copy-start.8 = (bf16[512,128]{1,0:T(8,128)(2,1)}, bf16[512,128]{1,0:T(8,128)(2,1)S(1)}, u32[]{:S(2)}) copy-start(bf16[512,128]{1,0:T(8,128)(2,1)S(1)} %collective-permute-done.r1_ref) | copy-start | bytes 393220
  24.7 0.7 copy-start.1
  25.4 11.0 %collective-permute-start.4 = (bf16[4,512,128]{2,1,0:T(8,128)(2,1)}, bf16[4,512,128]{2,1,0:T(8,128)(2,1)}, u32[]{:S(2)}, u32[]{:S(2)}) collective-permute-start(bf16[4,512,128]{2,1,0:T(8,128)(2,1)} %get-tuple-element.35), channel_id=1, source_target_pairs={{0,8},{8,0},{16,24},{24,16},{32,40},{40,32},{48,56},{56,48},{64,72... | collective-permute-start | bytes 1572872 | tf_op jit(solution)/shard_map/ppermute | solution.py:357
  25.4 11.0 %collective-permute-start.5 = (bf16[512,128]{1,0:T(8,128)(2,1)}, bf16[512,128]{1,0:T(8,128)(2,1)S(1)}, u32[]{:S(2)}, u32[]{:S(2)}) collective-permute-start(bf16[512,128]{1,0:T(8,128)(2,1)} %get-tuple-element.37), channel_id=1, source_target_pairs={{48,0},{56,8},{64,16},{72,24},{80,32},{88,40},{96,48},{104,56},{11... | collective-permute-start | bytes 393224 | tf_op jit(solution)/shard_map/ppermute | solution.py:354
  32.0 11.6 %copy-start.4 = (bf16[12,4096]{1,0:T(8,128)(2,1)S(1)}, bf16[12,4096]{1,0:T(8,128)(2,1)}, u32[]{:S(2)}) copy-start(bf16[12,4096]{1,0:T(8,128)(2,1)} %filters_ref.5) | copy-start | bytes 294916
  32.0 15.8 %collective-permute-start.9 = (bf16[2,512,128]{2,1,0:T(8,128)(2,1)}, bf16[2,512,128]{2,1,0:T(8,128)(2,1)S(1)}, u32[]{:S(2)}, u32[]{:S(2)}) collective-permute-start(bf16[2,512,128]{2,1,0:T(8,128)(2,1)} %copy-done.1), channel_id=1, source_target_pairs={{0,6},{1,7},{2,0},{3,1},{4,2},{5,3},{6,4},{7,5},{8,14},{9,15},{10,... | collective-permute-start | bytes 786440 | tf_op jit(solution)/shard_map/ppermute | solution.py:375
  34.8 13.0 %collective-permute-start.8 = (bf16[2,512,128]{2,1,0:T(8,128)(2,1)}, bf16[2,512,128]{2,1,0:T(8,128)(2,1)S(1)}, u32[]{:S(2)}, u32[]{:S(2)}) collective-permute-start(bf16[2,512,128]{2,1,0:T(8,128)(2,1)} %copy-done.1), channel_id=1, source_target_pairs={{0,4},{1,5},{2,6},{3,7},{4,0},{5,1},{6,2},{7,3},{8,12},{9,13},{10,... | collective-permute-start | bytes 786440 | tf_op jit(solution)/shard_map/ppermute | solution.py:375
  35.6 14.7 %collective-permute-start.7 = (bf16[2,512,128]{2,1,0:T(8,128)(2,1)}, bf16[2,512,128]{2,1,0:T(8,128)(2,1)S(1)}, u32[]{:S(2)}, u32[]{:S(2)}) collective-permute-start(bf16[2,512,128]{2,1,0:T(8,128)(2,1)} %copy-done.1), channel_id=1, source_target_pairs={{0,2},{1,3},{2,4},{3,5},{4,6},{5,7},{6,0},{7,1},{8,10},{9,11},{10,... | collective-permute-start | bytes 786440 | tf_op jit(solution)/shard_map/ppermute | solution.py:375
  36.5 7.1 %collective-permute-start.6 = (bf16[512,128]{1,0:T(8,128)(2,1)S(1)}, bf16[512,128]{1,0:T(8,128)(2,1)S(1)}, u32[]{:S(2)}, u32[]{:S(2)}) collective-permute-start(bf16[512,128]{1,0:T(8,128)(2,1)S(1)} %collective-permute-done.5.r3_ref), channel_id=1, source_target_pairs={{0,8},{8,0},{16,24},{24,16},{32,40},{40,32},{48,56},{56,48},{64,72... | collective-permute-start | bytes 393224 | tf_op jit(solution)/shard_map/ppermute | solution.py:357
  36.5 0.9 copy-start.7
  37.4 0.9 copy-start.9
  43.6 6.7 %copy-start.2 = (bf16[2,512,128]{2,1,0:T(8,128)(2,1)S(1)}, bf16[2,512,128]{2,1,0:T(8,128)(2,1)}, u32[]{:S(2)}) copy-start(bf16[2,512,128]{2,1,0:T(8,128)(2,1)} %copy-done.1) | copy-start | bytes 786436
  52.2 4.3 %collective-permute-start.10 = (bf16[4,4,6,32,128]{4,3,2,1,0:T(8,128)(2,1)S(1)}, bf16[4,4,6,32,128]{4,3,2,1,0:T(8,128)(2,1)S(1)}, u32[]{:S(2)}, u32[]{:S(2)}) collective-permute-start(bf16[4,4,6,32,128]{4,3,2,1,0:T(8,128)(2,1)S(1)} %get-tuple-element.39._), channel_id=1, source_target_pairs={{0,8},{8,0},{16,24},{24,16},{32,40},{40,32},{48,56},{56,48},{64,72... | collective-permute-start | bytes 2359304 | tf_op jit(solution)/shard_map/ppermute | solution.py:357
  56.5 2.7 %copy-start = (bf16[1024,12,128]{2,0,1:T(8,128)(2,1)S(1)}, bf16[1024,12,128]{2,0,1:T(8,128)(2,1)}, u32[]{:S(2)}) copy-start(bf16[1024,12,128]{2,0,1:T(8,128)(2,1)} %param.7) | copy-start | bytes 9437188
  58.6 3.0 %collective-permute-start.11 = (bf16[4,4,6,32,128]{4,3,2,1,0:T(8,128)(2,1)S(1)}, bf16[4,4,6,32,128]{4,3,2,1,0:T(8,128)(2,1)S(1)}, u32[]{:S(2)}, u32[]{:S(2)}) collective-permute-start(bf16[4,4,6,32,128]{4,3,2,1,0:T(8,128)(2,1)S(1)} %get-tuple-element.43._), channel_id=1, source_target_pairs={{0,8},{8,0},{16,24},{24,16},{32,40},{40,32},{48,56},{56,48},{64,72... | collective-permute-start | bytes 2359304 | tf_op jit(solution)/shard_map/ppermute | solution.py:357
  59.2 11.3 %collective-permute-start.13 = (bf16[2,4,6,32,128]{4,3,2,1,0:T(8,128)(2,1)S(1)}, bf16[2,4,6,32,128]{4,3,2,1,0:T(8,128)(2,1)S(1)}, u32[]{:S(2)}, u32[]{:S(2)}) collective-permute-start(bf16[2,4,6,32,128]{4,3,2,1,0:T(8,128)(2,1)S(1)} %get-tuple-element.42._), channel_id=1, source_target_pairs={{0,64},{8,72},{16,80},{24,88},{32,96},{40,104},{48,112},{56,120},{... | collective-permute-start | bytes 1179656 | tf_op jit(solution)/shard_map/ppermute | solution.py:360
  61.7 12.9 %collective-permute-start.16 = (bf16[2,4,6,32,128]{4,3,2,1,0:T(8,128)(2,1)S(1)}, bf16[2,4,6,32,128]{4,3,2,1,0:T(8,128)(2,1)S(1)}, u32[]{:S(2)}, u32[]{:S(2)}) collective-permute-start(bf16[2,4,6,32,128]{4,3,2,1,0:T(8,128)(2,1)S(1)} %get-tuple-element.46._), channel_id=1, source_target_pairs={{0,192},{8,200},{16,208},{24,216},{32,224},{40,232},{48,240},{56,2... | collective-permute-start | bytes 1179656 | tf_op jit(solution)/shard_map/ppermute | solution.py:360
  61.8 8.6 %collective-permute-start.12 = (bf16[2,512,128]{2,1,0:T(8,128)(2,1)S(1)}, bf16[2,512,128]{2,1,0:T(8,128)(2,1)S(1)}, u32[]{:S(2)}, u32[]{:S(2)}) collective-permute-start(bf16[2,512,128]{2,1,0:T(8,128)(2,1)S(1)} %get-tuple-element.48), channel_id=1, source_target_pairs={{0,2},{1,3},{2,0},{3,1},{4,6},{5,7},{6,4},{7,5},{8,10},{9,11},{10,... | collective-permute-start | bytes 786440 | tf_op jit(solution)/shard_map/ppermute | solution.py:366
  61.9 12.2 %collective-permute-start.14 = (bf16[2,512,128]{2,1,0:T(8,128)(2,1)S(1)}, bf16[2,512,128]{2,1,0:T(8,128)(2,1)S(1)}, u32[]{:S(2)}, u32[]{:S(2)}) collective-permute-start(bf16[2,512,128]{2,1,0:T(8,128)(2,1)S(1)} %get-tuple-element.44._), channel_id=1, source_target_pairs={{0,6},{1,7},{2,4},{3,5},{4,2},{5,3},{6,0},{7,1},{8,14},{9,15},{10,... | collective-permute-start | bytes 786440 | tf_op jit(solution)/shard_map/ppermute | solution.py:366
  70.6 11.2 %collective-permute-start.19 = (bf16[1,4,6,32,128]{4,3,2,1,0:T(8,128)(2,1)S(1)}, bf16[1,4,6,32,128]{4,3,2,1,0:T(8,128)(2,1)S(1)}, u32[]{:S(2)}, u32[]{:S(2)}) collective-permute-start(bf16[1,4,6,32,128]{4,3,2,1,0:T(8,128)(2,1)S(1)} %get-tuple-element.51._), channel_id=1, source_target_pairs={{0,192},{8,200},{16,208},{24,216},{32,224},{40,232},{48,240},{56,2... | collective-permute-start | bytes 589832 | tf_op jit(solution)/shard_map/ppermute | solution.py:360
  73.5 6.2 %collective-permute-start.17 = (bf16[1,512,128]{2,1,0:T(8,128)(2,1)S(1)}, bf16[1,512,128]{2,1,0:T(8,128)(2,1)S(1)}, u32[]{:S(2)}, u32[]{:S(2)}) collective-permute-start(bf16[1,512,128]{2,1,0:T(8,128)(2,1)S(1)} %get-tuple-element.49._), channel_id=1, source_target_pairs={{0,6},{1,7},{2,4},{3,5},{4,2},{5,3},{6,0},{7,1},{8,14},{9,15},{10,... | collective-permute-start | bytes 393224 | tf_op jit(solution)/shard_map/ppermute | solution.py:366
  74.8 8.4 %collective-permute-start.20 = (bf16[1,4,6,32,128]{4,3,2,1,0:T(8,128)(2,1)S(1)}, bf16[1,4,6,32,128]{4,3,2,1,0:T(8,128)(2,1)S(1)}, u32[]{:S(2)}, u32[]{:S(2)}) collective-permute-start(bf16[1,4,6,32,128]{4,3,2,1,0:T(8,128)(2,1)S(1)} %get-tuple-element.56._), channel_id=1, source_target_pairs={{0,64},{8,72},{16,80},{24,88},{32,96},{40,104},{48,112},{56,120},{... | collective-permute-start | bytes 589832 | tf_op jit(solution)/shard_map/ppermute | solution.py:360
  75.7 14.5 %collective-permute-start.15 = (bf16[1,512,128]{2,1,0:T(8,128)(2,1)S(1)}, bf16[1,512,128]{2,1,0:T(8,128)(2,1)S(1)}, u32[]{:S(2)}, u32[]{:S(2)}) collective-permute-start(bf16[1,512,128]{2,1,0:T(8,128)(2,1)S(1)} %get-tuple-element.54._), channel_id=1, source_target_pairs={{0,2},{1,3},{2,0},{3,1},{4,6},{5,7},{6,4},{7,5},{8,10},{9,11},{10,... | collective-permute-start | bytes 393224 | tf_op jit(solution)/shard_map/ppermute | solution.py:366
  79.7 11.8 %collective-permute-start.18 = (bf16[1,512,128]{2,1,0:T(8,128)(2,1)S(1)}, bf16[1,512,128]{2,1,0:T(8,128)(2,1)S(1)}, u32[]{:S(2)}, u32[]{:S(2)}) collective-permute-start(bf16[1,512,128]{2,1,0:T(8,128)(2,1)S(1)} %add.37._), channel_id=1, source_target_pairs={{0,1},{1,0},{2,3},{3,2},{4,5},{5,4},{6,7},{7,6},{8,9},{9,8},{10,11... | collective-permute-start | bytes 393224 | tf_op jit(solution)/shard_map/ppermute | solution.py:406
  81.8 8.0 %collective-permute-start.21 = (bf16[2,6,32,128]{3,2,1,0:T(8,128)(2,1)S(1)}, bf16[2,6,32,128]{3,2,1,0:T(8,128)(2,1)S(1)}, u32[]{:S(2)}, u32[]{:S(2)}) collective-permute-start(bf16[2,6,32,128]{3,2,1,0:T(8,128)(2,1)S(1)} %get-tuple-element.59._), channel_id=1, source_target_pairs={{0,16},{8,24},{16,0},{24,8},{32,48},{40,56},{48,32},{56,40},{64,80... | collective-permute-start | bytes 294920 | tf_op jit(solution)/shard_map/ppermute | solution.py:363
  83.2 9.1 %collective-permute-start.23 = (bf16[2,6,32,128]{3,2,1,0:T(8,128)(2,1)S(1)}, bf16[2,6,32,128]{3,2,1,0:T(8,128)(2,1)S(1)}, u32[]{:S(2)}, u32[]{:S(2)}) collective-permute-start(bf16[2,6,32,128]{3,2,1,0:T(8,128)(2,1)S(1)} %get-tuple-element.61._), channel_id=1, source_target_pairs={{0,16},{8,24},{16,0},{24,8},{32,48},{40,56},{48,32},{56,40},{64,80... | collective-permute-start | bytes 294920 | tf_op jit(solution)/shard_map/ppermute | solution.py:363
  89.8 5.5 %collective-permute-start.22 = (bf16[1,6,32,128]{3,2,1,0:T(8,128)(2,1)S(1)}, bf16[1,6,32,128]{3,2,1,0:T(8,128)(2,1)S(1)}, u32[]{:S(2)}, u32[]{:S(2)}) collective-permute-start(bf16[1,6,32,128]{3,2,1,0:T(8,128)(2,1)S(1)} %get-tuple-element.64._), channel_id=1, source_target_pairs={{0,32},{8,40},{16,48},{24,56},{32,0},{40,8},{48,16},{56,24},{64,96... | collective-permute-start | bytes 147464 | tf_op jit(solution)/shard_map/ppermute | solution.py:363
  92.3 5.1 %collective-permute-start.24 = (bf16[1,6,32,128]{3,2,1,0:T(8,128)(2,1)S(1)}, bf16[1,6,32,128]{3,2,1,0:T(8,128)(2,1)S(1)}, u32[]{:S(2)}, u32[]{:S(2)}) collective-permute-start(bf16[1,6,32,128]{3,2,1,0:T(8,128)(2,1)S(1)} %get-tuple-element.67), channel_id=1, source_target_pairs={{0,32},{8,40},{16,48},{24,56},{32,0},{40,8},{48,16},{56,24},{64,96... | collective-permute-start | bytes 147464 | tf_op jit(solution)/shard_map/ppermute | solution.py:363

commit v5 on v4

--- a/solution.py
+++ b/solution.py
@@ -87,30 +87,26 @@
     )(filters)
 
 
-def prep_kernel(_, own_ref, r1_ref, r2_ref, r4_ref, in_ref, far_in_ref, stack_ref, pair_ref, copy_ref):
-    copy_ref[...] = own_ref[...]
-    for s, part in enumerate((own_ref, r1_ref, r2_ref, r4_ref)):
-        stack_ref[s] = part[...]
-    pair_ref[0] = in_ref[...]
-    pair_ref[1] = far_in_ref[...]
-
-
-def prepare(after, *parts):
-    block = parts[0].shape
+def prep_kernel(pos_ref, _, __, *refs):
+    parts, stack_ref = refs[:-1], refs[-1]
+    core = lax.rem(pos_ref[1], NCORE)
+    for s in range(stack_ref.shape[0]):
+        stack_ref[s] = jnp.where(core == 0, parts[s + 1][...], parts[s][...])
+
+
+def for_sibling(pos, after, *parts):
     vmem = pl.BlockSpec(memory_space=pltpu.VMEM)
     return pl.pallas_call(
         prep_kernel,
-        out_shape=[
-            jax.ShapeDtypeStruct((4,) + block, BF16),
-            jax.ShapeDtypeStruct((2,) + block, BF16),
-            jax.ShapeDtypeStruct(block, BF16),
-        ],
-        in_specs=[pl.BlockSpec(memory_space=pl.ANY)] + [vmem] * 6,
-        out_specs=[vmem] * 3,
-        compiler_params=pltpu.CompilerParams(vmem_limit_bytes=VMEM_LIMIT),
-        cost_estimate=SMALL_COST,
-        name="prepare",
-    )(after, *parts)
+        out_shape=jax.ShapeDtypeStruct((len(parts) - 1,) + parts[0].shape, BF16),
+        in_specs=[pl.BlockSpec(memory_space=pltpu.SMEM)]
+        + [pl.BlockSpec(memory_space=pl.ANY)] * 2
+        + [vmem] * len(parts),
+        out_specs=vmem,
+        compiler_params=pltpu.CompilerParams(vmem_limit_bytes=VMEM_LIMIT),
+        cost_estimate=SMALL_COST,
+        name="for_sibling",
+    )(pos, *after, *parts)
 
 
 def pair_of_blocks(grad_ref, start, rows, width):
@@ -125,25 +121,20 @@
     return x, z_hi, chip // NZ_LO, lax.rem(chip, NZ_LO), core
 
 
-def lay_out(core, grad_ref, even_refs, odd_refs):
-    tok = even_refs[0].shape[0]
-    for s, part in enumerate(even_refs):
-        grad_ref[2 * s * tok : (2 * s + 1) * tok, :] = part[...]
-    for s in range(len(even_refs) - 1):
-        grad_ref[(2 * s + 1) * tok : (2 * s + 2) * tok, :] = jnp.where(
-            core == 0, odd_refs[s][...], odd_refs[s + 1][...]
-        )
-
-
-def near_kernel(pos_ref, table_ref, own_ref, r1_ref, r2_ref, sib_ref, *refs):
+def lay_out(grad_ref, refs):
+    tok = refs[0].shape[0]
+    for s, part in enumerate(refs):
+        grad_ref[s * tok : (s + 1) * tok, :] = part[...]
+
+
+def near_kernel(table_ref, own_ref, r1_ref, r2_ref, sib_ref, *refs):
     acc_refs, grad_ref = refs[:-1], refs[-1]
     filt_count, rows, width = table_ref.shape
     tok = own_ref.shape[0]
-    core = coords(pos_ref)[-1]
-    lay_out(core, grad_ref, (own_ref, r1_ref, r2_ref), [sib_ref.at[s] for s in range(3)])
+    lay_out(grad_ref, (own_ref, sib_ref.at[0], r1_ref, sib_ref.at[1], r2_ref))
     table = table_ref[...].reshape(filt_count * rows, width)
 
-    @pl.loop(0, tok // (2 * rows))
+    @pl.loop(0, tok // (2 * rows), unroll=True)
     def _(pair):
         start = pl.multiple_of(pair * (2 * rows), 2 * rows)
         both = pair_of_blocks(grad_ref, start, rows, width)
@@ -153,7 +144,7 @@
             acc_ref[pair] = result[group * part : (group + 1) * part]
 
 
-def near_conv(pos, table, halo, sibling, groups):
+def near_conv(table, halo, sibling, groups):
     filt_count, rows, width = table.shape
     tok = halo[0].shape[0]
     vmem = pl.BlockSpec(memory_space=pltpu.VMEM)
@@ -161,31 +152,30 @@
     return pl.pallas_call(
         near_kernel,
         out_shape=[acc] * groups,
-        in_specs=[pl.BlockSpec(memory_space=pltpu.SMEM)] + [vmem] * 5,
+        in_specs=[vmem] * 5,
         out_specs=[vmem] * groups,
         scratch_shapes=[pltpu.VMEM((5 * tok, LANE), BF16)],
         compiler_params=pltpu.CompilerParams(vmem_limit_bytes=VMEM_LIMIT),
         cost_estimate=LARGE_COST,
         name="near_conv",
-    )(pos, table, *halo, sibling)
+    )(table, *halo, sibling)
 
 
 def far_kernel(
-    first, pos_ref, _, filters_ref, acc_ref, r2_ref, r3_ref, r4_ref, sib_ref, sib_r3_ref,
+    first, _, filters_ref, acc_ref, r2_ref, r3_ref, r4_ref, sib_ref,
     corr_ref, grad_ref, table_ref,
 ):
     filt_count, rows, width = table_ref.shape
     tok = r2_ref.shape[0]
-    core = coords(pos_ref)[-1]
     edge = jnp.zeros((1, LANE), F32)
     start = filters_ref.shape[1] + LANE - width - LANE
     for k in range(filt_count):
         line = filters_ref[first + k : first + k + 1, start:].astype(F32)
         table_ref[k] = shifted_rows(jnp.concatenate([line, edge], axis=1), rows)[:, LANE:]
-    lay_out(core, grad_ref, (r2_ref, r3_ref, r4_ref), (sib_ref.at[2], sib_r3_ref, sib_ref.at[3]))
+    lay_out(grad_ref, (r2_ref, sib_ref.at[2], r3_ref, sib_ref.at[3], r4_ref))
     grad_ref[5 * tok :, :] = jnp.zeros((grad_ref.shape[0] - 5 * tok, LANE), BF16)
 
-    @pl.loop(0, tok // (2 * rows))
+    @pl.loop(0, tok // (2 * rows), unroll=True)
     def _(pair):
         start = pl.multiple_of(pair * (2 * rows), 2 * rows)
         both = pair_of_blocks(grad_ref, start, rows, width)
@@ -199,15 +189,14 @@
                 ]
 
 
-def far_conv(first, count, pos, after, filters, acc, halo, sibling, sibling_r3):
+def far_conv(first, count, after, filters, acc, halo, sibling):
     tok = halo[0].shape[0]
     width = filters.shape[1] // 2 + LANE
     vmem = pl.BlockSpec(memory_space=pltpu.VMEM)
     return pl.pallas_call(
         functools.partial(far_kernel, first),
         out_shape=jax.ShapeDtypeStruct((tok, count * LANE), BF16),
-        in_specs=[pl.BlockSpec(memory_space=pltpu.SMEM), pl.BlockSpec(memory_space=pl.ANY)]
-        + [vmem] * 7,
+        in_specs=[pl.BlockSpec(memory_space=pl.ANY)] + [vmem] * 6,
         out_specs=vmem,
         scratch_shapes=[
             pltpu.VMEM((5 * tok + ROWS, LANE), BF16),
@@ -216,7 +205,7 @@
         compiler_params=pltpu.CompilerParams(vmem_limit_bytes=VMEM_LIMIT),
         cost_estimate=SMALL_COST,
         name="far_conv",
-    )(pos, after, filters, acc, *halo, sibling, sibling_r3)
+    )(after, filters, acc, *halo, sibling)
 
 
 def product_kernel(
@@ -366,33 +355,26 @@
         return lax.ppermute(value, "tp", x_swap(crossed))
 
     count = filters.shape[0] // GROUPS
-    r1, r2, r4 = (later(grad_out, steps) for steps in (1, 2, 4))
+    pair = jnp.stack([inputs, lax.ppermute(inputs, "tp", Z_HI_SWAP)])
+    gathered = [pair] + [lax.ppermute(pair, "tp", along_x(s)) for s in range(1, NX)]
     table = near_table(filters)
-    stack, pair, grad_copy = prepare(
-        table, grad_out, r1, r2, r4, inputs, lax.ppermute(inputs, "tp", Z_HI_SWAP)
+    halo = [grad_out] + [later(grad_out, steps) for steps in range(1, 5)]
+    beside = sibling(for_sibling(pos, (table, pair), *halo))
+    accs = near_conv(table, halo[:3], beside, GROUPS)
+
+    def conv(group, after):
+        return far_conv(group * count, count, after, filters, accs[group], halo[2:], beside)
+
+    corr_0 = conv(0, table)
+    corr_1 = conv(1, corr_0)
+    keep_0, send_0 = product(False, pos, corr_1, corr_0, gathered)
+    near, near_send, far, far_send = input_shares(
+        pos, send_0, [corr_0, corr_1], projection.transpose(1, 0, 2)
     )
-    beside = sibling(stack)
-    gathered = [pair] + [lax.ppermute(pair, "tp", along_x(s)) for s in range(1, NX)]
-    r3 = later(grad_copy, 3)
-    beside_r3 = sibling(r3)
-    accs = near_conv(pos, table, (grad_out, r1, r2), beside, GROUPS)
-
-    def conv(group, after):
-        return far_conv(
-            group * count, count, pos, after, filters, accs[group], (r2, r3, r4), beside, beside_r3
-        )
-
-    corr_0 = conv(0, table)
-    keep_0, send_0 = product(False, pos, table, corr_0, gathered)
-    corr_1 = conv(1, send_0)
-    stay_0, leave_0 = halve(corr_1, keep_0, sibling(send_0))
+    stay_0, leave_0 = halve(near_send, keep_0, sibling(send_0))
     y_0 = y_swapped(leave_0, False)
     keep_1, send_1 = product(True, pos, leave_0, corr_1, gathered)
-
-    near, near_send, far, far_send = input_shares(
-        pos, send_1, [corr_0, corr_1], projection.transpose(1, 0, 2)
-    )
-    stay_1, leave_1 = halve(near_send, keep_1, sibling(send_1))
+    stay_1, leave_1 = halve(send_1, keep_1, sibling(send_1))
     y_1 = y_swapped(leave_1, True)
     far, leave = halve(leave_1, far, x_swapped(far_send, False))
     x_far = x_swapped(leave, True)

time: 99.1 us -> 95.3 us (0.962)
  Pallas kernels: 22.4 us -> 17.4 us
  local copies, waits for them, and re-layouts: 3.44 us -> 1.82 us
  starting transfers between devices: 41.3 us -> 42.6 us
  waiting for transfers between devices: 28.5 us -> 29.8 us
    pallas_call x2, Pallas kernels: 8.34 us -> 4.18 us  [far_conv(): pl.pallas_call(functools.partial(far_kernel, first), out_shape=jax.ShapeD...]
    ppermute x4, starting transfers between devices: 2.06 us -> 6.06 us  [x_swapped(): return lax.ppermute(value, 'tp', x_swap(crossed))]
    ppermute x4, waiting for transfers between devices: 11.1 us -> 8.55 us  [x_swapped(): return lax.ppermute(value, 'tp', x_swap(crossed))]
    ppermute x4, starting transfers between devices: 17.5 us -> 15.3 us  [later(): return lax.ppermute(value, 'ctx', from_later_chip(steps))]
    ppermute x1, waiting for transfers between devices: 4.23 us -> 6.33 us  [per_device(): pair = jnp.stack([inputs, lax.ppermute(inputs, 'tp', Z_HI_SWAP)])]
    ppermute x4 -> x3, waiting for transfers between devices: 0.01 us -> 1.91 us  [sibling(): return lax.ppermute(value, 'ctx', CORE_SWAP)]
    unnamed x20 -> x10, local copies, waits for them, and re-layouts: 3.44 us -> 1.82 us
    ppermute x3, starting transfers between devices: 4.47 us -> 5.73 us  [per_device(): lax.ppermute(pair, 'tp', along_x(s))]
  transfers between devices with their start and end apart: 25 -> 24, of which waited for: 9 -> 10; matrix products, arithmetic and copies ran while one was open for 1% -> 2% of each run, Pallas kernels for 18% -> 13%
where the time goes in v5:
time: 95.3 us; the launch traced here: 95.1 us
  starting transfers between devices  42.6 us (45%)
  waiting for transfers between devices  29.8 us (31%)
  Pallas kernels  17.4 us (18%)
  other arithmetic  2.48 us (3%)
  local copies, waits for them, and re-layouts  1.82 us (2%)
    ppermute x4, starting transfers between devices, later(): return lax.ppermute(value, 'ctx', from_later_chip(steps))  15.3 us
    ppermute x4, waiting for transfers between devices, z_swapped(): return lax.ppermute(value, 'ctx', z_swap(bit))  9.2 us
    ppermute x4, waiting for transfers between devices, x_swapped(): return lax.ppermute(value, 'tp', x_swap(crossed))  8.55 us
    ppermute x1, waiting for transfers between devices, per_device(): pair = jnp.stack([inputs, lax.ppermute(inputs, 'tp', Z_HI_SWAP)])  6.33 us
    ppermute x4, starting transfers between devices, x_swapped(): return lax.ppermute(value, 'tp', x_swap(crossed))  6.06 us
    ppermute x3, starting transfers between devices, per_device(): lax.ppermute(pair, 'tp', along_x(s))  5.73 us
    ppermute x1, starting transfers between devices, per_device(): pair = jnp.stack([inputs, lax.ppermute(inputs, 'tp', Z_HI_SWAP)])  5.48 us
    pallas_call x1, Pallas kernels, near_conv(): pl.pallas_call(near_kernel, out_shape=[acc] * groups, in_specs=[vmem] * 5...  4.34 us
  transfers between devices with their start and end apart: 24, of which 10 were waited for; matrix products, arithmetic and copies ran while one was open for 2% of the time, Pallas kernels for 13%

profile of v5, /device:TPU:24, one launch (start us, length us, event | category | flops | bytes accessed | tf_op | source)
XLA Modules:
  0.0 95.1 jit_solution(12851069260376965327)
XLA Ops:
  0.6 5.4 %collective-permute-start.1 = (bf16[512,128]{1,0:T(8,128)(2,1)}, bf16[512,128]{1,0:T(8,128)(2,1)S(1)}, u32[]{:S(2)}, u32[]{:S(2)}) collective-permute-start(bf16[512,128]{1,0:T(8,128)(2,1)} %own_ref.1), channel_id=1, source_target_pairs={{32,0},{40,8},{48,16},{56,24},{64,32},{72,40},{80,48},{88,56},{96,... | collective-permute-start | bytes 393224 | tf_op jit(solution)/shard_map/ppermute | solution.py:343
  6.0 3.7 %collective-permute-start.3 = (bf16[512,128]{1,0:T(8,128)(2,1)}, bf16[512,128]{1,0:T(8,128)(2,1)S(1)}, u32[]{:S(2)}, u32[]{:S(2)}) collective-permute-start(bf16[512,128]{1,0:T(8,128)(2,1)} %own_ref.1), channel_id=1, source_target_pairs={{48,0},{56,8},{64,16},{72,24},{80,32},{88,40},{96,48},{104,56},{11... | collective-permute-start | bytes 393224 | tf_op jit(solution)/shard_map/ppermute | solution.py:343
  9.7 2.4 %collective-permute-start.4 = (bf16[512,128]{1,0:T(8,128)(2,1)}, bf16[512,128]{1,0:T(8,128)(2,1)S(1)}, u32[]{:S(2)}, u32[]{:S(2)}) collective-permute-start(bf16[512,128]{1,0:T(8,128)(2,1)} %own_ref.1), channel_id=1, source_target_pairs={{64,0},{72,8},{80,16},{88,24},{96,32},{104,40},{112,48},{120,56},{... | collective-permute-start | bytes 393224 | tf_op jit(solution)/shard_map/ppermute | solution.py:343
  12.1 3.8 %collective-permute-start = (bf16[512,128]{1,0:T(8,128)(2,1)}, bf16[512,128]{1,0:T(8,128)(2,1)}, u32[]{:S(2)}, u32[]{:S(2)}) collective-permute-start(bf16[512,128]{1,0:T(8,128)(2,1)} %own_ref.1), channel_id=1, source_target_pairs={{16,0},{24,8},{32,16},{40,24},{48,32},{56,40},{64,48},{72,56},{80,... | collective-permute-start | bytes 393224 | tf_op jit(solution)/shard_map/ppermute | solution.py:343
  15.9 5.5 %collective-permute-start.2 = (bf16[512,128]{1,0:T(8,128)(2,1)}, bf16[512,128]{1,0:T(8,128)(2,1)}, u32[]{:S(2)}, u32[]{:S(2)}) collective-permute-start(bf16[512,128]{1,0:T(8,128)(2,1)} %param.4), channel_id=1, source_target_pairs={{0,1},{1,0},{2,3},{3,2},{4,5},{5,4},{6,7},{7,6},{8,9},{9,8},{10,11... | collective-permute-start | bytes 393224 | tf_op jit(solution)/shard_map/ppermute | solution.py:358
  21.4 0.9 copy-done.1
  22.3 0.9 near_table.1._.table_ref
  23.2 0.0 copy-start.4
  23.2 0.1 pad_add_fusion.pos_ref
  23.3 6.3 %collective-permute-done.2 = bf16[512,128]{1,0:T(8,128)(2,1)} collective-permute-done((bf16[512,128]{1,0:T(8,128)(2,1)}, bf16[512,128]{1,0:T(8,128)(2,1)}, u32[]{:S(2)}, u32[]{:S(2)}) %collective-permute-start.2) | collective-permute-done | bytes 131104 | tf_op jit(solution)/shard_map/ppermute | solution.py:358
  29.6 1.0 %pad_maximum_fusion.__.x0_ref = bf16[2,512,128]{2,1,0:T(8,128)(2,1)S(1)} fusion(bf16[1,512,128]{2,1,0:T(8,128)(2,1)} %bitcast.3, bf16[1,512,128]{2,1,0:T(8,128)(2,1)} %bitcast.22), kind=kLoop, calls=%fused_computation | loop fusion | flops 131072 | bytes 524288 | tf_op jit(solution)/shard_map/stack | solution.py:358
  30.6 0.0 collective-permute-done.1.refs_2_.r2_ref
  30.6 0.0 collective-permute-done.3.refs_3_.r3_ref
  30.7 0.0 collective-permute-done.refs_1_.r1_ref
  30.7 0.0 copy-start.3
  30.7 0.9 copy-done.3
  31.6 1.0 %for_sibling.1 = bf16[4,512,128]{2,1,0:T(8,128)(2,1)S(1)} custom-call(s32[2]{0:T(128)S(1)} %pad_add_fusion.pos_ref, bf16[12,64,2048]{2,1,0:T(8,128)(2,1)S(1)} %near_table.1._.table_ref, bf16[2,512,128]{2,1,0:T(8,128)(2,1)S(1)} %pad_maximum_fusion.__.x0_ref, bf16[512,128]{1,0:T(8,128)(2,1)S(1)} %copy-done.3, ...), custom_call_target="tpu_custom_call" | custom-call | flops 1000 | bytes 1000 | tf_op jit(solution)/shard_map/for_sibling/pallas_call | solution.py:99
  32.6 0.0 copy-start.2
  32.6 0.1 collective-permute-start.5
  32.7 1.6 %collective-permute-start.6 = (bf16[2,512,128]{2,1,0:T(8,128)(2,1)S(1)}, bf16[2,512,128]{2,1,0:T(8,128)(2,1)S(1)}, u32[]{:S(2)}, u32[]{:S(2)}) collective-permute-start(bf16[2,512,128]{2,1,0:T(8,128)(2,1)S(1)} %pad_maximum_fusion.__.x0_ref), channel_id=1, source_target_pairs={{0,2},{1,3},{2,4},{3,5},{4,6},{5,7},{6,0},{7,1},{8,10},{9,11},{10,... | collective-permute-start | bytes 786440 | tf_op jit(solution)/shard_map/ppermute | solution.py:359
  34.3 2.7 %collective-permute-start.7 = (bf16[2,512,128]{2,1,0:T(8,128)(2,1)S(1)}, bf16[2,512,128]{2,1,0:T(8,128)(2,1)S(1)}, u32[]{:S(2)}, u32[]{:S(2)}) collective-permute-start(bf16[2,512,128]{2,1,0:T(8,128)(2,1)S(1)} %pad_maximum_fusion.__.x0_ref), channel_id=1, source_target_pairs={{0,4},{1,5},{2,6},{3,7},{4,0},{5,1},{6,2},{7,3},{8,12},{9,13},{10,... | collective-permute-start | bytes 786440 | tf_op jit(solution)/shard_map/ppermute | solution.py:359
  37.0 1.4 %collective-permute-start.8 = (bf16[2,512,128]{2,1,0:T(8,128)(2,1)S(1)}, bf16[2,512,128]{2,1,0:T(8,128)(2,1)S(1)}, u32[]{:S(2)}, u32[]{:S(2)}) collective-permute-start(bf16[2,512,128]{2,1,0:T(8,128)(2,1)S(1)} %pad_maximum_fusion.__.x0_ref), channel_id=1, source_target_pairs={{0,6},{1,7},{2,0},{3,1},{4,2},{5,3},{6,4},{7,5},{8,14},{9,15},{10,... | collective-permute-start | bytes 786440 | tf_op jit(solution)/shard_map/ppermute | solution.py:359
  38.5 0.0 collective-permute-done.5.sib_ref
  38.5 4.3 %near_conv.1 = (f32[4,384,256]{2,1,0:T(8,128)S(1)}, f32[4,384,256]{2,1,0:T(8,128)S(1)}) custom-call(bf16[12,64,2048]{2,1,0:T(8,128)(2,1)S(1)} %near_table.1._.table_ref, bf16[512,128]{1,0:T(8,128)(2,1)S(1)} %copy-done.4, bf16[512,128]{1,0:T(8,128)(2,1)} %collective-permute-done.refs_1_.r1_ref, bf16[512,128]{1,0:T(8,128)(2,1)S(1)} %collective-permute-done.1.refs_2_.r2_ref, ...), custom_call_target="tpu_custom_call" | custom-call | flops 4000000000 | bytes 8000000 | tf_op jit(solution)/shard_map/near_conv/pallas_call | solution.py:152
  42.8 2.1 %far_conv.2._.corr_ref.refs_0_ = bf16[512,768]{1,0:T(8,128)(2,1)S(1)} custom-call(bf16[12,64,2048]{2,1,0:T(8,128)(2,1)S(1)} %near_table.1._.table_ref, bf16[12,4096]{1,0:T(8,128)(2,1)S(1)} %copy-done.2, f32[4,384,256]{2,1,0:T(8,128)S(1)} %get-tuple-element.32.acc_ref, bf16[512,128]{1,0:T(8,128)(2,1)S(1)} %collective-permute-done.1.refs_2_.r2_ref, ...), custom_call_target="tpu_custom_call" | custom-call | flops 1000 | bytes 1000 | tf_op jit(solution)/shard_map/far_conv/pallas_call | solution.py:196
  44.9 0.0 copy-start
  44.9 2.1 %far_conv.3._.refs_1_.corr_ref = bf16[512,768]{1,0:T(8,128)(2,1)S(1)} custom-call(bf16[512,768]{1,0:T(8,128)(2,1)S(1)} %far_conv.2._.corr_ref.refs_0_, bf16[12,4096]{1,0:T(8,128)(2,1)S(1)} %copy-done.2, f32[4,384,256]{2,1,0:T(8,128)S(1)} %get-tuple-element.33.acc_ref, bf16[512,128]{1,0:T(8,128)(2,1)S(1)} %collective-permute-done.1.refs_2_.r2_ref, ...), custom_call_target="tpu_custom_call" | custom-call | flops 1000 | bytes 1000 | tf_op jit(solution)/shard_map/far_conv/pallas_call | solution.py:196
  47.0 2.2 %collective-permute-done.7.x2_ref = bf16[2,512,128]{2,1,0:T(8,128)(2,1)S(1)} collective-permute-done((bf16[2,512,128]{2,1,0:T(8,128)(2,1)S(1)}, bf16[2,512,128]{2,1,0:T(8,128)(2,1)S(1)}, u32[]{:S(2)}, u32[]{:S(2)}) %collective-permute-start.7) | collective-permute-done | bytes 262176 | tf_op jit(solution)/shard_map/ppermute | solution.py:359
  49.3 1.9 %product.2 = (bf16[4,4,6,32,128]{4,3,2,1,0:T(8,128)(2,1)S(1)}, bf16[4,4,6,32,128]{4,3,2,1,0:T(8,128)(2,1)S(1)}) custom-call(s32[2]{0:T(128)S(1)} %pad_add_fusion.pos_ref, bf16[512,768]{1,0:T(8,128)(2,1)S(1)} %far_conv.3._.refs_1_.corr_ref, bf16[512,768]{1,0:T(8,128)(2,1)S(1)} %far_conv.2._.corr_ref.refs_0_, ...), custom_call_target="tpu_custom_call" | custom-call | flops 1000 | bytes 1000 | tf_op jit(solution)/shard_map/product/pallas_call | solution.py:241
  51.2 0.3 collective-permute-start.9
  51.5 2.4 %input_shares.1 = (f32[2,512,128]{2,1,0:T(8,128)S(1)}, bf16[2,512,128]{2,1,0:T(8,128)(2,1)S(1)}, f32[2,512,128]{2,1,0:T(8,128)S(1)}, bf16[2,512,128]{2,1,0:T(8,128)(2,1)S(1)}) custom-call(s32[2]{0:T(128)S(1)} %pad_add_fusion.pos_ref, bf16[4,4,6,32,128]{4,3,2,1,0:T(8,128)(2,1)S(1)} %get-tuple-element.34._, bf16[512,768]{1,0:T(8,128)(2,1)S(1)} %far_conv.2._.corr_ref.refs_0_, ...), custom_call_target="tpu_custom_call" | custom-call | flops 1000 | bytes 1000 | tf_op jit(solution)/shard_map/input_shares/pallas_call | solution.py:322
  53.9 0.0 collective-permute-done.9.other_ref
  53.9 0.2 halve.10
  54.1 1.9 %product.3 = (bf16[4,4,6,32,128]{4,3,2,1,0:T(8,128)(2,1)S(1)}, bf16[4,4,6,32,128]{4,3,2,1,0:T(8,128)(2,1)S(1)}) custom-call(s32[2]{0:T(128)S(1)} %pad_add_fusion.pos_ref, bf16[2,4,6,32,128]{4,3,2,1,0:T(8,128)(2,1)S(1)} %get-tuple-element.37._, bf16[512,768]{1,0:T(8,128)(2,1)S(1)} %far_conv.3._.refs_1_.corr_ref, ...), custom_call_target="tpu_custom_call" | custom-call | flops 1000 | bytes 1000 | tf_op jit(solution)/shard_map/product/pallas_call | solution.py:241
  56.0 0.6 collective-permute-start.10
  56.6 1.9 %collective-permute-done.10.other_ref = bf16[4,4,6,32,128]{4,3,2,1,0:T(8,128)(2,1)S(1)} collective-permute-done((bf16[4,4,6,32,128]{4,3,2,1,0:T(8,128)(2,1)S(1)}, bf16[4,4,6,32,128]{4,3,2,1,0:T(8,128)(2,1)S(1)}, u32[]{:S(2)}, u32[]{:S(2)}) %collective-permute-start.10) | collective-permute-done | bytes 786464 | tf_op jit(solution)/shard_map/ppermute | solution.py:346
  58.5 0.2 halve.11
  58.7 0.1 collective-permute-start.15
  58.8 1.4 %collective-permute-start.11 = (bf16[2,512,128]{2,1,0:T(8,128)(2,1)S(1)}, bf16[2,512,128]{2,1,0:T(8,128)(2,1)S(1)}, u32[]{:S(2)}, u32[]{:S(2)}) collective-permute-start(bf16[2,512,128]{2,1,0:T(8,128)(2,1)S(1)} %get-tuple-element.42), channel_id=1, source_target_pairs={{0,2},{1,3},{2,0},{3,1},{4,6},{5,7},{6,4},{7,5},{8,10},{9,11},{10,... | collective-permute-start | bytes 786440 | tf_op jit(solution)/shard_map/ppermute | solution.py:355
  60.2 1.9 %collective-permute-start.13 = (bf16[2,512,128]{2,1,0:T(8,128)(2,1)S(1)}, bf16[2,512,128]{2,1,0:T(8,128)(2,1)S(1)}, u32[]{:S(2)}, u32[]{:S(2)}) collective-permute-start(bf16[2,512,128]{2,1,0:T(8,128)(2,1)S(1)} %get-tuple-element.35._), channel_id=1, source_target_pairs={{0,6},{1,7},{2,4},{3,5},{4,2},{5,3},{6,0},{7,1},{8,14},{9,15},{10,... | collective-permute-start | bytes 786440 | tf_op jit(solution)/shard_map/ppermute | solution.py:355
  62.1 5.3 %collective-permute-done.11.other_ref = bf16[2,512,128]{2,1,0:T(8,128)(2,1)S(1)} collective-permute-done((bf16[2,512,128]{2,1,0:T(8,128)(2,1)S(1)}, bf16[2,512,128]{2,1,0:T(8,128)(2,1)S(1)}, u32[]{:S(2)}, u32[]{:S(2)}) %collective-permute-start.11) | collective-permute-done | bytes 262176 | tf_op jit(solution)/shard_map/ppermute | solution.py:355
  67.5 0.2 collective-permute-done.12.other_ref
  67.7 0.1 halve.13
  67.8 2.7 %collective-permute-start.18 = (bf16[1,4,6,32,128]{4,3,2,1,0:T(8,128)(2,1)S(1)}, bf16[1,4,6,32,128]{4,3,2,1,0:T(8,128)(2,1)S(1)}, u32[]{:S(2)}, u32[]{:S(2)}) collective-permute-start(bf16[1,4,6,32,128]{4,3,2,1,0:T(8,128)(2,1)S(1)} %get-tuple-element.45._), channel_id=1, source_target_pairs={{0,192},{8,200},{16,208},{24,216},{32,224},{40,232},{48,240},{56,2... | collective-permute-start | bytes 589832 | tf_op jit(solution)/shard_map/ppermute | solution.py:349
  70.5 2.3 %collective-permute-start.16 = (bf16[1,512,128]{2,1,0:T(8,128)(2,1)S(1)}, bf16[1,512,128]{2,1,0:T(8,128)(2,1)S(1)}, u32[]{:S(2)}, u32[]{:S(2)}) collective-permute-start(bf16[1,512,128]{2,1,0:T(8,128)(2,1)S(1)} %get-tuple-element.43._), channel_id=1, source_target_pairs={{0,6},{1,7},{2,4},{3,5},{4,2},{5,3},{6,0},{7,1},{8,14},{9,15},{10,... | collective-permute-start | bytes 393224 | tf_op jit(solution)/shard_map/ppermute | solution.py:355
  72.8 0.0 collective-permute-done.13.other_ref
  72.8 0.1 halve.15
  72.9 0.1 collective-permute-start.19
  73.0 0.5 collective-permute-start.14
  73.5 3.2 %collective-permute-done.16.other_ref = bf16[1,512,128]{2,1,0:T(8,128)(2,1)S(1)} collective-permute-done((bf16[1,512,128]{2,1,0:T(8,128)(2,1)S(1)}, bf16[1,512,128]{2,1,0:T(8,128)(2,1)S(1)}, u32[]{:S(2)}, u32[]{:S(2)}) %collective-permute-start.16) | collective-permute-done | bytes 131104 | tf_op jit(solution)/shard_map/ppermute | solution.py:355
  76.7 2.3 %collective-permute-start.17 = (bf16[1,512,128]{2,1,0:T(8,128)(2,1)S(1)}, bf16[1,512,128]{2,1,0:T(8,128)(2,1)S(1)}, u32[]{:S(2)}, u32[]{:S(2)}) collective-permute-start(bf16[1,512,128]{2,1,0:T(8,128)(2,1)S(1)} %add.37._), channel_id=1, source_target_pairs={{0,1},{1,0},{2,3},{3,2},{4,5},{5,4},{6,7},{7,6},{8,9},{9,8},{10,11... | collective-permute-start | bytes 393224 | tf_op jit(solution)/shard_map/ppermute | solution.py:388
  79.0 0.0 collective-permute-done.18
  79.0 0.2 collective-permute-start.20
  79.2 0.0 collective-permute-done.19
  79.3 2.0 %collective-permute-start.22 = (bf16[2,6,32,128]{3,2,1,0:T(8,128)(2,1)S(1)}, bf16[2,6,32,128]{3,2,1,0:T(8,128)(2,1)S(1)}, u32[]{:S(2)}, u32[]{:S(2)}) collective-permute-start(bf16[2,6,32,128]{3,2,1,0:T(8,128)(2,1)S(1)} %get-tuple-element.55._), channel_id=1, source_target_pairs={{0,16},{8,24},{16,0},{24,8},{32,48},{40,56},{48,32},{56,40},{64,80... | collective-permute-start | bytes 294920 | tf_op jit(solution)/shard_map/ppermute | solution.py:352
  81.3 5.3 %collective-permute-done.20.other_ref = bf16[2,6,32,128]{3,2,1,0:T(8,128)(2,1)S(1)} collective-permute-done((bf16[2,6,32,128]{3,2,1,0:T(8,128)(2,1)S(1)}, bf16[2,6,32,128]{3,2,1,0:T(8,128)(2,1)S(1)}, u32[]{:S(2)}, u32[]{:S(2)}) %collective-permute-start.20) | collective-permute-done | bytes 98336 | tf_op jit(solution)/shard_map/ppermute | solution.py:352
  86.6 0.6 collective-permute-start.21
  87.2 0.0 collective-permute-done.14
  87.2 1.4 %collective-permute-done.17 = bf16[1,512,128]{2,1,0:T(8,128)(2,1)S(1)} collective-permute-done((bf16[1,512,128]{2,1,0:T(8,128)(2,1)S(1)}, bf16[1,512,128]{2,1,0:T(8,128)(2,1)S(1)}, u32[]{:S(2)}, u32[]{:S(2)}) %collective-permute-start.17) | collective-permute-done | bytes 131104 | tf_op jit(solution)/shard_map/ppermute | solution.py:388
  88.6 0.7 fusion
  89.3 1.2 %collective-permute-start.23 = (bf16[1,6,32,128]{3,2,1,0:T(8,128)(2,1)S(1)}, bf16[1,6,32,128]{3,2,1,0:T(8,128)(2,1)S(1)}, u32[]{:S(2)}, u32[]{:S(2)}) collective-permute-start(bf16[1,6,32,128]{3,2,1,0:T(8,128)(2,1)S(1)} %get-tuple-element.61), channel_id=1, source_target_pairs={{0,32},{8,40},{16,48},{24,56},{32,0},{40,8},{48,16},{56,24},{64,96... | collective-permute-start | bytes 147464 | tf_op jit(solution)/shard_map/ppermute | solution.py:352
  90.5 1.2 %collective-permute-done.21 = bf16[1,6,32,128]{3,2,1,0:T(8,128)(2,1)S(1)} collective-permute-done((bf16[1,6,32,128]{3,2,1,0:T(8,128)(2,1)S(1)}, bf16[1,6,32,128]{3,2,1,0:T(8,128)(2,1)S(1)}, u32[]{:S(2)}, u32[]{:S(2)}) %collective-permute-start.21) | collective-permute-done | bytes 49184 | tf_op jit(solution)/shard_map/ppermute | solution.py:352
  91.7 2.7 %collective-permute-done.23 = bf16[1,6,32,128]{3,2,1,0:T(8,128)(2,1)S(1)} collective-permute-done((bf16[1,6,32,128]{3,2,1,0:T(8,128)(2,1)S(1)}, bf16[1,6,32,128]{3,2,1,0:T(8,128)(2,1)S(1)}, u32[]{:S(2)}, u32[]{:S(2)}) %collective-permute-start.23) | collective-permute-done | bytes 49184 | tf_op jit(solution)/shard_map/ppermute | solution.py:352
  94.4 0.7 maximum_bitcast_fusion
  (19 shorter events, 0.3 us)
Async XLA Ops:
  0.6 30.0 %collective-permute-start.1 = (bf16[512,128]{1,0:T(8,128)(2,1)}, bf16[512,128]{1,0:T(8,128)(2,1)S(1)}, u32[]{:S(2)}, u32[]{:S(2)}) collective-permute-start(bf16[512,128]{1,0:T(8,128)(2,1)} %own_ref.1), channel_id=1, source_target_pairs={{32,0},{40,8},{48,16},{56,24},{64,32},{72,40},{80,48},{88,56},{96,... | collective-permute-start | bytes 393224 | tf_op jit(solution)/shard_map/ppermute | solution.py:343
  6.0 24.6 %collective-permute-start.3 = (bf16[512,128]{1,0:T(8,128)(2,1)}, bf16[512,128]{1,0:T(8,128)(2,1)S(1)}, u32[]{:S(2)}, u32[]{:S(2)}) collective-permute-start(bf16[512,128]{1,0:T(8,128)(2,1)} %own_ref.1), channel_id=1, source_target_pairs={{48,0},{56,8},{64,16},{72,24},{80,32},{88,40},{96,48},{104,56},{11... | collective-permute-start | bytes 393224 | tf_op jit(solution)/shard_map/ppermute | solution.py:343
  9.7 20.9 %collective-permute-start.4 = (bf16[512,128]{1,0:T(8,128)(2,1)}, bf16[512,128]{1,0:T(8,128)(2,1)S(1)}, u32[]{:S(2)}, u32[]{:S(2)}) collective-permute-start(bf16[512,128]{1,0:T(8,128)(2,1)} %own_ref.1), channel_id=1, source_target_pairs={{64,0},{72,8},{80,16},{88,24},{96,32},{104,40},{112,48},{120,56},{... | collective-permute-start | bytes 393224 | tf_op jit(solution)/shard_map/ppermute | solution.py:343
  12.1 18.6 %collective-permute-start = (bf16[512,128]{1,0:T(8,128)(2,1)}, bf16[512,128]{1,0:T(8,128)(2,1)}, u32[]{:S(2)}, u32[]{:S(2)}) collective-permute-start(bf16[512,128]{1,0:T(8,128)(2,1)} %own_ref.1), channel_id=1, source_target_pairs={{16,0},{24,8},{32,16},{40,24},{48,32},{56,40},{64,48},{72,56},{80,... | collective-permute-start | bytes 393224 | tf_op jit(solution)/shard_map/ppermute | solution.py:343
  15.9 13.7 %collective-permute-start.2 = (bf16[512,128]{1,0:T(8,128)(2,1)}, bf16[512,128]{1,0:T(8,128)(2,1)}, u32[]{:S(2)}, u32[]{:S(2)}) collective-permute-start(bf16[512,128]{1,0:T(8,128)(2,1)} %param.4), channel_id=1, source_target_pairs={{0,1},{1,0},{2,3},{3,2},{4,5},{5,4},{6,7},{7,6},{8,9},{9,8},{10,11... | collective-permute-start | bytes 393224 | tf_op jit(solution)/shard_map/ppermute | solution.py:358
  21.4 0.9 copy-start.1
  23.2 15.2 %copy-start.4 = (bf16[512,128]{1,0:T(8,128)(2,1)S(1)}, bf16[512,128]{1,0:T(8,128)(2,1)}, u32[]{:S(2)}) copy-start(bf16[512,128]{1,0:T(8,128)(2,1)} %own_ref.1) | copy-start | bytes 393220
  30.7 0.9 copy-start.3
  32.6 10.2 %copy-start.2 = (bf16[12,4096]{1,0:T(8,128)(2,1)S(1)}, bf16[12,4096]{1,0:T(8,128)(2,1)}, u32[]{:S(2)}) copy-start(bf16[12,4096]{1,0:T(8,128)(2,1)} %filters_ref.5) | copy-start | bytes 294916
  32.6 5.8 %collective-permute-start.5 = (bf16[4,512,128]{2,1,0:T(8,128)(2,1)S(1)}, bf16[4,512,128]{2,1,0:T(8,128)(2,1)S(1)}, u32[]{:S(2)}, u32[]{:S(2)}) collective-permute-start(bf16[4,512,128]{2,1,0:T(8,128)(2,1)S(1)} %for_sibling.1), channel_id=1, source_target_pairs={{0,8},{8,0},{16,24},{24,16},{32,40},{40,32},{48,56},{56,48},{64,72... | collective-permute-start | bytes 1572872 | tf_op jit(solution)/shard_map/ppermute | solution.py:346
  32.7 14.3 %collective-permute-start.6 = (bf16[2,512,128]{2,1,0:T(8,128)(2,1)S(1)}, bf16[2,512,128]{2,1,0:T(8,128)(2,1)S(1)}, u32[]{:S(2)}, u32[]{:S(2)}) collective-permute-start(bf16[2,512,128]{2,1,0:T(8,128)(2,1)S(1)} %pad_maximum_fusion.__.x0_ref), channel_id=1, source_target_pairs={{0,2},{1,3},{2,4},{3,5},{4,6},{5,7},{6,0},{7,1},{8,10},{9,11},{10,... | collective-permute-start | bytes 786440 | tf_op jit(solution)/shard_map/ppermute | solution.py:359
  34.3 15.0 %collective-permute-start.7 = (bf16[2,512,128]{2,1,0:T(8,128)(2,1)S(1)}, bf16[2,512,128]{2,1,0:T(8,128)(2,1)S(1)}, u32[]{:S(2)}, u32[]{:S(2)}) collective-permute-start(bf16[2,512,128]{2,1,0:T(8,128)(2,1)S(1)} %pad_maximum_fusion.__.x0_ref), channel_id=1, source_target_pairs={{0,4},{1,5},{2,6},{3,7},{4,0},{5,1},{6,2},{7,3},{8,12},{9,13},{10,... | collective-permute-start | bytes 786440 | tf_op jit(solution)/shard_map/ppermute | solution.py:359
  37.0 12.2 %collective-permute-start.8 = (bf16[2,512,128]{2,1,0:T(8,128)(2,1)S(1)}, bf16[2,512,128]{2,1,0:T(8,128)(2,1)S(1)}, u32[]{:S(2)}, u32[]{:S(2)}) collective-permute-start(bf16[2,512,128]{2,1,0:T(8,128)(2,1)S(1)} %pad_maximum_fusion.__.x0_ref), channel_id=1, source_target_pairs={{0,6},{1,7},{2,0},{3,1},{4,2},{5,3},{6,4},{7,5},{8,14},{9,15},{10,... | collective-permute-start | bytes 786440 | tf_op jit(solution)/shard_map/ppermute | solution.py:359
  44.9 6.6 %copy-start = (bf16[1024,12,128]{2,0,1:T(8,128)(2,1)S(1)}, bf16[1024,12,128]{2,0,1:T(8,128)(2,1)}, u32[]{:S(2)}) copy-start(bf16[1024,12,128]{2,0,1:T(8,128)(2,1)} %param.7) | copy-start | bytes 9437188
  51.2 2.7 %collective-permute-start.9 = (bf16[4,4,6,32,128]{4,3,2,1,0:T(8,128)(2,1)S(1)}, bf16[4,4,6,32,128]{4,3,2,1,0:T(8,128)(2,1)S(1)}, u32[]{:S(2)}, u32[]{:S(2)}) collective-permute-start(bf16[4,4,6,32,128]{4,3,2,1,0:T(8,128)(2,1)S(1)} %get-tuple-element.34._), channel_id=1, source_target_pairs={{0,8},{8,0},{16,24},{24,16},{32,40},{40,32},{48,56},{56,48},{64,72... | collective-permute-start | bytes 2359304 | tf_op jit(solution)/shard_map/ppermute | solution.py:346
  56.0 2.5 %collective-permute-start.10 = (bf16[4,4,6,32,128]{4,3,2,1,0:T(8,128)(2,1)S(1)}, bf16[4,4,6,32,128]{4,3,2,1,0:T(8,128)(2,1)S(1)}, u32[]{:S(2)}, u32[]{:S(2)}) collective-permute-start(bf16[4,4,6,32,128]{4,3,2,1,0:T(8,128)(2,1)S(1)} %get-tuple-element.38._), channel_id=1, source_target_pairs={{0,8},{8,0},{16,24},{24,16},{32,40},{40,32},{48,56},{56,48},{64,72... | collective-permute-start | bytes 2359304 | tf_op jit(solution)/shard_map/ppermute | solution.py:346
  56.6 11.1 %collective-permute-start.12 = (bf16[2,4,6,32,128]{4,3,2,1,0:T(8,128)(2,1)S(1)}, bf16[2,4,6,32,128]{4,3,2,1,0:T(8,128)(2,1)S(1)}, u32[]{:S(2)}, u32[]{:S(2)}) collective-permute-start(bf16[2,4,6,32,128]{4,3,2,1,0:T(8,128)(2,1)S(1)} %get-tuple-element.37._), channel_id=1, source_target_pairs={{0,64},{8,72},{16,80},{24,88},{32,96},{40,104},{48,112},{56,120},{... | collective-permute-start | bytes 1179656 | tf_op jit(solution)/shard_map/ppermute | solution.py:349
  58.7 14.2 %collective-permute-start.15 = (bf16[2,4,6,32,128]{4,3,2,1,0:T(8,128)(2,1)S(1)}, bf16[2,4,6,32,128]{4,3,2,1,0:T(8,128)(2,1)S(1)}, u32[]{:S(2)}, u32[]{:S(2)}) collective-permute-start(bf16[2,4,6,32,128]{4,3,2,1,0:T(8,128)(2,1)S(1)} %get-tuple-element.40._), channel_id=1, source_target_pairs={{0,192},{8,200},{16,208},{24,216},{32,224},{40,232},{48,240},{56,2... | collective-permute-start | bytes 1179656 | tf_op jit(solution)/shard_map/ppermute | solution.py:349
  58.8 8.7 %collective-permute-start.11 = (bf16[2,512,128]{2,1,0:T(8,128)(2,1)S(1)}, bf16[2,512,128]{2,1,0:T(8,128)(2,1)S(1)}, u32[]{:S(2)}, u32[]{:S(2)}) collective-permute-start(bf16[2,512,128]{2,1,0:T(8,128)(2,1)S(1)} %get-tuple-element.42), channel_id=1, source_target_pairs={{0,2},{1,3},{2,0},{3,1},{4,6},{5,7},{6,4},{7,5},{8,10},{9,11},{10,... | collective-permute-start | bytes 786440 | tf_op jit(solution)/shard_map/ppermute | solution.py:355
  60.2 12.6 %collective-permute-start.13 = (bf16[2,512,128]{2,1,0:T(8,128)(2,1)S(1)}, bf16[2,512,128]{2,1,0:T(8,128)(2,1)S(1)}, u32[]{:S(2)}, u32[]{:S(2)}) collective-permute-start(bf16[2,512,128]{2,1,0:T(8,128)(2,1)S(1)} %get-tuple-element.35._), channel_id=1, source_target_pairs={{0,6},{1,7},{2,4},{3,5},{4,2},{5,3},{6,0},{7,1},{8,14},{9,15},{10,... | collective-permute-start | bytes 786440 | tf_op jit(solution)/shard_map/ppermute | solution.py:355
  67.8 11.2 %collective-permute-start.18 = (bf16[1,4,6,32,128]{4,3,2,1,0:T(8,128)(2,1)S(1)}, bf16[1,4,6,32,128]{4,3,2,1,0:T(8,128)(2,1)S(1)}, u32[]{:S(2)}, u32[]{:S(2)}) collective-permute-start(bf16[1,4,6,32,128]{4,3,2,1,0:T(8,128)(2,1)S(1)} %get-tuple-element.45._), channel_id=1, source_target_pairs={{0,192},{8,200},{16,208},{24,216},{32,224},{40,232},{48,240},{56,2... | collective-permute-start | bytes 589832 | tf_op jit(solution)/shard_map/ppermute | solution.py:349
  70.5 6.2 %collective-permute-start.16 = (bf16[1,512,128]{2,1,0:T(8,128)(2,1)S(1)}, bf16[1,512,128]{2,1,0:T(8,128)(2,1)S(1)}, u32[]{:S(2)}, u32[]{:S(2)}) collective-permute-start(bf16[1,512,128]{2,1,0:T(8,128)(2,1)S(1)} %get-tuple-element.43._), channel_id=1, source_target_pairs={{0,6},{1,7},{2,4},{3,5},{4,2},{5,3},{6,0},{7,1},{8,14},{9,15},{10,... | collective-permute-start | bytes 393224 | tf_op jit(solution)/shard_map/ppermute | solution.py:355
  72.9 6.3 %collective-permute-start.19 = (bf16[1,4,6,32,128]{4,3,2,1,0:T(8,128)(2,1)S(1)}, bf16[1,4,6,32,128]{4,3,2,1,0:T(8,128)(2,1)S(1)}, u32[]{:S(2)}, u32[]{:S(2)}) collective-permute-start(bf16[1,4,6,32,128]{4,3,2,1,0:T(8,128)(2,1)S(1)} %get-tuple-element.50._), channel_id=1, source_target_pairs={{0,64},{8,72},{16,80},{24,88},{32,96},{40,104},{48,112},{56,120},{... | collective-permute-start | bytes 589832 | tf_op jit(solution)/shard_map/ppermute | solution.py:349
  73.0 14.2 %collective-permute-start.14 = (bf16[1,512,128]{2,1,0:T(8,128)(2,1)S(1)}, bf16[1,512,128]{2,1,0:T(8,128)(2,1)S(1)}, u32[]{:S(2)}, u32[]{:S(2)}) collective-permute-start(bf16[1,512,128]{2,1,0:T(8,128)(2,1)S(1)} %get-tuple-element.48._), channel_id=1, source_target_pairs={{0,2},{1,3},{2,0},{3,1},{4,6},{5,7},{6,4},{7,5},{8,10},{9,11},{10,... | collective-permute-start | bytes 393224 | tf_op jit(solution)/shard_map/ppermute | solution.py:355
  76.7 11.8 %collective-permute-start.17 = (bf16[1,512,128]{2,1,0:T(8,128)(2,1)S(1)}, bf16[1,512,128]{2,1,0:T(8,128)(2,1)S(1)}, u32[]{:S(2)}, u32[]{:S(2)}) collective-permute-start(bf16[1,512,128]{2,1,0:T(8,128)(2,1)S(1)} %add.37._), channel_id=1, source_target_pairs={{0,1},{1,0},{2,3},{3,2},{4,5},{5,4},{6,7},{7,6},{8,9},{9,8},{10,11... | collective-permute-start | bytes 393224 | tf_op jit(solution)/shard_map/ppermute | solution.py:388
  79.0 7.6 %collective-permute-start.20 = (bf16[2,6,32,128]{3,2,1,0:T(8,128)(2,1)S(1)}, bf16[2,6,32,128]{3,2,1,0:T(8,128)(2,1)S(1)}, u32[]{:S(2)}, u32[]{:S(2)}) collective-permute-start(bf16[2,6,32,128]{3,2,1,0:T(8,128)(2,1)S(1)} %get-tuple-element.53._), channel_id=1, source_target_pairs={{0,16},{8,24},{16,0},{24,8},{32,48},{40,56},{48,32},{56,40},{64,80... | collective-permute-start | bytes 294920 | tf_op jit(solution)/shard_map/ppermute | solution.py:352
  79.3 10.0 %collective-permute-start.22 = (bf16[2,6,32,128]{3,2,1,0:T(8,128)(2,1)S(1)}, bf16[2,6,32,128]{3,2,1,0:T(8,128)(2,1)S(1)}, u32[]{:S(2)}, u32[]{:S(2)}) collective-permute-start(bf16[2,6,32,128]{3,2,1,0:T(8,128)(2,1)S(1)} %get-tuple-element.55._), channel_id=1, source_target_pairs={{0,16},{8,24},{16,0},{24,8},{32,48},{40,56},{48,32},{56,40},{64,80... | collective-permute-start | bytes 294920 | tf_op jit(solution)/shard_map/ppermute | solution.py:352
  86.6 5.1 %collective-permute-start.21 = (bf16[1,6,32,128]{3,2,1,0:T(8,128)(2,1)S(1)}, bf16[1,6,32,128]{3,2,1,0:T(8,128)(2,1)S(1)}, u32[]{:S(2)}, u32[]{:S(2)}) collective-permute-start(bf16[1,6,32,128]{3,2,1,0:T(8,128)(2,1)S(1)} %get-tuple-element.58._), channel_id=1, source_target_pairs={{0,32},{8,40},{16,48},{24,56},{32,0},{40,8},{48,16},{56,24},{64,96... | collective-permute-start | bytes 147464 | tf_op jit(solution)/shard_map/ppermute | solution.py:352
  89.3 5.1 %collective-permute-start.23 = (bf16[1,6,32,128]{3,2,1,0:T(8,128)(2,1)S(1)}, bf16[1,6,32,128]{3,2,1,0:T(8,128)(2,1)S(1)}, u32[]{:S(2)}, u32[]{:S(2)}) collective-permute-start(bf16[1,6,32,128]{3,2,1,0:T(8,128)(2,1)S(1)} %get-tuple-element.61), channel_id=1, source_target_pairs={{0,32},{8,40},{16,48},{24,56},{32,0},{40,8},{48,16},{56,24},{64,96... | collective-permute-start | bytes 147464 | tf_op jit(solution)/shard_map/ppermute | solution.py:352

commit v6 on v5

--- a/solution.py
+++ b/solution.py
@@ -65,7 +65,9 @@
     return pltpu.roll(block, 0, 1, stride=1, stride_axis=0).astype(BF16)
 
 
-def table_kernel(filters_ref, near_ref):
+def table_kernel(filters_ref, grad_ref, in_ref, near_ref, grad_copy_ref, in_copy_ref):
+    grad_copy_ref[...] = grad_ref[...]
+    in_copy_ref[...] = in_ref[...]
     filt_count, rows, near = near_ref.shape
     edge = jnp.zeros((1, LANE), F32)
     for k in range(filt_count):
@@ -73,40 +75,45 @@
         near_ref[k] = shifted_rows(jnp.concatenate([line, edge], axis=1), rows)[:, :near]
 
 
-def near_table(filters):
+def near_table(filters, grad_out, inputs):
     filt_count, taps = filters.shape
+    block = jax.ShapeDtypeStruct(grad_out.shape, BF16)
     vmem = pl.BlockSpec(memory_space=pltpu.VMEM)
     return pl.pallas_call(
         table_kernel,
-        out_shape=jax.ShapeDtypeStruct((filt_count, ROWS, taps // 2), BF16),
-        in_specs=[vmem],
-        out_specs=vmem,
+        out_shape=(jax.ShapeDtypeStruct((filt_count, ROWS, taps // 2), BF16), block, block),
+        in_specs=[vmem] * 3,
+        out_specs=[vmem] * 3,
         compiler_params=pltpu.CompilerParams(vmem_limit_bytes=VMEM_LIMIT),
         cost_estimate=LARGE_COST,
         name="near_table",
-    )(filters)
-
-
-def prep_kernel(pos_ref, _, __, *refs):
-    parts, stack_ref = refs[:-1], refs[-1]
+    )(filters, grad_out, inputs)
+
+
+def prep_kernel(pos_ref, own_ref, r1_ref, r2_ref, r3_ref, r4_ref, in_ref, far_in_ref, stack_ref, pair_ref):
+    parts = own_ref, r1_ref, r2_ref, r3_ref, r4_ref
     core = lax.rem(pos_ref[1], NCORE)
     for s in range(stack_ref.shape[0]):
         stack_ref[s] = jnp.where(core == 0, parts[s + 1][...], parts[s][...])
-
-
-def for_sibling(pos, after, *parts):
+    pair_ref[0] = in_ref[...]
+    pair_ref[1] = far_in_ref[...]
+
+
+def prepare(pos, *parts):
+    block = parts[0].shape
     vmem = pl.BlockSpec(memory_space=pltpu.VMEM)
     return pl.pallas_call(
         prep_kernel,
-        out_shape=jax.ShapeDtypeStruct((len(parts) - 1,) + parts[0].shape, BF16),
-        in_specs=[pl.BlockSpec(memory_space=pltpu.SMEM)]
-        + [pl.BlockSpec(memory_space=pl.ANY)] * 2
-        + [vmem] * len(parts),
-        out_specs=vmem,
-        compiler_params=pltpu.CompilerParams(vmem_limit_bytes=VMEM_LIMIT),
-        cost_estimate=SMALL_COST,
-        name="for_sibling",
-    )(pos, *after, *parts)
+        out_shape=(
+            jax.ShapeDtypeStruct((4,) + block, BF16),
+            jax.ShapeDtypeStruct((2,) + block, BF16),
+        ),
+        in_specs=[pl.BlockSpec(memory_space=pltpu.SMEM)] + [vmem] * len(parts),
+        out_specs=(vmem, vmem),
+        compiler_params=pltpu.CompilerParams(vmem_limit_bytes=VMEM_LIMIT),
+        cost_estimate=SMALL_COST,
+        name="prepare",
+    )(pos, *parts)
 
 
 def pair_of_blocks(grad_ref, start, rows, width):
@@ -355,11 +362,11 @@
         return lax.ppermute(value, "tp", x_swap(crossed))
 
     count = filters.shape[0] // GROUPS
-    pair = jnp.stack([inputs, lax.ppermute(inputs, "tp", Z_HI_SWAP)])
+    table, grad_copy, in_copy = near_table(filters, grad_out, inputs)
+    halo = [grad_copy] + [later(grad_out, steps) for steps in range(1, 5)]
+    stack, pair = prepare(pos, *halo, in_copy, lax.ppermute(inputs, "tp", Z_HI_SWAP))
     gathered = [pair] + [lax.ppermute(pair, "tp", along_x(s)) for s in range(1, NX)]
-    table = near_table(filters)
-    halo = [grad_out] + [later(grad_out, steps) for steps in range(1, 5)]
-    beside = sibling(for_sibling(pos, (table, pair), *halo))
+    beside = sibling(stack)
     accs = near_conv(table, halo[:3], beside, GROUPS)
 
     def conv(group, after):
@@ -367,22 +374,23 @@
 
     corr_0 = conv(0, table)
     corr_1 = conv(1, corr_0)
-    keep_0, send_0 = product(False, pos, corr_1, corr_0, gathered)
     near, near_send, far, far_send = input_shares(
-        pos, send_0, [corr_0, corr_1], projection.transpose(1, 0, 2)
+        pos, corr_1, [corr_0, corr_1], projection.transpose(1, 0, 2)
     )
-    stay_0, leave_0 = halve(near_send, keep_0, sibling(send_0))
+    x_far, x_near = x_swapped(far_send, False), x_swapped(near_send, True)
+    keep_0, send_0 = product(False, pos, near_send, corr_0, gathered)
+    keep_1, send_1 = product(True, pos, send_0, corr_1, gathered)
+    stay_0, leave_0 = halve(send_1, keep_0, sibling(send_0))
     y_0 = y_swapped(leave_0, False)
-    keep_1, send_1 = product(True, pos, leave_0, corr_1, gathered)
-    stay_1, leave_1 = halve(send_1, keep_1, sibling(send_1))
+    stay_1, leave_1 = halve(leave_0, keep_1, sibling(send_1))
     y_1 = y_swapped(leave_1, True)
-    far, leave = halve(leave_1, far, x_swapped(far_send, False))
+    far, leave = halve(leave_1, far, x_far)
     x_far = x_swapped(leave, True)
+    near, leave = halve(leave, near, x_near)
+    x_near = x_swapped(leave, False)
     stay_0, leave_0 = halve(leave, stay_0, y_0)
     y_0 = y_swapped(leave_0, True)
-    near, leave = halve(leave_0, near, x_swapped(near_send, True))
-    x_near = x_swapped(leave, False)
-    stay_1, leave_1 = halve(leave, stay_1, y_1)
+    stay_1, leave_1 = halve(leave_0, stay_1, y_1)
     y_1 = y_swapped(leave_1, False)
     far = add(leave_1, far, x_far)
     opposite = lax.ppermute(far, "tp", Z_HI_SWAP)

time: 95.3 us -> 95.4 us (level)
  local copies, waits for them, and re-layouts: 1.82 us -> 5.83 us
  waiting for transfers between devices: 29.8 us -> 27.8 us
  starting transfers between devices: 42.6 us -> 41.4 us
  other arithmetic: 2.48 us -> 1.49 us
    unnamed x10 -> x18, local copies, waits for them, and re-layouts: 1.82 us -> 5.83 us
    ppermute x1, waiting for transfers between devices: 6.33 us -> 3.2 us  [per_device(): lax.ppermute(inputs, 'tp', Z_HI_SWAP)]
    ppermute x4, waiting for transfers between devices: 8.55 us -> 11.6 us  [x_swapped(): return lax.ppermute(value, 'tp', x_swap(crossed))]
    ppermute x3, waiting for transfers between devices: 2.23 us -> 0.01 us  [per_device(): lax.ppermute(pair, 'tp', along_x(s))]
    another operation x1 -> x0, other arithmetic: 0.99 us -> none  [per_device(): pair = jnp.stack([inputs, lax.ppermute(inputs, 'tp', Z_HI_SWAP)])]
    ppermute x4, starting transfers between devices: 6.06 us -> 5.1 us  [x_swapped(): return lax.ppermute(value, 'tp', x_swap(crossed))]
  transfers between devices with their start and end apart: 24 -> 24, of which waited for: 10 -> 9; matrix products, arithmetic and copies ran while one was open for 2% -> 1% of each run, Pallas kernels for 13% -> 15%
where the time goes in v6:
time: 95.4 us; the launch traced here: 95.1 us
  starting transfers between devices  41.4 us (43%)
  waiting for transfers between devices  27.8 us (29%)
  Pallas kernels  17.5 us (18%)
  local copies, waits for them, and re-layouts  5.83 us (6%)
  other arithmetic  1.49 us (2%)
    ppermute x4, starting transfers between devices, later(): return lax.ppermute(value, 'ctx', from_later_chip(steps))  15.2 us
    ppermute x4, waiting for transfers between devices, x_swapped(): return lax.ppermute(value, 'tp', x_swap(crossed))  11.6 us
    ppermute x4, waiting for transfers between devices, z_swapped(): return lax.ppermute(value, 'ctx', z_swap(bit))  9.73 us
    unnamed x18, local copies, waits for them, and re-layouts  5.83 us
    ppermute x3, starting transfers between devices, per_device(): lax.ppermute(pair, 'tp', along_x(s))  5.73 us
    ppermute x1, starting transfers between devices, per_device(): lax.ppermute(inputs, 'tp', Z_HI_SWAP)  5.48 us
    ppermute x4, starting transfers between devices, x_swapped(): return lax.ppermute(value, 'tp', x_swap(crossed))  5.1 us
    pallas_call x1, Pallas kernels, near_conv(): pl.pallas_call(near_kernel, out_shape=[acc] * groups, in_specs=[vmem] * 5...  4.37 us
  transfers between devices with their start and end apart: 24, of which 9 were waited for; matrix products, arithmetic and copies ran while one was open for 1% of the time, Pallas kernels for 15%

profile of v6, /device:TPU:24, one launch (start us, length us, event | category | flops | bytes accessed | tf_op | source)
XLA Modules:
  0.0 95.1 jit_solution(14583738307860775291)
XLA Ops:
  0.6 5.4 %collective-permute-start.1 = (bf16[512,128]{1,0:T(8,128)(2,1)}, bf16[512,128]{1,0:T(8,128)(2,1)S(1)}, u32[]{:S(2)}, u32[]{:S(2)}) collective-permute-start(bf16[512,128]{1,0:T(8,128)(2,1)} %grad_ref.1), channel_id=1, source_target_pairs={{32,0},{40,8},{48,16},{56,24},{64,32},{72,40},{80,48},{88,56},{96,... | collective-permute-start | bytes 393224 | tf_op jit(solution)/shard_map/ppermute | solution.py:350
  6.0 3.7 %collective-permute-start.2 = (bf16[512,128]{1,0:T(8,128)(2,1)}, bf16[512,128]{1,0:T(8,128)(2,1)S(1)}, u32[]{:S(2)}, u32[]{:S(2)}) collective-permute-start(bf16[512,128]{1,0:T(8,128)(2,1)} %grad_ref.1), channel_id=1, source_target_pairs={{48,0},{56,8},{64,16},{72,24},{80,32},{88,40},{96,48},{104,56},{11... | collective-permute-start | bytes 393224 | tf_op jit(solution)/shard_map/ppermute | solution.py:350
  9.7 2.4 %collective-permute-start.3 = (bf16[512,128]{1,0:T(8,128)(2,1)}, bf16[512,128]{1,0:T(8,128)(2,1)S(1)}, u32[]{:S(2)}, u32[]{:S(2)}) collective-permute-start(bf16[512,128]{1,0:T(8,128)(2,1)} %grad_ref.1), channel_id=1, source_target_pairs={{64,0},{72,8},{80,16},{88,24},{96,32},{104,40},{112,48},{120,56},{... | collective-permute-start | bytes 393224 | tf_op jit(solution)/shard_map/ppermute | solution.py:350
  12.1 3.8 %collective-permute-start = (bf16[512,128]{1,0:T(8,128)(2,1)}, bf16[512,128]{1,0:T(8,128)(2,1)}, u32[]{:S(2)}, u32[]{:S(2)}) collective-permute-start(bf16[512,128]{1,0:T(8,128)(2,1)} %grad_ref.1), channel_id=1, source_target_pairs={{16,0},{24,8},{32,16},{40,24},{48,32},{56,40},{64,48},{72,56},{80,... | collective-permute-start | bytes 393224 | tf_op jit(solution)/shard_map/ppermute | solution.py:350
  15.9 5.5 %collective-permute-start.4 = (bf16[512,128]{1,0:T(8,128)(2,1)}, bf16[512,128]{1,0:T(8,128)(2,1)}, u32[]{:S(2)}, u32[]{:S(2)}) collective-permute-start(bf16[512,128]{1,0:T(8,128)(2,1)} %in_ref.1), channel_id=1, source_target_pairs={{0,1},{1,0},{2,3},{3,2},{4,5},{5,4},{6,7},{7,6},{8,9},{9,8},{10,11... | collective-permute-start | bytes 393224 | tf_op jit(solution)/shard_map/ppermute | solution.py:367
  21.4 0.9 copy-done.1
  22.3 0.9 copy-done.7
  23.2 0.9 copy-done.8
  24.1 0.9 near_table.1
  25.0 0.0 copy-start.3
  25.0 0.6 copy-done.3
  25.7 0.7 copy-done.5
  26.3 0.1 pad_add_fusion.pos_ref
  26.4 0.0 collective-permute-done.1.r2_ref
  26.4 0.0 collective-permute-done.2.r3_ref
  26.4 0.0 collective-permute-done.3.r4_ref
  26.4 3.2 %collective-permute-done.4.far_in_ref = bf16[512,128]{1,0:T(8,128)(2,1)} collective-permute-done((bf16[512,128]{1,0:T(8,128)(2,1)}, bf16[512,128]{1,0:T(8,128)(2,1)}, u32[]{:S(2)}, u32[]{:S(2)}) %collective-permute-start.4) | collective-permute-done | bytes 131104 | tf_op jit(solution)/shard_map/ppermute | solution.py:367
  29.6 0.9 copy-done.4
  30.5 0.9 copy-done.6
  31.4 1.1 %prepare.1 = (bf16[4,512,128]{2,1,0:T(8,128)(2,1)S(1)}, bf16[2,512,128]{2,1,0:T(8,128)(2,1)S(1)}) custom-call(s32[2]{0:T(128)S(1)} %pad_add_fusion.pos_ref, bf16[512,128]{1,0:T(8,128)(2,1)S(1)} %copy-done.4, bf16[512,128]{1,0:T(8,128)(2,1)} %collective-permute-done.r1_ref, bf16[512,128]{1,0:T(8,128)(2,1)S(1)} %collective-permute-done.1.r2_ref, ...), custom_call_target="tpu_custom_call" | custom-call | flops 1000 | bytes 1000 | tf_op jit(solution)/shard_map/prepare/pallas_call | solution.py:105
  32.5 0.1 collective-permute-start.5
  32.6 1.6 %collective-permute-start.6 = (bf16[2,512,128]{2,1,0:T(8,128)(2,1)S(1)}, bf16[2,512,128]{2,1,0:T(8,128)(2,1)S(1)}, u32[]{:S(2)}, u32[]{:S(2)}) collective-permute-start(bf16[2,512,128]{2,1,0:T(8,128)(2,1)S(1)} %get-tuple-element.44.x0_ref), channel_id=1, source_target_pairs={{0,2},{1,3},{2,4},{3,5},{4,6},{5,7},{6,0},{7,1},{8,10},{9,11},{10,... | collective-permute-start | bytes 786440 | tf_op jit(solution)/shard_map/ppermute | solution.py:368
  34.2 2.7 %collective-permute-start.7 = (bf16[2,512,128]{2,1,0:T(8,128)(2,1)S(1)}, bf16[2,512,128]{2,1,0:T(8,128)(2,1)S(1)}, u32[]{:S(2)}, u32[]{:S(2)}) collective-permute-start(bf16[2,512,128]{2,1,0:T(8,128)(2,1)S(1)} %get-tuple-element.44.x0_ref), channel_id=1, source_target_pairs={{0,4},{1,5},{2,6},{3,7},{4,0},{5,1},{6,2},{7,3},{8,12},{9,13},{10,... | collective-permute-start | bytes 786440 | tf_op jit(solution)/shard_map/ppermute | solution.py:368
  36.9 1.4 %collective-permute-start.8 = (bf16[2,512,128]{2,1,0:T(8,128)(2,1)S(1)}, bf16[2,512,128]{2,1,0:T(8,128)(2,1)S(1)}, u32[]{:S(2)}, u32[]{:S(2)}) collective-permute-start(bf16[2,512,128]{2,1,0:T(8,128)(2,1)S(1)} %get-tuple-element.44.x0_ref), channel_id=1, source_target_pairs={{0,6},{1,7},{2,0},{3,1},{4,2},{5,3},{6,4},{7,5},{8,14},{9,15},{10,... | collective-permute-start | bytes 786440 | tf_op jit(solution)/shard_map/ppermute | solution.py:368
  38.4 0.0 collective-permute-done.5.sib_ref
  38.4 4.4 %near_conv.1 = (f32[4,384,256]{2,1,0:T(8,128)S(1)}, f32[4,384,256]{2,1,0:T(8,128)S(1)}) custom-call(bf16[12,64,2048]{2,1,0:T(8,128)(2,1)S(1)} %get-tuple-element.37.table_ref._, bf16[512,128]{1,0:T(8,128)(2,1)S(1)} %copy-done.4, bf16[512,128]{1,0:T(8,128)(2,1)} %collective-permute-done.r1_ref, bf16[512,128]{1,0:T(8,128)(2,1)S(1)} %collective-permute-done.1.r2_ref, ...), custom_call_target="tpu_custom_call" | custom-call | flops 4000000000 | bytes 8000000 | tf_op jit(solution)/shard_map/near_conv/pallas_call | solution.py:159
  42.8 2.1 %far_conv.2._.refs_0_.corr_ref = bf16[512,768]{1,0:T(8,128)(2,1)S(1)} custom-call(bf16[12,64,2048]{2,1,0:T(8,128)(2,1)S(1)} %get-tuple-element.37.table_ref._, bf16[12,4096]{1,0:T(8,128)(2,1)S(1)} %copy-done.2, f32[4,384,256]{2,1,0:T(8,128)S(1)} %get-tuple-element.41.acc_ref, bf16[512,128]{1,0:T(8,128)(2,1)S(1)} %collective-permute-done.1.r2_ref, ...), custom_call_target="tpu_custom_call" | custom-call | flops 1000 | bytes 1000 | tf_op jit(solution)/shard_map/far_conv/pallas_call | solution.py:203
  44.9 0.0 copy-start
  44.9 2.1 %far_conv.3._.refs_1_.corr_ref = bf16[512,768]{1,0:T(8,128)(2,1)S(1)} custom-call(bf16[512,768]{1,0:T(8,128)(2,1)S(1)} %far_conv.2._.refs_0_.corr_ref, bf16[12,4096]{1,0:T(8,128)(2,1)S(1)} %copy-done.2, f32[4,384,256]{2,1,0:T(8,128)S(1)} %get-tuple-element.42.acc_ref, bf16[512,128]{1,0:T(8,128)(2,1)S(1)} %collective-permute-done.1.r2_ref, ...), custom_call_target="tpu_custom_call" | custom-call | flops 1000 | bytes 1000 | tf_op jit(solution)/shard_map/far_conv/pallas_call | solution.py:203
  47.0 2.4 %input_shares.1 = (f32[2,512,128]{2,1,0:T(8,128)S(1)}, bf16[2,512,128]{2,1,0:T(8,128)(2,1)S(1)}, f32[2,512,128]{2,1,0:T(8,128)S(1)}, bf16[2,512,128]{2,1,0:T(8,128)(2,1)S(1)}) custom-call(s32[2]{0:T(128)S(1)} %pad_add_fusion.pos_ref, bf16[512,768]{1,0:T(8,128)(2,1)S(1)} %far_conv.3._.refs_1_.corr_ref, bf16[512,768]{1,0:T(8,128)(2,1)S(1)} %far_conv.2._.refs_0_.corr_ref, ...), custom_call_target="tpu_custom_call" | custom-call | flops 1000 | bytes 1000 | tf_op jit(solution)/shard_map/input_shares/pallas_call | solution.py:329
  49.4 0.0 collective-permute-done.7.x2_ref
  49.4 1.9 %product.2 = (bf16[4,4,6,32,128]{4,3,2,1,0:T(8,128)(2,1)S(1)}, bf16[4,4,6,32,128]{4,3,2,1,0:T(8,128)(2,1)S(1)}) custom-call(s32[2]{0:T(128)S(1)} %pad_add_fusion.pos_ref, bf16[2,512,128]{2,1,0:T(8,128)(2,1)S(1)} %get-tuple-element.43._, bf16[512,768]{1,0:T(8,128)(2,1)S(1)} %far_conv.2._.refs_0_.corr_ref, bf16[2,512,128]{2,1,0:T(8,128)(2,1)S(1)} %get-tuple-element.44.x0_ref, ...), custom_call_target="tpu_custom_call" | custom-call | flops 1000 | bytes 1000 | tf_op jit(solution)/shard_map/product/pallas_call | solution.py:248
  51.3 0.1 collective-permute-start.9
  51.4 1.9 %product.3 = (bf16[4,4,6,32,128]{4,3,2,1,0:T(8,128)(2,1)S(1)}, bf16[4,4,6,32,128]{4,3,2,1,0:T(8,128)(2,1)S(1)}) custom-call(s32[2]{0:T(128)S(1)} %pad_add_fusion.pos_ref, bf16[4,4,6,32,128]{4,3,2,1,0:T(8,128)(2,1)S(1)} %get-tuple-element.45._, bf16[512,768]{1,0:T(8,128)(2,1)S(1)} %far_conv.3._.refs_1_.corr_ref, ...), custom_call_target="tpu_custom_call" | custom-call | flops 1000 | bytes 1000 | tf_op jit(solution)/shard_map/product/pallas_call | solution.py:248
  53.4 0.6 collective-permute-start.10
  54.0 0.2 halve.10
  54.1 0.1 collective-permute-start.14
  54.2 1.6 %collective-permute-done.10.other_ref = bf16[4,4,6,32,128]{4,3,2,1,0:T(8,128)(2,1)S(1)} collective-permute-done((bf16[4,4,6,32,128]{4,3,2,1,0:T(8,128)(2,1)S(1)}, bf16[4,4,6,32,128]{4,3,2,1,0:T(8,128)(2,1)S(1)}, u32[]{:S(2)}, u32[]{:S(2)}) %collective-permute-start.10) | collective-permute-done | bytes 786464 | tf_op jit(solution)/shard_map/ppermute | solution.py:353
  55.9 0.2 halve.11
  56.0 0.1 collective-permute-start.15
  56.1 1.2 %collective-permute-start.11 = (bf16[2,512,128]{2,1,0:T(8,128)(2,1)S(1)}, bf16[2,512,128]{2,1,0:T(8,128)(2,1)S(1)}, u32[]{:S(2)}, u32[]{:S(2)}) collective-permute-start(bf16[2,512,128]{2,1,0:T(8,128)(2,1)S(1)} %get-tuple-element.52), channel_id=1, source_target_pairs={{0,2},{1,3},{2,0},{3,1},{4,6},{5,7},{6,4},{7,5},{8,10},{9,11},{10,... | collective-permute-start | bytes 786440 | tf_op jit(solution)/shard_map/ppermute | solution.py:362
  57.4 1.9 %collective-permute-start.12 = (bf16[2,512,128]{2,1,0:T(8,128)(2,1)S(1)}, bf16[2,512,128]{2,1,0:T(8,128)(2,1)S(1)}, u32[]{:S(2)}, u32[]{:S(2)}) collective-permute-start(bf16[2,512,128]{2,1,0:T(8,128)(2,1)S(1)} %get-tuple-element.43._), channel_id=1, source_target_pairs={{0,6},{1,7},{2,4},{3,5},{4,2},{5,3},{6,0},{7,1},{8,14},{9,15},{10,... | collective-permute-start | bytes 786440 | tf_op jit(solution)/shard_map/ppermute | solution.py:362
  59.3 5.5 %collective-permute-done.11.other_ref = bf16[2,512,128]{2,1,0:T(8,128)(2,1)S(1)} collective-permute-done((bf16[2,512,128]{2,1,0:T(8,128)(2,1)S(1)}, bf16[2,512,128]{2,1,0:T(8,128)(2,1)S(1)}, u32[]{:S(2)}, u32[]{:S(2)}) %collective-permute-start.11) | collective-permute-done | bytes 262176 | tf_op jit(solution)/shard_map/ppermute | solution.py:362
  64.8 0.1 halve.12
  64.9 2.0 %collective-permute-done.12.other_ref = bf16[2,512,128]{2,1,0:T(8,128)(2,1)S(1)} collective-permute-done((bf16[2,512,128]{2,1,0:T(8,128)(2,1)S(1)}, bf16[2,512,128]{2,1,0:T(8,128)(2,1)S(1)}, u32[]{:S(2)}, u32[]{:S(2)}) %collective-permute-start.12) | collective-permute-done | bytes 262176 | tf_op jit(solution)/shard_map/ppermute | solution.py:362
  66.9 0.1 halve.13
  67.0 0.1 halve.14
  67.0 2.9 %collective-permute-start.18 = (bf16[1,4,6,32,128]{4,3,2,1,0:T(8,128)(2,1)S(1)}, bf16[1,4,6,32,128]{4,3,2,1,0:T(8,128)(2,1)S(1)}, u32[]{:S(2)}, u32[]{:S(2)}) collective-permute-start(bf16[1,4,6,32,128]{4,3,2,1,0:T(8,128)(2,1)S(1)} %get-tuple-element.58._), channel_id=1, source_target_pairs={{0,192},{8,200},{16,208},{24,216},{32,224},{40,232},{48,240},{56,2... | collective-permute-start | bytes 589832 | tf_op jit(solution)/shard_map/ppermute | solution.py:356
  70.0 1.9 %collective-permute-start.16 = (bf16[1,512,128]{2,1,0:T(8,128)(2,1)S(1)}, bf16[1,512,128]{2,1,0:T(8,128)(2,1)S(1)}, u32[]{:S(2)}, u32[]{:S(2)}) collective-permute-start(bf16[1,512,128]{2,1,0:T(8,128)(2,1)S(1)} %get-tuple-element.53._), channel_id=1, source_target_pairs={{0,6},{1,7},{2,4},{3,5},{4,2},{5,3},{6,0},{7,1},{8,14},{9,15},{10,... | collective-permute-start | bytes 393224 | tf_op jit(solution)/shard_map/ppermute | solution.py:362
  71.9 0.1 halve.15
  71.9 0.1 collective-permute-start.19
  72.0 0.1 collective-permute-start.13
  72.1 4.0 %collective-permute-done.16.other_ref = bf16[1,512,128]{2,1,0:T(8,128)(2,1)S(1)} collective-permute-done((bf16[1,512,128]{2,1,0:T(8,128)(2,1)S(1)}, bf16[1,512,128]{2,1,0:T(8,128)(2,1)S(1)}, u32[]{:S(2)}, u32[]{:S(2)}) %collective-permute-start.16) | collective-permute-done | bytes 131104 | tf_op jit(solution)/shard_map/ppermute | solution.py:362
  76.2 2.3 %collective-permute-start.17 = (bf16[1,512,128]{2,1,0:T(8,128)(2,1)S(1)}, bf16[1,512,128]{2,1,0:T(8,128)(2,1)S(1)}, u32[]{:S(2)}, u32[]{:S(2)}) collective-permute-start(bf16[1,512,128]{2,1,0:T(8,128)(2,1)S(1)} %add.37._), channel_id=1, source_target_pairs={{0,1},{1,0},{2,3},{3,2},{4,5},{5,4},{6,7},{7,6},{8,9},{9,8},{10,11... | collective-permute-start | bytes 393224 | tf_op jit(solution)/shard_map/ppermute | solution.py:396
  78.5 0.2 collective-permute-start.20
  78.7 2.0 %collective-permute-start.22 = (bf16[2,6,32,128]{3,2,1,0:T(8,128)(2,1)S(1)}, bf16[2,6,32,128]{3,2,1,0:T(8,128)(2,1)S(1)}, u32[]{:S(2)}, u32[]{:S(2)}) collective-permute-start(bf16[2,6,32,128]{3,2,1,0:T(8,128)(2,1)S(1)} %get-tuple-element.65._), channel_id=1, source_target_pairs={{0,16},{8,24},{16,0},{24,8},{32,48},{40,56},{48,32},{56,40},{64,80... | collective-permute-start | bytes 294920 | tf_op jit(solution)/shard_map/ppermute | solution.py:359
  80.8 5.5 %collective-permute-done.20.other_ref = bf16[2,6,32,128]{3,2,1,0:T(8,128)(2,1)S(1)} collective-permute-done((bf16[2,6,32,128]{3,2,1,0:T(8,128)(2,1)S(1)}, bf16[2,6,32,128]{3,2,1,0:T(8,128)(2,1)S(1)}, u32[]{:S(2)}, u32[]{:S(2)}) %collective-permute-start.20) | collective-permute-done | bytes 98336 | tf_op jit(solution)/shard_map/ppermute | solution.py:359
  86.2 0.1 collective-permute-start.21
  86.4 1.7 %collective-permute-done.17 = bf16[1,512,128]{2,1,0:T(8,128)(2,1)S(1)} collective-permute-done((bf16[1,512,128]{2,1,0:T(8,128)(2,1)S(1)}, bf16[1,512,128]{2,1,0:T(8,128)(2,1)S(1)}, u32[]{:S(2)}, u32[]{:S(2)}) %collective-permute-start.17) | collective-permute-done | bytes 131104 | tf_op jit(solution)/shard_map/ppermute | solution.py:396
  88.0 0.7 fusion
  88.7 1.3 %collective-permute-start.23 = (bf16[1,6,32,128]{3,2,1,0:T(8,128)(2,1)S(1)}, bf16[1,6,32,128]{3,2,1,0:T(8,128)(2,1)S(1)}, u32[]{:S(2)}, u32[]{:S(2)}) collective-permute-start(bf16[1,6,32,128]{3,2,1,0:T(8,128)(2,1)S(1)} %get-tuple-element.71), channel_id=1, source_target_pairs={{0,32},{8,40},{16,48},{24,56},{32,0},{40,8},{48,16},{56,24},{64,96... | collective-permute-start | bytes 147464 | tf_op jit(solution)/shard_map/ppermute | solution.py:359
  90.1 1.3 %collective-permute-done.21 = bf16[1,6,32,128]{3,2,1,0:T(8,128)(2,1)S(1)} collective-permute-done((bf16[1,6,32,128]{3,2,1,0:T(8,128)(2,1)S(1)}, bf16[1,6,32,128]{3,2,1,0:T(8,128)(2,1)S(1)}, u32[]{:S(2)}, u32[]{:S(2)}) %collective-permute-start.21) | collective-permute-done | bytes 49184 | tf_op jit(solution)/shard_map/ppermute | solution.py:359
  91.3 3.0 %collective-permute-done.23 = bf16[1,6,32,128]{3,2,1,0:T(8,128)(2,1)S(1)} collective-permute-done((bf16[1,6,32,128]{3,2,1,0:T(8,128)(2,1)S(1)}, bf16[1,6,32,128]{3,2,1,0:T(8,128)(2,1)S(1)}, u32[]{:S(2)}, u32[]{:S(2)}) %collective-permute-start.23) | collective-permute-done | bytes 49184 | tf_op jit(solution)/shard_map/ppermute | solution.py:359
  94.4 0.7 maximum_bitcast_fusion
  (26 shorter events, 0.2 us)
Async XLA Ops:
  0.6 25.8 %collective-permute-start.1 = (bf16[512,128]{1,0:T(8,128)(2,1)}, bf16[512,128]{1,0:T(8,128)(2,1)S(1)}, u32[]{:S(2)}, u32[]{:S(2)}) collective-permute-start(bf16[512,128]{1,0:T(8,128)(2,1)} %grad_ref.1), channel_id=1, source_target_pairs={{32,0},{40,8},{48,16},{56,24},{64,32},{72,40},{80,48},{88,56},{96,... | collective-permute-start | bytes 393224 | tf_op jit(solution)/shard_map/ppermute | solution.py:350
  6.0 20.4 %collective-permute-start.2 = (bf16[512,128]{1,0:T(8,128)(2,1)}, bf16[512,128]{1,0:T(8,128)(2,1)S(1)}, u32[]{:S(2)}, u32[]{:S(2)}) collective-permute-start(bf16[512,128]{1,0:T(8,128)(2,1)} %grad_ref.1), channel_id=1, source_target_pairs={{48,0},{56,8},{64,16},{72,24},{80,32},{88,40},{96,48},{104,56},{11... | collective-permute-start | bytes 393224 | tf_op jit(solution)/shard_map/ppermute | solution.py:350
  9.7 16.7 %collective-permute-start.3 = (bf16[512,128]{1,0:T(8,128)(2,1)}, bf16[512,128]{1,0:T(8,128)(2,1)S(1)}, u32[]{:S(2)}, u32[]{:S(2)}) collective-permute-start(bf16[512,128]{1,0:T(8,128)(2,1)} %grad_ref.1), channel_id=1, source_target_pairs={{64,0},{72,8},{80,16},{88,24},{96,32},{104,40},{112,48},{120,56},{... | collective-permute-start | bytes 393224 | tf_op jit(solution)/shard_map/ppermute | solution.py:350
  12.1 14.3 %collective-permute-start = (bf16[512,128]{1,0:T(8,128)(2,1)}, bf16[512,128]{1,0:T(8,128)(2,1)}, u32[]{:S(2)}, u32[]{:S(2)}) collective-permute-start(bf16[512,128]{1,0:T(8,128)(2,1)} %grad_ref.1), channel_id=1, source_target_pairs={{16,0},{24,8},{32,16},{40,24},{48,32},{56,40},{64,48},{72,56},{80,... | collective-permute-start | bytes 393224 | tf_op jit(solution)/shard_map/ppermute | solution.py:350
  15.9 13.7 %collective-permute-start.4 = (bf16[512,128]{1,0:T(8,128)(2,1)}, bf16[512,128]{1,0:T(8,128)(2,1)}, u32[]{:S(2)}, u32[]{:S(2)}) collective-permute-start(bf16[512,128]{1,0:T(8,128)(2,1)} %in_ref.1), channel_id=1, source_target_pairs={{0,1},{1,0},{2,3},{3,2},{4,5},{5,4},{6,7},{7,6},{8,9},{9,8},{10,11... | collective-permute-start | bytes 393224 | tf_op jit(solution)/shard_map/ppermute | solution.py:367
  21.4 0.9 copy-start.1
  22.3 0.9 copy-start.7
  23.2 0.9 copy-start.8
  25.0 0.7 copy-start.3
  25.7 0.7 copy-start.5
  29.6 0.9 copy-start.4
  30.5 0.9 copy-start.6
  32.5 5.8 %collective-permute-start.5 = (bf16[4,512,128]{2,1,0:T(8,128)(2,1)S(1)}, bf16[4,512,128]{2,1,0:T(8,128)(2,1)S(1)}, u32[]{:S(2)}, u32[]{:S(2)}) collective-permute-start(bf16[4,512,128]{2,1,0:T(8,128)(2,1)S(1)} %get-tuple-element.40), channel_id=1, source_target_pairs={{0,8},{8,0},{16,24},{24,16},{32,40},{40,32},{48,56},{56,48},{64,72... | collective-permute-start | bytes 1572872 | tf_op jit(solution)/shard_map/ppermute | solution.py:353
  32.6 16.7 %collective-permute-start.6 = (bf16[2,512,128]{2,1,0:T(8,128)(2,1)S(1)}, bf16[2,512,128]{2,1,0:T(8,128)(2,1)S(1)}, u32[]{:S(2)}, u32[]{:S(2)}) collective-permute-start(bf16[2,512,128]{2,1,0:T(8,128)(2,1)S(1)} %get-tuple-element.44.x0_ref), channel_id=1, source_target_pairs={{0,2},{1,3},{2,4},{3,5},{4,6},{5,7},{6,0},{7,1},{8,10},{9,11},{10,... | collective-permute-start | bytes 786440 | tf_op jit(solution)/shard_map/ppermute | solution.py:368
  34.2 15.2 %collective-permute-start.7 = (bf16[2,512,128]{2,1,0:T(8,128)(2,1)S(1)}, bf16[2,512,128]{2,1,0:T(8,128)(2,1)S(1)}, u32[]{:S(2)}, u32[]{:S(2)}) collective-permute-start(bf16[2,512,128]{2,1,0:T(8,128)(2,1)S(1)} %get-tuple-element.44.x0_ref), channel_id=1, source_target_pairs={{0,4},{1,5},{2,6},{3,7},{4,0},{5,1},{6,2},{7,3},{8,12},{9,13},{10,... | collective-permute-start | bytes 786440 | tf_op jit(solution)/shard_map/ppermute | solution.py:368
  36.9 12.4 %collective-permute-start.8 = (bf16[2,512,128]{2,1,0:T(8,128)(2,1)S(1)}, bf16[2,512,128]{2,1,0:T(8,128)(2,1)S(1)}, u32[]{:S(2)}, u32[]{:S(2)}) collective-permute-start(bf16[2,512,128]{2,1,0:T(8,128)(2,1)S(1)} %get-tuple-element.44.x0_ref), channel_id=1, source_target_pairs={{0,6},{1,7},{2,0},{3,1},{4,2},{5,3},{6,4},{7,5},{8,14},{9,15},{10,... | collective-permute-start | bytes 786440 | tf_op jit(solution)/shard_map/ppermute | solution.py:368
  38.4 4.4 %copy-start.2 = (bf16[12,4096]{1,0:T(8,128)(2,1)S(1)}, bf16[12,4096]{1,0:T(8,128)(2,1)}, u32[]{:S(2)}) copy-start(bf16[12,4096]{1,0:T(8,128)(2,1)} %filters_ref.5) | copy-start | bytes 294916
  44.9 2.1 %copy-start = (bf16[1024,12,128]{2,0,1:T(8,128)(2,1)S(1)}, bf16[1024,12,128]{2,0,1:T(8,128)(2,1)}, u32[]{:S(2)}) copy-start(bf16[1024,12,128]{2,0,1:T(8,128)(2,1)} %param.7) | copy-start | bytes 9437188
  51.3 2.6 %collective-permute-start.9 = (bf16[4,4,6,32,128]{4,3,2,1,0:T(8,128)(2,1)S(1)}, bf16[4,4,6,32,128]{4,3,2,1,0:T(8,128)(2,1)S(1)}, u32[]{:S(2)}, u32[]{:S(2)}) collective-permute-start(bf16[4,4,6,32,128]{4,3,2,1,0:T(8,128)(2,1)S(1)} %get-tuple-element.45._), channel_id=1, source_target_pairs={{0,8},{8,0},{16,24},{24,16},{32,40},{40,32},{48,56},{56,48},{64,72... | collective-permute-start | bytes 2359304 | tf_op jit(solution)/shard_map/ppermute | solution.py:353
  53.4 2.5 %collective-permute-start.10 = (bf16[4,4,6,32,128]{4,3,2,1,0:T(8,128)(2,1)S(1)}, bf16[4,4,6,32,128]{4,3,2,1,0:T(8,128)(2,1)S(1)}, u32[]{:S(2)}, u32[]{:S(2)}) collective-permute-start(bf16[4,4,6,32,128]{4,3,2,1,0:T(8,128)(2,1)S(1)} %get-tuple-element.46._), channel_id=1, source_target_pairs={{0,8},{8,0},{16,24},{24,16},{32,40},{40,32},{48,56},{56,48},{64,72... | collective-permute-start | bytes 2359304 | tf_op jit(solution)/shard_map/ppermute | solution.py:353
  54.1 12.8 %collective-permute-start.14 = (bf16[2,4,6,32,128]{4,3,2,1,0:T(8,128)(2,1)S(1)}, bf16[2,4,6,32,128]{4,3,2,1,0:T(8,128)(2,1)S(1)}, u32[]{:S(2)}, u32[]{:S(2)}) collective-permute-start(bf16[2,4,6,32,128]{4,3,2,1,0:T(8,128)(2,1)S(1)} %get-tuple-element.48._), channel_id=1, source_target_pairs={{0,64},{8,72},{16,80},{24,88},{32,96},{40,104},{48,112},{56,120},{... | collective-permute-start | bytes 1179656 | tf_op jit(solution)/shard_map/ppermute | solution.py:356
  56.0 15.8 %collective-permute-start.15 = (bf16[2,4,6,32,128]{4,3,2,1,0:T(8,128)(2,1)S(1)}, bf16[2,4,6,32,128]{4,3,2,1,0:T(8,128)(2,1)S(1)}, u32[]{:S(2)}, u32[]{:S(2)}) collective-permute-start(bf16[2,4,6,32,128]{4,3,2,1,0:T(8,128)(2,1)S(1)} %get-tuple-element.50._), channel_id=1, source_target_pairs={{0,192},{8,200},{16,208},{24,216},{32,224},{40,232},{48,240},{56,2... | collective-permute-start | bytes 1179656 | tf_op jit(solution)/shard_map/ppermute | solution.py:356
  56.1 8.7 %collective-permute-start.11 = (bf16[2,512,128]{2,1,0:T(8,128)(2,1)S(1)}, bf16[2,512,128]{2,1,0:T(8,128)(2,1)S(1)}, u32[]{:S(2)}, u32[]{:S(2)}) collective-permute-start(bf16[2,512,128]{2,1,0:T(8,128)(2,1)S(1)} %get-tuple-element.52), channel_id=1, source_target_pairs={{0,2},{1,3},{2,0},{3,1},{4,6},{5,7},{6,4},{7,5},{8,10},{9,11},{10,... | collective-permute-start | bytes 786440 | tf_op jit(solution)/shard_map/ppermute | solution.py:362
  57.4 9.5 %collective-permute-start.12 = (bf16[2,512,128]{2,1,0:T(8,128)(2,1)S(1)}, bf16[2,512,128]{2,1,0:T(8,128)(2,1)S(1)}, u32[]{:S(2)}, u32[]{:S(2)}) collective-permute-start(bf16[2,512,128]{2,1,0:T(8,128)(2,1)S(1)} %get-tuple-element.43._), channel_id=1, source_target_pairs={{0,6},{1,7},{2,4},{3,5},{4,2},{5,3},{6,0},{7,1},{8,14},{9,15},{10,... | collective-permute-start | bytes 786440 | tf_op jit(solution)/shard_map/ppermute | solution.py:362
  67.0 11.4 %collective-permute-start.18 = (bf16[1,4,6,32,128]{4,3,2,1,0:T(8,128)(2,1)S(1)}, bf16[1,4,6,32,128]{4,3,2,1,0:T(8,128)(2,1)S(1)}, u32[]{:S(2)}, u32[]{:S(2)}) collective-permute-start(bf16[1,4,6,32,128]{4,3,2,1,0:T(8,128)(2,1)S(1)} %get-tuple-element.58._), channel_id=1, source_target_pairs={{0,192},{8,200},{16,208},{24,216},{32,224},{40,232},{48,240},{56,2... | collective-permute-start | bytes 589832 | tf_op jit(solution)/shard_map/ppermute | solution.py:356
  70.0 6.2 %collective-permute-start.16 = (bf16[1,512,128]{2,1,0:T(8,128)(2,1)S(1)}, bf16[1,512,128]{2,1,0:T(8,128)(2,1)S(1)}, u32[]{:S(2)}, u32[]{:S(2)}) collective-permute-start(bf16[1,512,128]{2,1,0:T(8,128)(2,1)S(1)} %get-tuple-element.53._), channel_id=1, source_target_pairs={{0,6},{1,7},{2,4},{3,5},{4,2},{5,3},{6,0},{7,1},{8,14},{9,15},{10,... | collective-permute-start | bytes 393224 | tf_op jit(solution)/shard_map/ppermute | solution.py:362
  71.9 6.8 %collective-permute-start.19 = (bf16[1,4,6,32,128]{4,3,2,1,0:T(8,128)(2,1)S(1)}, bf16[1,4,6,32,128]{4,3,2,1,0:T(8,128)(2,1)S(1)}, u32[]{:S(2)}, u32[]{:S(2)}) collective-permute-start(bf16[1,4,6,32,128]{4,3,2,1,0:T(8,128)(2,1)S(1)} %get-tuple-element.60._), channel_id=1, source_target_pairs={{0,64},{8,72},{16,80},{24,88},{32,96},{40,104},{48,112},{56,120},{... | collective-permute-start | bytes 589832 | tf_op jit(solution)/shard_map/ppermute | solution.py:356
  72.0 14.3 %collective-permute-start.13 = (bf16[1,512,128]{2,1,0:T(8,128)(2,1)S(1)}, bf16[1,512,128]{2,1,0:T(8,128)(2,1)S(1)}, u32[]{:S(2)}, u32[]{:S(2)}) collective-permute-start(bf16[1,512,128]{2,1,0:T(8,128)(2,1)S(1)} %get-tuple-element.56._), channel_id=1, source_target_pairs={{0,2},{1,3},{2,0},{3,1},{4,6},{5,7},{6,4},{7,5},{8,10},{9,11},{10,... | collective-permute-start | bytes 393224 | tf_op jit(solution)/shard_map/ppermute | solution.py:362
  76.2 11.8 %collective-permute-start.17 = (bf16[1,512,128]{2,1,0:T(8,128)(2,1)S(1)}, bf16[1,512,128]{2,1,0:T(8,128)(2,1)S(1)}, u32[]{:S(2)}, u32[]{:S(2)}) collective-permute-start(bf16[1,512,128]{2,1,0:T(8,128)(2,1)S(1)} %add.37._), channel_id=1, source_target_pairs={{0,1},{1,0},{2,3},{3,2},{4,5},{5,4},{6,7},{7,6},{8,9},{9,8},{10,11... | collective-permute-start | bytes 393224 | tf_op jit(solution)/shard_map/ppermute | solution.py:396
  78.5 7.7 %collective-permute-start.20 = (bf16[2,6,32,128]{3,2,1,0:T(8,128)(2,1)S(1)}, bf16[2,6,32,128]{3,2,1,0:T(8,128)(2,1)S(1)}, u32[]{:S(2)}, u32[]{:S(2)}) collective-permute-start(bf16[2,6,32,128]{3,2,1,0:T(8,128)(2,1)S(1)} %get-tuple-element.63._), channel_id=1, source_target_pairs={{0,16},{8,24},{16,0},{24,8},{32,48},{40,56},{48,32},{56,40},{64,80... | collective-permute-start | bytes 294920 | tf_op jit(solution)/shard_map/ppermute | solution.py:359
  78.7 10.0 %collective-permute-start.22 = (bf16[2,6,32,128]{3,2,1,0:T(8,128)(2,1)S(1)}, bf16[2,6,32,128]{3,2,1,0:T(8,128)(2,1)S(1)}, u32[]{:S(2)}, u32[]{:S(2)}) collective-permute-start(bf16[2,6,32,128]{3,2,1,0:T(8,128)(2,1)S(1)} %get-tuple-element.65._), channel_id=1, source_target_pairs={{0,16},{8,24},{16,0},{24,8},{32,48},{40,56},{48,32},{56,40},{64,80... | collective-permute-start | bytes 294920 | tf_op jit(solution)/shard_map/ppermute | solution.py:359
  86.2 5.1 %collective-permute-start.21 = (bf16[1,6,32,128]{3,2,1,0:T(8,128)(2,1)S(1)}, bf16[1,6,32,128]{3,2,1,0:T(8,128)(2,1)S(1)}, u32[]{:S(2)}, u32[]{:S(2)}) collective-permute-start(bf16[1,6,32,128]{3,2,1,0:T(8,128)(2,1)S(1)} %get-tuple-element.68._), channel_id=1, source_target_pairs={{0,32},{8,40},{16,48},{24,56},{32,0},{40,8},{48,16},{56,24},{64,96... | collective-permute-start | bytes 147464 | tf_op jit(solution)/shard_map/ppermute | solution.py:359
  88.7 5.6 %collective-permute-start.23 = (bf16[1,6,32,128]{3,2,1,0:T(8,128)(2,1)S(1)}, bf16[1,6,32,128]{3,2,1,0:T(8,128)(2,1)S(1)}, u32[]{:S(2)}, u32[]{:S(2)}) collective-permute-start(bf16[1,6,32,128]{3,2,1,0:T(8,128)(2,1)S(1)} %get-tuple-element.71), channel_id=1, source_target_pairs={{0,32},{8,40},{16,48},{24,56},{32,0},{40,8},{48,16},{56,24},{64,96... | collective-permute-start | bytes 147464 | tf_op jit(solution)/shard_map/ppermute | solution.py:359

commit v7 on v5

--- a/solution.py
+++ b/solution.py
@@ -65,7 +65,7 @@
     return pltpu.roll(block, 0, 1, stride=1, stride_axis=0).astype(BF16)
 
 
-def table_kernel(filters_ref, near_ref):
+def table_kernel(_, filters_ref, near_ref):
     filt_count, rows, near = near_ref.shape
     edge = jnp.zeros((1, LANE), F32)
     for k in range(filt_count):
@@ -73,40 +73,46 @@
         near_ref[k] = shifted_rows(jnp.concatenate([line, edge], axis=1), rows)[:, :near]
 
 
-def near_table(filters):
+def near_table(after, filters):
     filt_count, taps = filters.shape
     vmem = pl.BlockSpec(memory_space=pltpu.VMEM)
     return pl.pallas_call(
         table_kernel,
         out_shape=jax.ShapeDtypeStruct((filt_count, ROWS, taps // 2), BF16),
-        in_specs=[vmem],
+        in_specs=[pl.BlockSpec(memory_space=pl.ANY), vmem],
         out_specs=vmem,
         compiler_params=pltpu.CompilerParams(vmem_limit_bytes=VMEM_LIMIT),
-        cost_estimate=LARGE_COST,
+        cost_estimate=SMALL_COST,
         name="near_table",
-    )(filters)
-
-
-def prep_kernel(pos_ref, _, __, *refs):
-    parts, stack_ref = refs[:-1], refs[-1]
+    )(after, filters)
+
+
+def prep_kernel(pos_ref, _, own_ref, r1_ref, r2_ref, r3_ref, r4_ref, stack_ref, held_ref, arrived):
+    copy = pltpu.make_async_copy(own_ref, held_ref, arrived)
+    copy.start()
+    parts = r1_ref, r2_ref, r3_ref, r4_ref
     core = lax.rem(pos_ref[1], NCORE)
-    for s in range(stack_ref.shape[0]):
-        stack_ref[s] = jnp.where(core == 0, parts[s + 1][...], parts[s][...])
+    for s in range(1, stack_ref.shape[0]):
+        stack_ref[s] = jnp.where(core == 0, parts[s][...], parts[s - 1][...])
+    copy.wait()
+    stack_ref[0] = jnp.where(core == 0, r1_ref[...], held_ref[...])
 
 
 def for_sibling(pos, after, *parts):
+    block = parts[0].shape
     vmem = pl.BlockSpec(memory_space=pltpu.VMEM)
     return pl.pallas_call(
         prep_kernel,
-        out_shape=jax.ShapeDtypeStruct((len(parts) - 1,) + parts[0].shape, BF16),
+        out_shape=jax.ShapeDtypeStruct((4,) + block, BF16),
         in_specs=[pl.BlockSpec(memory_space=pltpu.SMEM)]
         + [pl.BlockSpec(memory_space=pl.ANY)] * 2
-        + [vmem] * len(parts),
+        + [vmem] * 4,
         out_specs=vmem,
+        scratch_shapes=[pltpu.VMEM(block, BF16), pltpu.SemaphoreType.DMA],
         compiler_params=pltpu.CompilerParams(vmem_limit_bytes=VMEM_LIMIT),
         cost_estimate=SMALL_COST,
         name="for_sibling",
-    )(pos, *after, *parts)
+    )(pos, after, *parts)
 
 
 def pair_of_blocks(grad_ref, start, rows, width):
@@ -144,7 +150,7 @@
             acc_ref[pair] = result[group * part : (group + 1) * part]
 
 
-def near_conv(table, halo, sibling, groups):
+def near_conv(after, table, halo, sibling, groups):
     filt_count, rows, width = table.shape
     tok = halo[0].shape[0]
     vmem = pl.BlockSpec(memory_space=pltpu.VMEM)
@@ -152,13 +158,13 @@
     return pl.pallas_call(
         near_kernel,
         out_shape=[acc] * groups,
-        in_specs=[vmem] * 5,
+        in_specs=[pl.BlockSpec(memory_space=pl.ANY)] * len(after) + [vmem] * 5,
         out_specs=[vmem] * groups,
         scratch_shapes=[pltpu.VMEM((5 * tok, LANE), BF16)],
         compiler_params=pltpu.CompilerParams(vmem_limit_bytes=VMEM_LIMIT),
         cost_estimate=LARGE_COST,
         name="near_conv",
-    )(table, *halo, sibling)
+    )(*after, table, *halo, sibling)
 
 
 def far_kernel(
@@ -357,39 +363,39 @@
     count = filters.shape[0] // GROUPS
     pair = jnp.stack([inputs, lax.ppermute(inputs, "tp", Z_HI_SWAP)])
     gathered = [pair] + [lax.ppermute(pair, "tp", along_x(s)) for s in range(1, NX)]
-    table = near_table(filters)
+    table = near_table(pair, filters)
     halo = [grad_out] + [later(grad_out, steps) for steps in range(1, 5)]
-    beside = sibling(for_sibling(pos, (table, pair), *halo))
-    accs = near_conv(table, halo[:3], beside, GROUPS)
+    beside = sibling(for_sibling(pos, table, *halo))
+    accs = near_conv(gathered[1:1], table, halo[:3], beside, GROUPS)
 
     def conv(group, after):
         return far_conv(group * count, count, after, filters, accs[group], halo[2:], beside)
 
     corr_0 = conv(0, table)
     corr_1 = conv(1, corr_0)
-    keep_0, send_0 = product(False, pos, corr_1, corr_0, gathered)
     near, near_send, far, far_send = input_shares(
-        pos, send_0, [corr_0, corr_1], projection.transpose(1, 0, 2)
+        pos, corr_1, [corr_0, corr_1], projection.transpose(1, 0, 2)
     )
-    stay_0, leave_0 = halve(near_send, keep_0, sibling(send_0))
+    x_far, x_near = x_swapped(far_send, False), x_swapped(near_send, True)
+    keep_0, send_0 = product(False, pos, near_send, corr_0, gathered)
+    keep_1, send_1 = product(True, pos, send_0, corr_1, gathered)
+    stay_0, leave_0 = halve(send_1, keep_0, sibling(send_0))
     y_0 = y_swapped(leave_0, False)
-    keep_1, send_1 = product(True, pos, leave_0, corr_1, gathered)
-    stay_1, leave_1 = halve(send_1, keep_1, sibling(send_1))
+    stay_1, leave_1 = halve(leave_0, keep_1, sibling(send_1))
     y_1 = y_swapped(leave_1, True)
-    far, leave = halve(leave_1, far, x_swapped(far_send, False))
+    far, leave = halve(leave_1, far, x_far)
     x_far = x_swapped(leave, True)
+    near, leave = halve(leave, near, x_near)
+    x_near = x_swapped(leave, False)
     stay_0, leave_0 = halve(leave, stay_0, y_0)
     y_0 = y_swapped(leave_0, True)
-    near, leave = halve(leave_0, near, x_swapped(near_send, True))
-    x_near = x_swapped(leave, False)
-    stay_1, leave_1 = halve(leave, stay_1, y_1)
+    stay_1, leave_1 = halve(leave_0, stay_1, y_1)
     y_1 = y_swapped(leave_1, False)
-    far = add(leave_1, far, x_far)
+    stay_0, leave_0 = halve(leave_1, stay_0[0], y_0[0])
+    z_0 = z_swapped(leave_0, 1)
+    far = add(leave_0, far, x_far)
     opposite = lax.ppermute(far, "tp", Z_HI_SWAP)
-
-    stay_0, leave_0 = halve(far, stay_0[0], y_0[0])
-    z_0 = z_swapped(leave_0, 1)
-    stay_1, leave_1 = halve(leave_0, stay_1[0], y_1[0])
+    stay_1, leave_1 = halve(far, stay_1[0], y_1[0])
     z_1 = z_swapped(leave_1, 1)
     stay_0, leave_0 = halve(leave_1, stay_0, z_0)
     z_0 = z_swapped(leave_0, 2)

time: 95.3 us -> 89.6 us (0.940); the launches traced: 95.1 us -> 88.3 us
  waiting for transfers between devices: 29.8 us -> 24.2 us
  Pallas kernels: 17.4 us -> 16.3 us
    ppermute x1, waiting for transfers between devices: 6.33 us -> 0.01 us  [per_device(): pair = jnp.stack([inputs, lax.ppermute(inputs, 'tp', Z_HI_SWAP)])]
    ppermute x4, waiting for transfers between devices: 0.22 us -> 2.21 us  [y_swapped(): return lax.ppermute(value, 'ctx', y_swap(crossed))]
    ppermute x4, waiting for transfers between devices: 0.01 us -> 1.92 us  [later(): return lax.ppermute(value, 'ctx', from_later_chip(steps))]
    ppermute x4, starting transfers between devices: 15.3 us -> 13.4 us  [later(): return lax.ppermute(value, 'ctx', from_later_chip(steps))]
    ppermute x1, starting transfers between devices: 5.48 us -> 7.28 us  [per_device(): pair = jnp.stack([inputs, lax.ppermute(inputs, 'tp', Z_HI_SWAP)])]
    ppermute x3, waiting for transfers between devices: 2.23 us -> 0.78 us  [per_device(): lax.ppermute(pair, 'tp', along_x(s))]
    ppermute x1, waiting for transfers between devices: 1.37 us -> 0.01 us  [per_device(): opposite = lax.ppermute(far, 'tp', Z_HI_SWAP)]
    ppermute x4, starting transfers between devices: 2.93 us -> 4.08 us  [y_swapped(): return lax.ppermute(value, 'ctx', y_swap(crossed))]
  transfers between devices with their start and end apart: 24 -> 24, of which waited for: 10 -> 11; matrix products, arithmetic and copies ran while one was open for 2% -> 2% of each run, Pallas kernels for 13% -> 15%
where the time goes in v7:
time: 89.6 us; the launch traced here: 88.3 us
  starting transfers between devices  43.5 us (49%)
  waiting for transfers between devices  24.2 us (27%)
  Pallas kernels  16.3 us (18%)
  other arithmetic  2.42 us (3%)
  local copies, waits for them, and re-layouts  0.91 us (1%)
    ppermute x4, starting transfers between devices, later(): return lax.ppermute(value, 'ctx', from_later_chip(steps))  13.4 us
    ppermute x4, waiting for transfers between devices, x_swapped(): return lax.ppermute(value, 'tp', x_swap(crossed))  9.56 us
    ppermute x4, waiting for transfers between devices, z_swapped(): return lax.ppermute(value, 'ctx', z_swap(bit))  8.83 us
    ppermute x1, starting transfers between devices, per_device(): pair = jnp.stack([inputs, lax.ppermute(inputs, 'tp', Z_HI_SWAP)])  7.28 us
    ppermute x3, starting transfers between devices, per_device(): lax.ppermute(pair, 'tp', along_x(s))  5.73 us
    ppermute x4, starting transfers between devices, x_swapped(): return lax.ppermute(value, 'tp', x_swap(crossed))  5.2 us
    ppermute x4, starting transfers between devices, z_swapped(): return lax.ppermute(value, 'ctx', z_swap(bit))  4.28 us
    pallas_call x2, Pallas kernels, far_conv(): pl.pallas_call(functools.partial(far_kernel, first), out_shape=jax.ShapeD...  4.16 us
  transfers between devices with their start and end apart: 24, of which 11 were waited for; matrix products, arithmetic and copies ran while one was open for 2% of the time, Pallas kernels for 15%

profile of v7, /device:TPU:24, one launch (start us, length us, event | category | flops | bytes accessed | tf_op | source)
XLA Modules:
  0.0 88.3 jit_solution(11775617639608934337)
XLA Ops:
  0.6 7.3 %collective-permute-start = (bf16[512,128]{1,0:T(8,128)(2,1)}, bf16[512,128]{1,0:T(8,128)(2,1)S(1)}, u32[]{:S(2)}, u32[]{:S(2)}) collective-permute-start(bf16[512,128]{1,0:T(8,128)(2,1)} %param.4), channel_id=1, source_target_pairs={{0,1},{1,0},{2,3},{3,2},{4,5},{5,4},{6,7},{7,6},{8,9},{9,8},{10,11... | collective-permute-start | bytes 393224 | tf_op jit(solution)/shard_map/ppermute | solution.py:364
  7.9 3.5 %collective-permute-start.2 = (bf16[512,128]{1,0:T(8,128)(2,1)}, bf16[512,128]{1,0:T(8,128)(2,1)S(1)}, u32[]{:S(2)}, u32[]{:S(2)}) collective-permute-start(bf16[512,128]{1,0:T(8,128)(2,1)} %own_ref.3), channel_id=1, source_target_pairs={{32,0},{40,8},{48,16},{56,24},{64,32},{72,40},{80,48},{88,56},{96,... | collective-permute-start | bytes 393224 | tf_op jit(solution)/shard_map/ppermute | solution.py:349
  11.5 2.8 %collective-permute-start.3 = (bf16[512,128]{1,0:T(8,128)(2,1)}, bf16[512,128]{1,0:T(8,128)(2,1)S(1)}, u32[]{:S(2)}, u32[]{:S(2)}) collective-permute-start(bf16[512,128]{1,0:T(8,128)(2,1)} %own_ref.3), channel_id=1, source_target_pairs={{48,0},{56,8},{64,16},{72,24},{80,32},{88,40},{96,48},{104,56},{11... | collective-permute-start | bytes 393224 | tf_op jit(solution)/shard_map/ppermute | solution.py:349
  14.3 2.4 %collective-permute-start.4 = (bf16[512,128]{1,0:T(8,128)(2,1)}, bf16[512,128]{1,0:T(8,128)(2,1)S(1)}, u32[]{:S(2)}, u32[]{:S(2)}) collective-permute-start(bf16[512,128]{1,0:T(8,128)(2,1)} %own_ref.3), channel_id=1, source_target_pairs={{64,0},{72,8},{80,16},{88,24},{96,32},{104,40},{112,48},{120,56},{... | collective-permute-start | bytes 393224 | tf_op jit(solution)/shard_map/ppermute | solution.py:349
  16.7 4.7 %collective-permute-start.1 = (bf16[512,128]{1,0:T(8,128)(2,1)}, bf16[512,128]{1,0:T(8,128)(2,1)S(1)}, u32[]{:S(2)}, u32[]{:S(2)}) collective-permute-start(bf16[512,128]{1,0:T(8,128)(2,1)} %own_ref.3), channel_id=1, source_target_pairs={{16,0},{24,8},{32,16},{40,24},{48,32},{56,40},{64,48},{72,56},{80,... | collective-permute-start | bytes 393224 | tf_op jit(solution)/shard_map/ppermute | solution.py:349
  21.4 0.1 pad_add_fusion.pos_ref
  21.5 0.0 collective-permute-done
  21.5 0.9 %pad_maximum_fusion._.x0_ref = bf16[2,512,128]{2,1,0:T(8,128)(2,1)S(1)} fusion(bf16[1,512,128]{2,1,0:T(8,128)(2,1)S(1)} %bitcast.23, bf16[1,512,128]{2,1,0:T(8,128)(2,1)} %bitcast.22), kind=kLoop, calls=%fused_computation | loop fusion | flops 131072 | bytes 524288 | tf_op jit(solution)/shard_map/stack | solution.py:364
  22.4 0.0 copy-start.1
  22.4 0.9 %copy-done.1 = bf16[12,4096]{1,0:T(8,128)(2,1)S(1)} copy-done((bf16[12,4096]{1,0:T(8,128)(2,1)S(1)}, bf16[12,4096]{1,0:T(8,128)(2,1)}, u32[]{:S(2)}) %copy-start.1) | copy-done | bytes 98328
  23.3 0.9 %near_table.1._.table_ref = bf16[12,64,2048]{2,1,0:T(8,128)(2,1)S(1)} custom-call(bf16[2,512,128]{2,1,0:T(8,128)(2,1)S(1)} %pad_maximum_fusion._.x0_ref, bf16[12,4096]{1,0:T(8,128)(2,1)S(1)} %copy-done.1), custom_call_target="tpu_custom_call" | custom-call | flops 1000 | bytes 1000 | tf_op jit(solution)/shard_map/near_table/pallas_call | solution.py:79
  24.2 0.0 collective-permute-done.2.r2_ref
  24.2 0.0 collective-permute-done.3.r3_ref
  24.2 0.0 collective-permute-done.4.r4_ref
  24.3 1.9 %collective-permute-done.1.r1_ref = bf16[512,128]{1,0:T(8,128)(2,1)S(1)} collective-permute-done((bf16[512,128]{1,0:T(8,128)(2,1)}, bf16[512,128]{1,0:T(8,128)(2,1)S(1)}, u32[]{:S(2)}, u32[]{:S(2)}) %collective-permute-start.1) | collective-permute-done | bytes 131104 | tf_op jit(solution)/shard_map/ppermute | solution.py:349
  26.2 0.8 for_sibling.1
  27.0 0.1 collective-permute-start.5
  27.1 1.6 %collective-permute-start.6 = (bf16[2,512,128]{2,1,0:T(8,128)(2,1)S(1)}, bf16[2,512,128]{2,1,0:T(8,128)(2,1)S(1)}, u32[]{:S(2)}, u32[]{:S(2)}) collective-permute-start(bf16[2,512,128]{2,1,0:T(8,128)(2,1)S(1)} %pad_maximum_fusion._.x0_ref), channel_id=1, source_target_pairs={{0,2},{1,3},{2,4},{3,5},{4,6},{5,7},{6,0},{7,1},{8,10},{9,11},{10,... | collective-permute-start | bytes 786440 | tf_op jit(solution)/shard_map/ppermute | solution.py:365
  28.7 2.7 %collective-permute-start.7 = (bf16[2,512,128]{2,1,0:T(8,128)(2,1)S(1)}, bf16[2,512,128]{2,1,0:T(8,128)(2,1)S(1)}, u32[]{:S(2)}, u32[]{:S(2)}) collective-permute-start(bf16[2,512,128]{2,1,0:T(8,128)(2,1)S(1)} %pad_maximum_fusion._.x0_ref), channel_id=1, source_target_pairs={{0,4},{1,5},{2,6},{3,7},{4,0},{5,1},{6,2},{7,3},{8,12},{9,13},{10,... | collective-permute-start | bytes 786440 | tf_op jit(solution)/shard_map/ppermute | solution.py:365
  31.4 1.4 %collective-permute-start.8 = (bf16[2,512,128]{2,1,0:T(8,128)(2,1)S(1)}, bf16[2,512,128]{2,1,0:T(8,128)(2,1)S(1)}, u32[]{:S(2)}, u32[]{:S(2)}) collective-permute-start(bf16[2,512,128]{2,1,0:T(8,128)(2,1)S(1)} %pad_maximum_fusion._.x0_ref), channel_id=1, source_target_pairs={{0,6},{1,7},{2,0},{3,1},{4,2},{5,3},{6,4},{7,5},{8,14},{9,15},{10,... | collective-permute-start | bytes 786440 | tf_op jit(solution)/shard_map/ppermute | solution.py:365
  32.9 0.0 collective-permute-done.5.sib_ref
  32.9 3.4 %near_conv.1 = (f32[4,384,256]{2,1,0:T(8,128)S(1)}, f32[4,384,256]{2,1,0:T(8,128)S(1)}) custom-call(bf16[12,64,2048]{2,1,0:T(8,128)(2,1)S(1)} %near_table.1._.table_ref, bf16[512,128]{1,0:T(8,128)(2,1)S(1)} %copy-done.2, bf16[512,128]{1,0:T(8,128)(2,1)S(1)} %collective-permute-done.1.r1_ref, bf16[512,128]{1,0:T(8,128)(2,1)S(1)} %collective-permute-done.2.r2_ref, ...), custom_call_target="tpu_custom_call" | custom-call | flops 4000000000 | bytes 8000000 | tf_op jit(solution)/shard_map/near_conv/pallas_call | solution.py:158
  36.3 2.1 %far_conv.2._.refs_0_.corr_ref = bf16[512,768]{1,0:T(8,128)(2,1)S(1)} custom-call(bf16[12,64,2048]{2,1,0:T(8,128)(2,1)S(1)} %near_table.1._.table_ref, bf16[12,4096]{1,0:T(8,128)(2,1)S(1)} %copy-done.1, f32[4,384,256]{2,1,0:T(8,128)S(1)} %get-tuple-element.32.acc_ref, bf16[512,128]{1,0:T(8,128)(2,1)S(1)} %collective-permute-done.2.r2_ref, ...), custom_call_target="tpu_custom_call" | custom-call | flops 1000 | bytes 1000 | tf_op jit(solution)/shard_map/far_conv/pallas_call | solution.py:202
  38.4 0.0 copy-start
  38.4 2.1 %far_conv.3._.refs_1_.corr_ref = bf16[512,768]{1,0:T(8,128)(2,1)S(1)} custom-call(bf16[512,768]{1,0:T(8,128)(2,1)S(1)} %far_conv.2._.refs_0_.corr_ref, bf16[12,4096]{1,0:T(8,128)(2,1)S(1)} %copy-done.1, f32[4,384,256]{2,1,0:T(8,128)S(1)} %get-tuple-element.33.acc_ref, bf16[512,128]{1,0:T(8,128)(2,1)S(1)} %collective-permute-done.2.r2_ref, ...), custom_call_target="tpu_custom_call" | custom-call | flops 1000 | bytes 1000 | tf_op jit(solution)/shard_map/far_conv/pallas_call | solution.py:202
  40.5 2.4 %input_shares.1 = (f32[2,512,128]{2,1,0:T(8,128)S(1)}, bf16[2,512,128]{2,1,0:T(8,128)(2,1)S(1)}, f32[2,512,128]{2,1,0:T(8,128)S(1)}, bf16[2,512,128]{2,1,0:T(8,128)(2,1)S(1)}) custom-call(s32[2]{0:T(128)S(1)} %pad_add_fusion.pos_ref, bf16[512,768]{1,0:T(8,128)(2,1)S(1)} %far_conv.3._.refs_1_.corr_ref, bf16[512,768]{1,0:T(8,128)(2,1)S(1)} %far_conv.2._.refs_0_.corr_ref, ...), custom_call_target="tpu_custom_call" | custom-call | flops 1000 | bytes 1000 | tf_op jit(solution)/shard_map/input_shares/pallas_call | solution.py:328
  42.9 0.0 collective-permute-done.6.x1_ref
  42.9 0.8 collective-permute-done.7.x2_ref
  43.7 0.0 collective-permute-done.8.x3_ref
  43.7 1.9 %product.2 = (bf16[4,4,6,32,128]{4,3,2,1,0:T(8,128)(2,1)S(1)}, bf16[4,4,6,32,128]{4,3,2,1,0:T(8,128)(2,1)S(1)}) custom-call(s32[2]{0:T(128)S(1)} %pad_add_fusion.pos_ref, bf16[2,512,128]{2,1,0:T(8,128)(2,1)S(1)} %get-tuple-element.34._, bf16[512,768]{1,0:T(8,128)(2,1)S(1)} %far_conv.2._.refs_0_.corr_ref, bf16[2,512,128]{2,1,0:T(8,128)(2,1)S(1)} %pad_maximum_fusion._.x0_ref, ...), custom_call_target="tpu_custom_call" | custom-call | flops 1000 | bytes 1000 | tf_op jit(solution)/shard_map/product/pallas_call | solution.py:247
  45.6 0.1 collective-permute-start.9
  45.7 1.9 %product.3 = (bf16[4,4,6,32,128]{4,3,2,1,0:T(8,128)(2,1)S(1)}, bf16[4,4,6,32,128]{4,3,2,1,0:T(8,128)(2,1)S(1)}) custom-call(s32[2]{0:T(128)S(1)} %pad_add_fusion.pos_ref, bf16[4,4,6,32,128]{4,3,2,1,0:T(8,128)(2,1)S(1)} %get-tuple-element.35._, bf16[512,768]{1,0:T(8,128)(2,1)S(1)} %far_conv.3._.refs_1_.corr_ref, ...), custom_call_target="tpu_custom_call" | custom-call | flops 1000 | bytes 1000 | tf_op jit(solution)/shard_map/product/pallas_call | solution.py:247
  47.6 0.6 collective-permute-start.10
  48.2 0.0 collective-permute-done.9.other_ref
  48.2 0.2 halve.10
  48.4 0.8 collective-permute-start.14
  49.2 0.9 %collective-permute-done.10.other_ref = bf16[4,4,6,32,128]{4,3,2,1,0:T(8,128)(2,1)S(1)} collective-permute-done((bf16[4,4,6,32,128]{4,3,2,1,0:T(8,128)(2,1)S(1)}, bf16[4,4,6,32,128]{4,3,2,1,0:T(8,128)(2,1)S(1)}, u32[]{:S(2)}, u32[]{:S(2)}) %collective-permute-start.10) | collective-permute-done | bytes 786464 | tf_op jit(solution)/shard_map/ppermute | solution.py:352
  50.1 0.2 halve.11
  50.3 0.2 collective-permute-start.15
  50.5 1.3 %collective-permute-start.11 = (bf16[2,512,128]{2,1,0:T(8,128)(2,1)S(1)}, bf16[2,512,128]{2,1,0:T(8,128)(2,1)S(1)}, u32[]{:S(2)}, u32[]{:S(2)}) collective-permute-start(bf16[2,512,128]{2,1,0:T(8,128)(2,1)S(1)} %get-tuple-element.42), channel_id=1, source_target_pairs={{0,2},{1,3},{2,0},{3,1},{4,6},{5,7},{6,4},{7,5},{8,10},{9,11},{10,... | collective-permute-start | bytes 786440 | tf_op jit(solution)/shard_map/ppermute | solution.py:361
  51.9 1.9 %collective-permute-start.12 = (bf16[2,512,128]{2,1,0:T(8,128)(2,1)S(1)}, bf16[2,512,128]{2,1,0:T(8,128)(2,1)S(1)}, u32[]{:S(2)}, u32[]{:S(2)}) collective-permute-start(bf16[2,512,128]{2,1,0:T(8,128)(2,1)S(1)} %get-tuple-element.34._), channel_id=1, source_target_pairs={{0,6},{1,7},{2,4},{3,5},{4,2},{5,3},{6,0},{7,1},{8,14},{9,15},{10,... | collective-permute-start | bytes 786440 | tf_op jit(solution)/shard_map/ppermute | solution.py:361
  53.8 5.3 %collective-permute-done.11.other_ref = bf16[2,512,128]{2,1,0:T(8,128)(2,1)S(1)} collective-permute-done((bf16[2,512,128]{2,1,0:T(8,128)(2,1)S(1)}, bf16[2,512,128]{2,1,0:T(8,128)(2,1)S(1)}, u32[]{:S(2)}, u32[]{:S(2)}) %collective-permute-start.11) | collective-permute-done | bytes 262176 | tf_op jit(solution)/shard_map/ppermute | solution.py:361
  59.1 0.1 halve.12
  59.1 2.2 %collective-permute-done.12.other_ref = bf16[2,512,128]{2,1,0:T(8,128)(2,1)S(1)} collective-permute-done((bf16[2,512,128]{2,1,0:T(8,128)(2,1)S(1)}, bf16[2,512,128]{2,1,0:T(8,128)(2,1)S(1)}, u32[]{:S(2)}, u32[]{:S(2)}) %collective-permute-start.12) | collective-permute-done | bytes 262176 | tf_op jit(solution)/shard_map/ppermute | solution.py:361
  61.4 0.0 collective-permute-done.14.other_ref
  61.4 0.1 halve.14
  61.5 2.9 %collective-permute-start.16 = (bf16[1,4,6,32,128]{4,3,2,1,0:T(8,128)(2,1)S(1)}, bf16[1,4,6,32,128]{4,3,2,1,0:T(8,128)(2,1)S(1)}, u32[]{:S(2)}, u32[]{:S(2)}) collective-permute-start(bf16[1,4,6,32,128]{4,3,2,1,0:T(8,128)(2,1)S(1)} %get-tuple-element.48._), channel_id=1, source_target_pairs={{0,192},{8,200},{16,208},{24,216},{32,224},{40,232},{48,240},{56,2... | collective-permute-start | bytes 589832 | tf_op jit(solution)/shard_map/ppermute | solution.py:355
  64.4 0.1 halve.15
  64.5 0.1 collective-permute-start.19
  64.6 2.0 %collective-permute-start.17 = (bf16[1,512,128]{2,1,0:T(8,128)(2,1)S(1)}, bf16[1,512,128]{2,1,0:T(8,128)(2,1)S(1)}, u32[]{:S(2)}, u32[]{:S(2)}) collective-permute-start(bf16[1,512,128]{2,1,0:T(8,128)(2,1)S(1)} %get-tuple-element.43._), channel_id=1, source_target_pairs={{0,6},{1,7},{2,4},{3,5},{4,2},{5,3},{6,0},{7,1},{8,14},{9,15},{10,... | collective-permute-start | bytes 393224 | tf_op jit(solution)/shard_map/ppermute | solution.py:361
  66.6 0.0 collective-permute-start.13
  66.6 2.2 %collective-permute-done.16 = bf16[1,4,6,32,128]{4,3,2,1,0:T(8,128)(2,1)S(1)} collective-permute-done((bf16[1,4,6,32,128]{4,3,2,1,0:T(8,128)(2,1)S(1)}, bf16[1,4,6,32,128]{4,3,2,1,0:T(8,128)(2,1)S(1)}, u32[]{:S(2)}, u32[]{:S(2)}) %collective-permute-start.16) | collective-permute-done | bytes 196640 | tf_op jit(solution)/shard_map/ppermute | solution.py:355
  68.8 2.0 %collective-permute-done.17.other_ref = bf16[1,512,128]{2,1,0:T(8,128)(2,1)S(1)} collective-permute-done((bf16[1,512,128]{2,1,0:T(8,128)(2,1)S(1)}, bf16[1,512,128]{2,1,0:T(8,128)(2,1)S(1)}, u32[]{:S(2)}, u32[]{:S(2)}) %collective-permute-start.17) | collective-permute-done | bytes 131104 | tf_op jit(solution)/shard_map/ppermute | solution.py:361
  70.9 2.7 %collective-permute-start.18 = (bf16[1,512,128]{2,1,0:T(8,128)(2,1)S(1)}, bf16[1,512,128]{2,1,0:T(8,128)(2,1)S(1)}, u32[]{:S(2)}, u32[]{:S(2)}) collective-permute-start(bf16[1,512,128]{2,1,0:T(8,128)(2,1)S(1)} %add.37._), channel_id=1, source_target_pairs={{0,1},{1,0},{2,3},{3,2},{4,5},{5,4},{6,7},{7,6},{8,9},{9,8},{10,11... | collective-permute-start | bytes 393224 | tf_op jit(solution)/shard_map/ppermute | solution.py:397
  73.6 0.6 collective-permute-start.20
  74.3 1.5 %collective-permute-start.22 = (bf16[2,6,32,128]{3,2,1,0:T(8,128)(2,1)S(1)}, bf16[2,6,32,128]{3,2,1,0:T(8,128)(2,1)S(1)}, u32[]{:S(2)}, u32[]{:S(2)}) collective-permute-start(bf16[2,6,32,128]{3,2,1,0:T(8,128)(2,1)S(1)} %get-tuple-element.55._), channel_id=1, source_target_pairs={{0,16},{8,24},{16,0},{24,8},{32,48},{40,56},{48,32},{56,40},{64,80... | collective-permute-start | bytes 294920 | tf_op jit(solution)/shard_map/ppermute | solution.py:358
  75.8 5.6 %collective-permute-done.20.other_ref = bf16[2,6,32,128]{3,2,1,0:T(8,128)(2,1)S(1)} collective-permute-done((bf16[2,6,32,128]{3,2,1,0:T(8,128)(2,1)S(1)}, bf16[2,6,32,128]{3,2,1,0:T(8,128)(2,1)S(1)}, u32[]{:S(2)}, u32[]{:S(2)}) %collective-permute-start.20) | collective-permute-done | bytes 98336 | tf_op jit(solution)/shard_map/ppermute | solution.py:358
  81.4 0.1 collective-permute-start.21
  81.5 0.9 %collective-permute-done.22.other_ref = bf16[2,6,32,128]{3,2,1,0:T(8,128)(2,1)S(1)} collective-permute-done((bf16[2,6,32,128]{3,2,1,0:T(8,128)(2,1)S(1)}, bf16[2,6,32,128]{3,2,1,0:T(8,128)(2,1)S(1)}, u32[]{:S(2)}, u32[]{:S(2)}) %collective-permute-start.22) | collective-permute-done | bytes 98336 | tf_op jit(solution)/shard_map/ppermute | solution.py:358
  82.5 2.1 %collective-permute-start.23 = (bf16[1,6,32,128]{3,2,1,0:T(8,128)(2,1)S(1)}, bf16[1,6,32,128]{3,2,1,0:T(8,128)(2,1)S(1)}, u32[]{:S(2)}, u32[]{:S(2)}) collective-permute-start(bf16[1,6,32,128]{3,2,1,0:T(8,128)(2,1)S(1)} %get-tuple-element.61), channel_id=1, source_target_pairs={{0,32},{8,40},{16,48},{24,56},{32,0},{40,8},{48,16},{56,24},{64,96... | collective-permute-start | bytes 147464 | tf_op jit(solution)/shard_map/ppermute | solution.py:358
  84.6 0.7 fusion
  85.3 1.2 %collective-permute-done.21 = bf16[1,6,32,128]{3,2,1,0:T(8,128)(2,1)S(1)} collective-permute-done((bf16[1,6,32,128]{3,2,1,0:T(8,128)(2,1)S(1)}, bf16[1,6,32,128]{3,2,1,0:T(8,128)(2,1)S(1)}, u32[]{:S(2)}, u32[]{:S(2)}) %collective-permute-start.21) | collective-permute-done | bytes 49184 | tf_op jit(solution)/shard_map/ppermute | solution.py:358
  86.5 1.0 %collective-permute-done.23 = bf16[1,6,32,128]{3,2,1,0:T(8,128)(2,1)S(1)} collective-permute-done((bf16[1,6,32,128]{3,2,1,0:T(8,128)(2,1)S(1)}, bf16[1,6,32,128]{3,2,1,0:T(8,128)(2,1)S(1)}, u32[]{:S(2)}, u32[]{:S(2)}) %collective-permute-start.23) | collective-permute-done | bytes 49184 | tf_op jit(solution)/shard_map/ppermute | solution.py:358
  87.6 0.7 maximum_bitcast_fusion
  (15 shorter events, 0.2 us)
Async XLA Ops:
  0.6 25.5 %copy-start.2 = (bf16[512,128]{1,0:T(8,128)(2,1)S(1)}, bf16[512,128]{1,0:T(8,128)(2,1)}, u32[]{:S(2)}) copy-start(bf16[512,128]{1,0:T(8,128)(2,1)} %own_ref.3) | copy-start | bytes 393220
  0.6 20.8 %collective-permute-start = (bf16[512,128]{1,0:T(8,128)(2,1)}, bf16[512,128]{1,0:T(8,128)(2,1)S(1)}, u32[]{:S(2)}, u32[]{:S(2)}) collective-permute-start(bf16[512,128]{1,0:T(8,128)(2,1)} %param.4), channel_id=1, source_target_pairs={{0,1},{1,0},{2,3},{3,2},{4,5},{5,4},{6,7},{7,6},{8,9},{9,8},{10,11... | collective-permute-start | bytes 393224 | tf_op jit(solution)/shard_map/ppermute | solution.py:364
  7.9 16.3 %collective-permute-start.2 = (bf16[512,128]{1,0:T(8,128)(2,1)}, bf16[512,128]{1,0:T(8,128)(2,1)S(1)}, u32[]{:S(2)}, u32[]{:S(2)}) collective-permute-start(bf16[512,128]{1,0:T(8,128)(2,1)} %own_ref.3), channel_id=1, source_target_pairs={{32,0},{40,8},{48,16},{56,24},{64,32},{72,40},{80,48},{88,56},{96,... | collective-permute-start | bytes 393224 | tf_op jit(solution)/shard_map/ppermute | solution.py:349
  11.5 12.8 %collective-permute-start.3 = (bf16[512,128]{1,0:T(8,128)(2,1)}, bf16[512,128]{1,0:T(8,128)(2,1)S(1)}, u32[]{:S(2)}, u32[]{:S(2)}) collective-permute-start(bf16[512,128]{1,0:T(8,128)(2,1)} %own_ref.3), channel_id=1, source_target_pairs={{48,0},{56,8},{64,16},{72,24},{80,32},{88,40},{96,48},{104,56},{11... | collective-permute-start | bytes 393224 | tf_op jit(solution)/shard_map/ppermute | solution.py:349
  14.3 10.0 %collective-permute-start.4 = (bf16[512,128]{1,0:T(8,128)(2,1)}, bf16[512,128]{1,0:T(8,128)(2,1)S(1)}, u32[]{:S(2)}, u32[]{:S(2)}) collective-permute-start(bf16[512,128]{1,0:T(8,128)(2,1)} %own_ref.3), channel_id=1, source_target_pairs={{64,0},{72,8},{80,16},{88,24},{96,32},{104,40},{112,48},{120,56},{... | collective-permute-start | bytes 393224 | tf_op jit(solution)/shard_map/ppermute | solution.py:349
  16.7 9.5 %collective-permute-start.1 = (bf16[512,128]{1,0:T(8,128)(2,1)}, bf16[512,128]{1,0:T(8,128)(2,1)S(1)}, u32[]{:S(2)}, u32[]{:S(2)}) collective-permute-start(bf16[512,128]{1,0:T(8,128)(2,1)} %own_ref.3), channel_id=1, source_target_pairs={{16,0},{24,8},{32,16},{40,24},{48,32},{56,40},{64,48},{72,56},{80,... | collective-permute-start | bytes 393224 | tf_op jit(solution)/shard_map/ppermute | solution.py:349
  22.4 0.9 %copy-start.1 = (bf16[12,4096]{1,0:T(8,128)(2,1)S(1)}, bf16[12,4096]{1,0:T(8,128)(2,1)}, u32[]{:S(2)}) copy-start(bf16[12,4096]{1,0:T(8,128)(2,1)} %filters_ref.5) | copy-start | bytes 294916
  27.0 5.8 %collective-permute-start.5 = (bf16[4,512,128]{2,1,0:T(8,128)(2,1)S(1)}, bf16[4,512,128]{2,1,0:T(8,128)(2,1)S(1)}, u32[]{:S(2)}, u32[]{:S(2)}) collective-permute-start(bf16[4,512,128]{2,1,0:T(8,128)(2,1)S(1)} %for_sibling.1), channel_id=1, source_target_pairs={{0,8},{8,0},{16,24},{24,16},{32,40},{40,32},{48,56},{56,48},{64,72... | collective-permute-start | bytes 1572872 | tf_op jit(solution)/shard_map/ppermute | solution.py:352
  27.1 15.8 %collective-permute-start.6 = (bf16[2,512,128]{2,1,0:T(8,128)(2,1)S(1)}, bf16[2,512,128]{2,1,0:T(8,128)(2,1)S(1)}, u32[]{:S(2)}, u32[]{:S(2)}) collective-permute-start(bf16[2,512,128]{2,1,0:T(8,128)(2,1)S(1)} %pad_maximum_fusion._.x0_ref), channel_id=1, source_target_pairs={{0,2},{1,3},{2,4},{3,5},{4,6},{5,7},{6,0},{7,1},{8,10},{9,11},{10,... | collective-permute-start | bytes 786440 | tf_op jit(solution)/shard_map/ppermute | solution.py:365
  28.7 15.0 %collective-permute-start.7 = (bf16[2,512,128]{2,1,0:T(8,128)(2,1)S(1)}, bf16[2,512,128]{2,1,0:T(8,128)(2,1)S(1)}, u32[]{:S(2)}, u32[]{:S(2)}) collective-permute-start(bf16[2,512,128]{2,1,0:T(8,128)(2,1)S(1)} %pad_maximum_fusion._.x0_ref), channel_id=1, source_target_pairs={{0,4},{1,5},{2,6},{3,7},{4,0},{5,1},{6,2},{7,3},{8,12},{9,13},{10,... | collective-permute-start | bytes 786440 | tf_op jit(solution)/shard_map/ppermute | solution.py:365
  31.4 12.2 %collective-permute-start.8 = (bf16[2,512,128]{2,1,0:T(8,128)(2,1)S(1)}, bf16[2,512,128]{2,1,0:T(8,128)(2,1)S(1)}, u32[]{:S(2)}, u32[]{:S(2)}) collective-permute-start(bf16[2,512,128]{2,1,0:T(8,128)(2,1)S(1)} %pad_maximum_fusion._.x0_ref), channel_id=1, source_target_pairs={{0,6},{1,7},{2,0},{3,1},{4,2},{5,3},{6,4},{7,5},{8,14},{9,15},{10,... | collective-permute-start | bytes 786440 | tf_op jit(solution)/shard_map/ppermute | solution.py:365
  38.4 2.1 %copy-start = (bf16[1024,12,128]{2,0,1:T(8,128)(2,1)S(1)}, bf16[1024,12,128]{2,0,1:T(8,128)(2,1)}, u32[]{:S(2)}) copy-start(bf16[1024,12,128]{2,0,1:T(8,128)(2,1)} %param.7) | copy-start | bytes 9437188
  45.6 2.6 %collective-permute-start.9 = (bf16[4,4,6,32,128]{4,3,2,1,0:T(8,128)(2,1)S(1)}, bf16[4,4,6,32,128]{4,3,2,1,0:T(8,128)(2,1)S(1)}, u32[]{:S(2)}, u32[]{:S(2)}) collective-permute-start(bf16[4,4,6,32,128]{4,3,2,1,0:T(8,128)(2,1)S(1)} %get-tuple-element.35._), channel_id=1, source_target_pairs={{0,8},{8,0},{16,24},{24,16},{32,40},{40,32},{48,56},{56,48},{64,72... | collective-permute-start | bytes 2359304 | tf_op jit(solution)/shard_map/ppermute | solution.py:352
  47.6 2.5 %collective-permute-start.10 = (bf16[4,4,6,32,128]{4,3,2,1,0:T(8,128)(2,1)S(1)}, bf16[4,4,6,32,128]{4,3,2,1,0:T(8,128)(2,1)S(1)}, u32[]{:S(2)}, u32[]{:S(2)}) collective-permute-start(bf16[4,4,6,32,128]{4,3,2,1,0:T(8,128)(2,1)S(1)} %get-tuple-element.36._), channel_id=1, source_target_pairs={{0,8},{8,0},{16,24},{24,16},{32,40},{40,32},{48,56},{56,48},{64,72... | collective-permute-start | bytes 2359304 | tf_op jit(solution)/shard_map/ppermute | solution.py:352
  48.4 13.0 %collective-permute-start.14 = (bf16[2,4,6,32,128]{4,3,2,1,0:T(8,128)(2,1)S(1)}, bf16[2,4,6,32,128]{4,3,2,1,0:T(8,128)(2,1)S(1)}, u32[]{:S(2)}, u32[]{:S(2)}) collective-permute-start(bf16[2,4,6,32,128]{4,3,2,1,0:T(8,128)(2,1)S(1)} %get-tuple-element.38._), channel_id=1, source_target_pairs={{0,64},{8,72},{16,80},{24,88},{32,96},{40,104},{48,112},{56,120},{... | collective-permute-start | bytes 1179656 | tf_op jit(solution)/shard_map/ppermute | solution.py:355
  50.3 14.1 %collective-permute-start.15 = (bf16[2,4,6,32,128]{4,3,2,1,0:T(8,128)(2,1)S(1)}, bf16[2,4,6,32,128]{4,3,2,1,0:T(8,128)(2,1)S(1)}, u32[]{:S(2)}, u32[]{:S(2)}) collective-permute-start(bf16[2,4,6,32,128]{4,3,2,1,0:T(8,128)(2,1)S(1)} %get-tuple-element.40._), channel_id=1, source_target_pairs={{0,192},{8,200},{16,208},{24,216},{32,224},{40,232},{48,240},{56,2... | collective-permute-start | bytes 1179656 | tf_op jit(solution)/shard_map/ppermute | solution.py:355
  50.5 8.5 %collective-permute-start.11 = (bf16[2,512,128]{2,1,0:T(8,128)(2,1)S(1)}, bf16[2,512,128]{2,1,0:T(8,128)(2,1)S(1)}, u32[]{:S(2)}, u32[]{:S(2)}) collective-permute-start(bf16[2,512,128]{2,1,0:T(8,128)(2,1)S(1)} %get-tuple-element.42), channel_id=1, source_target_pairs={{0,2},{1,3},{2,0},{3,1},{4,6},{5,7},{6,4},{7,5},{8,10},{9,11},{10,... | collective-permute-start | bytes 786440 | tf_op jit(solution)/shard_map/ppermute | solution.py:361
  51.9 9.5 %collective-permute-start.12 = (bf16[2,512,128]{2,1,0:T(8,128)(2,1)S(1)}, bf16[2,512,128]{2,1,0:T(8,128)(2,1)S(1)}, u32[]{:S(2)}, u32[]{:S(2)}) collective-permute-start(bf16[2,512,128]{2,1,0:T(8,128)(2,1)S(1)} %get-tuple-element.34._), channel_id=1, source_target_pairs={{0,6},{1,7},{2,4},{3,5},{4,2},{5,3},{6,0},{7,1},{8,14},{9,15},{10,... | collective-permute-start | bytes 786440 | tf_op jit(solution)/shard_map/ppermute | solution.py:361
  61.5 7.3 %collective-permute-start.16 = (bf16[1,4,6,32,128]{4,3,2,1,0:T(8,128)(2,1)S(1)}, bf16[1,4,6,32,128]{4,3,2,1,0:T(8,128)(2,1)S(1)}, u32[]{:S(2)}, u32[]{:S(2)}) collective-permute-start(bf16[1,4,6,32,128]{4,3,2,1,0:T(8,128)(2,1)S(1)} %get-tuple-element.48._), channel_id=1, source_target_pairs={{0,192},{8,200},{16,208},{24,216},{32,224},{40,232},{48,240},{56,2... | collective-permute-start | bytes 589832 | tf_op jit(solution)/shard_map/ppermute | solution.py:355
  64.5 9.7 %collective-permute-start.19 = (bf16[1,4,6,32,128]{4,3,2,1,0:T(8,128)(2,1)S(1)}, bf16[1,4,6,32,128]{4,3,2,1,0:T(8,128)(2,1)S(1)}, u32[]{:S(2)}, u32[]{:S(2)}) collective-permute-start(bf16[1,4,6,32,128]{4,3,2,1,0:T(8,128)(2,1)S(1)} %get-tuple-element.50._), channel_id=1, source_target_pairs={{0,64},{8,72},{16,80},{24,88},{32,96},{40,104},{48,112},{56,120},{... | collective-permute-start | bytes 589832 | tf_op jit(solution)/shard_map/ppermute | solution.py:355
  64.6 6.3 %collective-permute-start.17 = (bf16[1,512,128]{2,1,0:T(8,128)(2,1)S(1)}, bf16[1,512,128]{2,1,0:T(8,128)(2,1)S(1)}, u32[]{:S(2)}, u32[]{:S(2)}) collective-permute-start(bf16[1,512,128]{2,1,0:T(8,128)(2,1)S(1)} %get-tuple-element.43._), channel_id=1, source_target_pairs={{0,6},{1,7},{2,4},{3,5},{4,2},{5,3},{6,0},{7,1},{8,14},{9,15},{10,... | collective-permute-start | bytes 393224 | tf_op jit(solution)/shard_map/ppermute | solution.py:361
  66.6 18.0 %collective-permute-start.13 = (bf16[1,512,128]{2,1,0:T(8,128)(2,1)S(1)}, bf16[1,512,128]{2,1,0:T(8,128)(2,1)S(1)}, u32[]{:S(2)}, u32[]{:S(2)}) collective-permute-start(bf16[1,512,128]{2,1,0:T(8,128)(2,1)S(1)} %get-tuple-element.46._), channel_id=1, source_target_pairs={{0,2},{1,3},{2,0},{3,1},{4,6},{5,7},{6,4},{7,5},{8,10},{9,11},{10,... | collective-permute-start | bytes 393224 | tf_op jit(solution)/shard_map/ppermute | solution.py:361
  70.9 13.7 %collective-permute-start.18 = (bf16[1,512,128]{2,1,0:T(8,128)(2,1)S(1)}, bf16[1,512,128]{2,1,0:T(8,128)(2,1)S(1)}, u32[]{:S(2)}, u32[]{:S(2)}) collective-permute-start(bf16[1,512,128]{2,1,0:T(8,128)(2,1)S(1)} %add.37._), channel_id=1, source_target_pairs={{0,1},{1,0},{2,3},{3,2},{4,5},{5,4},{6,7},{7,6},{8,9},{9,8},{10,11... | collective-permute-start | bytes 393224 | tf_op jit(solution)/shard_map/ppermute | solution.py:397
  73.6 7.8 %collective-permute-start.20 = (bf16[2,6,32,128]{3,2,1,0:T(8,128)(2,1)S(1)}, bf16[2,6,32,128]{3,2,1,0:T(8,128)(2,1)S(1)}, u32[]{:S(2)}, u32[]{:S(2)}) collective-permute-start(bf16[2,6,32,128]{3,2,1,0:T(8,128)(2,1)S(1)} %get-tuple-element.52._), channel_id=1, source_target_pairs={{0,16},{8,24},{16,0},{24,8},{32,48},{40,56},{48,32},{56,40},{64,80... | collective-permute-start | bytes 294920 | tf_op jit(solution)/shard_map/ppermute | solution.py:358
  74.3 8.2 %collective-permute-start.22 = (bf16[2,6,32,128]{3,2,1,0:T(8,128)(2,1)S(1)}, bf16[2,6,32,128]{3,2,1,0:T(8,128)(2,1)S(1)}, u32[]{:S(2)}, u32[]{:S(2)}) collective-permute-start(bf16[2,6,32,128]{3,2,1,0:T(8,128)(2,1)S(1)} %get-tuple-element.55._), channel_id=1, source_target_pairs={{0,16},{8,24},{16,0},{24,8},{32,48},{40,56},{48,32},{56,40},{64,80... | collective-permute-start | bytes 294920 | tf_op jit(solution)/shard_map/ppermute | solution.py:358
  81.4 5.1 %collective-permute-start.21 = (bf16[1,6,32,128]{3,2,1,0:T(8,128)(2,1)S(1)}, bf16[1,6,32,128]{3,2,1,0:T(8,128)(2,1)S(1)}, u32[]{:S(2)}, u32[]{:S(2)}) collective-permute-start(bf16[1,6,32,128]{3,2,1,0:T(8,128)(2,1)S(1)} %get-tuple-element.58._), channel_id=1, source_target_pairs={{0,32},{8,40},{16,48},{24,56},{32,0},{40,8},{48,16},{56,24},{64,96... | collective-permute-start | bytes 147464 | tf_op jit(solution)/shard_map/ppermute | solution.py:358
  82.5 5.1 %collective-permute-start.23 = (bf16[1,6,32,128]{3,2,1,0:T(8,128)(2,1)S(1)}, bf16[1,6,32,128]{3,2,1,0:T(8,128)(2,1)S(1)}, u32[]{:S(2)}, u32[]{:S(2)}) collective-permute-start(bf16[1,6,32,128]{3,2,1,0:T(8,128)(2,1)S(1)} %get-tuple-element.61), channel_id=1, source_target_pairs={{0,32},{8,40},{16,48},{24,56},{32,0},{40,8},{48,16},{56,24},{64,96... | collective-permute-start | bytes 147464 | tf_op jit(solution)/shard_map/ppermute | solution.py:358

commit v8 on v7

--- a/solution.py
+++ b/solution.py
@@ -263,7 +263,7 @@
     leave_ref[...] = (mine_ref[half:].astype(F32) + other_ref[half:].astype(F32)).astype(BF16)
 
 
-def halve(after, mine, other):
+def halve(after, mine, other, cost=SMALL_COST):
     half = (mine.shape[0] // 2,) + mine.shape[1:]
     vmem = pl.BlockSpec(memory_space=pltpu.VMEM)
     return pl.pallas_call(
@@ -272,7 +272,7 @@
         in_specs=[pl.BlockSpec(memory_space=pl.ANY), vmem, vmem],
         out_specs=(vmem, vmem),
         compiler_params=pltpu.CompilerParams(vmem_limit_bytes=VMEM_LIMIT),
-        cost_estimate=SMALL_COST,
+        cost_estimate=cost,
         name="halve",
     )(after, mine, other)
 
@@ -289,9 +289,32 @@
         in_specs=[pl.BlockSpec(memory_space=pl.ANY), vmem, vmem],
         out_specs=vmem,
         compiler_params=pltpu.CompilerParams(vmem_limit_bytes=VMEM_LIMIT),
-        cost_estimate=SMALL_COST,
+        cost_estimate=LARGE_COST,
         name="add",
     )(after, mine, other)
+
+
+def join_kernel(_, *refs):
+    at, sum_ref = 0, refs[-1]
+    for mine_ref, other_ref in zip(refs[0:-1:2], refs[1:-1:2]):
+        count = mine_ref.shape[1]
+        sum_ref[at : at + count] = mine_ref[0] + other_ref[0].astype(F32)
+        at += count
+
+
+def join(after, *pairs):
+    counts = [mine.shape[1] for mine, _ in pairs]
+    rest = pairs[0][0].shape[2:]
+    vmem = pl.BlockSpec(memory_space=pltpu.VMEM)
+    return pl.pallas_call(
+        join_kernel,
+        out_shape=jax.ShapeDtypeStruct((sum(counts),) + rest, F32),
+        in_specs=[pl.BlockSpec(memory_space=pl.ANY)] + [vmem] * (2 * len(pairs)),
+        out_specs=vmem,
+        compiler_params=pltpu.CompilerParams(vmem_limit_bytes=VMEM_LIMIT),
+        cost_estimate=SMALL_COST,
+        name="join",
+    )(after, *[part for pair in pairs for part in pair])
 
 
 def share_kernel(pos_ref, _, *refs):
@@ -383,7 +406,7 @@
     y_0 = y_swapped(leave_0, False)
     stay_1, leave_1 = halve(leave_0, keep_1, sibling(send_1))
     y_1 = y_swapped(leave_1, True)
-    far, leave = halve(leave_1, far, x_far)
+    far, leave = halve(leave_1, far, x_far, LARGE_COST)
     x_far = x_swapped(leave, True)
     near, leave = halve(leave, near, x_near)
     x_near = x_swapped(leave, False)
@@ -391,18 +414,17 @@
     y_0 = y_swapped(leave_0, True)
     stay_1, leave_1 = halve(leave_0, stay_1, y_1)
     y_1 = y_swapped(leave_1, False)
-    stay_0, leave_0 = halve(leave_1, stay_0[0], y_0[0])
+    far = add(leave_1, far, x_far)
+    opposite = lax.ppermute(far, "tp", Z_HI_SWAP)
+    stay_0, leave_0 = halve(far, stay_0[0], y_0[0])
     z_0 = z_swapped(leave_0, 1)
-    far = add(leave_0, far, x_far)
-    opposite = lax.ppermute(far, "tp", Z_HI_SWAP)
-    stay_1, leave_1 = halve(far, stay_1[0], y_1[0])
+    stay_1, leave_1 = halve(leave_0, stay_1[0], y_1[0])
     z_1 = z_swapped(leave_1, 1)
     stay_0, leave_0 = halve(leave_1, stay_0, z_0)
     z_0 = z_swapped(leave_0, 2)
     stay_1, leave_1 = halve(leave_0, stay_1, z_1)
     z_1 = z_swapped(leave_1, 2)
-    parts = [stay_0[0] + z_0[0].astype(F32), stay_1[0] + z_1[0].astype(F32)]
-    grad_proj = jnp.concatenate(parts, axis=0).transpose(1, 0, 2)
+    grad_proj = join(near, (stay_0, z_0), (stay_1, z_1)).transpose(1, 0, 2)
     total = near[0] + x_near[0].astype(F32) + opposite[0].astype(F32)
     return total.astype(BF16), grad_proj
 

time: 89.6 us -> 84.8 us (0.946); the launches traced: 88.3 us -> 84.4 us
  waiting for transfers between devices: 24.2 us -> 19.8 us
    ppermute x4, waiting for transfers between devices: 9.56 us -> 2.57 us  [x_swapped(): return lax.ppermute(value, 'tp', x_swap(crossed))]
    ppermute x4, waiting for transfers between devices: 2.21 us -> 6.71 us  [y_swapped(): return lax.ppermute(value, 'ctx', y_swap(crossed))]
    ppermute x4, starting transfers between devices: 4.08 us -> 2.47 us  [y_swapped(): return lax.ppermute(value, 'ctx', y_swap(crossed))]
    ppermute x4, starting transfers between devices: 4.28 us -> 5.51 us  [z_swapped(): return lax.ppermute(value, 'ctx', z_swap(bit))]
    ppermute x4, waiting for transfers between devices: 8.83 us -> 7.85 us  [z_swapped(): return lax.ppermute(value, 'ctx', z_swap(bit))]
    ppermute x3, waiting for transfers between devices: 0.92 us -> 0.01 us  [sibling(): return lax.ppermute(value, 'ctx', CORE_SWAP)]
  transfers between devices with their start and end apart: 24 -> 24, of which waited for: 11 -> 9; matrix products, arithmetic and copies ran while one was open for 2% -> 2% of each run, Pallas kernels for 15% -> 16%
where the time goes in v8:
time: 84.8 us; the launch traced here: 84.4 us
  starting transfers between devices  44.1 us (52%)
  waiting for transfers between devices  19.8 us (23%)
  Pallas kernels  17 us (20%)
  other arithmetic  1.71 us (2%)
  local copies, waits for them, and re-layouts  0.91 us (1%)
  between operations  0.86 us (1%)
    ppermute x4, starting transfers between devices, later(): return lax.ppermute(value, 'ctx', from_later_chip(steps))  13.4 us
    ppermute x4, waiting for transfers between devices, z_swapped(): return lax.ppermute(value, 'ctx', z_swap(bit))  7.85 us
    ppermute x1, starting transfers between devices, per_device(): pair = jnp.stack([inputs, lax.ppermute(inputs, 'tp', Z_HI_SWAP)])  7.28 us
    ppermute x4, waiting for transfers between devices, y_swapped(): return lax.ppermute(value, 'ctx', y_swap(crossed))  6.71 us
    ppermute x4, starting transfers between devices, x_swapped(): return lax.ppermute(value, 'tp', x_swap(crossed))  6.03 us
    ppermute x3, starting transfers between devices, per_device(): lax.ppermute(pair, 'tp', along_x(s))  5.73 us
    ppermute x4, starting transfers between devices, z_swapped(): return lax.ppermute(value, 'ctx', z_swap(bit))  5.51 us
    pallas_call x2, Pallas kernels, far_conv(): pl.pallas_call(functools.partial(far_kernel, first), out_shape=jax.ShapeD...  4.16 us
  transfers between devices with their start and end apart: 24, of which 9 were waited for; matrix products, arithmetic and copies ran while one was open for 2% of the time, Pallas kernels for 16%

profile of v8, /device:TPU:24, one launch (start us, length us, event | category | flops | bytes accessed | tf_op | source)
XLA Modules:
  0.0 84.4 jit_solution(6689621965126336738)
XLA Ops:
  0.6 7.3 %collective-permute-start = (bf16[512,128]{1,0:T(8,128)(2,1)}, bf16[512,128]{1,0:T(8,128)(2,1)S(1)}, u32[]{:S(2)}, u32[]{:S(2)}) collective-permute-start(bf16[512,128]{1,0:T(8,128)(2,1)} %param.4), channel_id=1, source_target_pairs={{0,1},{1,0},{2,3},{3,2},{4,5},{5,4},{6,7},{7,6},{8,9},{9,8},{10,11... | collective-permute-start | bytes 393224 | tf_op jit(solution)/shard_map/ppermute | solution.py:387
  7.9 3.5 %collective-permute-start.2 = (bf16[512,128]{1,0:T(8,128)(2,1)}, bf16[512,128]{1,0:T(8,128)(2,1)S(1)}, u32[]{:S(2)}, u32[]{:S(2)}) collective-permute-start(bf16[512,128]{1,0:T(8,128)(2,1)} %own_ref.3), channel_id=1, source_target_pairs={{32,0},{40,8},{48,16},{56,24},{64,32},{72,40},{80,48},{88,56},{96,... | collective-permute-start | bytes 393224 | tf_op jit(solution)/shard_map/ppermute | solution.py:372
  11.5 2.8 %collective-permute-start.3 = (bf16[512,128]{1,0:T(8,128)(2,1)}, bf16[512,128]{1,0:T(8,128)(2,1)S(1)}, u32[]{:S(2)}, u32[]{:S(2)}) collective-permute-start(bf16[512,128]{1,0:T(8,128)(2,1)} %own_ref.3), channel_id=1, source_target_pairs={{48,0},{56,8},{64,16},{72,24},{80,32},{88,40},{96,48},{104,56},{11... | collective-permute-start | bytes 393224 | tf_op jit(solution)/shard_map/ppermute | solution.py:372
  14.3 2.4 %collective-permute-start.4 = (bf16[512,128]{1,0:T(8,128)(2,1)}, bf16[512,128]{1,0:T(8,128)(2,1)S(1)}, u32[]{:S(2)}, u32[]{:S(2)}) collective-permute-start(bf16[512,128]{1,0:T(8,128)(2,1)} %own_ref.3), channel_id=1, source_target_pairs={{64,0},{72,8},{80,16},{88,24},{96,32},{104,40},{112,48},{120,56},{... | collective-permute-start | bytes 393224 | tf_op jit(solution)/shard_map/ppermute | solution.py:372
  16.7 4.7 %collective-permute-start.1 = (bf16[512,128]{1,0:T(8,128)(2,1)}, bf16[512,128]{1,0:T(8,128)(2,1)S(1)}, u32[]{:S(2)}, u32[]{:S(2)}) collective-permute-start(bf16[512,128]{1,0:T(8,128)(2,1)} %own_ref.3), channel_id=1, source_target_pairs={{16,0},{24,8},{32,16},{40,24},{48,32},{56,40},{64,48},{72,56},{80,... | collective-permute-start | bytes 393224 | tf_op jit(solution)/shard_map/ppermute | solution.py:372
  21.4 0.1 pad_add_fusion.pos_ref
  21.5 0.0 collective-permute-done
  21.5 0.9 %pad_maximum_fusion._.x0_ref = bf16[2,512,128]{2,1,0:T(8,128)(2,1)S(1)} fusion(bf16[1,512,128]{2,1,0:T(8,128)(2,1)S(1)} %bitcast.19, bf16[1,512,128]{2,1,0:T(8,128)(2,1)} %bitcast.18), kind=kLoop, calls=%fused_computation | loop fusion | flops 131072 | bytes 524288 | tf_op jit(solution)/shard_map/stack | solution.py:387
  22.4 0.0 copy-start.1
  22.4 0.9 %copy-done.1 = bf16[12,4096]{1,0:T(8,128)(2,1)S(1)} copy-done((bf16[12,4096]{1,0:T(8,128)(2,1)S(1)}, bf16[12,4096]{1,0:T(8,128)(2,1)}, u32[]{:S(2)}) %copy-start.1) | copy-done | bytes 98328
  23.3 0.9 %near_table.1._.table_ref = bf16[12,64,2048]{2,1,0:T(8,128)(2,1)S(1)} custom-call(bf16[2,512,128]{2,1,0:T(8,128)(2,1)S(1)} %pad_maximum_fusion._.x0_ref, bf16[12,4096]{1,0:T(8,128)(2,1)S(1)} %copy-done.1), custom_call_target="tpu_custom_call" | custom-call | flops 1000 | bytes 1000 | tf_op jit(solution)/shard_map/near_table/pallas_call | solution.py:79
  24.2 0.0 collective-permute-done.2.r2_ref
  24.2 0.0 collective-permute-done.3.r3_ref
  24.2 0.0 collective-permute-done.4.r4_ref
  24.3 1.9 %collective-permute-done.1.r1_ref = bf16[512,128]{1,0:T(8,128)(2,1)S(1)} collective-permute-done((bf16[512,128]{1,0:T(8,128)(2,1)}, bf16[512,128]{1,0:T(8,128)(2,1)S(1)}, u32[]{:S(2)}, u32[]{:S(2)}) %collective-permute-start.1) | collective-permute-done | bytes 131104 | tf_op jit(solution)/shard_map/ppermute | solution.py:372
  26.2 0.8 for_sibling.1
  27.0 0.1 collective-permute-start.5
  27.1 1.6 %collective-permute-start.6 = (bf16[2,512,128]{2,1,0:T(8,128)(2,1)S(1)}, bf16[2,512,128]{2,1,0:T(8,128)(2,1)S(1)}, u32[]{:S(2)}, u32[]{:S(2)}) collective-permute-start(bf16[2,512,128]{2,1,0:T(8,128)(2,1)S(1)} %pad_maximum_fusion._.x0_ref), channel_id=1, source_target_pairs={{0,2},{1,3},{2,4},{3,5},{4,6},{5,7},{6,0},{7,1},{8,10},{9,11},{10,... | collective-permute-start | bytes 786440 | tf_op jit(solution)/shard_map/ppermute | solution.py:388
  28.7 2.7 %collective-permute-start.7 = (bf16[2,512,128]{2,1,0:T(8,128)(2,1)S(1)}, bf16[2,512,128]{2,1,0:T(8,128)(2,1)S(1)}, u32[]{:S(2)}, u32[]{:S(2)}) collective-permute-start(bf16[2,512,128]{2,1,0:T(8,128)(2,1)S(1)} %pad_maximum_fusion._.x0_ref), channel_id=1, source_target_pairs={{0,4},{1,5},{2,6},{3,7},{4,0},{5,1},{6,2},{7,3},{8,12},{9,13},{10,... | collective-permute-start | bytes 786440 | tf_op jit(solution)/shard_map/ppermute | solution.py:388
  31.4 1.4 %collective-permute-start.8 = (bf16[2,512,128]{2,1,0:T(8,128)(2,1)S(1)}, bf16[2,512,128]{2,1,0:T(8,128)(2,1)S(1)}, u32[]{:S(2)}, u32[]{:S(2)}) collective-permute-start(bf16[2,512,128]{2,1,0:T(8,128)(2,1)S(1)} %pad_maximum_fusion._.x0_ref), channel_id=1, source_target_pairs={{0,6},{1,7},{2,0},{3,1},{4,2},{5,3},{6,4},{7,5},{8,14},{9,15},{10,... | collective-permute-start | bytes 786440 | tf_op jit(solution)/shard_map/ppermute | solution.py:388
  32.9 3.4 %near_conv.1 = (f32[4,384,256]{2,1,0:T(8,128)S(1)}, f32[4,384,256]{2,1,0:T(8,128)S(1)}) custom-call(bf16[12,64,2048]{2,1,0:T(8,128)(2,1)S(1)} %near_table.1._.table_ref, bf16[512,128]{1,0:T(8,128)(2,1)S(1)} %copy-done.2, bf16[512,128]{1,0:T(8,128)(2,1)S(1)} %collective-permute-done.1.r1_ref, bf16[512,128]{1,0:T(8,128)(2,1)S(1)} %collective-permute-done.2.r2_ref, ...), custom_call_target="tpu_custom_call" | custom-call | flops 4000000000 | bytes 8000000 | tf_op jit(solution)/shard_map/near_conv/pallas_call | solution.py:158
  36.3 2.1 %far_conv.2._.refs_0_.corr_ref = bf16[512,768]{1,0:T(8,128)(2,1)S(1)} custom-call(bf16[12,64,2048]{2,1,0:T(8,128)(2,1)S(1)} %near_table.1._.table_ref, bf16[12,4096]{1,0:T(8,128)(2,1)S(1)} %copy-done.1, f32[4,384,256]{2,1,0:T(8,128)S(1)} %get-tuple-element.32.acc_ref, bf16[512,128]{1,0:T(8,128)(2,1)S(1)} %collective-permute-done.2.r2_ref, ...), custom_call_target="tpu_custom_call" | custom-call | flops 1000 | bytes 1000 | tf_op jit(solution)/shard_map/far_conv/pallas_call | solution.py:202
  38.4 0.0 copy-start
  38.4 2.1 %far_conv.3._.refs_1_.corr_ref = bf16[512,768]{1,0:T(8,128)(2,1)S(1)} custom-call(bf16[512,768]{1,0:T(8,128)(2,1)S(1)} %far_conv.2._.refs_0_.corr_ref, bf16[12,4096]{1,0:T(8,128)(2,1)S(1)} %copy-done.1, f32[4,384,256]{2,1,0:T(8,128)S(1)} %get-tuple-element.33.acc_ref, bf16[512,128]{1,0:T(8,128)(2,1)S(1)} %collective-permute-done.2.r2_ref, ...), custom_call_target="tpu_custom_call" | custom-call | flops 1000 | bytes 1000 | tf_op jit(solution)/shard_map/far_conv/pallas_call | solution.py:202
  40.5 2.4 %input_shares.1 = (f32[2,512,128]{2,1,0:T(8,128)S(1)}, bf16[2,512,128]{2,1,0:T(8,128)(2,1)S(1)}, f32[2,512,128]{2,1,0:T(8,128)S(1)}, bf16[2,512,128]{2,1,0:T(8,128)(2,1)S(1)}) custom-call(s32[2]{0:T(128)S(1)} %pad_add_fusion.pos_ref, bf16[512,768]{1,0:T(8,128)(2,1)S(1)} %far_conv.3._.refs_1_.corr_ref, bf16[512,768]{1,0:T(8,128)(2,1)S(1)} %far_conv.2._.refs_0_.corr_ref, ...), custom_call_target="tpu_custom_call" | custom-call | flops 1000 | bytes 1000 | tf_op jit(solution)/shard_map/input_shares/pallas_call | solution.py:351
  42.9 0.0 collective-permute-done.6.x1_ref
  42.9 0.8 collective-permute-done.7.x2_ref
  43.7 1.9 %product.2 = (bf16[4,4,6,32,128]{4,3,2,1,0:T(8,128)(2,1)S(1)}, bf16[4,4,6,32,128]{4,3,2,1,0:T(8,128)(2,1)S(1)}) custom-call(s32[2]{0:T(128)S(1)} %pad_add_fusion.pos_ref, bf16[2,512,128]{2,1,0:T(8,128)(2,1)S(1)} %get-tuple-element.34._, bf16[512,768]{1,0:T(8,128)(2,1)S(1)} %far_conv.2._.refs_0_.corr_ref, bf16[2,512,128]{2,1,0:T(8,128)(2,1)S(1)} %pad_maximum_fusion._.x0_ref, ...), custom_call_target="tpu_custom_call" | custom-call | flops 1000 | bytes 1000 | tf_op jit(solution)/shard_map/product/pallas_call | solution.py:247
  45.6 0.1 collective-permute-start.9
  45.7 1.9 %product.3 = (bf16[4,4,6,32,128]{4,3,2,1,0:T(8,128)(2,1)S(1)}, bf16[4,4,6,32,128]{4,3,2,1,0:T(8,128)(2,1)S(1)}) custom-call(s32[2]{0:T(128)S(1)} %pad_add_fusion.pos_ref, bf16[4,4,6,32,128]{4,3,2,1,0:T(8,128)(2,1)S(1)} %get-tuple-element.35._, bf16[512,768]{1,0:T(8,128)(2,1)S(1)} %far_conv.3._.refs_1_.corr_ref, ...), custom_call_target="tpu_custom_call" | custom-call | flops 1000 | bytes 1000 | tf_op jit(solution)/shard_map/product/pallas_call | solution.py:247
  47.6 0.6 collective-permute-start.10
  48.2 1.3 %collective-permute-start.11 = (bf16[2,512,128]{2,1,0:T(8,128)(2,1)S(1)}, bf16[2,512,128]{2,1,0:T(8,128)(2,1)S(1)}, u32[]{:S(2)}, u32[]{:S(2)}) collective-permute-start(bf16[2,512,128]{2,1,0:T(8,128)(2,1)S(1)} %get-tuple-element.42), channel_id=1, source_target_pairs={{0,2},{1,3},{2,0},{3,1},{4,6},{5,7},{6,4},{7,5},{8,10},{9,11},{10,... | collective-permute-start | bytes 786440 | tf_op jit(solution)/shard_map/ppermute | solution.py:384
  49.6 1.9 %collective-permute-start.12 = (bf16[2,512,128]{2,1,0:T(8,128)(2,1)S(1)}, bf16[2,512,128]{2,1,0:T(8,128)(2,1)S(1)}, u32[]{:S(2)}, u32[]{:S(2)}) collective-permute-start(bf16[2,512,128]{2,1,0:T(8,128)(2,1)S(1)} %get-tuple-element.34._), channel_id=1, source_target_pairs={{0,6},{1,7},{2,4},{3,5},{4,2},{5,3},{6,0},{7,1},{8,14},{9,15},{10,... | collective-permute-start | bytes 786440 | tf_op jit(solution)/shard_map/ppermute | solution.py:384
  51.5 0.0 collective-permute-done.9.other_ref
  51.5 0.2 halve.10
  51.6 0.8 collective-permute-start.14
  52.5 0.0 collective-permute-done.10.other_ref
  52.5 0.2 halve.11
  52.6 1.3 %collective-permute-start.15 = (bf16[2,4,6,32,128]{4,3,2,1,0:T(8,128)(2,1)S(1)}, bf16[2,4,6,32,128]{4,3,2,1,0:T(8,128)(2,1)S(1)}, u32[]{:S(2)}, u32[]{:S(2)}) collective-permute-start(bf16[2,4,6,32,128]{4,3,2,1,0:T(8,128)(2,1)S(1)} %get-tuple-element.40._), channel_id=1, source_target_pairs={{0,192},{8,200},{16,208},{24,216},{32,224},{40,232},{48,240},{56,2... | collective-permute-start | bytes 1179656 | tf_op jit(solution)/shard_map/ppermute | solution.py:378
  54.0 2.6 %collective-permute-done.11.other_ref = bf16[2,512,128]{2,1,0:T(8,128)(2,1)S(1)} collective-permute-done((bf16[2,512,128]{2,1,0:T(8,128)(2,1)S(1)}, bf16[2,512,128]{2,1,0:T(8,128)(2,1)S(1)}, u32[]{:S(2)}, u32[]{:S(2)}) %collective-permute-start.11) | collective-permute-done | bytes 262176 | tf_op jit(solution)/shard_map/ppermute | solution.py:384
  56.5 0.1 halve.12
  56.6 2.4 %collective-permute-start.16 = (bf16[1,512,128]{2,1,0:T(8,128)(2,1)S(1)}, bf16[1,512,128]{2,1,0:T(8,128)(2,1)S(1)}, u32[]{:S(2)}, u32[]{:S(2)}) collective-permute-start(bf16[1,512,128]{2,1,0:T(8,128)(2,1)S(1)} %get-tuple-element.43._), channel_id=1, source_target_pairs={{0,6},{1,7},{2,4},{3,5},{4,2},{5,3},{6,0},{7,1},{8,14},{9,15},{10,... | collective-permute-start | bytes 393224 | tf_op jit(solution)/shard_map/ppermute | solution.py:384
  59.0 0.1 halve.13
  59.0 0.4 collective-permute-start.13
  59.5 2.8 %collective-permute-done.14.other_ref = bf16[2,4,6,32,128]{4,3,2,1,0:T(8,128)(2,1)S(1)} collective-permute-done((bf16[2,4,6,32,128]{4,3,2,1,0:T(8,128)(2,1)S(1)}, bf16[2,4,6,32,128]{4,3,2,1,0:T(8,128)(2,1)S(1)}, u32[]{:S(2)}, u32[]{:S(2)}) %collective-permute-start.14) | collective-permute-done | bytes 393248 | tf_op jit(solution)/shard_map/ppermute | solution.py:378
  62.3 0.1 halve.14
  62.3 0.1 collective-permute-start.18
  62.5 2.0 %collective-permute-done.15.other_ref = bf16[2,4,6,32,128]{4,3,2,1,0:T(8,128)(2,1)S(1)} collective-permute-done((bf16[2,4,6,32,128]{4,3,2,1,0:T(8,128)(2,1)S(1)}, bf16[2,4,6,32,128]{4,3,2,1,0:T(8,128)(2,1)S(1)}, u32[]{:S(2)}, u32[]{:S(2)}) %collective-permute-start.15) | collective-permute-done | bytes 393248 | tf_op jit(solution)/shard_map/ppermute | solution.py:378
  64.4 0.1 halve.15
  64.5 0.2 collective-permute-start.19
  64.7 0.0 collective-permute-done.16.other_ref
  64.7 2.9 %collective-permute-start.17 = (bf16[1,512,128]{2,1,0:T(8,128)(2,1)S(1)}, bf16[1,512,128]{2,1,0:T(8,128)(2,1)S(1)}, u32[]{:S(2)}, u32[]{:S(2)}) collective-permute-start(bf16[1,512,128]{2,1,0:T(8,128)(2,1)S(1)} %add.19._), channel_id=1, source_target_pairs={{0,1},{1,0},{2,3},{3,2},{4,5},{5,4},{6,7},{7,6},{8,9},{9,8},{10,11... | collective-permute-start | bytes 393224 | tf_op jit(solution)/shard_map/ppermute | solution.py:418
  67.6 1.7 %collective-permute-done.18 = bf16[1,4,6,32,128]{4,3,2,1,0:T(8,128)(2,1)S(1)} collective-permute-done((bf16[1,4,6,32,128]{4,3,2,1,0:T(8,128)(2,1)S(1)}, bf16[1,4,6,32,128]{4,3,2,1,0:T(8,128)(2,1)S(1)}, u32[]{:S(2)}, u32[]{:S(2)}) %collective-permute-start.18) | collective-permute-done | bytes 196640 | tf_op jit(solution)/shard_map/ppermute | solution.py:378
  69.4 0.7 collective-permute-start.20
  70.1 0.2 collective-permute-done.19
  70.3 1.3 %collective-permute-start.22 = (bf16[2,6,32,128]{3,2,1,0:T(8,128)(2,1)S(1)}, bf16[2,6,32,128]{3,2,1,0:T(8,128)(2,1)S(1)}, u32[]{:S(2)}, u32[]{:S(2)}) collective-permute-start(bf16[2,6,32,128]{3,2,1,0:T(8,128)(2,1)S(1)} %get-tuple-element.55._), channel_id=1, source_target_pairs={{0,16},{8,24},{16,0},{24,8},{32,48},{40,56},{48,32},{56,40},{64,80... | collective-permute-start | bytes 294920 | tf_op jit(solution)/shard_map/ppermute | solution.py:381
  71.6 4.1 %collective-permute-done.20.other_ref = bf16[2,6,32,128]{3,2,1,0:T(8,128)(2,1)S(1)} collective-permute-done((bf16[2,6,32,128]{3,2,1,0:T(8,128)(2,1)S(1)}, bf16[2,6,32,128]{3,2,1,0:T(8,128)(2,1)S(1)}, u32[]{:S(2)}, u32[]{:S(2)}) %collective-permute-start.20) | collective-permute-done | bytes 98336 | tf_op jit(solution)/shard_map/ppermute | solution.py:381
  75.7 2.4 %collective-permute-start.21 = (bf16[1,6,32,128]{3,2,1,0:T(8,128)(2,1)S(1)}, bf16[1,6,32,128]{3,2,1,0:T(8,128)(2,1)S(1)}, u32[]{:S(2)}, u32[]{:S(2)}) collective-permute-start(bf16[1,6,32,128]{3,2,1,0:T(8,128)(2,1)S(1)} %get-tuple-element.58._), channel_id=1, source_target_pairs={{0,32},{8,40},{16,48},{24,56},{32,0},{40,8},{48,16},{56,24},{64,96... | collective-permute-start | bytes 147464 | tf_op jit(solution)/shard_map/ppermute | solution.py:381
  78.1 1.1 %collective-permute-start.23 = (bf16[1,6,32,128]{3,2,1,0:T(8,128)(2,1)S(1)}, bf16[1,6,32,128]{3,2,1,0:T(8,128)(2,1)S(1)}, u32[]{:S(2)}, u32[]{:S(2)}) collective-permute-start(bf16[1,6,32,128]{3,2,1,0:T(8,128)(2,1)S(1)} %get-tuple-element.61), channel_id=1, source_target_pairs={{0,32},{8,40},{16,48},{24,56},{32,0},{40,8},{48,16},{56,24},{64,96... | collective-permute-start | bytes 147464 | tf_op jit(solution)/shard_map/ppermute | solution.py:381
  79.2 0.0 collective-permute-done.13
  79.2 0.7 fusion
  79.9 3.8 %collective-permute-done.23.refs_3_ = bf16[1,6,32,128]{3,2,1,0:T(8,128)(2,1)S(1)} collective-permute-done((bf16[1,6,32,128]{3,2,1,0:T(8,128)(2,1)S(1)}, bf16[1,6,32,128]{3,2,1,0:T(8,128)(2,1)S(1)}, u32[]{:S(2)}, u32[]{:S(2)}) %collective-permute-start.23) | collective-permute-done | bytes 49184 | tf_op jit(solution)/shard_map/ppermute | solution.py:381
  83.7 0.0 collective-permute-done.21.refs_1_
  83.7 0.7 join.1
  (13 shorter events, 0.2 us)
Async XLA Ops:
  0.6 25.5 %copy-start.2 = (bf16[512,128]{1,0:T(8,128)(2,1)S(1)}, bf16[512,128]{1,0:T(8,128)(2,1)}, u32[]{:S(2)}) copy-start(bf16[512,128]{1,0:T(8,128)(2,1)} %own_ref.3) | copy-start | bytes 393220
  0.6 20.8 %collective-permute-start = (bf16[512,128]{1,0:T(8,128)(2,1)}, bf16[512,128]{1,0:T(8,128)(2,1)S(1)}, u32[]{:S(2)}, u32[]{:S(2)}) collective-permute-start(bf16[512,128]{1,0:T(8,128)(2,1)} %param.4), channel_id=1, source_target_pairs={{0,1},{1,0},{2,3},{3,2},{4,5},{5,4},{6,7},{7,6},{8,9},{9,8},{10,11... | collective-permute-start | bytes 393224 | tf_op jit(solution)/shard_map/ppermute | solution.py:387
  7.9 16.3 %collective-permute-start.2 = (bf16[512,128]{1,0:T(8,128)(2,1)}, bf16[512,128]{1,0:T(8,128)(2,1)S(1)}, u32[]{:S(2)}, u32[]{:S(2)}) collective-permute-start(bf16[512,128]{1,0:T(8,128)(2,1)} %own_ref.3), channel_id=1, source_target_pairs={{32,0},{40,8},{48,16},{56,24},{64,32},{72,40},{80,48},{88,56},{96,... | collective-permute-start | bytes 393224 | tf_op jit(solution)/shard_map/ppermute | solution.py:372
  11.5 12.8 %collective-permute-start.3 = (bf16[512,128]{1,0:T(8,128)(2,1)}, bf16[512,128]{1,0:T(8,128)(2,1)S(1)}, u32[]{:S(2)}, u32[]{:S(2)}) collective-permute-start(bf16[512,128]{1,0:T(8,128)(2,1)} %own_ref.3), channel_id=1, source_target_pairs={{48,0},{56,8},{64,16},{72,24},{80,32},{88,40},{96,48},{104,56},{11... | collective-permute-start | bytes 393224 | tf_op jit(solution)/shard_map/ppermute | solution.py:372
  14.3 10.0 %collective-permute-start.4 = (bf16[512,128]{1,0:T(8,128)(2,1)}, bf16[512,128]{1,0:T(8,128)(2,1)S(1)}, u32[]{:S(2)}, u32[]{:S(2)}) collective-permute-start(bf16[512,128]{1,0:T(8,128)(2,1)} %own_ref.3), channel_id=1, source_target_pairs={{64,0},{72,8},{80,16},{88,24},{96,32},{104,40},{112,48},{120,56},{... | collective-permute-start | bytes 393224 | tf_op jit(solution)/shard_map/ppermute | solution.py:372
  16.7 9.5 %collective-permute-start.1 = (bf16[512,128]{1,0:T(8,128)(2,1)}, bf16[512,128]{1,0:T(8,128)(2,1)S(1)}, u32[]{:S(2)}, u32[]{:S(2)}) collective-permute-start(bf16[512,128]{1,0:T(8,128)(2,1)} %own_ref.3), channel_id=1, source_target_pairs={{16,0},{24,8},{32,16},{40,24},{48,32},{56,40},{64,48},{72,56},{80,... | collective-permute-start | bytes 393224 | tf_op jit(solution)/shard_map/ppermute | solution.py:372
  22.4 0.9 %copy-start.1 = (bf16[12,4096]{1,0:T(8,128)(2,1)S(1)}, bf16[12,4096]{1,0:T(8,128)(2,1)}, u32[]{:S(2)}) copy-start(bf16[12,4096]{1,0:T(8,128)(2,1)} %filters_ref.5) | copy-start | bytes 294916
  27.0 5.8 %collective-permute-start.5 = (bf16[4,512,128]{2,1,0:T(8,128)(2,1)S(1)}, bf16[4,512,128]{2,1,0:T(8,128)(2,1)S(1)}, u32[]{:S(2)}, u32[]{:S(2)}) collective-permute-start(bf16[4,512,128]{2,1,0:T(8,128)(2,1)S(1)} %for_sibling.1), channel_id=1, source_target_pairs={{0,8},{8,0},{16,24},{24,16},{32,40},{40,32},{48,56},{56,48},{64,72... | collective-permute-start | bytes 1572872 | tf_op jit(solution)/shard_map/ppermute | solution.py:375
  27.1 15.8 %collective-permute-start.6 = (bf16[2,512,128]{2,1,0:T(8,128)(2,1)S(1)}, bf16[2,512,128]{2,1,0:T(8,128)(2,1)S(1)}, u32[]{:S(2)}, u32[]{:S(2)}) collective-permute-start(bf16[2,512,128]{2,1,0:T(8,128)(2,1)S(1)} %pad_maximum_fusion._.x0_ref), channel_id=1, source_target_pairs={{0,2},{1,3},{2,4},{3,5},{4,6},{5,7},{6,0},{7,1},{8,10},{9,11},{10,... | collective-permute-start | bytes 786440 | tf_op jit(solution)/shard_map/ppermute | solution.py:388
  28.7 15.0 %collective-permute-start.7 = (bf16[2,512,128]{2,1,0:T(8,128)(2,1)S(1)}, bf16[2,512,128]{2,1,0:T(8,128)(2,1)S(1)}, u32[]{:S(2)}, u32[]{:S(2)}) collective-permute-start(bf16[2,512,128]{2,1,0:T(8,128)(2,1)S(1)} %pad_maximum_fusion._.x0_ref), channel_id=1, source_target_pairs={{0,4},{1,5},{2,6},{3,7},{4,0},{5,1},{6,2},{7,3},{8,12},{9,13},{10,... | collective-permute-start | bytes 786440 | tf_op jit(solution)/shard_map/ppermute | solution.py:388
  31.4 12.2 %collective-permute-start.8 = (bf16[2,512,128]{2,1,0:T(8,128)(2,1)S(1)}, bf16[2,512,128]{2,1,0:T(8,128)(2,1)S(1)}, u32[]{:S(2)}, u32[]{:S(2)}) collective-permute-start(bf16[2,512,128]{2,1,0:T(8,128)(2,1)S(1)} %pad_maximum_fusion._.x0_ref), channel_id=1, source_target_pairs={{0,6},{1,7},{2,0},{3,1},{4,2},{5,3},{6,4},{7,5},{8,14},{9,15},{10,... | collective-permute-start | bytes 786440 | tf_op jit(solution)/shard_map/ppermute | solution.py:388
  38.4 2.1 %copy-start = (bf16[1024,12,128]{2,0,1:T(8,128)(2,1)S(1)}, bf16[1024,12,128]{2,0,1:T(8,128)(2,1)}, u32[]{:S(2)}) copy-start(bf16[1024,12,128]{2,0,1:T(8,128)(2,1)} %param.7) | copy-start | bytes 9437188
  45.6 5.9 %collective-permute-start.9 = (bf16[4,4,6,32,128]{4,3,2,1,0:T(8,128)(2,1)S(1)}, bf16[4,4,6,32,128]{4,3,2,1,0:T(8,128)(2,1)S(1)}, u32[]{:S(2)}, u32[]{:S(2)}) collective-permute-start(bf16[4,4,6,32,128]{4,3,2,1,0:T(8,128)(2,1)S(1)} %get-tuple-element.35._), channel_id=1, source_target_pairs={{0,8},{8,0},{16,24},{24,16},{32,40},{40,32},{48,56},{56,48},{64,72... | collective-permute-start | bytes 2359304 | tf_op jit(solution)/shard_map/ppermute | solution.py:375
  47.6 4.8 %collective-permute-start.10 = (bf16[4,4,6,32,128]{4,3,2,1,0:T(8,128)(2,1)S(1)}, bf16[4,4,6,32,128]{4,3,2,1,0:T(8,128)(2,1)S(1)}, u32[]{:S(2)}, u32[]{:S(2)}) collective-permute-start(bf16[4,4,6,32,128]{4,3,2,1,0:T(8,128)(2,1)S(1)} %get-tuple-element.36._), channel_id=1, source_target_pairs={{0,8},{8,0},{16,24},{24,16},{32,40},{40,32},{48,56},{56,48},{64,72... | collective-permute-start | bytes 2359304 | tf_op jit(solution)/shard_map/ppermute | solution.py:375
  48.2 8.3 %collective-permute-start.11 = (bf16[2,512,128]{2,1,0:T(8,128)(2,1)S(1)}, bf16[2,512,128]{2,1,0:T(8,128)(2,1)S(1)}, u32[]{:S(2)}, u32[]{:S(2)}) collective-permute-start(bf16[2,512,128]{2,1,0:T(8,128)(2,1)S(1)} %get-tuple-element.42), channel_id=1, source_target_pairs={{0,2},{1,3},{2,0},{3,1},{4,6},{5,7},{6,4},{7,5},{8,10},{9,11},{10,... | collective-permute-start | bytes 786440 | tf_op jit(solution)/shard_map/ppermute | solution.py:384
  49.6 9.4 %collective-permute-start.12 = (bf16[2,512,128]{2,1,0:T(8,128)(2,1)S(1)}, bf16[2,512,128]{2,1,0:T(8,128)(2,1)S(1)}, u32[]{:S(2)}, u32[]{:S(2)}) collective-permute-start(bf16[2,512,128]{2,1,0:T(8,128)(2,1)S(1)} %get-tuple-element.34._), channel_id=1, source_target_pairs={{0,6},{1,7},{2,4},{3,5},{4,2},{5,3},{6,0},{7,1},{8,14},{9,15},{10,... | collective-permute-start | bytes 786440 | tf_op jit(solution)/shard_map/ppermute | solution.py:384
  51.6 10.6 %collective-permute-start.14 = (bf16[2,4,6,32,128]{4,3,2,1,0:T(8,128)(2,1)S(1)}, bf16[2,4,6,32,128]{4,3,2,1,0:T(8,128)(2,1)S(1)}, u32[]{:S(2)}, u32[]{:S(2)}) collective-permute-start(bf16[2,4,6,32,128]{4,3,2,1,0:T(8,128)(2,1)S(1)} %get-tuple-element.38._), channel_id=1, source_target_pairs={{0,64},{8,72},{16,80},{24,88},{32,96},{40,104},{48,112},{56,120},{... | collective-permute-start | bytes 1179656 | tf_op jit(solution)/shard_map/ppermute | solution.py:378
  52.6 11.8 %collective-permute-start.15 = (bf16[2,4,6,32,128]{4,3,2,1,0:T(8,128)(2,1)S(1)}, bf16[2,4,6,32,128]{4,3,2,1,0:T(8,128)(2,1)S(1)}, u32[]{:S(2)}, u32[]{:S(2)}) collective-permute-start(bf16[2,4,6,32,128]{4,3,2,1,0:T(8,128)(2,1)S(1)} %get-tuple-element.40._), channel_id=1, source_target_pairs={{0,192},{8,200},{16,208},{24,216},{32,224},{40,232},{48,240},{56,2... | collective-permute-start | bytes 1179656 | tf_op jit(solution)/shard_map/ppermute | solution.py:378
  56.6 8.1 %collective-permute-start.16 = (bf16[1,512,128]{2,1,0:T(8,128)(2,1)S(1)}, bf16[1,512,128]{2,1,0:T(8,128)(2,1)S(1)}, u32[]{:S(2)}, u32[]{:S(2)}) collective-permute-start(bf16[1,512,128]{2,1,0:T(8,128)(2,1)S(1)} %get-tuple-element.43._), channel_id=1, source_target_pairs={{0,6},{1,7},{2,4},{3,5},{4,2},{5,3},{6,0},{7,1},{8,14},{9,15},{10,... | collective-permute-start | bytes 393224 | tf_op jit(solution)/shard_map/ppermute | solution.py:384
  59.0 20.2 %collective-permute-start.13 = (bf16[1,512,128]{2,1,0:T(8,128)(2,1)S(1)}, bf16[1,512,128]{2,1,0:T(8,128)(2,1)S(1)}, u32[]{:S(2)}, u32[]{:S(2)}) collective-permute-start(bf16[1,512,128]{2,1,0:T(8,128)(2,1)S(1)} %get-tuple-element.46._), channel_id=1, source_target_pairs={{0,2},{1,3},{2,0},{3,1},{4,6},{5,7},{6,4},{7,5},{8,10},{9,11},{10,... | collective-permute-start | bytes 393224 | tf_op jit(solution)/shard_map/ppermute | solution.py:384
  62.3 7.0 %collective-permute-start.18 = (bf16[1,4,6,32,128]{4,3,2,1,0:T(8,128)(2,1)S(1)}, bf16[1,4,6,32,128]{4,3,2,1,0:T(8,128)(2,1)S(1)}, u32[]{:S(2)}, u32[]{:S(2)}) collective-permute-start(bf16[1,4,6,32,128]{4,3,2,1,0:T(8,128)(2,1)S(1)} %get-tuple-element.48._), channel_id=1, source_target_pairs={{0,192},{8,200},{16,208},{24,216},{32,224},{40,232},{48,240},{56,2... | collective-permute-start | bytes 589832 | tf_op jit(solution)/shard_map/ppermute | solution.py:378
  64.5 5.8 %collective-permute-start.19 = (bf16[1,4,6,32,128]{4,3,2,1,0:T(8,128)(2,1)S(1)}, bf16[1,4,6,32,128]{4,3,2,1,0:T(8,128)(2,1)S(1)}, u32[]{:S(2)}, u32[]{:S(2)}) collective-permute-start(bf16[1,4,6,32,128]{4,3,2,1,0:T(8,128)(2,1)S(1)} %get-tuple-element.50._), channel_id=1, source_target_pairs={{0,64},{8,72},{16,80},{24,88},{32,96},{40,104},{48,112},{56,120},{... | collective-permute-start | bytes 589832 | tf_op jit(solution)/shard_map/ppermute | solution.py:378
  64.7 14.5 %collective-permute-start.17 = (bf16[1,512,128]{2,1,0:T(8,128)(2,1)S(1)}, bf16[1,512,128]{2,1,0:T(8,128)(2,1)S(1)}, u32[]{:S(2)}, u32[]{:S(2)}) collective-permute-start(bf16[1,512,128]{2,1,0:T(8,128)(2,1)S(1)} %add.19._), channel_id=1, source_target_pairs={{0,1},{1,0},{2,3},{3,2},{4,5},{5,4},{6,7},{7,6},{8,9},{9,8},{10,11... | collective-permute-start | bytes 393224 | tf_op jit(solution)/shard_map/ppermute | solution.py:418
  69.4 6.3 %collective-permute-start.20 = (bf16[2,6,32,128]{3,2,1,0:T(8,128)(2,1)S(1)}, bf16[2,6,32,128]{3,2,1,0:T(8,128)(2,1)S(1)}, u32[]{:S(2)}, u32[]{:S(2)}) collective-permute-start(bf16[2,6,32,128]{3,2,1,0:T(8,128)(2,1)S(1)} %get-tuple-element.53._), channel_id=1, source_target_pairs={{0,16},{8,24},{16,0},{24,8},{32,48},{40,56},{48,32},{56,40},{64,80... | collective-permute-start | bytes 294920 | tf_op jit(solution)/shard_map/ppermute | solution.py:381
  70.3 7.8 %collective-permute-start.22 = (bf16[2,6,32,128]{3,2,1,0:T(8,128)(2,1)S(1)}, bf16[2,6,32,128]{3,2,1,0:T(8,128)(2,1)S(1)}, u32[]{:S(2)}, u32[]{:S(2)}) collective-permute-start(bf16[2,6,32,128]{3,2,1,0:T(8,128)(2,1)S(1)} %get-tuple-element.55._), channel_id=1, source_target_pairs={{0,16},{8,24},{16,0},{24,8},{32,48},{40,56},{48,32},{56,40},{64,80... | collective-permute-start | bytes 294920 | tf_op jit(solution)/shard_map/ppermute | solution.py:381
  75.7 8.1 %collective-permute-start.21 = (bf16[1,6,32,128]{3,2,1,0:T(8,128)(2,1)S(1)}, bf16[1,6,32,128]{3,2,1,0:T(8,128)(2,1)S(1)}, u32[]{:S(2)}, u32[]{:S(2)}) collective-permute-start(bf16[1,6,32,128]{3,2,1,0:T(8,128)(2,1)S(1)} %get-tuple-element.58._), channel_id=1, source_target_pairs={{0,32},{8,40},{16,48},{24,56},{32,0},{40,8},{48,16},{56,24},{64,96... | collective-permute-start | bytes 147464 | tf_op jit(solution)/shard_map/ppermute | solution.py:381
  78.1 5.6 %collective-permute-start.23 = (bf16[1,6,32,128]{3,2,1,0:T(8,128)(2,1)S(1)}, bf16[1,6,32,128]{3,2,1,0:T(8,128)(2,1)S(1)}, u32[]{:S(2)}, u32[]{:S(2)}) collective-permute-start(bf16[1,6,32,128]{3,2,1,0:T(8,128)(2,1)S(1)} %get-tuple-element.61), channel_id=1, source_target_pairs={{0,32},{8,40},{16,48},{24,56},{32,0},{40,8},{48,16},{56,24},{64,96... | collective-permute-start | bytes 147464 | tf_op jit(solution)/shard_map/ppermute | solution.py:381

commit v9 on v8

--- a/solution.py
+++ b/solution.py
@@ -87,34 +87,6 @@
     )(after, filters)
 
 
-def prep_kernel(pos_ref, _, own_ref, r1_ref, r2_ref, r3_ref, r4_ref, stack_ref, held_ref, arrived):
-    copy = pltpu.make_async_copy(own_ref, held_ref, arrived)
-    copy.start()
-    parts = r1_ref, r2_ref, r3_ref, r4_ref
-    core = lax.rem(pos_ref[1], NCORE)
-    for s in range(1, stack_ref.shape[0]):
-        stack_ref[s] = jnp.where(core == 0, parts[s][...], parts[s - 1][...])
-    copy.wait()
-    stack_ref[0] = jnp.where(core == 0, r1_ref[...], held_ref[...])
-
-
-def for_sibling(pos, after, *parts):
-    block = parts[0].shape
-    vmem = pl.BlockSpec(memory_space=pltpu.VMEM)
-    return pl.pallas_call(
-        prep_kernel,
-        out_shape=jax.ShapeDtypeStruct((4,) + block, BF16),
-        in_specs=[pl.BlockSpec(memory_space=pltpu.SMEM)]
-        + [pl.BlockSpec(memory_space=pl.ANY)] * 2
-        + [vmem] * 4,
-        out_specs=vmem,
-        scratch_shapes=[pltpu.VMEM(block, BF16), pltpu.SemaphoreType.DMA],
-        compiler_params=pltpu.CompilerParams(vmem_limit_bytes=VMEM_LIMIT),
-        cost_estimate=SMALL_COST,
-        name="for_sibling",
-    )(pos, after, *parts)
-
-
 def pair_of_blocks(grad_ref, start, rows, width):
     first = grad_ref[pl.ds(start, width), :]
     second = grad_ref[pl.ds(start + rows, width), :]
@@ -127,17 +99,22 @@
     return x, z_hi, chip // NZ_LO, lax.rem(chip, NZ_LO), core
 
 
-def lay_out(grad_ref, refs):
-    tok = refs[0].shape[0]
-    for s, part in enumerate(refs):
-        grad_ref[s * tok : (s + 1) * tok, :] = part[...]
-
-
-def near_kernel(table_ref, own_ref, r1_ref, r2_ref, sib_ref, *refs):
+def lay_out(core, grad_ref, even_refs, odd_refs):
+    tok = even_refs[0].shape[0]
+    for s, part in enumerate(even_refs):
+        grad_ref[2 * s * tok : (2 * s + 1) * tok, :] = part[...]
+    for s in range(len(even_refs) - 1):
+        grad_ref[(2 * s + 1) * tok : (2 * s + 2) * tok, :] = jnp.where(
+            core == 0, odd_refs[s][...], odd_refs[s + 1][...]
+        )
+
+
+def near_kernel(pos_ref, table_ref, own_ref, r1_ref, r2_ref, s0_ref, s1_ref, s2_ref, *refs):
     acc_refs, grad_ref = refs[:-1], refs[-1]
     filt_count, rows, width = table_ref.shape
     tok = own_ref.shape[0]
-    lay_out(grad_ref, (own_ref, sib_ref.at[0], r1_ref, sib_ref.at[1], r2_ref))
+    core = lax.rem(pos_ref[1], NCORE)
+    lay_out(core, grad_ref, (own_ref, r1_ref, r2_ref), (s0_ref, s1_ref, s2_ref))
     table = table_ref[...].reshape(filt_count * rows, width)
 
     @pl.loop(0, tok // (2 * rows), unroll=True)
@@ -150,7 +127,7 @@
             acc_ref[pair] = result[group * part : (group + 1) * part]
 
 
-def near_conv(after, table, halo, sibling, groups):
+def near_conv(pos, table, halo, sibling, groups):
     filt_count, rows, width = table.shape
     tok = halo[0].shape[0]
     vmem = pl.BlockSpec(memory_space=pltpu.VMEM)
@@ -158,17 +135,17 @@
     return pl.pallas_call(
         near_kernel,
         out_shape=[acc] * groups,
-        in_specs=[pl.BlockSpec(memory_space=pl.ANY)] * len(after) + [vmem] * 5,
+        in_specs=[pl.BlockSpec(memory_space=pltpu.SMEM)] + [vmem] * 7,
         out_specs=[vmem] * groups,
         scratch_shapes=[pltpu.VMEM((5 * tok, LANE), BF16)],
         compiler_params=pltpu.CompilerParams(vmem_limit_bytes=VMEM_LIMIT),
         cost_estimate=LARGE_COST,
         name="near_conv",
-    )(*after, table, *halo, sibling)
+    )(pos, table, *halo, *sibling)
 
 
 def far_kernel(
-    first, _, filters_ref, acc_ref, r2_ref, r3_ref, r4_ref, sib_ref,
+    first, pos_ref, _, filters_ref, acc_ref, r2_ref, r3_ref, r4_ref, s2_ref, s3_ref, s4_ref,
     corr_ref, grad_ref, table_ref,
 ):
     filt_count, rows, width = table_ref.shape
@@ -178,7 +155,8 @@
     for k in range(filt_count):
         line = filters_ref[first + k : first + k + 1, start:].astype(F32)
         table_ref[k] = shifted_rows(jnp.concatenate([line, edge], axis=1), rows)[:, LANE:]
-    lay_out(grad_ref, (r2_ref, sib_ref.at[2], r3_ref, sib_ref.at[3], r4_ref))
+    core = lax.rem(pos_ref[1], NCORE)
+    lay_out(core, grad_ref, (r2_ref, r3_ref, r4_ref), (s2_ref, s3_ref, s4_ref))
     grad_ref[5 * tok :, :] = jnp.zeros((grad_ref.shape[0] - 5 * tok, LANE), BF16)
 
     @pl.loop(0, tok // (2 * rows), unroll=True)
@@ -195,14 +173,15 @@
                 ]
 
 
-def far_conv(first, count, after, filters, acc, halo, sibling):
+def far_conv(first, count, pos, after, filters, acc, halo, sibling):
     tok = halo[0].shape[0]
     width = filters.shape[1] // 2 + LANE
     vmem = pl.BlockSpec(memory_space=pltpu.VMEM)
     return pl.pallas_call(
         functools.partial(far_kernel, first),
         out_shape=jax.ShapeDtypeStruct((tok, count * LANE), BF16),
-        in_specs=[pl.BlockSpec(memory_space=pl.ANY)] + [vmem] * 6,
+        in_specs=[pl.BlockSpec(memory_space=pltpu.SMEM), pl.BlockSpec(memory_space=pl.ANY)]
+        + [vmem] * 8,
         out_specs=vmem,
         scratch_shapes=[
             pltpu.VMEM((5 * tok + ROWS, LANE), BF16),
@@ -211,7 +190,7 @@
         compiler_params=pltpu.CompilerParams(vmem_limit_bytes=VMEM_LIMIT),
         cost_estimate=SMALL_COST,
         name="far_conv",
-    )(after, filters, acc, *halo, sibling)
+    )(pos, after, filters, acc, *halo, *sibling)
 
 
 def product_kernel(
@@ -388,11 +367,13 @@
     gathered = [pair] + [lax.ppermute(pair, "tp", along_x(s)) for s in range(1, NX)]
     table = near_table(pair, filters)
     halo = [grad_out] + [later(grad_out, steps) for steps in range(1, 5)]
-    beside = sibling(for_sibling(pos, table, *halo))
-    accs = near_conv(gathered[1:1], table, halo[:3], beside, GROUPS)
+    beside = [sibling(part) for part in halo]
+    accs = near_conv(pos, table, halo[:3], beside[:3], GROUPS)
 
     def conv(group, after):
-        return far_conv(group * count, count, after, filters, accs[group], halo[2:], beside)
+        return far_conv(
+            group * count, count, pos, after, filters, accs[group], halo[2:], beside[2:]
+        )
 
     corr_0 = conv(0, table)
     corr_1 = conv(1, corr_0)

time: 84.8 us -> 85.8 us (1.012); the launches traced: 84.4 us -> 84.5 us
  waiting for transfers between devices: 19.8 us -> 15.6 us
  starting transfers between devices: 44.1 us -> 47.5 us
  Pallas kernels: 17 us -> 17.9 us
    ppermute x4, starting transfers between devices: 5.51 us -> 9.76 us  [z_swapped(): return lax.ppermute(value, 'ctx', z_swap(bit))]
    ppermute x4, waiting for transfers between devices: 6.71 us -> 3.26 us  [y_swapped(): return lax.ppermute(value, 'ctx', y_swap(crossed))]
    ppermute x4, starting transfers between devices: 2.47 us -> 5.67 us  [y_swapped(): return lax.ppermute(value, 'ctx', y_swap(crossed))]
    ppermute x4, starting transfers between devices: 6.03 us -> 2.95 us  [x_swapped(): return lax.ppermute(value, 'tp', x_swap(crossed))]
    ppermute x4, starting transfers between devices: 13.4 us -> 11.6 us  [later(): return lax.ppermute(value, 'ctx', from_later_chip(steps))]
    ppermute x4, waiting for transfers between devices: 2.57 us -> 3.97 us  [x_swapped(): return lax.ppermute(value, 'tp', x_swap(crossed))]
    pallas_call x2, Pallas kernels: 4.16 us -> 5.29 us  [far_conv(): pl.pallas_call(functools.partial(far_kernel, first), out_shape=jax.ShapeD...]
    ppermute x4, waiting for transfers between devices: 7.85 us -> 6.8 us  [z_swapped(): return lax.ppermute(value, 'ctx', z_swap(bit))]
  transfers between devices with their start and end apart: 24 -> 28, of which waited for: 9 -> 8; matrix products, arithmetic and copies ran while one was open for 2% -> 2% of each run, Pallas kernels for 16% -> 18%
where the time goes in v9:
time: 85.8 us; the launch traced here: 84.5 us
  starting transfers between devices  47.5 us (55%)
  Pallas kernels  17.9 us (21%)
  waiting for transfers between devices  15.6 us (18%)
  other arithmetic  1.71 us (2%)
  local copies, waits for them, and re-layouts  0.91 us (1%)
  between operations  0.9 us (1%)
    ppermute x4, starting transfers between devices, later(): return lax.ppermute(value, 'ctx', from_later_chip(steps))  11.6 us
    ppermute x4, starting transfers between devices, z_swapped(): return lax.ppermute(value, 'ctx', z_swap(bit))  9.76 us
    ppermute x1, starting transfers between devices, per_device(): pair = jnp.stack([inputs, lax.ppermute(inputs, 'tp', Z_HI_SWAP)])  7.28 us
    ppermute x4, waiting for transfers between devices, z_swapped(): return lax.ppermute(value, 'ctx', z_swap(bit))  6.8 us
    ppermute x3, starting transfers between devices, per_device(): lax.ppermute(pair, 'tp', along_x(s))  5.73 us
    ppermute x4, starting transfers between devices, y_swapped(): return lax.ppermute(value, 'ctx', y_swap(crossed))  5.67 us
    pallas_call x2, Pallas kernels, far_conv(): pl.pallas_call(functools.partial(far_kernel, first), out_shape=jax.ShapeD...  5.29 us
    pallas_call x1, Pallas kernels, near_conv(): pl.pallas_call(near_kernel, out_shape=[acc] * groups, in_specs=[pl.BlockS...  4 us
  transfers between devices with their start and end apart: 28, of which 8 were waited for; matrix products, arithmetic and copies ran while one was open for 2% of the time, Pallas kernels for 18%

profile of v9, /device:TPU:24, one launch (start us, length us, event | category | flops | bytes accessed | tf_op | source)
XLA Modules:
  0.0 84.5 jit_solution(5678917500707009814)
XLA Ops:
  0.6 7.3 %collective-permute-start = (bf16[512,128]{1,0:T(8,128)(2,1)}, bf16[512,128]{1,0:T(8,128)(2,1)S(1)}, u32[]{:S(2)}, u32[]{:S(2)}) collective-permute-start(bf16[512,128]{1,0:T(8,128)(2,1)} %param.4), channel_id=1, source_target_pairs={{0,1},{1,0},{2,3},{3,2},{4,5},{5,4},{6,7},{7,6},{8,9},{9,8},{10,11... | collective-permute-start | bytes 393224 | tf_op jit(solution)/shard_map/ppermute | solution.py:366
  7.9 3.5 %collective-permute-start.2 = (bf16[512,128]{1,0:T(8,128)(2,1)}, bf16[512,128]{1,0:T(8,128)(2,1)S(1)}, u32[]{:S(2)}, u32[]{:S(2)}) collective-permute-start(bf16[512,128]{1,0:T(8,128)(2,1)} %own_ref.1), channel_id=1, source_target_pairs={{32,0},{40,8},{48,16},{56,24},{64,32},{72,40},{80,48},{88,56},{96,... | collective-permute-start | bytes 393224 | tf_op jit(solution)/shard_map/ppermute | solution.py:351
  11.5 3.8 %collective-permute-start.1 = (bf16[512,128]{1,0:T(8,128)(2,1)}, bf16[512,128]{1,0:T(8,128)(2,1)S(1)}, u32[]{:S(2)}, u32[]{:S(2)}) collective-permute-start(bf16[512,128]{1,0:T(8,128)(2,1)} %own_ref.1), channel_id=1, source_target_pairs={{16,0},{24,8},{32,16},{40,24},{48,32},{56,40},{64,48},{72,56},{80,... | collective-permute-start | bytes 393224 | tf_op jit(solution)/shard_map/ppermute | solution.py:351
  15.3 0.1 collective-permute-start.3
  15.4 1.9 %collective-permute-start.6 = (bf16[512,128]{1,0:T(8,128)(2,1)}, bf16[512,128]{1,0:T(8,128)(2,1)S(1)}, u32[]{:S(2)}, u32[]{:S(2)}) collective-permute-start(bf16[512,128]{1,0:T(8,128)(2,1)} %own_ref.1), channel_id=1, source_target_pairs={{48,0},{56,8},{64,16},{72,24},{80,32},{88,40},{96,48},{104,56},{11... | collective-permute-start | bytes 393224 | tf_op jit(solution)/shard_map/ppermute | solution.py:351
  17.3 0.0 collective-permute-done
  17.3 2.4 %collective-permute-start.7 = (bf16[512,128]{1,0:T(8,128)(2,1)}, bf16[512,128]{1,0:T(8,128)(2,1)S(1)}, u32[]{:S(2)}, u32[]{:S(2)}) collective-permute-start(bf16[512,128]{1,0:T(8,128)(2,1)} %own_ref.1), channel_id=1, source_target_pairs={{64,0},{72,8},{80,16},{88,24},{96,32},{104,40},{112,48},{120,56},{... | collective-permute-start | bytes 393224 | tf_op jit(solution)/shard_map/ppermute | solution.py:351
  19.7 1.0 %collective-permute-done.2.r2_ref = bf16[512,128]{1,0:T(8,128)(2,1)S(1)} collective-permute-done((bf16[512,128]{1,0:T(8,128)(2,1)}, bf16[512,128]{1,0:T(8,128)(2,1)S(1)}, u32[]{:S(2)}, u32[]{:S(2)}) %collective-permute-start.2) | collective-permute-done | bytes 131104 | tf_op jit(solution)/shard_map/ppermute | solution.py:351
  20.7 0.6 collective-permute-done.1.r1_ref
  21.3 0.1 pad_add_fusion.pos_ref
  21.3 0.9 %pad_maximum_fusion._.x0_ref = bf16[2,512,128]{2,1,0:T(8,128)(2,1)S(1)} fusion(bf16[1,512,128]{2,1,0:T(8,128)(2,1)S(1)} %bitcast.19, bf16[1,512,128]{2,1,0:T(8,128)(2,1)} %bitcast.18), kind=kLoop, calls=%fused_computation | loop fusion | flops 131072 | bytes 524288 | tf_op jit(solution)/shard_map/stack | solution.py:366
  22.3 0.0 copy-start.1
  22.3 0.9 %copy-done.1 = bf16[12,4096]{1,0:T(8,128)(2,1)S(1)} copy-done((bf16[12,4096]{1,0:T(8,128)(2,1)S(1)}, bf16[12,4096]{1,0:T(8,128)(2,1)}, u32[]{:S(2)}) %copy-start.1) | copy-done | bytes 98328
  23.2 0.9 %near_table.1.table_ref._ = bf16[12,64,2048]{2,1,0:T(8,128)(2,1)S(1)} custom-call(bf16[2,512,128]{2,1,0:T(8,128)(2,1)S(1)} %pad_maximum_fusion._.x0_ref, bf16[12,4096]{1,0:T(8,128)(2,1)S(1)} %copy-done.1), custom_call_target="tpu_custom_call" | custom-call | flops 1000 | bytes 1000 | tf_op jit(solution)/shard_map/near_table/pallas_call | solution.py:79
  24.1 1.6 %collective-permute-start.10 = (bf16[2,512,128]{2,1,0:T(8,128)(2,1)S(1)}, bf16[2,512,128]{2,1,0:T(8,128)(2,1)S(1)}, u32[]{:S(2)}, u32[]{:S(2)}) collective-permute-start(bf16[2,512,128]{2,1,0:T(8,128)(2,1)S(1)} %pad_maximum_fusion._.x0_ref), channel_id=1, source_target_pairs={{0,2},{1,3},{2,4},{3,5},{4,6},{5,7},{6,0},{7,1},{8,10},{9,11},{10,... | collective-permute-start | bytes 786440 | tf_op jit(solution)/shard_map/ppermute | solution.py:367
  25.7 0.0 collective-permute-done.6.r3_ref
  25.7 2.7 %collective-permute-start.11 = (bf16[2,512,128]{2,1,0:T(8,128)(2,1)S(1)}, bf16[2,512,128]{2,1,0:T(8,128)(2,1)S(1)}, u32[]{:S(2)}, u32[]{:S(2)}) collective-permute-start(bf16[2,512,128]{2,1,0:T(8,128)(2,1)S(1)} %pad_maximum_fusion._.x0_ref), channel_id=1, source_target_pairs={{0,4},{1,5},{2,6},{3,7},{4,0},{5,1},{6,2},{7,3},{8,12},{9,13},{10,... | collective-permute-start | bytes 786440 | tf_op jit(solution)/shard_map/ppermute | solution.py:367
  28.4 1.4 %collective-permute-start.12 = (bf16[2,512,128]{2,1,0:T(8,128)(2,1)S(1)}, bf16[2,512,128]{2,1,0:T(8,128)(2,1)S(1)}, u32[]{:S(2)}, u32[]{:S(2)}) collective-permute-start(bf16[2,512,128]{2,1,0:T(8,128)(2,1)S(1)} %pad_maximum_fusion._.x0_ref), channel_id=1, source_target_pairs={{0,6},{1,7},{2,0},{3,1},{4,2},{5,3},{6,4},{7,5},{8,14},{9,15},{10,... | collective-permute-start | bytes 786440 | tf_op jit(solution)/shard_map/ppermute | solution.py:367
  29.8 0.0 collective-permute-start.8
  29.9 0.0 collective-permute-done.4.s1_ref
  29.9 0.5 collective-permute-start.9
  30.4 4.0 %near_conv.1 = (f32[4,384,256]{2,1,0:T(8,128)S(1)}, f32[4,384,256]{2,1,0:T(8,128)S(1)}) custom-call(s32[2]{0:T(128)S(1)} %pad_add_fusion.pos_ref, bf16[12,64,2048]{2,1,0:T(8,128)(2,1)S(1)} %near_table.1.table_ref._, bf16[512,128]{1,0:T(8,128)(2,1)S(1)} %copy-done.2, bf16[512,128]{1,0:T(8,128)(2,1)S(1)} %collective-permute-done.1.r1_ref, ...), custom_call_target="tpu_custom_call" | custom-call | flops 4000000000 | bytes 8000000 | tf_op jit(solution)/shard_map/near_conv/pallas_call | solution.py:135
  34.4 0.0 collective-permute-done.9.s4_ref
  34.4 2.6 %far_conv.2._.refs_0_.corr_ref = bf16[512,768]{1,0:T(8,128)(2,1)S(1)} custom-call(s32[2]{0:T(128)S(1)} %pad_add_fusion.pos_ref, bf16[12,64,2048]{2,1,0:T(8,128)(2,1)S(1)} %near_table.1.table_ref._, bf16[12,4096]{1,0:T(8,128)(2,1)S(1)} %copy-done.1, f32[4,384,256]{2,1,0:T(8,128)S(1)} %get-tuple-element.32.acc_ref, ...), custom_call_target="tpu_custom_call" | custom-call | flops 1000 | bytes 1000 | tf_op jit(solution)/shard_map/far_conv/pallas_call | solution.py:180
  37.0 0.0 copy-start
  37.1 2.6 %far_conv.3._.refs_1_.corr_ref = bf16[512,768]{1,0:T(8,128)(2,1)S(1)} custom-call(s32[2]{0:T(128)S(1)} %pad_add_fusion.pos_ref, bf16[512,768]{1,0:T(8,128)(2,1)S(1)} %far_conv.2._.refs_0_.corr_ref, bf16[12,4096]{1,0:T(8,128)(2,1)S(1)} %copy-done.1, f32[4,384,256]{2,1,0:T(8,128)S(1)} %get-tuple-element.33.acc_ref, ...), custom_call_target="tpu_custom_call" | custom-call | flops 1000 | bytes 1000 | tf_op jit(solution)/shard_map/far_conv/pallas_call | solution.py:180
  39.7 2.4 %input_shares.1 = (f32[2,512,128]{2,1,0:T(8,128)S(1)}, bf16[2,512,128]{2,1,0:T(8,128)(2,1)S(1)}, f32[2,512,128]{2,1,0:T(8,128)S(1)}, bf16[2,512,128]{2,1,0:T(8,128)(2,1)S(1)}) custom-call(s32[2]{0:T(128)S(1)} %pad_add_fusion.pos_ref, bf16[512,768]{1,0:T(8,128)(2,1)S(1)} %far_conv.3._.refs_1_.corr_ref, bf16[512,768]{1,0:T(8,128)(2,1)S(1)} %far_conv.2._.refs_0_.corr_ref, ...), custom_call_target="tpu_custom_call" | custom-call | flops 1000 | bytes 1000 | tf_op jit(solution)/shard_map/input_shares/pallas_call | solution.py:330
  42.1 0.0 collective-permute-done.11.x2_ref
  42.1 0.0 collective-permute-done.12.x3_ref
  42.1 1.9 %product.2 = (bf16[4,4,6,32,128]{4,3,2,1,0:T(8,128)(2,1)S(1)}, bf16[4,4,6,32,128]{4,3,2,1,0:T(8,128)(2,1)S(1)}) custom-call(s32[2]{0:T(128)S(1)} %pad_add_fusion.pos_ref, bf16[2,512,128]{2,1,0:T(8,128)(2,1)S(1)} %get-tuple-element.34._, bf16[512,768]{1,0:T(8,128)(2,1)S(1)} %far_conv.2._.refs_0_.corr_ref, bf16[2,512,128]{2,1,0:T(8,128)(2,1)S(1)} %pad_maximum_fusion._.x0_ref, ...), custom_call_target="tpu_custom_call" | custom-call | flops 1000 | bytes 1000 | tf_op jit(solution)/shard_map/product/pallas_call | solution.py:226
  44.1 0.4 collective-permute-start.13
  44.4 1.9 %product.3 = (bf16[4,4,6,32,128]{4,3,2,1,0:T(8,128)(2,1)S(1)}, bf16[4,4,6,32,128]{4,3,2,1,0:T(8,128)(2,1)S(1)}) custom-call(s32[2]{0:T(128)S(1)} %pad_add_fusion.pos_ref, bf16[4,4,6,32,128]{4,3,2,1,0:T(8,128)(2,1)S(1)} %get-tuple-element.35._, bf16[512,768]{1,0:T(8,128)(2,1)S(1)} %far_conv.3._.refs_1_.corr_ref, ...), custom_call_target="tpu_custom_call" | custom-call | flops 1000 | bytes 1000 | tf_op jit(solution)/shard_map/product/pallas_call | solution.py:226
  46.4 0.3 collective-permute-start.14
  46.7 0.6 collective-permute-start.15
  47.3 1.2 %collective-permute-start.16 = (bf16[2,512,128]{2,1,0:T(8,128)(2,1)S(1)}, bf16[2,512,128]{2,1,0:T(8,128)(2,1)S(1)}, u32[]{:S(2)}, u32[]{:S(2)}) collective-permute-start(bf16[2,512,128]{2,1,0:T(8,128)(2,1)S(1)} %get-tuple-element.34._), channel_id=1, source_target_pairs={{0,6},{1,7},{2,4},{3,5},{4,2},{5,3},{6,0},{7,1},{8,14},{9,15},{10,... | collective-permute-start | bytes 786440 | tf_op jit(solution)/shard_map/ppermute | solution.py:363
  48.5 0.0 collective-permute-done.13.other_ref
  48.5 0.2 halve.10
  48.7 0.6 collective-permute-start.18
  49.2 0.2 halve.11
  49.4 2.4 %collective-permute-start.19 = (bf16[2,4,6,32,128]{4,3,2,1,0:T(8,128)(2,1)S(1)}, bf16[2,4,6,32,128]{4,3,2,1,0:T(8,128)(2,1)S(1)}, u32[]{:S(2)}, u32[]{:S(2)}) collective-permute-start(bf16[2,4,6,32,128]{4,3,2,1,0:T(8,128)(2,1)S(1)} %get-tuple-element.40._), channel_id=1, source_target_pairs={{0,192},{8,200},{16,208},{24,216},{32,224},{40,232},{48,240},{56,2... | collective-permute-start | bytes 1179656 | tf_op jit(solution)/shard_map/ppermute | solution.py:357
  51.8 3.3 %collective-permute-done.15.other_ref = bf16[2,512,128]{2,1,0:T(8,128)(2,1)S(1)} collective-permute-done((bf16[2,512,128]{2,1,0:T(8,128)(2,1)S(1)}, bf16[2,512,128]{2,1,0:T(8,128)(2,1)S(1)}, u32[]{:S(2)}, u32[]{:S(2)}) %collective-permute-start.15) | collective-permute-done | bytes 262176 | tf_op jit(solution)/shard_map/ppermute | solution.py:363
  55.2 0.1 halve.12
  55.3 0.8 collective-permute-start.20
  56.1 0.6 collective-permute-done.16.other_ref
  56.7 0.1 halve.13
  56.8 0.3 collective-permute-start.17
  57.1 2.3 %collective-permute-done.18.other_ref = bf16[2,4,6,32,128]{4,3,2,1,0:T(8,128)(2,1)S(1)} collective-permute-done((bf16[2,4,6,32,128]{4,3,2,1,0:T(8,128)(2,1)S(1)}, bf16[2,4,6,32,128]{4,3,2,1,0:T(8,128)(2,1)S(1)}, u32[]{:S(2)}, u32[]{:S(2)}) %collective-permute-start.18) | collective-permute-done | bytes 393248 | tf_op jit(solution)/shard_map/ppermute | solution.py:357
  59.4 0.1 halve.14
  59.5 2.6 %collective-permute-start.22 = (bf16[1,4,6,32,128]{4,3,2,1,0:T(8,128)(2,1)S(1)}, bf16[1,4,6,32,128]{4,3,2,1,0:T(8,128)(2,1)S(1)}, u32[]{:S(2)}, u32[]{:S(2)}) collective-permute-start(bf16[1,4,6,32,128]{4,3,2,1,0:T(8,128)(2,1)S(1)} %get-tuple-element.48._), channel_id=1, source_target_pairs={{0,192},{8,200},{16,208},{24,216},{32,224},{40,232},{48,240},{56,2... | collective-permute-start | bytes 589832 | tf_op jit(solution)/shard_map/ppermute | solution.py:357
  62.1 0.1 halve.15
  62.1 0.1 collective-permute-start.23
  62.2 0.0 collective-permute-done.20.other_ref
  62.3 3.2 %collective-permute-start.21 = (bf16[1,512,128]{2,1,0:T(8,128)(2,1)S(1)}, bf16[1,512,128]{2,1,0:T(8,128)(2,1)S(1)}, u32[]{:S(2)}, u32[]{:S(2)}) collective-permute-start(bf16[1,512,128]{2,1,0:T(8,128)(2,1)S(1)} %add.19._), channel_id=1, source_target_pairs={{0,1},{1,0},{2,3},{3,2},{4,5},{5,4},{6,7},{7,6},{8,9},{9,8},{10,11... | collective-permute-start | bytes 393224 | tf_op jit(solution)/shard_map/ppermute | solution.py:399
  65.5 0.9 %collective-permute-done.22 = bf16[1,4,6,32,128]{4,3,2,1,0:T(8,128)(2,1)S(1)} collective-permute-done((bf16[1,4,6,32,128]{4,3,2,1,0:T(8,128)(2,1)S(1)}, bf16[1,4,6,32,128]{4,3,2,1,0:T(8,128)(2,1)S(1)}, u32[]{:S(2)}, u32[]{:S(2)}) %collective-permute-start.22) | collective-permute-done | bytes 196640 | tf_op jit(solution)/shard_map/ppermute | solution.py:357
  66.5 5.5 %collective-permute-start.24 = (bf16[2,6,32,128]{3,2,1,0:T(8,128)(2,1)S(1)}, bf16[2,6,32,128]{3,2,1,0:T(8,128)(2,1)S(1)}, u32[]{:S(2)}, u32[]{:S(2)}) collective-permute-start(bf16[2,6,32,128]{3,2,1,0:T(8,128)(2,1)S(1)} %get-tuple-element.53._), channel_id=1, source_target_pairs={{0,16},{8,24},{16,0},{24,8},{32,48},{40,56},{48,32},{56,40},{64,80... | collective-permute-start | bytes 294920 | tf_op jit(solution)/shard_map/ppermute | solution.py:360
  72.0 0.0 collective-permute-done.23
  72.1 1.1 %collective-permute-start.26 = (bf16[2,6,32,128]{3,2,1,0:T(8,128)(2,1)S(1)}, bf16[2,6,32,128]{3,2,1,0:T(8,128)(2,1)S(1)}, u32[]{:S(2)}, u32[]{:S(2)}) collective-permute-start(bf16[2,6,32,128]{3,2,1,0:T(8,128)(2,1)S(1)} %get-tuple-element.55._), channel_id=1, source_target_pairs={{0,16},{8,24},{16,0},{24,8},{32,48},{40,56},{48,32},{56,40},{64,80... | collective-permute-start | bytes 294920 | tf_op jit(solution)/shard_map/ppermute | solution.py:360
  73.2 4.4 %collective-permute-done.24.other_ref = bf16[2,6,32,128]{3,2,1,0:T(8,128)(2,1)S(1)} collective-permute-done((bf16[2,6,32,128]{3,2,1,0:T(8,128)(2,1)S(1)}, bf16[2,6,32,128]{3,2,1,0:T(8,128)(2,1)S(1)}, u32[]{:S(2)}, u32[]{:S(2)}) %collective-permute-start.24) | collective-permute-done | bytes 98336 | tf_op jit(solution)/shard_map/ppermute | solution.py:360
  77.6 1.0 %collective-permute-start.25 = (bf16[1,6,32,128]{3,2,1,0:T(8,128)(2,1)S(1)}, bf16[1,6,32,128]{3,2,1,0:T(8,128)(2,1)S(1)}, u32[]{:S(2)}, u32[]{:S(2)}) collective-permute-start(bf16[1,6,32,128]{3,2,1,0:T(8,128)(2,1)S(1)} %get-tuple-element.58._), channel_id=1, source_target_pairs={{0,32},{8,40},{16,48},{24,56},{32,0},{40,8},{48,16},{56,24},{64,96... | collective-permute-start | bytes 147464 | tf_op jit(solution)/shard_map/ppermute | solution.py:360
  78.6 0.0 collective-permute-done.26.other_ref
  78.6 2.1 %collective-permute-start.27 = (bf16[1,6,32,128]{3,2,1,0:T(8,128)(2,1)S(1)}, bf16[1,6,32,128]{3,2,1,0:T(8,128)(2,1)S(1)}, u32[]{:S(2)}, u32[]{:S(2)}) collective-permute-start(bf16[1,6,32,128]{3,2,1,0:T(8,128)(2,1)S(1)} %get-tuple-element.61), channel_id=1, source_target_pairs={{0,32},{8,40},{16,48},{24,56},{32,0},{40,8},{48,16},{56,24},{64,96... | collective-permute-start | bytes 147464 | tf_op jit(solution)/shard_map/ppermute | solution.py:360
  80.7 0.7 fusion
  81.4 2.4 %collective-permute-done.27.refs_3_ = bf16[1,6,32,128]{3,2,1,0:T(8,128)(2,1)S(1)} collective-permute-done((bf16[1,6,32,128]{3,2,1,0:T(8,128)(2,1)S(1)}, bf16[1,6,32,128]{3,2,1,0:T(8,128)(2,1)S(1)}, u32[]{:S(2)}, u32[]{:S(2)}) %collective-permute-start.27) | collective-permute-done | bytes 49184 | tf_op jit(solution)/shard_map/ppermute | solution.py:360
  83.8 0.7 join.1
  (20 shorter events, 0.2 us)
Async XLA Ops:
  0.6 29.7 %copy-start.2 = (bf16[512,128]{1,0:T(8,128)(2,1)S(1)}, bf16[512,128]{1,0:T(8,128)(2,1)}, u32[]{:S(2)}) copy-start(bf16[512,128]{1,0:T(8,128)(2,1)} %own_ref.1) | copy-start | bytes 393220
  0.6 16.7 %collective-permute-start = (bf16[512,128]{1,0:T(8,128)(2,1)}, bf16[512,128]{1,0:T(8,128)(2,1)S(1)}, u32[]{:S(2)}, u32[]{:S(2)}) collective-permute-start(bf16[512,128]{1,0:T(8,128)(2,1)} %param.4), channel_id=1, source_target_pairs={{0,1},{1,0},{2,3},{3,2},{4,5},{5,4},{6,7},{7,6},{8,9},{9,8},{10,11... | collective-permute-start | bytes 393224 | tf_op jit(solution)/shard_map/ppermute | solution.py:366
  7.9 12.8 %collective-permute-start.2 = (bf16[512,128]{1,0:T(8,128)(2,1)}, bf16[512,128]{1,0:T(8,128)(2,1)S(1)}, u32[]{:S(2)}, u32[]{:S(2)}) collective-permute-start(bf16[512,128]{1,0:T(8,128)(2,1)} %own_ref.1), channel_id=1, source_target_pairs={{32,0},{40,8},{48,16},{56,24},{64,32},{72,40},{80,48},{88,56},{96,... | collective-permute-start | bytes 393224 | tf_op jit(solution)/shard_map/ppermute | solution.py:351
  11.5 9.8 %collective-permute-start.1 = (bf16[512,128]{1,0:T(8,128)(2,1)}, bf16[512,128]{1,0:T(8,128)(2,1)S(1)}, u32[]{:S(2)}, u32[]{:S(2)}) collective-permute-start(bf16[512,128]{1,0:T(8,128)(2,1)} %own_ref.1), channel_id=1, source_target_pairs={{16,0},{24,8},{32,16},{40,24},{48,32},{56,40},{64,48},{72,56},{80,... | collective-permute-start | bytes 393224 | tf_op jit(solution)/shard_map/ppermute | solution.py:351
  15.3 8.8 %collective-permute-start.3 = (bf16[512,128]{1,0:T(8,128)(2,1)}, bf16[512,128]{1,0:T(8,128)(2,1)S(1)}, u32[]{:S(2)}, u32[]{:S(2)}) collective-permute-start(bf16[512,128]{1,0:T(8,128)(2,1)} %own_ref.1), channel_id=1, source_target_pairs={{0,8},{8,0},{16,24},{24,16},{32,40},{40,32},{48,56},{56,48},{64,72... | collective-permute-start | bytes 393224 | tf_op jit(solution)/shard_map/ppermute | solution.py:354
  15.4 10.3 %collective-permute-start.6 = (bf16[512,128]{1,0:T(8,128)(2,1)}, bf16[512,128]{1,0:T(8,128)(2,1)S(1)}, u32[]{:S(2)}, u32[]{:S(2)}) collective-permute-start(bf16[512,128]{1,0:T(8,128)(2,1)} %own_ref.1), channel_id=1, source_target_pairs={{48,0},{56,8},{64,16},{72,24},{80,32},{88,40},{96,48},{104,56},{11... | collective-permute-start | bytes 393224 | tf_op jit(solution)/shard_map/ppermute | solution.py:351
  17.3 11.1 %collective-permute-start.7 = (bf16[512,128]{1,0:T(8,128)(2,1)}, bf16[512,128]{1,0:T(8,128)(2,1)S(1)}, u32[]{:S(2)}, u32[]{:S(2)}) collective-permute-start(bf16[512,128]{1,0:T(8,128)(2,1)} %own_ref.1), channel_id=1, source_target_pairs={{64,0},{72,8},{80,16},{88,24},{96,32},{104,40},{112,48},{120,56},{... | collective-permute-start | bytes 393224 | tf_op jit(solution)/shard_map/ppermute | solution.py:351
  20.7 9.2 %collective-permute-start.5 = (bf16[512,128]{1,0:T(8,128)(2,1)S(1)}, bf16[512,128]{1,0:T(8,128)(2,1)S(1)}, u32[]{:S(2)}, u32[]{:S(2)}) collective-permute-start(bf16[512,128]{1,0:T(8,128)(2,1)S(1)} %collective-permute-done.2.r2_ref), channel_id=1, source_target_pairs={{0,8},{8,0},{16,24},{24,16},{32,40},{40,32},{48,56},{56,48},{64,72... | collective-permute-start | bytes 393224 | tf_op jit(solution)/shard_map/ppermute | solution.py:354
  21.3 8.6 %collective-permute-start.4 = (bf16[512,128]{1,0:T(8,128)(2,1)S(1)}, bf16[512,128]{1,0:T(8,128)(2,1)S(1)}, u32[]{:S(2)}, u32[]{:S(2)}) collective-permute-start(bf16[512,128]{1,0:T(8,128)(2,1)S(1)} %collective-permute-done.1.r1_ref), channel_id=1, source_target_pairs={{0,8},{8,0},{16,24},{24,16},{32,40},{40,32},{48,56},{56,48},{64,72... | collective-permute-start | bytes 393224 | tf_op jit(solution)/shard_map/ppermute | solution.py:354
  22.3 0.9 %copy-start.1 = (bf16[12,4096]{1,0:T(8,128)(2,1)S(1)}, bf16[12,4096]{1,0:T(8,128)(2,1)}, u32[]{:S(2)}) copy-start(bf16[12,4096]{1,0:T(8,128)(2,1)} %filters_ref.5) | copy-start | bytes 294916
  24.1 18.0 %collective-permute-start.10 = (bf16[2,512,128]{2,1,0:T(8,128)(2,1)S(1)}, bf16[2,512,128]{2,1,0:T(8,128)(2,1)S(1)}, u32[]{:S(2)}, u32[]{:S(2)}) collective-permute-start(bf16[2,512,128]{2,1,0:T(8,128)(2,1)S(1)} %pad_maximum_fusion._.x0_ref), channel_id=1, source_target_pairs={{0,2},{1,3},{2,4},{3,5},{4,6},{5,7},{6,0},{7,1},{8,10},{9,11},{10,... | collective-permute-start | bytes 786440 | tf_op jit(solution)/shard_map/ppermute | solution.py:367
  25.7 16.4 %collective-permute-start.11 = (bf16[2,512,128]{2,1,0:T(8,128)(2,1)S(1)}, bf16[2,512,128]{2,1,0:T(8,128)(2,1)S(1)}, u32[]{:S(2)}, u32[]{:S(2)}) collective-permute-start(bf16[2,512,128]{2,1,0:T(8,128)(2,1)S(1)} %pad_maximum_fusion._.x0_ref), channel_id=1, source_target_pairs={{0,4},{1,5},{2,6},{3,7},{4,0},{5,1},{6,2},{7,3},{8,12},{9,13},{10,... | collective-permute-start | bytes 786440 | tf_op jit(solution)/shard_map/ppermute | solution.py:367
  28.4 13.7 %collective-permute-start.12 = (bf16[2,512,128]{2,1,0:T(8,128)(2,1)S(1)}, bf16[2,512,128]{2,1,0:T(8,128)(2,1)S(1)}, u32[]{:S(2)}, u32[]{:S(2)}) collective-permute-start(bf16[2,512,128]{2,1,0:T(8,128)(2,1)S(1)} %pad_maximum_fusion._.x0_ref), channel_id=1, source_target_pairs={{0,6},{1,7},{2,0},{3,1},{4,2},{5,3},{6,4},{7,5},{8,14},{9,15},{10,... | collective-permute-start | bytes 786440 | tf_op jit(solution)/shard_map/ppermute | solution.py:367
  29.8 4.5 %collective-permute-start.8 = (bf16[512,128]{1,0:T(8,128)(2,1)S(1)}, bf16[512,128]{1,0:T(8,128)(2,1)S(1)}, u32[]{:S(2)}, u32[]{:S(2)}) collective-permute-start(bf16[512,128]{1,0:T(8,128)(2,1)S(1)} %collective-permute-done.6.r3_ref), channel_id=1, source_target_pairs={{0,8},{8,0},{16,24},{24,16},{32,40},{40,32},{48,56},{56,48},{64,72... | collective-permute-start | bytes 393224 | tf_op jit(solution)/shard_map/ppermute | solution.py:354
  29.9 4.5 %collective-permute-start.9 = (bf16[512,128]{1,0:T(8,128)(2,1)S(1)}, bf16[512,128]{1,0:T(8,128)(2,1)S(1)}, u32[]{:S(2)}, u32[]{:S(2)}) collective-permute-start(bf16[512,128]{1,0:T(8,128)(2,1)S(1)} %collective-permute-done.7.r4_ref), channel_id=1, source_target_pairs={{0,8},{8,0},{16,24},{24,16},{32,40},{40,32},{48,56},{56,48},{64,72... | collective-permute-start | bytes 393224 | tf_op jit(solution)/shard_map/ppermute | solution.py:354
  37.0 2.7 %copy-start = (bf16[1024,12,128]{2,0,1:T(8,128)(2,1)S(1)}, bf16[1024,12,128]{2,0,1:T(8,128)(2,1)}, u32[]{:S(2)}) copy-start(bf16[1024,12,128]{2,0,1:T(8,128)(2,1)} %param.7) | copy-start | bytes 9437188
  44.1 4.4 %collective-permute-start.13 = (bf16[4,4,6,32,128]{4,3,2,1,0:T(8,128)(2,1)S(1)}, bf16[4,4,6,32,128]{4,3,2,1,0:T(8,128)(2,1)S(1)}, u32[]{:S(2)}, u32[]{:S(2)}) collective-permute-start(bf16[4,4,6,32,128]{4,3,2,1,0:T(8,128)(2,1)S(1)} %get-tuple-element.35._), channel_id=1, source_target_pairs={{0,8},{8,0},{16,24},{24,16},{32,40},{40,32},{48,56},{56,48},{64,72... | collective-permute-start | bytes 2359304 | tf_op jit(solution)/shard_map/ppermute | solution.py:354
  46.4 2.9 %collective-permute-start.14 = (bf16[4,4,6,32,128]{4,3,2,1,0:T(8,128)(2,1)S(1)}, bf16[4,4,6,32,128]{4,3,2,1,0:T(8,128)(2,1)S(1)}, u32[]{:S(2)}, u32[]{:S(2)}) collective-permute-start(bf16[4,4,6,32,128]{4,3,2,1,0:T(8,128)(2,1)S(1)} %get-tuple-element.36._), channel_id=1, source_target_pairs={{0,8},{8,0},{16,24},{24,16},{32,40},{40,32},{48,56},{56,48},{64,72... | collective-permute-start | bytes 2359304 | tf_op jit(solution)/shard_map/ppermute | solution.py:354
  46.7 8.5 %collective-permute-start.15 = (bf16[2,512,128]{2,1,0:T(8,128)(2,1)S(1)}, bf16[2,512,128]{2,1,0:T(8,128)(2,1)S(1)}, u32[]{:S(2)}, u32[]{:S(2)}) collective-permute-start(bf16[2,512,128]{2,1,0:T(8,128)(2,1)S(1)} %get-tuple-element.42), channel_id=1, source_target_pairs={{0,2},{1,3},{2,0},{3,1},{4,6},{5,7},{6,4},{7,5},{8,10},{9,11},{10,... | collective-permute-start | bytes 786440 | tf_op jit(solution)/shard_map/ppermute | solution.py:363
  47.3 9.4 %collective-permute-start.16 = (bf16[2,512,128]{2,1,0:T(8,128)(2,1)S(1)}, bf16[2,512,128]{2,1,0:T(8,128)(2,1)S(1)}, u32[]{:S(2)}, u32[]{:S(2)}) collective-permute-start(bf16[2,512,128]{2,1,0:T(8,128)(2,1)S(1)} %get-tuple-element.34._), channel_id=1, source_target_pairs={{0,6},{1,7},{2,4},{3,5},{4,2},{5,3},{6,0},{7,1},{8,14},{9,15},{10,... | collective-permute-start | bytes 786440 | tf_op jit(solution)/shard_map/ppermute | solution.py:363
  48.7 10.7 %collective-permute-start.18 = (bf16[2,4,6,32,128]{4,3,2,1,0:T(8,128)(2,1)S(1)}, bf16[2,4,6,32,128]{4,3,2,1,0:T(8,128)(2,1)S(1)}, u32[]{:S(2)}, u32[]{:S(2)}) collective-permute-start(bf16[2,4,6,32,128]{4,3,2,1,0:T(8,128)(2,1)S(1)} %get-tuple-element.38._), channel_id=1, source_target_pairs={{0,64},{8,72},{16,80},{24,88},{32,96},{40,104},{48,112},{56,120},{... | collective-permute-start | bytes 1179656 | tf_op jit(solution)/shard_map/ppermute | solution.py:357
  49.4 12.6 %collective-permute-start.19 = (bf16[2,4,6,32,128]{4,3,2,1,0:T(8,128)(2,1)S(1)}, bf16[2,4,6,32,128]{4,3,2,1,0:T(8,128)(2,1)S(1)}, u32[]{:S(2)}, u32[]{:S(2)}) collective-permute-start(bf16[2,4,6,32,128]{4,3,2,1,0:T(8,128)(2,1)S(1)} %get-tuple-element.40._), channel_id=1, source_target_pairs={{0,192},{8,200},{16,208},{24,216},{32,224},{40,232},{48,240},{56,2... | collective-permute-start | bytes 1179656 | tf_op jit(solution)/shard_map/ppermute | solution.py:357
  55.3 7.0 %collective-permute-start.20 = (bf16[1,512,128]{2,1,0:T(8,128)(2,1)S(1)}, bf16[1,512,128]{2,1,0:T(8,128)(2,1)S(1)}, u32[]{:S(2)}, u32[]{:S(2)}) collective-permute-start(bf16[1,512,128]{2,1,0:T(8,128)(2,1)S(1)} %get-tuple-element.43._), channel_id=1, source_target_pairs={{0,6},{1,7},{2,4},{3,5},{4,2},{5,3},{6,0},{7,1},{8,14},{9,15},{10,... | collective-permute-start | bytes 393224 | tf_op jit(solution)/shard_map/ppermute | solution.py:363
  56.8 23.9 %collective-permute-start.17 = (bf16[1,512,128]{2,1,0:T(8,128)(2,1)S(1)}, bf16[1,512,128]{2,1,0:T(8,128)(2,1)S(1)}, u32[]{:S(2)}, u32[]{:S(2)}) collective-permute-start(bf16[1,512,128]{2,1,0:T(8,128)(2,1)S(1)} %get-tuple-element.46._), channel_id=1, source_target_pairs={{0,2},{1,3},{2,0},{3,1},{4,6},{5,7},{6,4},{7,5},{8,10},{9,11},{10,... | collective-permute-start | bytes 393224 | tf_op jit(solution)/shard_map/ppermute | solution.py:363
  59.5 7.0 %collective-permute-start.22 = (bf16[1,4,6,32,128]{4,3,2,1,0:T(8,128)(2,1)S(1)}, bf16[1,4,6,32,128]{4,3,2,1,0:T(8,128)(2,1)S(1)}, u32[]{:S(2)}, u32[]{:S(2)}) collective-permute-start(bf16[1,4,6,32,128]{4,3,2,1,0:T(8,128)(2,1)S(1)} %get-tuple-element.48._), channel_id=1, source_target_pairs={{0,192},{8,200},{16,208},{24,216},{32,224},{40,232},{48,240},{56,2... | collective-permute-start | bytes 589832 | tf_op jit(solution)/shard_map/ppermute | solution.py:357
  62.1 9.9 %collective-permute-start.23 = (bf16[1,4,6,32,128]{4,3,2,1,0:T(8,128)(2,1)S(1)}, bf16[1,4,6,32,128]{4,3,2,1,0:T(8,128)(2,1)S(1)}, u32[]{:S(2)}, u32[]{:S(2)}) collective-permute-start(bf16[1,4,6,32,128]{4,3,2,1,0:T(8,128)(2,1)S(1)} %get-tuple-element.50._), channel_id=1, source_target_pairs={{0,64},{8,72},{16,80},{24,88},{32,96},{40,104},{48,112},{56,120},{... | collective-permute-start | bytes 589832 | tf_op jit(solution)/shard_map/ppermute | solution.py:357
  62.3 18.4 %collective-permute-start.21 = (bf16[1,512,128]{2,1,0:T(8,128)(2,1)S(1)}, bf16[1,512,128]{2,1,0:T(8,128)(2,1)S(1)}, u32[]{:S(2)}, u32[]{:S(2)}) collective-permute-start(bf16[1,512,128]{2,1,0:T(8,128)(2,1)S(1)} %add.19._), channel_id=1, source_target_pairs={{0,1},{1,0},{2,3},{3,2},{4,5},{5,4},{6,7},{7,6},{8,9},{9,8},{10,11... | collective-permute-start | bytes 393224 | tf_op jit(solution)/shard_map/ppermute | solution.py:399
  66.5 11.1 %collective-permute-start.24 = (bf16[2,6,32,128]{3,2,1,0:T(8,128)(2,1)S(1)}, bf16[2,6,32,128]{3,2,1,0:T(8,128)(2,1)S(1)}, u32[]{:S(2)}, u32[]{:S(2)}) collective-permute-start(bf16[2,6,32,128]{3,2,1,0:T(8,128)(2,1)S(1)} %get-tuple-element.53._), channel_id=1, source_target_pairs={{0,16},{8,24},{16,0},{24,8},{32,48},{40,56},{48,32},{56,40},{64,80... | collective-permute-start | bytes 294920 | tf_op jit(solution)/shard_map/ppermute | solution.py:360
  72.1 6.5 %collective-permute-start.26 = (bf16[2,6,32,128]{3,2,1,0:T(8,128)(2,1)S(1)}, bf16[2,6,32,128]{3,2,1,0:T(8,128)(2,1)S(1)}, u32[]{:S(2)}, u32[]{:S(2)}) collective-permute-start(bf16[2,6,32,128]{3,2,1,0:T(8,128)(2,1)S(1)} %get-tuple-element.55._), channel_id=1, source_target_pairs={{0,16},{8,24},{16,0},{24,8},{32,48},{40,56},{48,32},{56,40},{64,80... | collective-permute-start | bytes 294920 | tf_op jit(solution)/shard_map/ppermute | solution.py:360
  77.6 6.3 %collective-permute-start.25 = (bf16[1,6,32,128]{3,2,1,0:T(8,128)(2,1)S(1)}, bf16[1,6,32,128]{3,2,1,0:T(8,128)(2,1)S(1)}, u32[]{:S(2)}, u32[]{:S(2)}) collective-permute-start(bf16[1,6,32,128]{3,2,1,0:T(8,128)(2,1)S(1)} %get-tuple-element.58._), channel_id=1, source_target_pairs={{0,32},{8,40},{16,48},{24,56},{32,0},{40,8},{48,16},{56,24},{64,96... | collective-permute-start | bytes 147464 | tf_op jit(solution)/shard_map/ppermute | solution.py:360
  78.6 5.2 %collective-permute-start.27 = (bf16[1,6,32,128]{3,2,1,0:T(8,128)(2,1)S(1)}, bf16[1,6,32,128]{3,2,1,0:T(8,128)(2,1)S(1)}, u32[]{:S(2)}, u32[]{:S(2)}) collective-permute-start(bf16[1,6,32,128]{3,2,1,0:T(8,128)(2,1)S(1)} %get-tuple-element.61), channel_id=1, source_target_pairs={{0,32},{8,40},{16,48},{24,56},{32,0},{40,8},{48,16},{56,24},{64,96... | collective-permute-start | bytes 147464 | tf_op jit(solution)/shard_map/ppermute | solution.py:360

commit v10 on v8

--- a/solution.py
+++ b/solution.py
@@ -214,21 +214,24 @@
     )(after, filters, acc, *halo, sibling)
 
 
-def product_kernel(
-    crossed, pos_ref, _, corr_ref, x0_ref, x1_ref, x2_ref, x3_ref, keep_ref, send_ref, full_ref
-):
-    x, z_hi, y, z_lo, core = coords(pos_ref)
-    for s, part in enumerate((x0_ref, x1_ref, x2_ref, x3_ref)):
+def gathered_columns(pos_ref, part_refs, full_ref):
+    x, z_hi = coords(pos_ref)[:2]
+    for s, part in enumerate(part_refs):
         for h in range(NZ_HI):
             at = lax.rem(x + NX - s, NX) * NZ_HI + lax.rem(z_hi + h, NZ_HI)
             full_ref[:, pl.ds(pl.multiple_of(at * LANE, LANE), LANE)] = part[h]
 
+
+def products(crossed, pos_ref, corr_ref, full_ref, out_refs):
+    y, z_lo, core = coords(pos_ref)[2:]
+    stay_ref, leave_ref, send_stay_ref, send_leave_ref = out_refs
     deep = NZ_LO * NCORE * 32
     for s, at in enumerate(ring_slots(y, crossed)):
         part = full_ref[:, pl.ds(pl.multiple_of(at * deep, deep), deep)]
         result = lax.dot_general(
             part, corr_ref[...], (((0,), (0,)), ((), ())), preferred_element_type=F32
         ).astype(BF16)
+        keep_ref, send_ref = (stay_ref, send_stay_ref) if s < 2 else (leave_ref, send_leave_ref)
         for z in range(NZ_LO):
             shift = z ^ z_lo
             slot = lax.rem(shift, 2) * 2 + shift // 2
@@ -236,25 +239,56 @@
                 columns = slice(k * LANE, (k + 1) * LANE)
                 even = result[z * 64 : z * 64 + 32, columns]
                 odd = result[z * 64 + 32 : z * 64 + 64, columns]
-                keep_ref[s, slot, k] = jnp.where(core == 0, even, odd)
-                send_ref[s, slot, k] = jnp.where(core == 0, odd, even)
-
-
-def product(crossed, pos, after, corr, gathered):
+                keep_ref[s % 2, slot, k] = jnp.where(core == 0, even, odd)
+                send_ref[s % 2, slot, k] = jnp.where(core == 0, odd, even)
+
+
+def first_product_kernel(crossed, pos_ref, _, corr_ref, x0_ref, x1_ref, x2_ref, x3_ref, full_ref, *out_refs):
+    gathered_columns(pos_ref, (x0_ref, x1_ref, x2_ref, x3_ref), full_ref)
+    products(crossed, pos_ref, corr_ref, full_ref, out_refs)
+
+
+def next_product_kernel(crossed, pos_ref, _, corr_ref, full_ref, *out_refs):
+    products(crossed, pos_ref, corr_ref, full_ref, out_refs)
+
+
+def product(kernel, crossed, pos, after, corr, sources, keep_full):
     tok, width = corr.shape
-    part = jax.ShapeDtypeStruct((NY, NZ_LO, width // LANE, 32, LANE), BF16)
-    vmem = pl.BlockSpec(memory_space=pltpu.VMEM)
-    return pl.pallas_call(
-        functools.partial(product_kernel, crossed),
-        out_shape=(part, part),
+    part = jax.ShapeDtypeStruct((2, NZ_LO, width // LANE, 32, LANE), BF16)
+    vmem = pl.BlockSpec(memory_space=pltpu.VMEM)
+    full = [jax.ShapeDtypeStruct((tok, 1024), BF16)] if keep_full else []
+    outs = full + [part] * 4
+    return pl.pallas_call(
+        functools.partial(kernel, crossed),
+        out_shape=outs,
         in_specs=[pl.BlockSpec(memory_space=pltpu.SMEM), pl.BlockSpec(memory_space=pl.ANY)]
-        + [vmem] * 5,
-        out_specs=(vmem,) * 2,
-        scratch_shapes=[pltpu.VMEM((tok, 1024), BF16)],
+        + [vmem] * (1 + len(sources)),
+        out_specs=[vmem] * len(outs),
         compiler_params=pltpu.CompilerParams(vmem_limit_bytes=VMEM_LIMIT),
         cost_estimate=SMALL_COST,
         name="product",
-    )(pos, after, corr, *gathered)
+    )(pos, after, corr, *sources)
+
+
+def halve_three_kernel(_, mine_ref, beside_ref, other_ref, stay_ref, leave_ref):
+    half = leave_ref.shape[0]
+    for out_ref, rows in ((stay_ref, slice(0, half)), (leave_ref, slice(half, 2 * half))):
+        total = mine_ref[rows].astype(F32) + beside_ref[rows].astype(F32)
+        out_ref[...] = (total + other_ref[rows].astype(F32)).astype(out_ref.dtype)
+
+
+def halve_three(after, mine, beside, other):
+    half = (mine.shape[0] // 2,) + mine.shape[1:]
+    vmem = pl.BlockSpec(memory_space=pltpu.VMEM)
+    return pl.pallas_call(
+        halve_three_kernel,
+        out_shape=(jax.ShapeDtypeStruct(half, F32), jax.ShapeDtypeStruct(half, BF16)),
+        in_specs=[pl.BlockSpec(memory_space=pl.ANY), vmem, vmem, vmem],
+        out_specs=(vmem, vmem),
+        compiler_params=pltpu.CompilerParams(vmem_limit_bytes=VMEM_LIMIT),
+        cost_estimate=SMALL_COST,
+        name="halve_three",
+    )(after, mine, beside, other)
 
 
 def halve_kernel(_, mine_ref, other_ref, stay_ref, leave_ref):
@@ -278,10 +312,10 @@
 
 
 def add_kernel(_, mine_ref, other_ref, sum_ref):
-    sum_ref[...] = (mine_ref[...] + other_ref[...].astype(F32)).astype(BF16)
-
-
-def add(after, mine, other):
+    sum_ref[...] = (mine_ref[...].astype(F32) + other_ref[...].astype(F32)).astype(BF16)
+
+
+def add(after, mine, other, cost=SMALL_COST):
     vmem = pl.BlockSpec(memory_space=pltpu.VMEM)
     return pl.pallas_call(
         add_kernel,
@@ -289,7 +323,7 @@
         in_specs=[pl.BlockSpec(memory_space=pl.ANY), vmem, vmem],
         out_specs=vmem,
         compiler_params=pltpu.CompilerParams(vmem_limit_bytes=VMEM_LIMIT),
-        cost_estimate=LARGE_COST,
+        cost_estimate=cost,
         name="add",
     )(after, mine, other)
 
@@ -400,23 +434,28 @@
         pos, corr_1, [corr_0, corr_1], projection.transpose(1, 0, 2)
     )
     x_far, x_near = x_swapped(far_send, False), x_swapped(near_send, True)
-    keep_0, send_0 = product(False, pos, near_send, corr_0, gathered)
-    keep_1, send_1 = product(True, pos, send_0, corr_1, gathered)
-    stay_0, leave_0 = halve(send_1, keep_0, sibling(send_0))
+    full, stay_0, leave_0, send_stay_0, send_leave_0 = product(
+        first_product_kernel, False, pos, near_send, corr_0, gathered, True
+    )
+    stay_1, leave_1, send_stay_1, send_leave_1 = product(
+        next_product_kernel, True, pos, send_leave_0, corr_1, [full], False
+    )
+    leave_0 = add(send_leave_1, leave_0, sibling(send_leave_0))
     y_0 = y_swapped(leave_0, False)
-    stay_1, leave_1 = halve(leave_0, keep_1, sibling(send_1))
+    leave_1 = add(leave_0, leave_1, sibling(send_leave_1))
     y_1 = y_swapped(leave_1, True)
+    beside_0, beside_1 = sibling(send_stay_0), sibling(send_stay_1)
     far, leave = halve(leave_1, far, x_far, LARGE_COST)
     x_far = x_swapped(leave, True)
-    near, leave = halve(leave, near, x_near)
+    stay_0, leave_0 = halve_three(leave, stay_0, beside_0, y_0)
+    y_0 = y_swapped(leave_0, True)
+    stay_1, leave_1 = halve_three(leave_0, stay_1, beside_1, y_1)
+    y_1 = y_swapped(leave_1, False)
+    far = add(leave_1, far, x_far, LARGE_COST)
+    opposite = lax.ppermute(far, "tp", Z_HI_SWAP)
+    near, leave = halve(far, near, x_near)
     x_near = x_swapped(leave, False)
-    stay_0, leave_0 = halve(leave, stay_0, y_0)
-    y_0 = y_swapped(leave_0, True)
-    stay_1, leave_1 = halve(leave_0, stay_1, y_1)
-    y_1 = y_swapped(leave_1, False)
-    far = add(leave_1, far, x_far)
-    opposite = lax.ppermute(far, "tp", Z_HI_SWAP)
-    stay_0, leave_0 = halve(far, stay_0[0], y_0[0])
+    stay_0, leave_0 = halve(leave, stay_0[0], y_0[0])
     z_0 = z_swapped(leave_0, 1)
     stay_1, leave_1 = halve(leave_0, stay_1[0], y_1[0])
     z_1 = z_swapped(leave_1, 1)

time: 84.8 us -> 88 us (1.038)
  waiting for transfers between devices: 19.8 us -> 25.7 us
  starting transfers between devices: 44.1 us -> 41.3 us
    ppermute x4, waiting for transfers between devices: 2.57 us -> 8.88 us  [x_swapped(): return lax.ppermute(value, 'tp', x_swap(crossed))]
    ppermute x4, waiting for transfers between devices: 6.71 us -> 3.14 us  [y_swapped(): return lax.ppermute(value, 'ctx', y_swap(crossed))]
    ppermute x4, waiting for transfers between devices: 7.85 us -> 11 us  [z_swapped(): return lax.ppermute(value, 'ctx', z_swap(bit))]
    ppermute x4, starting transfers between devices: 5.51 us -> 3.61 us  [z_swapped(): return lax.ppermute(value, 'ctx', z_swap(bit))]
    ppermute x4, starting transfers between devices: 6.03 us -> 4.73 us  [x_swapped(): return lax.ppermute(value, 'tp', x_swap(crossed))]
    pallas_call x2 -> x4, Pallas kernels: 3.87 us -> 3.84 us  [the longest x2 3.57 us: product(): pl.pallas_call(functools.partial(kernel, crossed), out_shape=outs, in_spe...]
  transfers between devices with their start and end apart: 24 -> 26, of which waited for: 9 -> 10; matrix products, arithmetic and copies ran while one was open for 2% -> 2% of each run, Pallas kernels for 16% -> 15%
where the time goes in v10:
time: 88 us; the launch traced here: 87.2 us
  starting transfers between devices  41.3 us (47%)
  waiting for transfers between devices  25.7 us (29%)
  Pallas kernels  16.7 us (19%)
  other arithmetic  1.71 us (2%)
  local copies, waits for them, and re-layouts  0.92 us (1%)
  between operations  0.88 us (1%)
    ppermute x4, starting transfers between devices, later(): return lax.ppermute(value, 'ctx', from_later_chip(steps))  13.4 us
    ppermute x4, waiting for transfers between devices, z_swapped(): return lax.ppermute(value, 'ctx', z_swap(bit))  11 us
    ppermute x4, waiting for transfers between devices, x_swapped(): return lax.ppermute(value, 'tp', x_swap(crossed))  8.88 us
    ppermute x1, starting transfers between devices, per_device(): pair = jnp.stack([inputs, lax.ppermute(inputs, 'tp', Z_HI_SWAP)])  7.28 us
    ppermute x3, starting transfers between devices, per_device(): lax.ppermute(pair, 'tp', along_x(s))  5.73 us
    ppermute x4, starting transfers between devices, x_swapped(): return lax.ppermute(value, 'tp', x_swap(crossed))  4.73 us
    pallas_call x2, Pallas kernels, far_conv(): pl.pallas_call(functools.partial(far_kernel, first), out_shape=jax.ShapeD...  4.17 us
    ppermute x4, starting transfers between devices, z_swapped(): return lax.ppermute(value, 'ctx', z_swap(bit))  3.61 us
  transfers between devices with their start and end apart: 26, of which 10 were waited for; matrix products, arithmetic and copies ran while one was open for 2% of the time, Pallas kernels for 15%

profile of v10, /device:TPU:24, one launch (start us, length us, event | category | flops | bytes accessed | tf_op | source)
XLA Modules:
  0.0 87.2 jit_solution(4167006990805351032)
XLA Ops:
  0.6 7.3 %collective-permute-start = (bf16[512,128]{1,0:T(8,128)(2,1)}, bf16[512,128]{1,0:T(8,128)(2,1)S(1)}, u32[]{:S(2)}, u32[]{:S(2)}) collective-permute-start(bf16[512,128]{1,0:T(8,128)(2,1)} %param.4), channel_id=1, source_target_pairs={{0,1},{1,0},{2,3},{3,2},{4,5},{5,4},{6,7},{7,6},{8,9},{9,8},{10,11... | collective-permute-start | bytes 393224 | tf_op jit(solution)/shard_map/ppermute | solution.py:421
  7.9 3.5 %collective-permute-start.2 = (bf16[512,128]{1,0:T(8,128)(2,1)}, bf16[512,128]{1,0:T(8,128)(2,1)S(1)}, u32[]{:S(2)}, u32[]{:S(2)}) collective-permute-start(bf16[512,128]{1,0:T(8,128)(2,1)} %own_ref.3), channel_id=1, source_target_pairs={{32,0},{40,8},{48,16},{56,24},{64,32},{72,40},{80,48},{88,56},{96,... | collective-permute-start | bytes 393224 | tf_op jit(solution)/shard_map/ppermute | solution.py:406
  11.5 2.8 %collective-permute-start.3 = (bf16[512,128]{1,0:T(8,128)(2,1)}, bf16[512,128]{1,0:T(8,128)(2,1)S(1)}, u32[]{:S(2)}, u32[]{:S(2)}) collective-permute-start(bf16[512,128]{1,0:T(8,128)(2,1)} %own_ref.3), channel_id=1, source_target_pairs={{48,0},{56,8},{64,16},{72,24},{80,32},{88,40},{96,48},{104,56},{11... | collective-permute-start | bytes 393224 | tf_op jit(solution)/shard_map/ppermute | solution.py:406
  14.3 2.4 %collective-permute-start.4 = (bf16[512,128]{1,0:T(8,128)(2,1)}, bf16[512,128]{1,0:T(8,128)(2,1)S(1)}, u32[]{:S(2)}, u32[]{:S(2)}) collective-permute-start(bf16[512,128]{1,0:T(8,128)(2,1)} %own_ref.3), channel_id=1, source_target_pairs={{64,0},{72,8},{80,16},{88,24},{96,32},{104,40},{112,48},{120,56},{... | collective-permute-start | bytes 393224 | tf_op jit(solution)/shard_map/ppermute | solution.py:406
  16.7 4.7 %collective-permute-start.1 = (bf16[512,128]{1,0:T(8,128)(2,1)}, bf16[512,128]{1,0:T(8,128)(2,1)S(1)}, u32[]{:S(2)}, u32[]{:S(2)}) collective-permute-start(bf16[512,128]{1,0:T(8,128)(2,1)} %own_ref.3), channel_id=1, source_target_pairs={{16,0},{24,8},{32,16},{40,24},{48,32},{56,40},{64,48},{72,56},{80,... | collective-permute-start | bytes 393224 | tf_op jit(solution)/shard_map/ppermute | solution.py:406
  21.4 0.1 pad_add_fusion.pos_ref
  21.5 0.0 collective-permute-done
  21.5 0.9 %pad_maximum_fusion._.x0_ref = bf16[2,512,128]{2,1,0:T(8,128)(2,1)S(1)} fusion(bf16[1,512,128]{2,1,0:T(8,128)(2,1)S(1)} %bitcast.19, bf16[1,512,128]{2,1,0:T(8,128)(2,1)} %bitcast.18), kind=kLoop, calls=%fused_computation | loop fusion | flops 131072 | bytes 524288 | tf_op jit(solution)/shard_map/stack | solution.py:421
  22.4 0.0 copy-start.1
  22.4 0.9 %copy-done.1 = bf16[12,4096]{1,0:T(8,128)(2,1)S(1)} copy-done((bf16[12,4096]{1,0:T(8,128)(2,1)S(1)}, bf16[12,4096]{1,0:T(8,128)(2,1)}, u32[]{:S(2)}) %copy-start.1) | copy-done | bytes 98328
  23.3 0.9 %near_table.1._.table_ref = bf16[12,64,2048]{2,1,0:T(8,128)(2,1)S(1)} custom-call(bf16[2,512,128]{2,1,0:T(8,128)(2,1)S(1)} %pad_maximum_fusion._.x0_ref, bf16[12,4096]{1,0:T(8,128)(2,1)S(1)} %copy-done.1), custom_call_target="tpu_custom_call" | custom-call | flops 1000 | bytes 1000 | tf_op jit(solution)/shard_map/near_table/pallas_call | solution.py:79
  24.2 0.0 collective-permute-done.2.r2_ref
  24.3 1.9 %collective-permute-done.1.r1_ref = bf16[512,128]{1,0:T(8,128)(2,1)S(1)} collective-permute-done((bf16[512,128]{1,0:T(8,128)(2,1)}, bf16[512,128]{1,0:T(8,128)(2,1)S(1)}, u32[]{:S(2)}, u32[]{:S(2)}) %collective-permute-start.1) | collective-permute-done | bytes 131104 | tf_op jit(solution)/shard_map/ppermute | solution.py:406
  26.2 0.8 for_sibling.1
  27.0 0.1 collective-permute-start.5
  27.1 1.6 %collective-permute-start.6 = (bf16[2,512,128]{2,1,0:T(8,128)(2,1)S(1)}, bf16[2,512,128]{2,1,0:T(8,128)(2,1)S(1)}, u32[]{:S(2)}, u32[]{:S(2)}) collective-permute-start(bf16[2,512,128]{2,1,0:T(8,128)(2,1)S(1)} %pad_maximum_fusion._.x0_ref), channel_id=1, source_target_pairs={{0,2},{1,3},{2,4},{3,5},{4,6},{5,7},{6,0},{7,1},{8,10},{9,11},{10,... | collective-permute-start | bytes 786440 | tf_op jit(solution)/shard_map/ppermute | solution.py:422
  28.7 2.7 %collective-permute-start.7 = (bf16[2,512,128]{2,1,0:T(8,128)(2,1)S(1)}, bf16[2,512,128]{2,1,0:T(8,128)(2,1)S(1)}, u32[]{:S(2)}, u32[]{:S(2)}) collective-permute-start(bf16[2,512,128]{2,1,0:T(8,128)(2,1)S(1)} %pad_maximum_fusion._.x0_ref), channel_id=1, source_target_pairs={{0,4},{1,5},{2,6},{3,7},{4,0},{5,1},{6,2},{7,3},{8,12},{9,13},{10,... | collective-permute-start | bytes 786440 | tf_op jit(solution)/shard_map/ppermute | solution.py:422
  31.4 1.4 %collective-permute-start.8 = (bf16[2,512,128]{2,1,0:T(8,128)(2,1)S(1)}, bf16[2,512,128]{2,1,0:T(8,128)(2,1)S(1)}, u32[]{:S(2)}, u32[]{:S(2)}) collective-permute-start(bf16[2,512,128]{2,1,0:T(8,128)(2,1)S(1)} %pad_maximum_fusion._.x0_ref), channel_id=1, source_target_pairs={{0,6},{1,7},{2,0},{3,1},{4,2},{5,3},{6,4},{7,5},{8,14},{9,15},{10,... | collective-permute-start | bytes 786440 | tf_op jit(solution)/shard_map/ppermute | solution.py:422
  32.9 3.4 %near_conv.1 = (f32[4,384,256]{2,1,0:T(8,128)S(1)}, f32[4,384,256]{2,1,0:T(8,128)S(1)}) custom-call(bf16[12,64,2048]{2,1,0:T(8,128)(2,1)S(1)} %near_table.1._.table_ref, bf16[512,128]{1,0:T(8,128)(2,1)S(1)} %copy-done.3, bf16[512,128]{1,0:T(8,128)(2,1)S(1)} %collective-permute-done.1.r1_ref, bf16[512,128]{1,0:T(8,128)(2,1)S(1)} %collective-permute-done.2.r2_ref, ...), custom_call_target="tpu_custom_call" | custom-call | flops 4000000000 | bytes 8000000 | tf_op jit(solution)/shard_map/near_conv/pallas_call | solution.py:158
  36.3 0.0 copy-start.2
  36.3 2.1 %far_conv.2._.refs_0_.corr_ref = bf16[512,768]{1,0:T(8,128)(2,1)S(1)} custom-call(bf16[12,64,2048]{2,1,0:T(8,128)(2,1)S(1)} %near_table.1._.table_ref, bf16[12,4096]{1,0:T(8,128)(2,1)S(1)} %copy-done.1, f32[4,384,256]{2,1,0:T(8,128)S(1)} %get-tuple-element.33.acc_ref, bf16[512,128]{1,0:T(8,128)(2,1)S(1)} %collective-permute-done.2.r2_ref, ...), custom_call_target="tpu_custom_call" | custom-call | flops 1000 | bytes 1000 | tf_op jit(solution)/shard_map/far_conv/pallas_call | solution.py:202
  38.4 0.0 copy-start
  38.4 2.1 %far_conv.3._.refs_1_.corr_ref = bf16[512,768]{1,0:T(8,128)(2,1)S(1)} custom-call(bf16[512,768]{1,0:T(8,128)(2,1)S(1)} %far_conv.2._.refs_0_.corr_ref, bf16[12,4096]{1,0:T(8,128)(2,1)S(1)} %copy-done.2, f32[4,384,256]{2,1,0:T(8,128)S(1)} %get-tuple-element.34.acc_ref, bf16[512,128]{1,0:T(8,128)(2,1)S(1)} %collective-permute-done.2.r2_ref, ...), custom_call_target="tpu_custom_call" | custom-call | flops 1000 | bytes 1000 | tf_op jit(solution)/shard_map/far_conv/pallas_call | solution.py:202
  40.5 2.4 %input_shares.1 = (f32[2,512,128]{2,1,0:T(8,128)S(1)}, bf16[2,512,128]{2,1,0:T(8,128)(2,1)S(1)}, f32[2,512,128]{2,1,0:T(8,128)S(1)}, bf16[2,512,128]{2,1,0:T(8,128)(2,1)S(1)}) custom-call(s32[2]{0:T(128)S(1)} %pad_add_fusion.pos_ref, bf16[512,768]{1,0:T(8,128)(2,1)S(1)} %far_conv.3._.refs_1_.corr_ref, bf16[512,768]{1,0:T(8,128)(2,1)S(1)} %far_conv.2._.refs_0_.corr_ref, ...), custom_call_target="tpu_custom_call" | custom-call | flops 1000 | bytes 1000 | tf_op jit(solution)/shard_map/input_shares/pallas_call | solution.py:385
  42.9 0.7 collective-permute-done.7.x2_ref
  43.7 1.9 %product.2 = (bf16[512,1024]{1,0:T(8,128)(2,1)S(1)}, bf16[2,4,6,32,128]{4,3,2,1,0:T(8,128)(2,1)S(1)}, bf16[2,4,6,32,128]{4,3,2,1,0:T(8,128)(2,1)S(1)}, bf16[2,4,...) custom-call(s32[2]{0:T(128)S(1)} %pad_add_fusion.pos_ref, bf16[2,512,128]{2,1,0:T(8,128)(2,1)S(1)} %get-tuple-element.35._, ...), custom_call_target="tpu_custom_call" | custom-call | flops 1000 | bytes 1000 | tf_op jit(solution)/shard_map/product/pallas_call | solution.py:261
  45.6 0.1 collective-permute-start.9
  45.7 1.6 %product.3 = (bf16[2,4,6,32,128]{4,3,2,1,0:T(8,128)(2,1)S(1)}, bf16[2,4,6,32,128]{4,3,2,1,0:T(8,128)(2,1)S(1)}, bf16[2,4,6,32,128]{4,3,2,1,0:T(8,128)(2,1)S(1)}, bf16[2,4,6,32,128]{4,3,2,1,0:T(8,128)(2,1)S(1)}) custom-call(s32[2]{0:T(128)S(1)} %pad_add_fusion.pos_ref, bf16[2,4,6,32,128]{4,3,2,1,0:T(8,128)(2,1)S(1)} %get-tuple-element.36._, ...), custom_call_target="tpu_custom_call" | custom-call | flops 1000 | bytes 1000 | tf_op jit(solution)/shard_map/product/pallas_call | solution.py:261
  47.3 0.6 collective-permute-start.10
  47.9 1.3 %collective-permute-start.11 = (bf16[2,512,128]{2,1,0:T(8,128)(2,1)S(1)}, bf16[2,512,128]{2,1,0:T(8,128)(2,1)S(1)}, u32[]{:S(2)}, u32[]{:S(2)}) collective-permute-start(bf16[2,512,128]{2,1,0:T(8,128)(2,1)S(1)} %get-tuple-element.42), channel_id=1, source_target_pairs={{0,2},{1,3},{2,0},{3,1},{4,6},{5,7},{6,4},{7,5},{8,10},{9,11},{10,... | collective-permute-start | bytes 786440 | tf_op jit(solution)/shard_map/ppermute | solution.py:418
  49.2 0.5 collective-permute-start.14
  49.7 0.0 collective-permute-done.9.other_ref
  49.8 0.1 add.21._
  49.8 0.8 collective-permute-start.13
  50.7 0.1 add.22._
  50.8 1.4 %collective-permute-start.15 = (bf16[2,4,6,32,128]{4,3,2,1,0:T(8,128)(2,1)S(1)}, bf16[2,4,6,32,128]{4,3,2,1,0:T(8,128)(2,1)S(1)}, u32[]{:S(2)}, u32[]{:S(2)}) collective-permute-start(bf16[2,4,6,32,128]{4,3,2,1,0:T(8,128)(2,1)S(1)} %add.22._), channel_id=1, source_target_pairs={{0,192},{8,200},{16,208},{24,216},{32,224},{40,232},{48,240},{56,2... | collective-permute-start | bytes 1179656 | tf_op jit(solution)/shard_map/ppermute | solution.py:412
  52.2 4.1 %collective-permute-done.11.other_ref = bf16[2,512,128]{2,1,0:T(8,128)(2,1)S(1)} collective-permute-done((bf16[2,512,128]{2,1,0:T(8,128)(2,1)S(1)}, bf16[2,512,128]{2,1,0:T(8,128)(2,1)S(1)}, u32[]{:S(2)}, u32[]{:S(2)}) %collective-permute-start.11) | collective-permute-done | bytes 262176 | tf_op jit(solution)/shard_map/ppermute | solution.py:418
  56.2 0.1 halve.6
  56.3 2.3 %collective-permute-start.16 = (bf16[1,512,128]{2,1,0:T(8,128)(2,1)S(1)}, bf16[1,512,128]{2,1,0:T(8,128)(2,1)S(1)}, u32[]{:S(2)}, u32[]{:S(2)}) collective-permute-start(bf16[1,512,128]{2,1,0:T(8,128)(2,1)S(1)} %get-tuple-element.43._), channel_id=1, source_target_pairs={{0,6},{1,7},{2,4},{3,5},{4,2},{5,3},{6,0},{7,1},{8,14},{9,15},{10,... | collective-permute-start | bytes 393224 | tf_op jit(solution)/shard_map/ppermute | solution.py:418
  58.6 1.0 %collective-permute-start.17 = (bf16[2,512,128]{2,1,0:T(8,128)(2,1)S(1)}, bf16[2,512,128]{2,1,0:T(8,128)(2,1)S(1)}, u32[]{:S(2)}, u32[]{:S(2)}) collective-permute-start(bf16[2,512,128]{2,1,0:T(8,128)(2,1)S(1)} %get-tuple-element.35._), channel_id=1, source_target_pairs={{0,6},{1,7},{2,4},{3,5},{4,2},{5,3},{6,0},{7,1},{8,14},{9,15},{10,... | collective-permute-start | bytes 786440 | tf_op jit(solution)/shard_map/ppermute | solution.py:418
  59.6 1.3 %collective-permute-done.13.other_ref = bf16[2,4,6,32,128]{4,3,2,1,0:T(8,128)(2,1)S(1)} collective-permute-done((bf16[2,4,6,32,128]{4,3,2,1,0:T(8,128)(2,1)S(1)}, bf16[2,4,6,32,128]{4,3,2,1,0:T(8,128)(2,1)S(1)}, u32[]{:S(2)}, u32[]{:S(2)}) %collective-permute-start.13) | collective-permute-done | bytes 393248 | tf_op jit(solution)/shard_map/ppermute | solution.py:412
  61.0 0.1 halve_three.2
  61.1 0.1 collective-permute-start.20
  61.2 1.8 %collective-permute-done.15.other_ref = bf16[2,4,6,32,128]{4,3,2,1,0:T(8,128)(2,1)S(1)} collective-permute-done((bf16[2,4,6,32,128]{4,3,2,1,0:T(8,128)(2,1)S(1)}, bf16[2,4,6,32,128]{4,3,2,1,0:T(8,128)(2,1)S(1)}, u32[]{:S(2)}, u32[]{:S(2)}) %collective-permute-start.15) | collective-permute-done | bytes 393248 | tf_op jit(solution)/shard_map/ppermute | solution.py:412
  63.0 0.1 halve_three.3
  63.2 0.2 collective-permute-start.21
  63.3 0.3 collective-permute-done.16.other_ref
  63.7 4.5 %collective-permute-done.17.other_ref = bf16[2,512,128]{2,1,0:T(8,128)(2,1)S(1)} collective-permute-done((bf16[2,512,128]{2,1,0:T(8,128)(2,1)S(1)}, bf16[2,512,128]{2,1,0:T(8,128)(2,1)S(1)}, u32[]{:S(2)}, u32[]{:S(2)}) %collective-permute-start.17) | collective-permute-done | bytes 262176 | tf_op jit(solution)/shard_map/ppermute | solution.py:418
  68.2 0.1 halve.7
  68.2 0.1 collective-permute-start.18
  68.3 2.7 %collective-permute-start.19 = (bf16[1,512,128]{2,1,0:T(8,128)(2,1)S(1)}, bf16[1,512,128]{2,1,0:T(8,128)(2,1)S(1)}, u32[]{:S(2)}, u32[]{:S(2)}) collective-permute-start(bf16[1,512,128]{2,1,0:T(8,128)(2,1)S(1)} %add.23._), channel_id=1, source_target_pairs={{0,1},{1,0},{2,3},{3,2},{4,5},{5,4},{6,7},{7,6},{8,9},{9,8},{10,11... | collective-permute-start | bytes 393224 | tf_op jit(solution)/shard_map/ppermute | solution.py:455
  71.0 0.0 collective-permute-done.20
  71.1 0.7 collective-permute-start.22
  71.8 1.5 %collective-permute-start.24 = (bf16[2,6,32,128]{3,2,1,0:T(8,128)(2,1)S(1)}, bf16[2,6,32,128]{3,2,1,0:T(8,128)(2,1)S(1)}, u32[]{:S(2)}, u32[]{:S(2)}) collective-permute-start(bf16[2,6,32,128]{3,2,1,0:T(8,128)(2,1)S(1)} %get-tuple-element.57._), channel_id=1, source_target_pairs={{0,16},{8,24},{16,0},{24,8},{32,48},{40,56},{48,32},{56,40},{64,80... | collective-permute-start | bytes 294920 | tf_op jit(solution)/shard_map/ppermute | solution.py:415
  73.3 5.4 %collective-permute-done.22.other_ref = bf16[2,6,32,128]{3,2,1,0:T(8,128)(2,1)S(1)} collective-permute-done((bf16[2,6,32,128]{3,2,1,0:T(8,128)(2,1)S(1)}, bf16[2,6,32,128]{3,2,1,0:T(8,128)(2,1)S(1)}, u32[]{:S(2)}, u32[]{:S(2)}) %collective-permute-start.22) | collective-permute-done | bytes 98336 | tf_op jit(solution)/shard_map/ppermute | solution.py:415
  78.8 0.1 collective-permute-start.23
  78.9 1.7 %collective-permute-done.24.other_ref = bf16[2,6,32,128]{3,2,1,0:T(8,128)(2,1)S(1)} collective-permute-done((bf16[2,6,32,128]{3,2,1,0:T(8,128)(2,1)S(1)}, bf16[2,6,32,128]{3,2,1,0:T(8,128)(2,1)S(1)}, u32[]{:S(2)}, u32[]{:S(2)}) %collective-permute-start.24) | collective-permute-done | bytes 98336 | tf_op jit(solution)/shard_map/ppermute | solution.py:415
  80.6 1.3 %collective-permute-start.25 = (bf16[1,6,32,128]{3,2,1,0:T(8,128)(2,1)S(1)}, bf16[1,6,32,128]{3,2,1,0:T(8,128)(2,1)S(1)}, u32[]{:S(2)}, u32[]{:S(2)}) collective-permute-start(bf16[1,6,32,128]{3,2,1,0:T(8,128)(2,1)S(1)} %get-tuple-element.63), channel_id=1, source_target_pairs={{0,32},{8,40},{16,48},{24,56},{32,0},{40,8},{48,16},{56,24},{64,96... | collective-permute-start | bytes 147464 | tf_op jit(solution)/shard_map/ppermute | solution.py:415
  81.9 0.0 collective-permute-done.18
  81.9 0.0 collective-permute-done.19
  81.9 0.7 fusion
  82.6 3.9 %collective-permute-done.25.refs_3_ = bf16[1,6,32,128]{3,2,1,0:T(8,128)(2,1)S(1)} collective-permute-done((bf16[1,6,32,128]{3,2,1,0:T(8,128)(2,1)S(1)}, bf16[1,6,32,128]{3,2,1,0:T(8,128)(2,1)S(1)}, u32[]{:S(2)}, u32[]{:S(2)}) %collective-permute-start.25) | collective-permute-done | bytes 49184 | tf_op jit(solution)/shard_map/ppermute | solution.py:415
  86.5 0.0 collective-permute-done.23.refs_1_
  86.5 0.7 join.1
  (19 shorter events, 0.2 us)
Async XLA Ops:
  0.6 25.5 %copy-start.3 = (bf16[512,128]{1,0:T(8,128)(2,1)S(1)}, bf16[512,128]{1,0:T(8,128)(2,1)}, u32[]{:S(2)}) copy-start(bf16[512,128]{1,0:T(8,128)(2,1)} %own_ref.3) | copy-start | bytes 393220
  0.6 20.8 %collective-permute-start = (bf16[512,128]{1,0:T(8,128)(2,1)}, bf16[512,128]{1,0:T(8,128)(2,1)S(1)}, u32[]{:S(2)}, u32[]{:S(2)}) collective-permute-start(bf16[512,128]{1,0:T(8,128)(2,1)} %param.4), channel_id=1, source_target_pairs={{0,1},{1,0},{2,3},{3,2},{4,5},{5,4},{6,7},{7,6},{8,9},{9,8},{10,11... | collective-permute-start | bytes 393224 | tf_op jit(solution)/shard_map/ppermute | solution.py:421
  7.9 16.3 %collective-permute-start.2 = (bf16[512,128]{1,0:T(8,128)(2,1)}, bf16[512,128]{1,0:T(8,128)(2,1)S(1)}, u32[]{:S(2)}, u32[]{:S(2)}) collective-permute-start(bf16[512,128]{1,0:T(8,128)(2,1)} %own_ref.3), channel_id=1, source_target_pairs={{32,0},{40,8},{48,16},{56,24},{64,32},{72,40},{80,48},{88,56},{96,... | collective-permute-start | bytes 393224 | tf_op jit(solution)/shard_map/ppermute | solution.py:406
  11.5 12.8 %collective-permute-start.3 = (bf16[512,128]{1,0:T(8,128)(2,1)}, bf16[512,128]{1,0:T(8,128)(2,1)S(1)}, u32[]{:S(2)}, u32[]{:S(2)}) collective-permute-start(bf16[512,128]{1,0:T(8,128)(2,1)} %own_ref.3), channel_id=1, source_target_pairs={{48,0},{56,8},{64,16},{72,24},{80,32},{88,40},{96,48},{104,56},{11... | collective-permute-start | bytes 393224 | tf_op jit(solution)/shard_map/ppermute | solution.py:406
  14.3 10.0 %collective-permute-start.4 = (bf16[512,128]{1,0:T(8,128)(2,1)}, bf16[512,128]{1,0:T(8,128)(2,1)S(1)}, u32[]{:S(2)}, u32[]{:S(2)}) collective-permute-start(bf16[512,128]{1,0:T(8,128)(2,1)} %own_ref.3), channel_id=1, source_target_pairs={{64,0},{72,8},{80,16},{88,24},{96,32},{104,40},{112,48},{120,56},{... | collective-permute-start | bytes 393224 | tf_op jit(solution)/shard_map/ppermute | solution.py:406
  16.7 9.5 %collective-permute-start.1 = (bf16[512,128]{1,0:T(8,128)(2,1)}, bf16[512,128]{1,0:T(8,128)(2,1)S(1)}, u32[]{:S(2)}, u32[]{:S(2)}) collective-permute-start(bf16[512,128]{1,0:T(8,128)(2,1)} %own_ref.3), channel_id=1, source_target_pairs={{16,0},{24,8},{32,16},{40,24},{48,32},{56,40},{64,48},{72,56},{80,... | collective-permute-start | bytes 393224 | tf_op jit(solution)/shard_map/ppermute | solution.py:406
  22.4 0.9 %copy-start.1 = (bf16[12,4096]{1,0:T(8,128)(2,1)S(1)}, bf16[12,4096]{1,0:T(8,128)(2,1)}, u32[]{:S(2)}) copy-start(bf16[12,4096]{1,0:T(8,128)(2,1)} %filters_ref.5) | copy-start | bytes 294916
  27.0 5.8 %collective-permute-start.5 = (bf16[4,512,128]{2,1,0:T(8,128)(2,1)S(1)}, bf16[4,512,128]{2,1,0:T(8,128)(2,1)S(1)}, u32[]{:S(2)}, u32[]{:S(2)}) collective-permute-start(bf16[4,512,128]{2,1,0:T(8,128)(2,1)S(1)} %for_sibling.1), channel_id=1, source_target_pairs={{0,8},{8,0},{16,24},{24,16},{32,40},{40,32},{48,56},{56,48},{64,72... | collective-permute-start | bytes 1572872 | tf_op jit(solution)/shard_map/ppermute | solution.py:409
  27.1 15.8 %collective-permute-start.6 = (bf16[2,512,128]{2,1,0:T(8,128)(2,1)S(1)}, bf16[2,512,128]{2,1,0:T(8,128)(2,1)S(1)}, u32[]{:S(2)}, u32[]{:S(2)}) collective-permute-start(bf16[2,512,128]{2,1,0:T(8,128)(2,1)S(1)} %pad_maximum_fusion._.x0_ref), channel_id=1, source_target_pairs={{0,2},{1,3},{2,4},{3,5},{4,6},{5,7},{6,0},{7,1},{8,10},{9,11},{10,... | collective-permute-start | bytes 786440 | tf_op jit(solution)/shard_map/ppermute | solution.py:422
  28.7 15.0 %collective-permute-start.7 = (bf16[2,512,128]{2,1,0:T(8,128)(2,1)S(1)}, bf16[2,512,128]{2,1,0:T(8,128)(2,1)S(1)}, u32[]{:S(2)}, u32[]{:S(2)}) collective-permute-start(bf16[2,512,128]{2,1,0:T(8,128)(2,1)S(1)} %pad_maximum_fusion._.x0_ref), channel_id=1, source_target_pairs={{0,4},{1,5},{2,6},{3,7},{4,0},{5,1},{6,2},{7,3},{8,12},{9,13},{10,... | collective-permute-start | bytes 786440 | tf_op jit(solution)/shard_map/ppermute | solution.py:422
  31.4 12.2 %collective-permute-start.8 = (bf16[2,512,128]{2,1,0:T(8,128)(2,1)S(1)}, bf16[2,512,128]{2,1,0:T(8,128)(2,1)S(1)}, u32[]{:S(2)}, u32[]{:S(2)}) collective-permute-start(bf16[2,512,128]{2,1,0:T(8,128)(2,1)S(1)} %pad_maximum_fusion._.x0_ref), channel_id=1, source_target_pairs={{0,6},{1,7},{2,0},{3,1},{4,2},{5,3},{6,4},{7,5},{8,14},{9,15},{10,... | collective-permute-start | bytes 786440 | tf_op jit(solution)/shard_map/ppermute | solution.py:422
  36.3 2.1 %copy-start.2 = (bf16[12,4096]{1,0:T(8,128)(2,1)S(1)}, bf16[12,4096]{1,0:T(8,128)(2,1)}, u32[]{:S(2)}) copy-start(bf16[12,4096]{1,0:T(8,128)(2,1)} %filters_ref.5) | copy-start | bytes 294916
  38.4 2.1 %copy-start = (bf16[1024,12,128]{2,0,1:T(8,128)(2,1)S(1)}, bf16[1024,12,128]{2,0,1:T(8,128)(2,1)}, u32[]{:S(2)}) copy-start(bf16[1024,12,128]{2,0,1:T(8,128)(2,1)} %param.7) | copy-start | bytes 9437188
  45.6 4.1 %collective-permute-start.9 = (bf16[2,4,6,32,128]{4,3,2,1,0:T(8,128)(2,1)S(1)}, bf16[2,4,6,32,128]{4,3,2,1,0:T(8,128)(2,1)S(1)}, u32[]{:S(2)}, u32[]{:S(2)}) collective-permute-start(bf16[2,4,6,32,128]{4,3,2,1,0:T(8,128)(2,1)S(1)} %get-tuple-element.36._), channel_id=1, source_target_pairs={{0,8},{8,0},{16,24},{24,16},{32,40},{40,32},{48,56},{56,48},{64,72... | collective-permute-start | bytes 1179656 | tf_op jit(solution)/shard_map/ppermute | solution.py:409
  47.3 3.3 %collective-permute-start.10 = (bf16[2,4,6,32,128]{4,3,2,1,0:T(8,128)(2,1)S(1)}, bf16[2,4,6,32,128]{4,3,2,1,0:T(8,128)(2,1)S(1)}, u32[]{:S(2)}, u32[]{:S(2)}) collective-permute-start(bf16[2,4,6,32,128]{4,3,2,1,0:T(8,128)(2,1)S(1)} %get-tuple-element.38._), channel_id=1, source_target_pairs={{0,8},{8,0},{16,24},{24,16},{32,40},{40,32},{48,56},{56,48},{64,72... | collective-permute-start | bytes 1179656 | tf_op jit(solution)/shard_map/ppermute | solution.py:409
  47.9 8.3 %collective-permute-start.11 = (bf16[2,512,128]{2,1,0:T(8,128)(2,1)S(1)}, bf16[2,512,128]{2,1,0:T(8,128)(2,1)S(1)}, u32[]{:S(2)}, u32[]{:S(2)}) collective-permute-start(bf16[2,512,128]{2,1,0:T(8,128)(2,1)S(1)} %get-tuple-element.42), channel_id=1, source_target_pairs={{0,2},{1,3},{2,0},{3,1},{4,6},{5,7},{6,4},{7,5},{8,10},{9,11},{10,... | collective-permute-start | bytes 786440 | tf_op jit(solution)/shard_map/ppermute | solution.py:418
  49.2 9.4 %collective-permute-start.12 = (bf16[2,4,6,32,128]{4,3,2,1,0:T(8,128)(2,1)S(1)}, bf16[2,4,6,32,128]{4,3,2,1,0:T(8,128)(2,1)S(1)}, u32[]{:S(2)}, u32[]{:S(2)}) collective-permute-start(bf16[2,4,6,32,128]{4,3,2,1,0:T(8,128)(2,1)S(1)} %get-tuple-element.45), channel_id=1, source_target_pairs={{0,8},{8,0},{16,24},{24,16},{32,40},{40,32},{48,56},{56,48},{64,72... | collective-permute-start | bytes 1179656 | tf_op jit(solution)/shard_map/ppermute | solution.py:409
  49.2 12.0 %collective-permute-start.14 = (bf16[2,4,6,32,128]{4,3,2,1,0:T(8,128)(2,1)S(1)}, bf16[2,4,6,32,128]{4,3,2,1,0:T(8,128)(2,1)S(1)}, u32[]{:S(2)}, u32[]{:S(2)}) collective-permute-start(bf16[2,4,6,32,128]{4,3,2,1,0:T(8,128)(2,1)S(1)} %get-tuple-element.48), channel_id=1, source_target_pairs={{0,8},{8,0},{16,24},{24,16},{32,40},{40,32},{48,56},{56,48},{64,72... | collective-permute-start | bytes 1179656 | tf_op jit(solution)/shard_map/ppermute | solution.py:409
  49.8 11.1 %collective-permute-start.13 = (bf16[2,4,6,32,128]{4,3,2,1,0:T(8,128)(2,1)S(1)}, bf16[2,4,6,32,128]{4,3,2,1,0:T(8,128)(2,1)S(1)}, u32[]{:S(2)}, u32[]{:S(2)}) collective-permute-start(bf16[2,4,6,32,128]{4,3,2,1,0:T(8,128)(2,1)S(1)} %add.21._), channel_id=1, source_target_pairs={{0,64},{8,72},{16,80},{24,88},{32,96},{40,104},{48,112},{56,120},{... | collective-permute-start | bytes 1179656 | tf_op jit(solution)/shard_map/ppermute | solution.py:412
  50.8 12.3 %collective-permute-start.15 = (bf16[2,4,6,32,128]{4,3,2,1,0:T(8,128)(2,1)S(1)}, bf16[2,4,6,32,128]{4,3,2,1,0:T(8,128)(2,1)S(1)}, u32[]{:S(2)}, u32[]{:S(2)}) collective-permute-start(bf16[2,4,6,32,128]{4,3,2,1,0:T(8,128)(2,1)S(1)} %add.22._), channel_id=1, source_target_pairs={{0,192},{8,200},{16,208},{24,216},{32,224},{40,232},{48,240},{56,2... | collective-permute-start | bytes 1179656 | tf_op jit(solution)/shard_map/ppermute | solution.py:412
  56.3 7.4 %collective-permute-start.16 = (bf16[1,512,128]{2,1,0:T(8,128)(2,1)S(1)}, bf16[1,512,128]{2,1,0:T(8,128)(2,1)S(1)}, u32[]{:S(2)}, u32[]{:S(2)}) collective-permute-start(bf16[1,512,128]{2,1,0:T(8,128)(2,1)S(1)} %get-tuple-element.43._), channel_id=1, source_target_pairs={{0,6},{1,7},{2,4},{3,5},{4,2},{5,3},{6,0},{7,1},{8,14},{9,15},{10,... | collective-permute-start | bytes 393224 | tf_op jit(solution)/shard_map/ppermute | solution.py:418
  58.6 9.5 %collective-permute-start.17 = (bf16[2,512,128]{2,1,0:T(8,128)(2,1)S(1)}, bf16[2,512,128]{2,1,0:T(8,128)(2,1)S(1)}, u32[]{:S(2)}, u32[]{:S(2)}) collective-permute-start(bf16[2,512,128]{2,1,0:T(8,128)(2,1)S(1)} %get-tuple-element.35._), channel_id=1, source_target_pairs={{0,6},{1,7},{2,4},{3,5},{4,2},{5,3},{6,0},{7,1},{8,14},{9,15},{10,... | collective-permute-start | bytes 786440 | tf_op jit(solution)/shard_map/ppermute | solution.py:418
  61.1 9.9 %collective-permute-start.20 = (bf16[1,4,6,32,128]{4,3,2,1,0:T(8,128)(2,1)S(1)}, bf16[1,4,6,32,128]{4,3,2,1,0:T(8,128)(2,1)S(1)}, u32[]{:S(2)}, u32[]{:S(2)}) collective-permute-start(bf16[1,4,6,32,128]{4,3,2,1,0:T(8,128)(2,1)S(1)} %get-tuple-element.46._), channel_id=1, source_target_pairs={{0,192},{8,200},{16,208},{24,216},{32,224},{40,232},{48,240},{56,2... | collective-permute-start | bytes 589832 | tf_op jit(solution)/shard_map/ppermute | solution.py:412
  63.2 8.6 %collective-permute-start.21 = (bf16[1,4,6,32,128]{4,3,2,1,0:T(8,128)(2,1)S(1)}, bf16[1,4,6,32,128]{4,3,2,1,0:T(8,128)(2,1)S(1)}, u32[]{:S(2)}, u32[]{:S(2)}) collective-permute-start(bf16[1,4,6,32,128]{4,3,2,1,0:T(8,128)(2,1)S(1)} %get-tuple-element.49._), channel_id=1, source_target_pairs={{0,64},{8,72},{16,80},{24,88},{32,96},{40,104},{48,112},{56,120},{... | collective-permute-start | bytes 589832 | tf_op jit(solution)/shard_map/ppermute | solution.py:412
  68.2 13.7 %collective-permute-start.18 = (bf16[1,512,128]{2,1,0:T(8,128)(2,1)S(1)}, bf16[1,512,128]{2,1,0:T(8,128)(2,1)S(1)}, u32[]{:S(2)}, u32[]{:S(2)}) collective-permute-start(bf16[1,512,128]{2,1,0:T(8,128)(2,1)S(1)} %get-tuple-element.53._), channel_id=1, source_target_pairs={{0,2},{1,3},{2,0},{3,1},{4,6},{5,7},{6,4},{7,5},{8,10},{9,11},{10,... | collective-permute-start | bytes 393224 | tf_op jit(solution)/shard_map/ppermute | solution.py:418
  68.3 13.6 %collective-permute-start.19 = (bf16[1,512,128]{2,1,0:T(8,128)(2,1)S(1)}, bf16[1,512,128]{2,1,0:T(8,128)(2,1)S(1)}, u32[]{:S(2)}, u32[]{:S(2)}) collective-permute-start(bf16[1,512,128]{2,1,0:T(8,128)(2,1)S(1)} %add.23._), channel_id=1, source_target_pairs={{0,1},{1,0},{2,3},{3,2},{4,5},{5,4},{6,7},{7,6},{8,9},{9,8},{10,11... | collective-permute-start | bytes 393224 | tf_op jit(solution)/shard_map/ppermute | solution.py:455
  71.1 7.7 %collective-permute-start.22 = (bf16[2,6,32,128]{3,2,1,0:T(8,128)(2,1)S(1)}, bf16[2,6,32,128]{3,2,1,0:T(8,128)(2,1)S(1)}, u32[]{:S(2)}, u32[]{:S(2)}) collective-permute-start(bf16[2,6,32,128]{3,2,1,0:T(8,128)(2,1)S(1)} %get-tuple-element.55._), channel_id=1, source_target_pairs={{0,16},{8,24},{16,0},{24,8},{32,48},{40,56},{48,32},{56,40},{64,80... | collective-permute-start | bytes 294920 | tf_op jit(solution)/shard_map/ppermute | solution.py:415
  71.8 8.8 %collective-permute-start.24 = (bf16[2,6,32,128]{3,2,1,0:T(8,128)(2,1)S(1)}, bf16[2,6,32,128]{3,2,1,0:T(8,128)(2,1)S(1)}, u32[]{:S(2)}, u32[]{:S(2)}) collective-permute-start(bf16[2,6,32,128]{3,2,1,0:T(8,128)(2,1)S(1)} %get-tuple-element.57._), channel_id=1, source_target_pairs={{0,16},{8,24},{16,0},{24,8},{32,48},{40,56},{48,32},{56,40},{64,80... | collective-permute-start | bytes 294920 | tf_op jit(solution)/shard_map/ppermute | solution.py:415
  78.8 7.7 %collective-permute-start.23 = (bf16[1,6,32,128]{3,2,1,0:T(8,128)(2,1)S(1)}, bf16[1,6,32,128]{3,2,1,0:T(8,128)(2,1)S(1)}, u32[]{:S(2)}, u32[]{:S(2)}) collective-permute-start(bf16[1,6,32,128]{3,2,1,0:T(8,128)(2,1)S(1)} %get-tuple-element.60._), channel_id=1, source_target_pairs={{0,32},{8,40},{16,48},{24,56},{32,0},{40,8},{48,16},{56,24},{64,96... | collective-permute-start | bytes 147464 | tf_op jit(solution)/shard_map/ppermute | solution.py:415
  80.6 5.9 %collective-permute-start.25 = (bf16[1,6,32,128]{3,2,1,0:T(8,128)(2,1)S(1)}, bf16[1,6,32,128]{3,2,1,0:T(8,128)(2,1)S(1)}, u32[]{:S(2)}, u32[]{:S(2)}) collective-permute-start(bf16[1,6,32,128]{3,2,1,0:T(8,128)(2,1)S(1)} %get-tuple-element.63), channel_id=1, source_target_pairs={{0,32},{8,40},{16,48},{24,56},{32,0},{40,8},{48,16},{56,24},{64,96... | collective-permute-start | bytes 147464 | tf_op jit(solution)/shard_map/ppermute | solution.py:415

commit v11 on v10

--- a/solution.py
+++ b/solution.py
@@ -222,16 +222,14 @@
             full_ref[:, pl.ds(pl.multiple_of(at * LANE, LANE), LANE)] = part[h]
 
 
-def products(crossed, pos_ref, corr_ref, full_ref, out_refs):
+def products(crossed, pos_ref, corr_ref, full_ref, slots):
     y, z_lo, core = coords(pos_ref)[2:]
-    stay_ref, leave_ref, send_stay_ref, send_leave_ref = out_refs
     deep = NZ_LO * NCORE * 32
-    for s, at in enumerate(ring_slots(y, crossed)):
+    for at, (keep_ref, send_ref, s) in zip(ring_slots(y, crossed), slots):
         part = full_ref[:, pl.ds(pl.multiple_of(at * deep, deep), deep)]
         result = lax.dot_general(
             part, corr_ref[...], (((0,), (0,)), ((), ())), preferred_element_type=F32
         ).astype(BF16)
-        keep_ref, send_ref = (stay_ref, send_stay_ref) if s < 2 else (leave_ref, send_leave_ref)
         for z in range(NZ_LO):
             shift = z ^ z_lo
             slot = lax.rem(shift, 2) * 2 + shift // 2
@@ -239,25 +237,33 @@
                 columns = slice(k * LANE, (k + 1) * LANE)
                 even = result[z * 64 : z * 64 + 32, columns]
                 odd = result[z * 64 + 32 : z * 64 + 64, columns]
-                keep_ref[s % 2, slot, k] = jnp.where(core == 0, even, odd)
-                send_ref[s % 2, slot, k] = jnp.where(core == 0, odd, even)
-
-
-def first_product_kernel(crossed, pos_ref, _, corr_ref, x0_ref, x1_ref, x2_ref, x3_ref, full_ref, *out_refs):
+                keep_ref[s, slot, k] = jnp.where(core == 0, even, odd)
+                send_ref[s, slot, k] = jnp.where(core == 0, odd, even)
+
+
+def first_product_kernel(
+    crossed, pos_ref, _, corr_ref, x0_ref, x1_ref, x2_ref, x3_ref, full_ref, keep_ref, send_ref
+):
     gathered_columns(pos_ref, (x0_ref, x1_ref, x2_ref, x3_ref), full_ref)
-    products(crossed, pos_ref, corr_ref, full_ref, out_refs)
-
-
-def next_product_kernel(crossed, pos_ref, _, corr_ref, full_ref, *out_refs):
-    products(crossed, pos_ref, corr_ref, full_ref, out_refs)
-
-
-def product(kernel, crossed, pos, after, corr, sources, keep_full):
+    products(crossed, pos_ref, corr_ref, full_ref, [(keep_ref, send_ref, s) for s in range(NY)])
+
+
+def last_product_kernel(
+    crossed, pos_ref, _, corr_ref, full_ref, stay_ref, leave_ref, send_stay_ref, send_leave_ref
+):
+    slots = [(stay_ref, send_stay_ref, s) for s in range(2)]
+    slots += [(leave_ref, send_leave_ref, s) for s in range(2)]
+    products(crossed, pos_ref, corr_ref, full_ref, slots)
+
+
+def product(kernel, crossed, pos, after, corr, sources, first):
     tok, width = corr.shape
-    part = jax.ShapeDtypeStruct((2, NZ_LO, width // LANE, 32, LANE), BF16)
-    vmem = pl.BlockSpec(memory_space=pltpu.VMEM)
-    full = [jax.ShapeDtypeStruct((tok, 1024), BF16)] if keep_full else []
-    outs = full + [part] * 4
+    rest = (NZ_LO, width // LANE, 32, LANE)
+    vmem = pl.BlockSpec(memory_space=pltpu.VMEM)
+    outs = [jax.ShapeDtypeStruct((2,) + rest, BF16)] * 4
+    if first:
+        outs = [jax.ShapeDtypeStruct((tok, 1024), BF16)]
+        outs += [jax.ShapeDtypeStruct((NY,) + rest, BF16)] * 2
     return pl.pallas_call(
         functools.partial(kernel, crossed),
         out_shape=outs,
@@ -434,28 +440,28 @@
         pos, corr_1, [corr_0, corr_1], projection.transpose(1, 0, 2)
     )
     x_far, x_near = x_swapped(far_send, False), x_swapped(near_send, True)
-    full, stay_0, leave_0, send_stay_0, send_leave_0 = product(
+    full, keep_0, send_0 = product(
         first_product_kernel, False, pos, near_send, corr_0, gathered, True
     )
     stay_1, leave_1, send_stay_1, send_leave_1 = product(
-        next_product_kernel, True, pos, send_leave_0, corr_1, [full], False
+        last_product_kernel, True, pos, send_0, corr_1, [full], False
     )
-    leave_0 = add(send_leave_1, leave_0, sibling(send_leave_0))
+    stay_0, leave_0 = halve(send_leave_1, keep_0, sibling(send_0))
     y_0 = y_swapped(leave_0, False)
     leave_1 = add(leave_0, leave_1, sibling(send_leave_1))
     y_1 = y_swapped(leave_1, True)
-    beside_0, beside_1 = sibling(send_stay_0), sibling(send_stay_1)
+    beside_1 = sibling(send_stay_1)
     far, leave = halve(leave_1, far, x_far, LARGE_COST)
     x_far = x_swapped(leave, True)
-    stay_0, leave_0 = halve_three(leave, stay_0, beside_0, y_0)
+    near, leave = halve(leave, near, x_near)
+    x_near = x_swapped(leave, False)
+    stay_0, leave_0 = halve(leave, stay_0, y_0)
     y_0 = y_swapped(leave_0, True)
     stay_1, leave_1 = halve_three(leave_0, stay_1, beside_1, y_1)
     y_1 = y_swapped(leave_1, False)
     far = add(leave_1, far, x_far, LARGE_COST)
     opposite = lax.ppermute(far, "tp", Z_HI_SWAP)
-    near, leave = halve(far, near, x_near)
-    x_near = x_swapped(leave, False)
-    stay_0, leave_0 = halve(leave, stay_0[0], y_0[0])
+    stay_0, leave_0 = halve(far, stay_0[0], y_0[0])
     z_0 = z_swapped(leave_0, 1)
     stay_1, leave_1 = halve(leave_0, stay_1[0], y_1[0])
     z_1 = z_swapped(leave_1, 1)

time: 88 us -> 86.8 us (0.986)
  the two profiles are of different devices: /device:TPU:24 before, /device:TPU:1 now
where the time goes in v11:
time: 86.8 us; the launch traced here: 86.6 us
  starting transfers between devices  37.5 us (43%)
  waiting for transfers between devices  29 us (33%)
  Pallas kernels  16.7 us (19%)
  other arithmetic  1.71 us (2%)
  local copies, waits for them, and re-layouts  0.92 us (1%)
  between operations  0.89 us (1%)
    ppermute x4, waiting for transfers between devices, z_swapped(): return lax.ppermute(value, 'ctx', z_swap(bit))  11.9 us
    ppermute x4, waiting for transfers between devices, y_swapped(): return lax.ppermute(value, 'ctx', y_swap(crossed))  8.33 us
    ppermute x4, starting transfers between devices, y_swapped(): return lax.ppermute(value, 'ctx', y_swap(crossed))  8.25 us
    ppermute x4, waiting for transfers between devices, later(): return lax.ppermute(value, 'ctx', from_later_chip(steps))  7.93 us
    ppermute x1, starting transfers between devices, per_device(): pair = jnp.stack([inputs, lax.ppermute(inputs, 'tp', Z_HI_SWAP)])  7.83 us
    ppermute x4, starting transfers between devices, later(): return lax.ppermute(value, 'ctx', from_later_chip(steps))  5.16 us
    ppermute x3, starting transfers between devices, per_device(): lax.ppermute(pair, 'tp', along_x(s))  4.83 us
    pallas_call x2, Pallas kernels, far_conv(): pl.pallas_call(functools.partial(far_kernel, first), out_shape=jax.ShapeD...  4.16 us
  transfers between devices with their start and end apart: 25, of which 8 were waited for; matrix products, arithmetic and copies ran while one was open for 2% of the time, Pallas kernels for 15%

profile of v11, /device:TPU:1, one launch (start us, length us, event | category | flops | bytes accessed | tf_op | source)
XLA Modules:
  0.0 86.6 jit_solution(8606762236169375575)
XLA Ops:
  0.6 7.8 %collective-permute-start = (bf16[512,128]{1,0:T(8,128)(2,1)}, bf16[512,128]{1,0:T(8,128)(2,1)S(1)}, u32[]{:S(2)}, u32[]{:S(2)}) collective-permute-start(bf16[512,128]{1,0:T(8,128)(2,1)} %param.4), channel_id=1, source_target_pairs={{0,1},{1,0},{2,3},{3,2},{4,5},{5,4},{6,7},{7,6},{8,9},{9,8},{10,11... | collective-permute-start | bytes 393224 | tf_op jit(solution)/shard_map/ppermute | solution.py:427
  8.5 1.3 %collective-permute-start.2 = (bf16[512,128]{1,0:T(8,128)(2,1)}, bf16[512,128]{1,0:T(8,128)(2,1)S(1)}, u32[]{:S(2)}, u32[]{:S(2)}) collective-permute-start(bf16[512,128]{1,0:T(8,128)(2,1)} %own_ref.3), channel_id=1, source_target_pairs={{32,0},{40,8},{48,16},{56,24},{64,32},{72,40},{80,48},{88,56},{96,... | collective-permute-start | bytes 393224 | tf_op jit(solution)/shard_map/ppermute | solution.py:412
  9.8 1.3 %collective-permute-start.3 = (bf16[512,128]{1,0:T(8,128)(2,1)}, bf16[512,128]{1,0:T(8,128)(2,1)S(1)}, u32[]{:S(2)}, u32[]{:S(2)}) collective-permute-start(bf16[512,128]{1,0:T(8,128)(2,1)} %own_ref.3), channel_id=1, source_target_pairs={{48,0},{56,8},{64,16},{72,24},{80,32},{88,40},{96,48},{104,56},{11... | collective-permute-start | bytes 393224 | tf_op jit(solution)/shard_map/ppermute | solution.py:412
  11.1 1.3 %collective-permute-start.4 = (bf16[512,128]{1,0:T(8,128)(2,1)}, bf16[512,128]{1,0:T(8,128)(2,1)S(1)}, u32[]{:S(2)}, u32[]{:S(2)}) collective-permute-start(bf16[512,128]{1,0:T(8,128)(2,1)} %own_ref.3), channel_id=1, source_target_pairs={{64,0},{72,8},{80,16},{88,24},{96,32},{104,40},{112,48},{120,56},{... | collective-permute-start | bytes 393224 | tf_op jit(solution)/shard_map/ppermute | solution.py:412
  12.4 1.3 %collective-permute-start.1 = (bf16[512,128]{1,0:T(8,128)(2,1)}, bf16[512,128]{1,0:T(8,128)(2,1)S(1)}, u32[]{:S(2)}, u32[]{:S(2)}) collective-permute-start(bf16[512,128]{1,0:T(8,128)(2,1)} %own_ref.3), channel_id=1, source_target_pairs={{16,0},{24,8},{32,16},{40,24},{48,32},{56,40},{64,48},{72,56},{80,... | collective-permute-start | bytes 393224 | tf_op jit(solution)/shard_map/ppermute | solution.py:412
  13.7 0.1 pad_add_fusion.pos_ref
  13.7 0.9 %pad_maximum_fusion._.x0_ref = bf16[2,512,128]{2,1,0:T(8,128)(2,1)S(1)} fusion(bf16[1,512,128]{2,1,0:T(8,128)(2,1)S(1)} %bitcast.19, bf16[1,512,128]{2,1,0:T(8,128)(2,1)} %bitcast.18), kind=kLoop, calls=%fused_computation | loop fusion | flops 131072 | bytes 524288 | tf_op jit(solution)/shard_map/stack | solution.py:427
  14.7 0.0 copy-start.1
  14.7 0.9 %copy-done.1 = bf16[12,4096]{1,0:T(8,128)(2,1)S(1)} copy-done((bf16[12,4096]{1,0:T(8,128)(2,1)S(1)}, bf16[12,4096]{1,0:T(8,128)(2,1)}, u32[]{:S(2)}) %copy-start.1) | copy-done | bytes 98328
  15.6 0.9 %near_table.1._.table_ref = bf16[12,64,2048]{2,1,0:T(8,128)(2,1)S(1)} custom-call(bf16[2,512,128]{2,1,0:T(8,128)(2,1)S(1)} %pad_maximum_fusion._.x0_ref, bf16[12,4096]{1,0:T(8,128)(2,1)S(1)} %copy-done.1), custom_call_target="tpu_custom_call" | custom-call | flops 1000 | bytes 1000 | tf_op jit(solution)/shard_map/near_table/pallas_call | solution.py:79
  16.5 7.9 %collective-permute-done.2.r2_ref = bf16[512,128]{1,0:T(8,128)(2,1)S(1)} collective-permute-done((bf16[512,128]{1,0:T(8,128)(2,1)}, bf16[512,128]{1,0:T(8,128)(2,1)S(1)}, u32[]{:S(2)}, u32[]{:S(2)}) %collective-permute-start.2) | collective-permute-done | bytes 131104 | tf_op jit(solution)/shard_map/ppermute | solution.py:412
  24.4 0.0 collective-permute-done.3.r3_ref
  24.4 0.0 collective-permute-done.4.r4_ref
  24.4 0.0 collective-permute-done.1.r1_ref
  24.4 0.8 for_sibling.1
  25.3 1.5 %collective-permute-start.5 = (bf16[4,512,128]{2,1,0:T(8,128)(2,1)S(1)}, bf16[4,512,128]{2,1,0:T(8,128)(2,1)S(1)}, u32[]{:S(2)}, u32[]{:S(2)}) collective-permute-start(bf16[4,512,128]{2,1,0:T(8,128)(2,1)S(1)} %for_sibling.1), channel_id=1, source_target_pairs={{0,8},{8,0},{16,24},{24,16},{32,40},{40,32},{48,56},{56,48},{64,72... | collective-permute-start | bytes 1572872 | tf_op jit(solution)/shard_map/ppermute | solution.py:415
  26.8 1.2 %collective-permute-start.6 = (bf16[2,512,128]{2,1,0:T(8,128)(2,1)S(1)}, bf16[2,512,128]{2,1,0:T(8,128)(2,1)S(1)}, u32[]{:S(2)}, u32[]{:S(2)}) collective-permute-start(bf16[2,512,128]{2,1,0:T(8,128)(2,1)S(1)} %pad_maximum_fusion._.x0_ref), channel_id=1, source_target_pairs={{0,2},{1,3},{2,4},{3,5},{4,6},{5,7},{6,0},{7,1},{8,10},{9,11},{10,... | collective-permute-start | bytes 786440 | tf_op jit(solution)/shard_map/ppermute | solution.py:428
  28.1 2.5 %collective-permute-start.7 = (bf16[2,512,128]{2,1,0:T(8,128)(2,1)S(1)}, bf16[2,512,128]{2,1,0:T(8,128)(2,1)S(1)}, u32[]{:S(2)}, u32[]{:S(2)}) collective-permute-start(bf16[2,512,128]{2,1,0:T(8,128)(2,1)S(1)} %pad_maximum_fusion._.x0_ref), channel_id=1, source_target_pairs={{0,4},{1,5},{2,6},{3,7},{4,0},{5,1},{6,2},{7,3},{8,12},{9,13},{10,... | collective-permute-start | bytes 786440 | tf_op jit(solution)/shard_map/ppermute | solution.py:428
  30.5 1.2 %collective-permute-start.8 = (bf16[2,512,128]{2,1,0:T(8,128)(2,1)S(1)}, bf16[2,512,128]{2,1,0:T(8,128)(2,1)S(1)}, u32[]{:S(2)}, u32[]{:S(2)}) collective-permute-start(bf16[2,512,128]{2,1,0:T(8,128)(2,1)S(1)} %pad_maximum_fusion._.x0_ref), channel_id=1, source_target_pairs={{0,6},{1,7},{2,0},{3,1},{4,2},{5,3},{6,4},{7,5},{8,14},{9,15},{10,... | collective-permute-start | bytes 786440 | tf_op jit(solution)/shard_map/ppermute | solution.py:428
  31.7 3.4 %near_conv.1 = (f32[4,384,256]{2,1,0:T(8,128)S(1)}, f32[4,384,256]{2,1,0:T(8,128)S(1)}) custom-call(bf16[12,64,2048]{2,1,0:T(8,128)(2,1)S(1)} %near_table.1._.table_ref, bf16[512,128]{1,0:T(8,128)(2,1)S(1)} %copy-done.3, bf16[512,128]{1,0:T(8,128)(2,1)S(1)} %collective-permute-done.1.r1_ref, bf16[512,128]{1,0:T(8,128)(2,1)S(1)} %collective-permute-done.2.r2_ref, ...), custom_call_target="tpu_custom_call" | custom-call | flops 4000000000 | bytes 8000000 | tf_op jit(solution)/shard_map/near_conv/pallas_call | solution.py:158
  35.1 0.0 copy-start.2
  35.1 2.1 %far_conv.2._.refs_0_.corr_ref = bf16[512,768]{1,0:T(8,128)(2,1)S(1)} custom-call(bf16[12,64,2048]{2,1,0:T(8,128)(2,1)S(1)} %near_table.1._.table_ref, bf16[12,4096]{1,0:T(8,128)(2,1)S(1)} %copy-done.1, f32[4,384,256]{2,1,0:T(8,128)S(1)} %get-tuple-element.33.acc_ref, bf16[512,128]{1,0:T(8,128)(2,1)S(1)} %collective-permute-done.2.r2_ref, ...), custom_call_target="tpu_custom_call" | custom-call | flops 1000 | bytes 1000 | tf_op jit(solution)/shard_map/far_conv/pallas_call | solution.py:202
  37.2 0.0 copy-start
  37.2 2.1 %far_conv.3._.refs_1_.corr_ref = bf16[512,768]{1,0:T(8,128)(2,1)S(1)} custom-call(bf16[512,768]{1,0:T(8,128)(2,1)S(1)} %far_conv.2._.refs_0_.corr_ref, bf16[12,4096]{1,0:T(8,128)(2,1)S(1)} %copy-done.2, f32[4,384,256]{2,1,0:T(8,128)S(1)} %get-tuple-element.34.acc_ref, bf16[512,128]{1,0:T(8,128)(2,1)S(1)} %collective-permute-done.2.r2_ref, ...), custom_call_target="tpu_custom_call" | custom-call | flops 1000 | bytes 1000 | tf_op jit(solution)/shard_map/far_conv/pallas_call | solution.py:202
  39.3 2.4 %input_shares.1 = (f32[2,512,128]{2,1,0:T(8,128)S(1)}, bf16[2,512,128]{2,1,0:T(8,128)(2,1)S(1)}, f32[2,512,128]{2,1,0:T(8,128)S(1)}, bf16[2,512,128]{2,1,0:T(8,128)(2,1)S(1)}) custom-call(s32[2]{0:T(128)S(1)} %pad_add_fusion.pos_ref, bf16[512,768]{1,0:T(8,128)(2,1)S(1)} %far_conv.3._.refs_1_.corr_ref, bf16[512,768]{1,0:T(8,128)(2,1)S(1)} %far_conv.2._.refs_0_.corr_ref, ...), custom_call_target="tpu_custom_call" | custom-call | flops 1000 | bytes 1000 | tf_op jit(solution)/shard_map/input_shares/pallas_call | solution.py:391
  41.7 0.8 collective-permute-done.7.x2_ref
  42.5 0.0 collective-permute-done.8.x3_ref
  42.5 1.9 %product.2 = (bf16[512,1024]{1,0:T(8,128)(2,1)S(1)}, bf16[4,4,6,32,128]{4,3,2,1,0:T(8,128)(2,1)S(1)}, bf16[4,4,6,32,128]{4,3,2,1,0:T(8,128)(2,1)S(1)}) custom-call(s32[2]{0:T(128)S(1)} %pad_add_fusion.pos_ref, bf16[2,512,128]{2,1,0:T(8,128)(2,1)S(1)} %get-tuple-element.35._, bf16[512,768]{1,0:T(8,128)(2,1)S(1)} %far_conv.2._.refs_0_.corr_ref, ...), custom_call_target="tpu_custom_call" | custom-call | flops 1000 | bytes 1000 | tf_op jit(solution)/shard_map/product/pallas_call | solution.py:267
  44.5 1.0 %collective-permute-start.9 = (bf16[4,4,6,32,128]{4,3,2,1,0:T(8,128)(2,1)S(1)}, bf16[4,4,6,32,128]{4,3,2,1,0:T(8,128)(2,1)S(1)}, u32[]{:S(2)}, u32[]{:S(2)}) collective-permute-start(bf16[4,4,6,32,128]{4,3,2,1,0:T(8,128)(2,1)S(1)} %get-tuple-element.36._), channel_id=1, source_target_pairs={{0,8},{8,0},{16,24},{24,16},{32,40},{40,32},{48,56},{56,48},{64,72... | collective-permute-start | bytes 2359304 | tf_op jit(solution)/shard_map/ppermute | solution.py:415
  45.4 1.6 %product.3 = (bf16[2,4,6,32,128]{4,3,2,1,0:T(8,128)(2,1)S(1)}, bf16[2,4,6,32,128]{4,3,2,1,0:T(8,128)(2,1)S(1)}, bf16[2,4,6,32,128]{4,3,2,1,0:T(8,128)(2,1)S(1)}, bf16[2,4,6,32,128]{4,3,2,1,0:T(8,128)(2,1)S(1)}) custom-call(s32[2]{0:T(128)S(1)} %pad_add_fusion.pos_ref, bf16[4,4,6,32,128]{4,3,2,1,0:T(8,128)(2,1)S(1)} %get-tuple-element.36._, ...), custom_call_target="tpu_custom_call" | custom-call | flops 1000 | bytes 1000 | tf_op jit(solution)/shard_map/product/pallas_call | solution.py:267
  47.0 0.1 collective-permute-start.10
  47.1 1.1 %collective-permute-start.11 = (bf16[2,512,128]{2,1,0:T(8,128)(2,1)S(1)}, bf16[2,512,128]{2,1,0:T(8,128)(2,1)S(1)}, u32[]{:S(2)}, u32[]{:S(2)}) collective-permute-start(bf16[2,512,128]{2,1,0:T(8,128)(2,1)S(1)} %get-tuple-element.43), channel_id=1, source_target_pairs={{0,2},{1,3},{2,0},{3,1},{4,6},{5,7},{6,4},{7,5},{8,10},{9,11},{10,... | collective-permute-start | bytes 786440 | tf_op jit(solution)/shard_map/ppermute | solution.py:424
  48.3 1.6 %collective-permute-start.12 = (bf16[2,512,128]{2,1,0:T(8,128)(2,1)S(1)}, bf16[2,512,128]{2,1,0:T(8,128)(2,1)S(1)}, u32[]{:S(2)}, u32[]{:S(2)}) collective-permute-start(bf16[2,512,128]{2,1,0:T(8,128)(2,1)S(1)} %get-tuple-element.35._), channel_id=1, source_target_pairs={{0,6},{1,7},{2,4},{3,5},{4,2},{5,3},{6,0},{7,1},{8,14},{9,15},{10,... | collective-permute-start | bytes 786440 | tf_op jit(solution)/shard_map/ppermute | solution.py:424
  49.9 1.0 %collective-permute-start.15 = (bf16[2,4,6,32,128]{4,3,2,1,0:T(8,128)(2,1)S(1)}, bf16[2,4,6,32,128]{4,3,2,1,0:T(8,128)(2,1)S(1)}, u32[]{:S(2)}, u32[]{:S(2)}) collective-permute-start(bf16[2,4,6,32,128]{4,3,2,1,0:T(8,128)(2,1)S(1)} %get-tuple-element.51), channel_id=1, source_target_pairs={{0,8},{8,0},{16,24},{24,16},{32,40},{40,32},{48,56},{56,48},{64,72... | collective-permute-start | bytes 1179656 | tf_op jit(solution)/shard_map/ppermute | solution.py:415
  50.8 0.0 collective-permute-done.9.other_ref
  50.9 0.2 halve.8
  51.0 3.2 %collective-permute-start.14 = (bf16[2,4,6,32,128]{4,3,2,1,0:T(8,128)(2,1)S(1)}, bf16[2,4,6,32,128]{4,3,2,1,0:T(8,128)(2,1)S(1)}, u32[]{:S(2)}, u32[]{:S(2)}) collective-permute-start(bf16[2,4,6,32,128]{4,3,2,1,0:T(8,128)(2,1)S(1)} %get-tuple-element.40._), channel_id=1, source_target_pairs={{0,64},{8,72},{16,80},{24,88},{32,96},{40,104},{48,112},{56,120},{... | collective-permute-start | bytes 1179656 | tf_op jit(solution)/shard_map/ppermute | solution.py:418
  54.2 0.1 add.20._
  54.3 2.2 %collective-permute-start.16 = (bf16[2,4,6,32,128]{4,3,2,1,0:T(8,128)(2,1)S(1)}, bf16[2,4,6,32,128]{4,3,2,1,0:T(8,128)(2,1)S(1)}, u32[]{:S(2)}, u32[]{:S(2)}) collective-permute-start(bf16[2,4,6,32,128]{4,3,2,1,0:T(8,128)(2,1)S(1)} %add.20._), channel_id=1, source_target_pairs={{0,192},{8,200},{16,208},{24,216},{32,224},{40,232},{48,240},{56,2... | collective-permute-start | bytes 1179656 | tf_op jit(solution)/shard_map/ppermute | solution.py:418
  56.5 0.0 collective-permute-done.11.other_ref
  56.5 0.1 halve.9
  56.6 1.2 %collective-permute-start.17 = (bf16[1,512,128]{2,1,0:T(8,128)(2,1)S(1)}, bf16[1,512,128]{2,1,0:T(8,128)(2,1)S(1)}, u32[]{:S(2)}, u32[]{:S(2)}) collective-permute-start(bf16[1,512,128]{2,1,0:T(8,128)(2,1)S(1)} %get-tuple-element.44._), channel_id=1, source_target_pairs={{0,6},{1,7},{2,4},{3,5},{4,2},{5,3},{6,0},{7,1},{8,14},{9,15},{10,... | collective-permute-start | bytes 393224 | tf_op jit(solution)/shard_map/ppermute | solution.py:424
  57.7 0.0 collective-permute-done.12.other_ref
  57.8 0.1 collective-permute-start.13
  57.9 5.8 %collective-permute-done.14.other_ref = bf16[2,4,6,32,128]{4,3,2,1,0:T(8,128)(2,1)S(1)} collective-permute-done((bf16[2,4,6,32,128]{4,3,2,1,0:T(8,128)(2,1)S(1)}, bf16[2,4,6,32,128]{4,3,2,1,0:T(8,128)(2,1)S(1)}, u32[]{:S(2)}, u32[]{:S(2)}) %collective-permute-start.14) | collective-permute-done | bytes 393248 | tf_op jit(solution)/shard_map/ppermute | solution.py:418
  63.7 0.1 halve.11
  63.8 2.8 %collective-permute-start.19 = (bf16[1,4,6,32,128]{4,3,2,1,0:T(8,128)(2,1)S(1)}, bf16[1,4,6,32,128]{4,3,2,1,0:T(8,128)(2,1)S(1)}, u32[]{:S(2)}, u32[]{:S(2)}) collective-permute-start(bf16[1,4,6,32,128]{4,3,2,1,0:T(8,128)(2,1)S(1)} %get-tuple-element.49._), channel_id=1, source_target_pairs={{0,192},{8,200},{16,208},{24,216},{32,224},{40,232},{48,240},{56,2... | collective-permute-start | bytes 589832 | tf_op jit(solution)/shard_map/ppermute | solution.py:418
  66.5 0.0 collective-permute-done.15.beside_ref
  66.5 0.0 collective-permute-done.16.other_ref
  66.5 0.1 halve_three.1
  66.7 0.1 collective-permute-start.20
  66.8 2.4 %collective-permute-start.18 = (bf16[1,512,128]{2,1,0:T(8,128)(2,1)S(1)}, bf16[1,512,128]{2,1,0:T(8,128)(2,1)S(1)}, u32[]{:S(2)}, u32[]{:S(2)}) collective-permute-start(bf16[1,512,128]{2,1,0:T(8,128)(2,1)S(1)} %add.21._), channel_id=1, source_target_pairs={{0,1},{1,0},{2,3},{3,2},{4,5},{5,4},{6,7},{7,6},{8,9},{9,8},{10,11... | collective-permute-start | bytes 393224 | tf_op jit(solution)/shard_map/ppermute | solution.py:463
  69.3 1.7 %collective-permute-done.19 = bf16[1,4,6,32,128]{4,3,2,1,0:T(8,128)(2,1)S(1)} collective-permute-done((bf16[1,4,6,32,128]{4,3,2,1,0:T(8,128)(2,1)S(1)}, bf16[1,4,6,32,128]{4,3,2,1,0:T(8,128)(2,1)S(1)}, u32[]{:S(2)}, u32[]{:S(2)}) %collective-permute-start.19) | collective-permute-done | bytes 196640 | tf_op jit(solution)/shard_map/ppermute | solution.py:418
  71.0 0.3 collective-permute-start.21
  71.3 0.8 collective-permute-done.20
  72.2 0.6 collective-permute-start.23
  72.7 5.5 %collective-permute-done.21.other_ref = bf16[2,6,32,128]{3,2,1,0:T(8,128)(2,1)S(1)} collective-permute-done((bf16[2,6,32,128]{3,2,1,0:T(8,128)(2,1)S(1)}, bf16[2,6,32,128]{3,2,1,0:T(8,128)(2,1)S(1)}, u32[]{:S(2)}, u32[]{:S(2)}) %collective-permute-start.21) | collective-permute-done | bytes 98336 | tf_op jit(solution)/shard_map/ppermute | solution.py:421
  78.3 0.1 collective-permute-start.22
  78.4 2.0 %collective-permute-done.23.other_ref = bf16[2,6,32,128]{3,2,1,0:T(8,128)(2,1)S(1)} collective-permute-done((bf16[2,6,32,128]{3,2,1,0:T(8,128)(2,1)S(1)}, bf16[2,6,32,128]{3,2,1,0:T(8,128)(2,1)S(1)}, u32[]{:S(2)}, u32[]{:S(2)}) %collective-permute-start.23) | collective-permute-done | bytes 98336 | tf_op jit(solution)/shard_map/ppermute | solution.py:421
  80.4 0.5 collective-permute-start.24
  80.9 0.0 collective-permute-done.18
  80.9 0.7 fusion
  81.6 4.3 %collective-permute-done.24.refs_3_ = bf16[1,6,32,128]{3,2,1,0:T(8,128)(2,1)S(1)} collective-permute-done((bf16[1,6,32,128]{3,2,1,0:T(8,128)(2,1)S(1)}, bf16[1,6,32,128]{3,2,1,0:T(8,128)(2,1)S(1)}, u32[]{:S(2)}, u32[]{:S(2)}) %collective-permute-start.24) | collective-permute-done | bytes 49184 | tf_op jit(solution)/shard_map/ppermute | solution.py:421
  85.9 0.7 join.1
  (17 shorter events, 0.2 us)
Async XLA Ops:
  0.6 23.8 %copy-start.3 = (bf16[512,128]{1,0:T(8,128)(2,1)S(1)}, bf16[512,128]{1,0:T(8,128)(2,1)}, u32[]{:S(2)}) copy-start(bf16[512,128]{1,0:T(8,128)(2,1)} %own_ref.3) | copy-start | bytes 393220
  0.6 13.1 %collective-permute-start = (bf16[512,128]{1,0:T(8,128)(2,1)}, bf16[512,128]{1,0:T(8,128)(2,1)S(1)}, u32[]{:S(2)}, u32[]{:S(2)}) collective-permute-start(bf16[512,128]{1,0:T(8,128)(2,1)} %param.4), channel_id=1, source_target_pairs={{0,1},{1,0},{2,3},{3,2},{4,5},{5,4},{6,7},{7,6},{8,9},{9,8},{10,11... | collective-permute-start | bytes 393224 | tf_op jit(solution)/shard_map/ppermute | solution.py:427
  8.5 16.0 %collective-permute-start.2 = (bf16[512,128]{1,0:T(8,128)(2,1)}, bf16[512,128]{1,0:T(8,128)(2,1)S(1)}, u32[]{:S(2)}, u32[]{:S(2)}) collective-permute-start(bf16[512,128]{1,0:T(8,128)(2,1)} %own_ref.3), channel_id=1, source_target_pairs={{32,0},{40,8},{48,16},{56,24},{64,32},{72,40},{80,48},{88,56},{96,... | collective-permute-start | bytes 393224 | tf_op jit(solution)/shard_map/ppermute | solution.py:412
  9.8 14.7 %collective-permute-start.3 = (bf16[512,128]{1,0:T(8,128)(2,1)}, bf16[512,128]{1,0:T(8,128)(2,1)S(1)}, u32[]{:S(2)}, u32[]{:S(2)}) collective-permute-start(bf16[512,128]{1,0:T(8,128)(2,1)} %own_ref.3), channel_id=1, source_target_pairs={{48,0},{56,8},{64,16},{72,24},{80,32},{88,40},{96,48},{104,56},{11... | collective-permute-start | bytes 393224 | tf_op jit(solution)/shard_map/ppermute | solution.py:412
  11.1 13.4 %collective-permute-start.4 = (bf16[512,128]{1,0:T(8,128)(2,1)}, bf16[512,128]{1,0:T(8,128)(2,1)S(1)}, u32[]{:S(2)}, u32[]{:S(2)}) collective-permute-start(bf16[512,128]{1,0:T(8,128)(2,1)} %own_ref.3), channel_id=1, source_target_pairs={{64,0},{72,8},{80,16},{88,24},{96,32},{104,40},{112,48},{120,56},{... | collective-permute-start | bytes 393224 | tf_op jit(solution)/shard_map/ppermute | solution.py:412
  12.4 12.1 %collective-permute-start.1 = (bf16[512,128]{1,0:T(8,128)(2,1)}, bf16[512,128]{1,0:T(8,128)(2,1)S(1)}, u32[]{:S(2)}, u32[]{:S(2)}) collective-permute-start(bf16[512,128]{1,0:T(8,128)(2,1)} %own_ref.3), channel_id=1, source_target_pairs={{16,0},{24,8},{32,16},{40,24},{48,32},{56,40},{64,48},{72,56},{80,... | collective-permute-start | bytes 393224 | tf_op jit(solution)/shard_map/ppermute | solution.py:412
  14.7 0.9 %copy-start.1 = (bf16[12,4096]{1,0:T(8,128)(2,1)S(1)}, bf16[12,4096]{1,0:T(8,128)(2,1)}, u32[]{:S(2)}) copy-start(bf16[12,4096]{1,0:T(8,128)(2,1)} %filters_ref.5) | copy-start | bytes 294916
  25.3 6.4 %collective-permute-start.5 = (bf16[4,512,128]{2,1,0:T(8,128)(2,1)S(1)}, bf16[4,512,128]{2,1,0:T(8,128)(2,1)S(1)}, u32[]{:S(2)}, u32[]{:S(2)}) collective-permute-start(bf16[4,512,128]{2,1,0:T(8,128)(2,1)S(1)} %for_sibling.1), channel_id=1, source_target_pairs={{0,8},{8,0},{16,24},{24,16},{32,40},{40,32},{48,56},{56,48},{64,72... | collective-permute-start | bytes 1572872 | tf_op jit(solution)/shard_map/ppermute | solution.py:415
  26.8 14.9 %collective-permute-start.6 = (bf16[2,512,128]{2,1,0:T(8,128)(2,1)S(1)}, bf16[2,512,128]{2,1,0:T(8,128)(2,1)S(1)}, u32[]{:S(2)}, u32[]{:S(2)}) collective-permute-start(bf16[2,512,128]{2,1,0:T(8,128)(2,1)S(1)} %pad_maximum_fusion._.x0_ref), channel_id=1, source_target_pairs={{0,2},{1,3},{2,4},{3,5},{4,6},{5,7},{6,0},{7,1},{8,10},{9,11},{10,... | collective-permute-start | bytes 786440 | tf_op jit(solution)/shard_map/ppermute | solution.py:428
  28.1 14.5 %collective-permute-start.7 = (bf16[2,512,128]{2,1,0:T(8,128)(2,1)S(1)}, bf16[2,512,128]{2,1,0:T(8,128)(2,1)S(1)}, u32[]{:S(2)}, u32[]{:S(2)}) collective-permute-start(bf16[2,512,128]{2,1,0:T(8,128)(2,1)S(1)} %pad_maximum_fusion._.x0_ref), channel_id=1, source_target_pairs={{0,4},{1,5},{2,6},{3,7},{4,0},{5,1},{6,2},{7,3},{8,12},{9,13},{10,... | collective-permute-start | bytes 786440 | tf_op jit(solution)/shard_map/ppermute | solution.py:428
  30.5 12.0 %collective-permute-start.8 = (bf16[2,512,128]{2,1,0:T(8,128)(2,1)S(1)}, bf16[2,512,128]{2,1,0:T(8,128)(2,1)S(1)}, u32[]{:S(2)}, u32[]{:S(2)}) collective-permute-start(bf16[2,512,128]{2,1,0:T(8,128)(2,1)S(1)} %pad_maximum_fusion._.x0_ref), channel_id=1, source_target_pairs={{0,6},{1,7},{2,0},{3,1},{4,2},{5,3},{6,4},{7,5},{8,14},{9,15},{10,... | collective-permute-start | bytes 786440 | tf_op jit(solution)/shard_map/ppermute | solution.py:428
  35.1 2.1 %copy-start.2 = (bf16[12,4096]{1,0:T(8,128)(2,1)S(1)}, bf16[12,4096]{1,0:T(8,128)(2,1)}, u32[]{:S(2)}) copy-start(bf16[12,4096]{1,0:T(8,128)(2,1)} %filters_ref.5) | copy-start | bytes 294916
  37.2 2.1 %copy-start = (bf16[1024,12,128]{2,0,1:T(8,128)(2,1)S(1)}, bf16[1024,12,128]{2,0,1:T(8,128)(2,1)}, u32[]{:S(2)}) copy-start(bf16[1024,12,128]{2,0,1:T(8,128)(2,1)} %param.7) | copy-start | bytes 9437188
  44.5 6.4 %collective-permute-start.9 = (bf16[4,4,6,32,128]{4,3,2,1,0:T(8,128)(2,1)S(1)}, bf16[4,4,6,32,128]{4,3,2,1,0:T(8,128)(2,1)S(1)}, u32[]{:S(2)}, u32[]{:S(2)}) collective-permute-start(bf16[4,4,6,32,128]{4,3,2,1,0:T(8,128)(2,1)S(1)} %get-tuple-element.36._), channel_id=1, source_target_pairs={{0,8},{8,0},{16,24},{24,16},{32,40},{40,32},{48,56},{56,48},{64,72... | collective-permute-start | bytes 2359304 | tf_op jit(solution)/shard_map/ppermute | solution.py:415
  47.0 7.2 %collective-permute-start.10 = (bf16[2,4,6,32,128]{4,3,2,1,0:T(8,128)(2,1)S(1)}, bf16[2,4,6,32,128]{4,3,2,1,0:T(8,128)(2,1)S(1)}, u32[]{:S(2)}, u32[]{:S(2)}) collective-permute-start(bf16[2,4,6,32,128]{4,3,2,1,0:T(8,128)(2,1)S(1)} %get-tuple-element.38._), channel_id=1, source_target_pairs={{0,8},{8,0},{16,24},{24,16},{32,40},{40,32},{48,56},{56,48},{64,72... | collective-permute-start | bytes 1179656 | tf_op jit(solution)/shard_map/ppermute | solution.py:415
  47.1 9.4 %collective-permute-start.11 = (bf16[2,512,128]{2,1,0:T(8,128)(2,1)S(1)}, bf16[2,512,128]{2,1,0:T(8,128)(2,1)S(1)}, u32[]{:S(2)}, u32[]{:S(2)}) collective-permute-start(bf16[2,512,128]{2,1,0:T(8,128)(2,1)S(1)} %get-tuple-element.43), channel_id=1, source_target_pairs={{0,2},{1,3},{2,0},{3,1},{4,6},{5,7},{6,4},{7,5},{8,10},{9,11},{10,... | collective-permute-start | bytes 786440 | tf_op jit(solution)/shard_map/ppermute | solution.py:424
  48.3 9.4 %collective-permute-start.12 = (bf16[2,512,128]{2,1,0:T(8,128)(2,1)S(1)}, bf16[2,512,128]{2,1,0:T(8,128)(2,1)S(1)}, u32[]{:S(2)}, u32[]{:S(2)}) collective-permute-start(bf16[2,512,128]{2,1,0:T(8,128)(2,1)S(1)} %get-tuple-element.35._), channel_id=1, source_target_pairs={{0,6},{1,7},{2,4},{3,5},{4,2},{5,3},{6,0},{7,1},{8,14},{9,15},{10,... | collective-permute-start | bytes 786440 | tf_op jit(solution)/shard_map/ppermute | solution.py:424
  49.9 16.7 %collective-permute-start.15 = (bf16[2,4,6,32,128]{4,3,2,1,0:T(8,128)(2,1)S(1)}, bf16[2,4,6,32,128]{4,3,2,1,0:T(8,128)(2,1)S(1)}, u32[]{:S(2)}, u32[]{:S(2)}) collective-permute-start(bf16[2,4,6,32,128]{4,3,2,1,0:T(8,128)(2,1)S(1)} %get-tuple-element.51), channel_id=1, source_target_pairs={{0,8},{8,0},{16,24},{24,16},{32,40},{40,32},{48,56},{56,48},{64,72... | collective-permute-start | bytes 1179656 | tf_op jit(solution)/shard_map/ppermute | solution.py:415
  51.0 12.6 %collective-permute-start.14 = (bf16[2,4,6,32,128]{4,3,2,1,0:T(8,128)(2,1)S(1)}, bf16[2,4,6,32,128]{4,3,2,1,0:T(8,128)(2,1)S(1)}, u32[]{:S(2)}, u32[]{:S(2)}) collective-permute-start(bf16[2,4,6,32,128]{4,3,2,1,0:T(8,128)(2,1)S(1)} %get-tuple-element.40._), channel_id=1, source_target_pairs={{0,64},{8,72},{16,80},{24,88},{32,96},{40,104},{48,112},{56,120},{... | collective-permute-start | bytes 1179656 | tf_op jit(solution)/shard_map/ppermute | solution.py:418
  54.3 12.3 %collective-permute-start.16 = (bf16[2,4,6,32,128]{4,3,2,1,0:T(8,128)(2,1)S(1)}, bf16[2,4,6,32,128]{4,3,2,1,0:T(8,128)(2,1)S(1)}, u32[]{:S(2)}, u32[]{:S(2)}) collective-permute-start(bf16[2,4,6,32,128]{4,3,2,1,0:T(8,128)(2,1)S(1)} %add.20._), channel_id=1, source_target_pairs={{0,192},{8,200},{16,208},{24,216},{32,224},{40,232},{48,240},{56,2... | collective-permute-start | bytes 1179656 | tf_op jit(solution)/shard_map/ppermute | solution.py:418
  56.6 10.2 %collective-permute-start.17 = (bf16[1,512,128]{2,1,0:T(8,128)(2,1)S(1)}, bf16[1,512,128]{2,1,0:T(8,128)(2,1)S(1)}, u32[]{:S(2)}, u32[]{:S(2)}) collective-permute-start(bf16[1,512,128]{2,1,0:T(8,128)(2,1)S(1)} %get-tuple-element.44._), channel_id=1, source_target_pairs={{0,6},{1,7},{2,4},{3,5},{4,2},{5,3},{6,0},{7,1},{8,14},{9,15},{10,... | collective-permute-start | bytes 393224 | tf_op jit(solution)/shard_map/ppermute | solution.py:424
  57.8 23.1 %collective-permute-start.13 = (bf16[1,512,128]{2,1,0:T(8,128)(2,1)S(1)}, bf16[1,512,128]{2,1,0:T(8,128)(2,1)S(1)}, u32[]{:S(2)}, u32[]{:S(2)}) collective-permute-start(bf16[1,512,128]{2,1,0:T(8,128)(2,1)S(1)} %get-tuple-element.47._), channel_id=1, source_target_pairs={{0,2},{1,3},{2,0},{3,1},{4,6},{5,7},{6,4},{7,5},{8,10},{9,11},{10,... | collective-permute-start | bytes 393224 | tf_op jit(solution)/shard_map/ppermute | solution.py:424
  63.8 7.2 %collective-permute-start.19 = (bf16[1,4,6,32,128]{4,3,2,1,0:T(8,128)(2,1)S(1)}, bf16[1,4,6,32,128]{4,3,2,1,0:T(8,128)(2,1)S(1)}, u32[]{:S(2)}, u32[]{:S(2)}) collective-permute-start(bf16[1,4,6,32,128]{4,3,2,1,0:T(8,128)(2,1)S(1)} %get-tuple-element.49._), channel_id=1, source_target_pairs={{0,192},{8,200},{16,208},{24,216},{32,224},{40,232},{48,240},{56,2... | collective-permute-start | bytes 589832 | tf_op jit(solution)/shard_map/ppermute | solution.py:418
  66.7 5.4 %collective-permute-start.20 = (bf16[1,4,6,32,128]{4,3,2,1,0:T(8,128)(2,1)S(1)}, bf16[1,4,6,32,128]{4,3,2,1,0:T(8,128)(2,1)S(1)}, u32[]{:S(2)}, u32[]{:S(2)}) collective-permute-start(bf16[1,4,6,32,128]{4,3,2,1,0:T(8,128)(2,1)S(1)} %get-tuple-element.52._), channel_id=1, source_target_pairs={{0,64},{8,72},{16,80},{24,88},{32,96},{40,104},{48,112},{56,120},{... | collective-permute-start | bytes 589832 | tf_op jit(solution)/shard_map/ppermute | solution.py:418
  66.8 14.0 %collective-permute-start.18 = (bf16[1,512,128]{2,1,0:T(8,128)(2,1)S(1)}, bf16[1,512,128]{2,1,0:T(8,128)(2,1)S(1)}, u32[]{:S(2)}, u32[]{:S(2)}) collective-permute-start(bf16[1,512,128]{2,1,0:T(8,128)(2,1)S(1)} %add.21._), channel_id=1, source_target_pairs={{0,1},{1,0},{2,3},{3,2},{4,5},{5,4},{6,7},{7,6},{8,9},{9,8},{10,11... | collective-permute-start | bytes 393224 | tf_op jit(solution)/shard_map/ppermute | solution.py:463
  71.0 7.2 %collective-permute-start.21 = (bf16[2,6,32,128]{3,2,1,0:T(8,128)(2,1)S(1)}, bf16[2,6,32,128]{3,2,1,0:T(8,128)(2,1)S(1)}, u32[]{:S(2)}, u32[]{:S(2)}) collective-permute-start(bf16[2,6,32,128]{3,2,1,0:T(8,128)(2,1)S(1)} %get-tuple-element.55._), channel_id=1, source_target_pairs={{0,16},{8,24},{16,0},{24,8},{32,48},{40,56},{48,32},{56,40},{64,80... | collective-permute-start | bytes 294920 | tf_op jit(solution)/shard_map/ppermute | solution.py:421
  72.2 8.2 %collective-permute-start.23 = (bf16[2,6,32,128]{3,2,1,0:T(8,128)(2,1)S(1)}, bf16[2,6,32,128]{3,2,1,0:T(8,128)(2,1)S(1)}, u32[]{:S(2)}, u32[]{:S(2)}) collective-permute-start(bf16[2,6,32,128]{3,2,1,0:T(8,128)(2,1)S(1)} %get-tuple-element.57._), channel_id=1, source_target_pairs={{0,16},{8,24},{16,0},{24,8},{32,48},{40,56},{48,32},{56,40},{64,80... | collective-permute-start | bytes 294920 | tf_op jit(solution)/shard_map/ppermute | solution.py:421
  78.3 7.6 %collective-permute-start.22 = (bf16[1,6,32,128]{3,2,1,0:T(8,128)(2,1)S(1)}, bf16[1,6,32,128]{3,2,1,0:T(8,128)(2,1)S(1)}, u32[]{:S(2)}, u32[]{:S(2)}) collective-permute-start(bf16[1,6,32,128]{3,2,1,0:T(8,128)(2,1)S(1)} %get-tuple-element.60._), channel_id=1, source_target_pairs={{0,32},{8,40},{16,48},{24,56},{32,0},{40,8},{48,16},{56,24},{64,96... | collective-permute-start | bytes 147464 | tf_op jit(solution)/shard_map/ppermute | solution.py:421
  80.4 5.5 %collective-permute-start.24 = (bf16[1,6,32,128]{3,2,1,0:T(8,128)(2,1)S(1)}, bf16[1,6,32,128]{3,2,1,0:T(8,128)(2,1)S(1)}, u32[]{:S(2)}, u32[]{:S(2)}) collective-permute-start(bf16[1,6,32,128]{3,2,1,0:T(8,128)(2,1)S(1)} %get-tuple-element.63), channel_id=1, source_target_pairs={{0,32},{8,40},{16,48},{24,56},{32,0},{40,8},{48,16},{56,24},{64,96... | collective-permute-start | bytes 147464 | tf_op jit(solution)/shard_map/ppermute | solution.py:421
